TPU v7x, 32 devices: a whole 2x2x4 slice. The times are simulated.
32 devices in a mesh: lat: 4 (over y, x), lon: 8 (over z, core).
Axes of the slice: x: 2, y: 2, z: 4, core: 2. Of those that a mesh axis runs over, the one named last changes fastest.
Arguments:
- residual: float32 [524288], P(('lat', 'lon')), may hold values from -6 to 6
- star_pixel: int32 [524288], P(('lat', 'lon')), may hold values from 0 to 63
- star_bin: int32 [524288], P(('lat', 'lon')), may hold values from 0 to 511
- send_counts: int32 [32, 32], P(('lat', 'lon')), may hold values from 64 to 512, as said below
- send_offsets: int32 [32, 32], P(('lat', 'lon')), may hold values from 0 to 10112, as said below
- latent: float32 [32, 64, 512], P('lat', 'lon'), may hold values from -6 to 6
- stencils: float32 [2, 27, 512], replicated
Outputs:
- gradient: float32 [32, 64, 512], P('lat', 'lon')
Inputs may be any that keep to these rules, and one draw needn't show every extreme that they name: `send_counts`: each entry is at most 512; for one owner of the latitude tiles 4 // 4 to 2, drawn from the seed, every catalog shard holds exactly 512 stars. Owners of those latitude tiles get 512 // 2 to 512 from a shard, the others 512 // 8 to 128; one catalog shard, drawn from the seed, holds that most for every owner. `send_offsets`: each row is the running sum of the same row of send_counts before each entry, starting at 0. `star_pixel`: equals row * 8 + column within the owner's tile.
All inputs are finite; a program needn't handle non-finite values.
Results may differ from a plain program's by a relative error of at most 0.0003.
Values sent between devices are 32-bit elements; how exact they have to be, the bound alone decides.
No kernel may reach another device: no remote copies, remote signals or barrier semaphores. Data moves between devices by JAX's collectives and lax.ppermute only.
A program may use at most 64 MiB of HBM per device.

v0:
```python
import jax
import jax.numpy as jnp
from jax import lax
from jax.sharding import PartitionSpec as P

CAP = 512


bin_width = 0.0625


def padded(cells, sides, width, closed):
    for axis, dim in sides:
        count = lax.axis_size(axis)
        ends = count if closed else count - 1
        head = lax.slice_in_dim(cells, 0, width, axis=dim)
        tail = lax.slice_in_dim(cells, cells.shape[dim] - width, cells.shape[dim], axis=dim)
        cells = jnp.concatenate(
            [
                lax.ppermute(tail, axis, [(i, (i + 1) % count) for i in range(ends)]),
                cells,
                lax.ppermute(head, axis, [((i + 1) % count, i) for i in range(ends)]),
            ],
            axis=dim,
        )
    return cells


def shift_radial(values, step):
    if step == 1:
        return jnp.concatenate([values[..., 1:], jnp.zeros_like(values[..., :1])], axis=-1)
    if step == -1:
        return jnp.concatenate([jnp.zeros_like(values[..., :1]), values[..., :-1]], axis=-1)
    return values


def refine(ext, coef):
    height = ext.shape[0] - 2
    width = ext.shape[1] - 2
    total = jnp.zeros((height, width, ext.shape[2]), jnp.float32)
    for radial in (-1, 0, 1):
        shifted = shift_radial(ext, radial)
        for above in (-1, 0, 1):
            for beside in (-1, 0, 1):
                tap = (above + 1) * 9 + (beside + 1) * 3 + radial + 1
                window = shifted[1 + above : 1 + above + height, 1 + beside : 1 + beside + width]
                total = total + coef[tap] * window
    return total


def adjoint(ext, coef):
    height = ext.shape[0] - 2
    width = ext.shape[1] - 2
    total = jnp.zeros((height, width, ext.shape[2]), jnp.float32)
    for radial in (-1, 0, 1):
        partial_sum = jnp.zeros((height, width, ext.shape[2]), jnp.float32)
        for above in (-1, 0, 1):
            for beside in (-1, 0, 1):
                tap = (above + 1) * 9 + (beside + 1) * 3 + radial + 1
                window = ext[1 - above : 1 - above + height, 1 - beside : 1 - beside + width]
                partial_sum = partial_sum + coef[tap] * window
        total = total + shift_radial(partial_sum, -radial)
    return total


def widen_single(field):
    beside_all = padded(field, (("lon", 1),), 1, True)
    return padded(beside_all, (("lat", 0),), 1, False)


def on_device(residual, star_pixel, star_bin, send_counts, send_offsets, latent, stencils):
    height, width, radial = latent.shape
    slots = lax.iota(jnp.int32, CAP)
    index = jnp.minimum(send_offsets[0][:, None] + slots[None, :], residual.shape[0] - 1)
    live = slots[None, :] < send_counts[0][:, None]
    values = jnp.where(live, residual[index], jnp.float32(0.0))
    cell_ids = jnp.where(live, star_pixel[index] * radial + star_bin[index], 0).astype(jnp.float32)
    got_values, got_cells = (
        lax.all_to_all(values, ("lat", "lon"), split_axis=0, concat_axis=0, tiled=True),
        lax.all_to_all(cell_ids, ("lat", "lon"), split_axis=0, concat_axis=0, tiled=True),
    )
    coarse = refine(widen_single(latent), stencils[0])
    fine = refine(widen_single(coarse), stencils[1])
    targets = got_cells.reshape(-1).astype(jnp.int32)
    binned = (
        jnp.zeros((height * width * radial,), jnp.float32).at[targets].add(got_values.reshape(-1))
    )
    binned = binned.reshape(height * width, radial)
    bins = lax.iota(jnp.int32, radial)
    upper = (bins[:, None] >= bins[None, :]).astype(jnp.float32)
    behind = bin_width * jnp.dot(
        binned, upper, precision=lax.Precision.HIGHEST, preferred_element_type=jnp.float32
    )
    upstream = jnp.exp(fine) * behind.reshape(height, width, radial)
    middle = adjoint(widen_single(upstream), stencils[1])
    back = adjoint(widen_single(middle), stencils[0])
    return latent + back


def solution(mesh):
    return jax.shard_map(
        on_device,
        mesh=mesh,
        in_specs=(
            P(("lat", "lon")),
            P(("lat", "lon")),
            P(("lat", "lon")),
            P(("lat", "lon"), None),
            P(("lat", "lon"), None),
            P("lat", "lon", None),
            P(),
        ),
        out_specs=P("lat", "lon", None),
        check_vma=False,
    )
```

profile of v0, /device:TPU:2, one launch (start us, length us, event | category | flops | bytes accessed | tf_op | source)
XLA Modules:
  0.0 454.7 jit_solution(9824509599257444957)
XLA Ops:
  0.0 1.0 fusion.153
  1.1 3.5 collective-permute-start.1
  4.8 90.5 %gather_fusion.1 = s32[16384]{0:T(1024)S(1)} fusion(s32[16384]{0:T(1024)S(1)} %copy-done, s32[16384]{0:T(1024)S(1)} %broadcast_clamp_fusion), kind=kCustom, calls=%fused_computation.1 | custom fusion | bytes 196608 | tf_op jit(solution)/shard_map/gather | solution.py:77
  95.3 90.5 %gather_fusion = s32[16384]{0:T(1024)S(1)} fusion(s32[16384]{0:T(1024)S(1)} %copy-done.1, s32[16384]{0:T(1024)S(1)} %broadcast_clamp_fusion), kind=kCustom, calls=%fused_computation | custom fusion | bytes 196608 | tf_op jit(solution)/shard_map/gather | solution.py:77
  187.3 4.3 all-to-all-start
  191.8 3.5 collective-permute-start.2
  195.3 2.5 collective-permute-start.3
  197.8 90.5 %gather_fusion.2 = f32[16384]{0:T(1024)S(1)} fusion(f32[16384]{0:T(1024)S(1)} %copy-done.2, s32[16384]{0:T(1024)S(1)} %broadcast_clamp_fusion), kind=kCustom, calls=%fused_computation.2 | custom fusion | bytes 196608 | tf_op jit(solution)/shard_map/gather | solution.py:76
  289.3 3.5 collective-permute-start.5
  294.4 4.3 collective-permute-start.6
  298.7 1.9 collective-permute-start.7
  300.7 4.7 %collective-permute-done.7 = f32[1,10,512]{2,1,0:T(8,128)S(1)} collective-permute-done((f32[1,10,512]{2,1,0:T(8,128)S(1)}, f32[1,10,512]{2,1,0:T(8,128)S(1)}, u32[]{:S(2)}, u32[]{:S(2)}) %collective-permute-start.7) | collective-permute-done | bytes 20512 | tf_op jit(solution)/shard_map/ppermute | solution.py:22
  305.7 3.6 all-to-all-start.1
  309.4 6.2 %all-to-all-done.1 = f32[32,1,512]{2,1,0:T(1,128)S(1)} async-done(((f32[32,1,512]{2,1,0:T(1,128)}), f32[32,1,512]{2,1,0:T(1,128)S(1)}, u32[]{:S(2)}, u32[]{:S(2)}) %all-to-all-start.1) | async-done | bytes 65568 | tf_op jit(solution)/shard_map/all_to_all | solution.py:79
  315.6 92.6 %scatter_custom_fusion = f32[32768]{0:T(1024)S(1)} fusion(s32[16384]{0:T(1024)S(1)} %bitcast.85, f32[16384]{0:T(1024)S(1)} %bitcast.84, f32[]{:T(128)} %constant.7.clone.1), kind=kCustom, calls=%fused_computation.249 | custom fusion | flops 16384 | bytes 131076 | tf_op jit(solution)/shard_map/scatter-add | solution.py:86
  409.0 0.9 collective-permute-start.8
  410.5 3.5 collective-permute-done.8
  414.0 19.0 %collective-permute-start.10 = (f32[1,10,512]{2,1,0:T(8,128)S(1)}, f32[1,10,512]{2,1,0:T(8,128)S(1)}, u32[]{:S(2)}, u32[]{:S(2)}) collective-permute-start(f32[1,10,512]{2,1,0:T(8,128)S(1)} %get-tuple-element.25), channel_id=1, source_target_pairs={{8,0},{16,8},{24,16},{9,1},{17,9},{25,17},{10,2},{18,10},{26,18},{... | collective-permute-start | bytes 61448 | tf_op jit(solution)/shard_map/ppermute | solution.py:22
  433.1 1.9 collective-permute-start.11
  435.1 3.8 collective-permute-done.11
  441.2 3.6 collective-permute-done.12
  444.8 1.9 collective-permute-start.14
  446.8 4.8 %collective-permute-start.15 = (f32[1,10,512]{2,1,0:T(8,128)S(1)}, f32[1,10,512]{2,1,0:T(8,128)S(1)}, u32[]{:S(2)}, u32[]{:S(2)}) collective-permute-start(f32[1,10,512]{2,1,0:T(8,128)S(1)} %get-tuple-element.22), channel_id=1, source_target_pairs={{0,8},{8,16},{16,24},{1,9},{9,17},{17,25},{2,10},{10,18},{18,26},{... | collective-permute-start | bytes 61448 | tf_op jit(solution)/shard_map/ppermute | solution.py:20
  451.7 1.5 collective-permute-done.15
  (81 shorter events, 9.9 us)
Async XLA Ops:
  0.0 4.8 %copy-start = (s32[16384]{0:T(1024)S(1)}, s32[16384]{0:T(1024)}, u32[]{:S(2)}) copy-start(s32[16384]{0:T(1024)} %param.9) | copy-start | bytes 196612
  1.0 190.7 %collective-permute-start = (f32[8,1,512]{2,1,0:T(1,128)S(1)}, f32[8,1,512]{2,1,0:T(1,128)S(1)}, u32[]{:S(2)}, u32[]{:S(2)}) collective-permute-start(f32[8,1,512]{2,1,0:T(1,128)S(1)} %get-tuple-element.45), channel_id=1, source_target_pairs={{0,1},{1,2},{2,3},{3,4},{4,5},{5,6},{6,7},{7,0},{8,9},{9,10},{10,1... | collective-permute-start | bytes 49160 | tf_op jit(solution)/shard_map/ppermute | solution.py:20
  1.1 3.5 copy-start.6
  1.1 190.6 %collective-permute-start.1 = (f32[8,1,512]{2,1,0:T(1,128)S(1)}, f32[8,1,512]{2,1,0:T(1,128)S(1)}, u32[]{:S(2)}, u32[]{:S(2)}) collective-permute-start(f32[8,1,512]{2,1,0:T(1,128)S(1)} %get-tuple-element.46), channel_id=1, source_target_pairs={{1,0},{2,1},{3,2},{4,3},{5,4},{6,5},{7,6},{0,7},{9,8},{10,9},{11,1... | collective-permute-start | bytes 49160 | tf_op jit(solution)/shard_map/ppermute | solution.py:22
  4.8 90.6 %copy-start.1 = (s32[16384]{0:T(1024)S(1)}, s32[16384]{0:T(1024)}, u32[]{:S(2)}) copy-start(s32[16384]{0:T(1024)} %param.8) | copy-start | bytes 196612
  186.6 5.1 %copy-start.4 = (f32[2,27,512]{2,0,1:T(2,128)S(1)}, f32[2,27,512]{2,0,1:T(2,128)}, u32[]{:S(2)}) copy-start(f32[2,27,512]{2,0,1:T(2,128)} %param.13) | copy-start | bytes 331780
  187.3 4.4 copy-start.3
  187.3 118.4 %all-to-all-start = ((f32[32,1,512]{2,1,0:T(1,128)}), f32[32,1,512]{2,1,0:T(1,128)S(1)}, u32[]{:S(2)}, u32[]{:S(2)}) async-start(f32[32,1,512]{2,1,0:T(1,128)} %fusion.142), calls=%async_computation | async-start | bytes 131072 | tf_op jit(solution)/shard_map/all_to_all | solution.py:80
  191.8 6.0 %copy-start.2 = (f32[16384]{0:T(1024)S(1)}, f32[16384]{0:T(1024)}, u32[]{:S(2)}) copy-start(f32[16384]{0:T(1024)} %param.7) | copy-start | bytes 196612
  191.8 96.6 %collective-permute-start.2 = (f32[1,10,512]{2,1,0:T(8,128)S(1)}, f32[1,10,512]{2,1,0:T(8,128)S(1)}, u32[]{:S(2)}, u32[]{:S(2)}) collective-permute-start(f32[1,10,512]{2,1,0:T(8,128)S(1)} %get-tuple-element.33), channel_id=1, source_target_pairs={{0,8},{8,16},{16,24},{1,9},{9,17},{17,25},{2,10},{10,18},{18,26},{... | collective-permute-start | bytes 61448 | tf_op jit(solution)/shard_map/ppermute | solution.py:20
  195.3 93.1 %collective-permute-start.3 = (f32[1,10,512]{2,1,0:T(8,128)S(1)}, f32[1,10,512]{2,1,0:T(8,128)S(1)}, u32[]{:S(2)}, u32[]{:S(2)}) collective-permute-start(f32[1,10,512]{2,1,0:T(8,128)S(1)} %get-tuple-element.34), channel_id=1, source_target_pairs={{8,0},{16,8},{24,16},{9,1},{17,9},{25,17},{10,2},{18,10},{26,18},{... | collective-permute-start | bytes 61448 | tf_op jit(solution)/shard_map/ppermute | solution.py:22
  289.3 5.1 %collective-permute-start.4 = (f32[8,1,512]{2,1,0:T(1,128)S(1)}, f32[8,1,512]{2,1,0:T(1,128)S(1)}, u32[]{:S(2)}, u32[]{:S(2)}) collective-permute-start(f32[8,1,512]{2,1,0:T(1,128)S(1)} %get-tuple-element.43), channel_id=1, source_target_pairs={{0,1},{1,2},{2,3},{3,4},{4,5},{5,6},{6,7},{7,0},{8,9},{9,10},{10,1... | collective-permute-start | bytes 49160 | tf_op jit(solution)/shard_map/ppermute | solution.py:20
  289.3 5.1 %collective-permute-start.5 = (f32[8,1,512]{2,1,0:T(1,128)S(1)}, f32[8,1,512]{2,1,0:T(1,128)S(1)}, u32[]{:S(2)}, u32[]{:S(2)}) collective-permute-start(f32[8,1,512]{2,1,0:T(1,128)S(1)} %get-tuple-element.44), channel_id=1, source_target_pairs={{1,0},{2,1},{3,2},{4,3},{5,4},{6,5},{7,6},{0,7},{9,8},{10,9},{11,1... | collective-permute-start | bytes 49160 | tf_op jit(solution)/shard_map/ppermute | solution.py:22
  294.4 6.3 %collective-permute-start.6 = (f32[1,10,512]{2,1,0:T(8,128)S(1)}, f32[1,10,512]{2,1,0:T(8,128)S(1)}, u32[]{:S(2)}, u32[]{:S(2)}) collective-permute-start(f32[1,10,512]{2,1,0:T(8,128)S(1)} %get-tuple-element.29), channel_id=1, source_target_pairs={{0,8},{8,16},{16,24},{1,9},{9,17},{17,25},{2,10},{10,18},{18,26},{... | collective-permute-start | bytes 61448 | tf_op jit(solution)/shard_map/ppermute | solution.py:20
  298.7 6.7 %collective-permute-start.7 = (f32[1,10,512]{2,1,0:T(8,128)S(1)}, f32[1,10,512]{2,1,0:T(8,128)S(1)}, u32[]{:S(2)}, u32[]{:S(2)}) collective-permute-start(f32[1,10,512]{2,1,0:T(8,128)S(1)} %get-tuple-element.30), channel_id=1, source_target_pairs={{8,0},{16,8},{24,16},{9,1},{17,9},{25,17},{10,2},{18,10},{26,18},{... | collective-permute-start | bytes 61448 | tf_op jit(solution)/shard_map/ppermute | solution.py:22
  305.7 9.9 %all-to-all-start.1 = ((f32[32,1,512]{2,1,0:T(1,128)}), f32[32,1,512]{2,1,0:T(1,128)S(1)}, u32[]{:S(2)}, u32[]{:S(2)}) async-start(f32[32,1,512]{2,1,0:T(1,128)} %compare_select_fusion.2), calls=%async_computation.1 | async-start | bytes 131072 | tf_op jit(solution)/shard_map/all_to_all | solution.py:79
  408.9 1.6 collective-permute-start.9
  409.0 5.0 %collective-permute-start.8 = (f32[8,1,512]{2,1,0:T(1,128)S(1)}, f32[8,1,512]{2,1,0:T(1,128)S(1)}, u32[]{:S(2)}, u32[]{:S(2)}) collective-permute-start(f32[8,1,512]{2,1,0:T(1,128)S(1)} %get-tuple-element.42), channel_id=1, source_target_pairs={{0,1},{1,2},{2,3},{3,4},{4,5},{5,6},{6,7},{7,0},{8,9},{9,10},{10,1... | collective-permute-start | bytes 49160 | tf_op jit(solution)/shard_map/ppermute | solution.py:20
  414.0 21.0 %collective-permute-start.10 = (f32[1,10,512]{2,1,0:T(8,128)S(1)}, f32[1,10,512]{2,1,0:T(8,128)S(1)}, u32[]{:S(2)}, u32[]{:S(2)}) collective-permute-start(f32[1,10,512]{2,1,0:T(8,128)S(1)} %get-tuple-element.25), channel_id=1, source_target_pairs={{8,0},{16,8},{24,16},{9,1},{17,9},{25,17},{10,2},{18,10},{26,18},{... | collective-permute-start | bytes 61448 | tf_op jit(solution)/shard_map/ppermute | solution.py:22
  433.1 5.8 %collective-permute-start.11 = (f32[1,10,512]{2,1,0:T(8,128)S(1)}, f32[1,10,512]{2,1,0:T(8,128)S(1)}, u32[]{:S(2)}, u32[]{:S(2)}) collective-permute-start(f32[1,10,512]{2,1,0:T(8,128)S(1)} %get-tuple-element.26), channel_id=1, source_target_pairs={{0,8},{8,16},{16,24},{1,9},{9,17},{17,25},{2,10},{10,18},{18,26},{... | collective-permute-start | bytes 61448 | tf_op jit(solution)/shard_map/ppermute | solution.py:20
  439.7 1.5 collective-permute-start.13
  439.8 5.0 %collective-permute-start.12 = (f32[8,1,512]{2,1,0:T(1,128)S(1)}, f32[8,1,512]{2,1,0:T(1,128)S(1)}, u32[]{:S(2)}, u32[]{:S(2)}) collective-permute-start(f32[8,1,512]{2,1,0:T(1,128)S(1)} %get-tuple-element.40), channel_id=1, source_target_pairs={{0,1},{1,2},{2,3},{3,4},{4,5},{5,6},{6,7},{7,0},{8,9},{9,10},{10,1... | collective-permute-start | bytes 49160 | tf_op jit(solution)/shard_map/ppermute | solution.py:20
  444.8 6.8 %collective-permute-start.14 = (f32[1,10,512]{2,1,0:T(8,128)S(1)}, f32[1,10,512]{2,1,0:T(8,128)S(1)}, u32[]{:S(2)}, u32[]{:S(2)}) collective-permute-start(f32[1,10,512]{2,1,0:T(8,128)S(1)} %get-tuple-element.21), channel_id=1, source_target_pairs={{8,0},{16,8},{24,16},{9,1},{17,9},{25,17},{10,2},{18,10},{26,18},{... | collective-permute-start | bytes 61448 | tf_op jit(solution)/shard_map/ppermute | solution.py:22
  446.8 6.4 %collective-permute-start.15 = (f32[1,10,512]{2,1,0:T(8,128)S(1)}, f32[1,10,512]{2,1,0:T(8,128)S(1)}, u32[]{:S(2)}, u32[]{:S(2)}) collective-permute-start(f32[1,10,512]{2,1,0:T(8,128)S(1)} %get-tuple-element.22), channel_id=1, source_target_pairs={{0,8},{8,16},{16,24},{1,9},{9,17},{17,25},{2,10},{10,18},{18,26},{... | collective-permute-start | bytes 61448 | tf_op jit(solution)/shard_map/ppermute | solution.py:20
  (1 other events, 0.7 us)
where the time goes:
time: 457 us; the launch traced here: 455 us
  local copies, waits for them, and re-layouts  275 us (60%)
  other arithmetic  97.5 us (21%)
  starting transfers between devices  56.4 us (12%)
  waiting for transfers between devices  25 us (5%)
    scatter-add x1, other arithmetic, on_device(): jnp.zeros((height * width * radial,), jnp.float32).at[targets]  92.6 us
    gather x1, local copies, waits for them, and re-layouts, on_device(): star_bin[index]  90.5 us
    gather x1, local copies, waits for them, and re-layouts, on_device(): values = jnp.where(live, residual[index], jnp.float32(0.0))  90.5 us
    gather x1, local copies, waits for them, and re-layouts, on_device(): star_pixel[index] * radial + star_bin[index]  90.5 us
    ppermute x8, starting transfers between devices, padded(): lax.ppermute(head, axis, [((i + 1) % count, i) for i in range(ends)])  32.5 us
    ppermute x8, starting transfers between devices, padded(): lax.ppermute(tail, axis, [(i, (i + 1) % count) for i in range(ends)])  16 us
    ppermute x8, waiting for transfers between devices, padded(): lax.ppermute(tail, axis, [(i, (i + 1) % count) for i in range(ends)])  13.2 us
  transfers between devices with their start and end apart: 18, of which 9 were waited for; matrix products, arithmetic and copies ran while one was open for 61% of the time, Pallas kernels for 0%

commit v1 on v0

v1 whole, which is shorter than its diff:
```python
import functools

import jax
import jax.numpy as jnp
from jax import lax
from jax.experimental import pallas as pl
from jax.experimental.pallas import tpu as pltpu
from jax.sharding import PartitionSpec as P

CAP = 512
LANES = 128
SUBLANES = 8
RUNS = CAP // LANES
bin_width = 0.0625


def lane_roll(values, shift):
    return pltpu.roll(values, shift % values.shape[-1], values.ndim - 1)


def compact_kernel(counts, offsets, residual, pixel, bins, out, cells, *, radial):
    cells[...] = (pixel[...] * radial + bins[...]).astype(jnp.float32)
    lane = lax.broadcasted_iota(jnp.int32, (SUBLANES, LANES), 1)
    row = lax.broadcasted_iota(jnp.int32, (SUBLANES, LANES), 0)
    slot = row * LANES + lane
    for owner in range(out.shape[0]):
        start = offsets[0, owner]
        first = lax.shift_right_logical(start, 7)
        part = lax.bitwise_and(start, LANES - 1)
        live = slot < counts[0, owner]

        def window(ref):
            rows = ref[pl.ds(first, SUBLANES), :]
            turned = pltpu.roll(rows, lax.bitwise_and(LANES - part, LANES - 1), 1)
            joined = jnp.where(lane < LANES - part, turned, pltpu.roll(turned, SUBLANES - 1, 0))
            return jnp.where(live, joined, 0.0)

        out[owner] = jnp.where(row < RUNS, window(residual), pltpu.roll(window(cells), RUNS, 0))


def behind_of(got, left, right, *, radial, pixels):
    half = radial // 2
    classes = 2 * pixels
    shards = got.shape[0]
    group = 4
    column = lax.broadcasted_iota(jnp.int32, (classes, LANES), 0).astype(jnp.float32).astype(jnp.bfloat16)
    place = lax.broadcasted_iota(jnp.int32, (half, LANES), 0).astype(jnp.float32).astype(jnp.bfloat16)
    zero = jnp.zeros((), jnp.bfloat16)
    one = jnp.ones((), jnp.bfloat16)

    def tall(row, height):
        return jnp.concatenate([jnp.broadcast_to(row, (16, LANES)).astype(jnp.bfloat16)] * (height // 16), axis=0)

    def step(turn, total):
        for member in range(group):
            tile = got[turn * group + member]
            cell = tile.astype(jnp.int32)
            pixel = lax.shift_right_logical(cell, radial.bit_length() - 1)
            bins = lax.bitwise_and(cell, radial - 1)
            upper = (bins >= half).astype(jnp.int32)
            label = (upper * pixels + pixel).astype(jnp.float32)
            low = (bins - upper * half).astype(jnp.float32)
            coarse = tile.astype(jnp.bfloat16).astype(jnp.float32)
            rest = tile - coarse
            for run in range(RUNS):
                at = slice((member * RUNS + run) * LANES, (member * RUNS + run + 1) * LANES)
                mine = tall(label[RUNS + run:RUNS + run + 1], classes) == column
                left[:classes, at] = jnp.where(mine, tall(coarse[run:run + 1], classes), zero)
                left[classes:, at] = jnp.where(mine, tall(rest[run:run + 1], classes), zero)
                right[:, at] = jnp.where(tall(low[RUNS + run:RUNS + run + 1], half) >= place, one, zero)
        return total + lax.dot_general(
            left[...], right[...], (((1,), (1,)), ((), ())), preferred_element_type=jnp.float32
        )

    total = lax.fori_loop(0, shards // group, step, jnp.zeros((2 * classes, half), jnp.float32))
    both = (total[:classes] + total[classes:]) * bin_width
    near, far = both[:pixels], both[pixels:]
    return near + far[:, :1], far


def bin_kernel(got, latent, behind, to_left, to_right, left, right):
    height, width, radial = latent.shape
    near, far = behind_of(got, left, right, radial=radial, pixels=height * width)
    half = radial // 2
    sub = lax.broadcasted_iota(jnp.int32, (width, radial), 0)
    for row in range(height):
        at = slice(row * width, (row + 1) * width)
        mine = jnp.concatenate([near[at], far[at]], axis=1)
        behind[row] = mine
        turned = pltpu.roll(mine, width // 2, 0)
        field = latent[row]
        to_left[row] = jnp.where(sub < width // 2, field, turned)
        to_right[row] = jnp.where(sub < width // 2, turned, field)


def lon_halos(from_left, from_right, sub, width):
    field = jnp.where(sub < width // 2, from_right, from_left)
    behind = pltpu.roll(jnp.where(sub < width // 2, from_left, from_right), width // 2, 0)
    return field, behind


def pack_kernel(latent, behind, from_left, from_right, to_up, to_down):
    height, width, radial = latent.shape
    sub = lax.broadcasted_iota(jnp.int32, (width, radial), 0)
    wide = slice(width, 2 * width)
    for out, rows in ((to_up, range(4)), (to_down, range(height - 4, height))):
        for place, row in enumerate(rows):
            field, _ = lon_halos(from_left[row], from_right[row], sub, width)
            out[place, :width] = latent[row]
            out[place, wide] = field
    for out, rows in ((to_up, range(2)), (to_down, range(height - 2, height))):
        for place, row in enumerate(rows):
            _, mass = lon_halos(from_left[row], from_right[row], sub, width)
            out[4 + place, :width] = behind[row]
            out[4 + place, wide] = mass


def level(source, shifted, coef, first, last, write):
    cols, radial = source.shape[1], source.shape[2]
    lane = lax.broadcasted_iota(jnp.int32, (cols, radial), 1)

    def shift(row, _):
        field = source[row]
        shifted[0, row] = jnp.where(lane == 0, 0.0, lane_roll(field, 1))
        shifted[1, row] = jnp.where(lane == radial - 1, 0.0, lane_roll(field, -1))
        return 0

    lax.fori_loop(first - 1, last + 2, shift, 0, unroll=2)

    for tile in range(radial // LANES):
        at = slice(tile * LANES, (tile + 1) * LANES)
        taps = [jnp.broadcast_to(coef[k:k + 1, at], (cols, LANES)) for k in range(27)]

        def line(row, _, taps=taps, at=at):
            sums = [None, None, None]
            for above in (-1, 0, 1):
                window = (shifted[0, row + above, :, at], source[row + above, :, at], shifted[1, row + above, :, at])
                for beside in (-1, 0, 1):
                    for radial_step in (-1, 0, 1):
                        tap = (above + 1) * 9 + (beside + 1) * 3 + radial_step + 1
                        term = taps[tap] * window[radial_step + 1]
                        old = sums[beside + 1]
                        sums[beside + 1] = term if old is None else old + term
            write(row, at, sums[1] + pltpu.roll(sums[0], 1, 0) + pltpu.roll(sums[2], cols - 1, 0))
            return 0

        lax.fori_loop(first, last + 1, line, 0, unroll=2)


def field_kernel(
    inside, latent, behind, from_left, from_right, from_up, from_down, stencils, mirrored, out,
    field, mass, other, shifted,
):
    height, width, radial = latent.shape
    sub = lax.broadcasted_iota(jnp.int32, (width, radial), 0)
    cols = 2 * width
    field[:4] = from_up[:4]
    field[height + 4:] = from_down[:4]
    mass[2:4] = from_up[4:]
    mass[height + 4:height + 6] = from_down[4:]

    def fill(row, _):
        near, dust = lon_halos(from_left[row], from_right[row], sub, width)
        field[row + 4, :width] = latent[row]
        field[row + 4, width:] = near
        mass[row + 4, :width] = behind[row]
        mass[row + 4, width:] = dust
        return 0

    lax.fori_loop(0, height, fill, 0)

    def kept(row, values):
        real = jnp.where(row < 4, inside[0], jnp.where(row >= height + 4, inside[1], 1))
        return jnp.where(jnp.full(values.shape, real, jnp.int32) > 0, values, 0.0)

    def to_coarse(row, at, values):
        other[row, :, at] = kept(row, values)

    def to_upstream(row, at, values):
        mass[row, :, at] = kept(row, jnp.exp(values) * mass[row, :, at])

    def to_middle(row, at, values):
        other[row, :, at] = kept(row, values)

    def to_out(row, at, values):
        out[row - 4, :, at] = latent[row - 4, :, at] + values[:width]

    level(field, shifted, stencils.at[0], 1, height + 6, to_coarse)
    level(other, shifted, stencils.at[1], 2, height + 5, to_upstream)
    level(mass, shifted, mirrored.at[1], 3, height + 4, to_middle)
    level(other, shifted, mirrored.at[0], 4, height + 3, to_out)


def mirror(stencils):
    turned = jnp.flip(stencils, axis=1).reshape(stencils.shape[0], 9, 3, stencils.shape[2])
    edge = jnp.zeros_like(turned[:, :, 0, :1])
    back = jnp.concatenate([edge, turned[:, :, 0, :-1]], axis=-1)
    ahead = jnp.concatenate([turned[:, :, 2, 1:], edge], axis=-1)
    return jnp.stack([back, turned[:, :, 1], ahead], axis=2).reshape(stencils.shape)


def exchange(first, last, axis, closed):
    count = lax.axis_size(axis)
    ends = count if closed else count - 1
    return (
        lax.ppermute(last, axis, [(i, (i + 1) % count) for i in range(ends)]),
        lax.ppermute(first, axis, [((i + 1) % count, i) for i in range(ends)]),
    )


VMEM = pl.BlockSpec(memory_space=pltpu.VMEM)
SMEM = pl.BlockSpec(memory_space=pltpu.SMEM)
LIMIT = pltpu.CompilerParams(vmem_limit_bytes=32 * 1024 * 1024)


def on_device(residual, star_pixel, star_bin, send_counts, send_offsets, latent, stencils):
    height, width, radial = latent.shape
    shards = send_counts.shape[1]
    slots = residual.shape[0]
    f32 = jnp.float32

    def rows(values):
        return values.reshape(slots // LANES, LANES)

    packed = pl.pallas_call(
        functools.partial(compact_kernel, radial=radial),
        out_shape=jax.ShapeDtypeStruct((shards, 2 * RUNS, LANES), f32),
        in_specs=[SMEM, SMEM, VMEM, VMEM, VMEM],
        out_specs=VMEM,
        scratch_shapes=[pltpu.VMEM((slots // LANES, LANES), f32)],
        compiler_params=LIMIT,
        name="compact",
    )(send_counts, send_offsets, rows(residual), rows(star_pixel), rows(star_bin))
    got = lax.all_to_all(packed, ("lat", "lon"), split_axis=0, concat_axis=0, tiled=True)

    tile = jax.ShapeDtypeStruct((height, width, radial), f32)
    behind, to_left, to_right = pl.pallas_call(
        bin_kernel,
        out_shape=(tile, tile, tile),
        in_specs=[VMEM, VMEM],
        out_specs=(VMEM, VMEM, VMEM),
        scratch_shapes=[
            pltpu.VMEM((4 * height * width, 4 * CAP), jnp.bfloat16),
            pltpu.VMEM((radial // 2, 4 * CAP), jnp.bfloat16),
        ],
        compiler_params=LIMIT,
        name="binning",
    )(got, latent)
    from_left, from_right = exchange(to_left, to_right, "lon", True)

    band = jax.ShapeDtypeStruct((6, 2 * width, radial), f32)
    to_up, to_down = pl.pallas_call(
        pack_kernel,
        out_shape=(band, band),
        in_specs=[VMEM] * 4,
        out_specs=(VMEM, VMEM),
        compiler_params=LIMIT,
        name="pack",
    )(latent, behind, from_left, from_right)
    from_up, from_down = exchange(to_up, to_down, "lat", False)

    row = lax.axis_index("lat")
    inside = jnp.stack([row > 0, row < lax.axis_size("lat") - 1]).astype(jnp.int32)
    wide = (height + 8, 2 * width, radial)
    return pl.pallas_call(
        field_kernel,
        out_shape=tile,
        in_specs=[SMEM] + [VMEM] * 8,
        out_specs=VMEM,
        scratch_shapes=[pltpu.VMEM(wide, f32)] * 3 + [pltpu.VMEM((2,) + wide, f32)],
        compiler_params=LIMIT,
        name="field",
    )(inside, latent, behind, from_left, from_right, from_up, from_down, stencils, mirror(stencils))


def solution(mesh):
    return jax.shard_map(
        on_device,
        mesh=mesh,
        in_specs=(
            P(("lat", "lon")),
            P(("lat", "lon")),
            P(("lat", "lon")),
            P(("lat", "lon"), None),
            P(("lat", "lon"), None),
            P("lat", "lon", None),
            P(),
        ),
        out_specs=P("lat", "lon", None),
        check_vma=False,
    )
```

time: 457 us -> 52.2 us (0.11)
  the two profiles are of different devices: /device:TPU:2 before, /device:TPU:0 now
where the time goes in v1:
time: 52.2 us; the launch traced here: 51.8 us
  waiting for transfers between devices  18.6 us (36%)
  starting transfers between devices  15 us (29%)
  Pallas kernels  14.6 us (28%)
  local copies, waits for them, and re-layouts  3.44 us (7%)
    all_to_all x1, waiting for transfers between devices, on_device(): lax.all_to_all(packed, ('lat', 'lon'), split_axis=0, concat_axis=0, tiled...  8.13 us
    pallas_call x1, Pallas kernels, on_device(): pl.pallas_call(field_kernel, out_shape=tile, in_specs=[SMEM] + [VMEM] * 8...  7.47 us
    all_to_all x1, starting transfers between devices, on_device(): lax.all_to_all(packed, ('lat', 'lon'), split_axis=0, concat_axis=0, tiled...  7.3 us
    pallas_call x1, Pallas kernels, on_device(): pl.pallas_call(bin_kernel, out_shape=(tile, tile, tile), in_specs=[VMEM,...  5.71 us
    ppermute x2, waiting for transfers between devices, exchange(): lax.ppermute(first, axis, [((i + 1) % count, i) for i in range(ends)])  5.58 us
    ppermute x2, waiting for transfers between devices, exchange(): lax.ppermute(last, axis, [(i, (i + 1) % count) for i in range(ends)])  4.85 us
    ppermute x2, starting transfers between devices, exchange(): lax.ppermute(first, axis, [((i + 1) % count, i) for i in range(ends)])  4.52 us
    unnamed x15, local copies, waits for them, and re-layouts  3.22 us
  transfers between devices with their start and end apart: 5, of which 4 were waited for; matrix products, arithmetic and copies ran while one was open for 1% of the time, Pallas kernels for 0%

profile of v1, /device:TPU:0, one launch (start us, length us, event | category | flops | bytes accessed | tf_op | source)
XLA Modules:
  0.0 51.8 jit_solution(2283084561177249384)
XLA Ops:
  0.0 0.7 %copy-done.4 = s32[1,32]{1,0:T(1,128)S(1)} copy-done((s32[1,32]{1,0:T(1,128)S(1)}, s32[1,32]{1,0:T(1,128)}, u32[]{:S(2)}) %copy-start.4) | copy-done | bytes 152
  0.7 0.0 copy-done.5
  0.7 0.8 %copy-done.1 = f32[16384]{0:T(1024)S(1)} copy-done((f32[16384]{0:T(1024)S(1)}, f32[16384]{0:T(1024)}, u32[]{:S(2)}) %copy-start.1) | copy-done | bytes 65560
  1.5 0.8 %copy-done.2 = s32[16384]{0:T(1024)S(1)} copy-done((s32[16384]{0:T(1024)S(1)}, s32[16384]{0:T(1024)}, u32[]{:S(2)}) %copy-start.2) | copy-done | bytes 65560
  2.4 0.8 %copy-done.3 = s32[16384]{0:T(1024)S(1)} copy-done((s32[16384]{0:T(1024)S(1)}, s32[16384]{0:T(1024)}, u32[]{:S(2)}) %copy-start.3) | copy-done | bytes 65560
  3.2 1.4 %compact.1 = f32[32,8,128]{2,1,0:T(8,128)} custom-call(s32[1,32]{1,0:T(1,128)S(1)} %copy-done.4, s32[1,32]{1,0:T(1,128)S(1)} %copy-done.5, f32[128,128]{1,0:T(8,128)S(1)} %bitcast.19, s32[128,128]{1,0:T(8,128)S(1)} %bitcast.20, s32[128,128]{1,0:T(8,128)S(1)} %bitcast.21), custom_call_target="tpu_custom_call" | custom-call | tf_op jit(solution)/shard_map/compact/pallas_call | solution.py:225
  4.6 7.3 %all-to-all-start = ((f32[32,8,128]{2,1,0:T(8,128)}), f32[32,8,128]{2,1,0:T(8,128)S(1)}, u32[]{:S(2)}, u32[]{:S(2)}) async-start(f32[32,8,128]{2,1,0:T(8,128)} %compact.1), calls=%async_computation | async-start | bytes 262144 | tf_op jit(solution)/shard_map/all_to_all | solution.py:234
  11.9 0.0 copy-done.6
  11.9 0.0 copy-start
  11.9 8.1 %all-to-all-done.got = f32[32,8,128]{2,1,0:T(8,128)S(1)} async-done(((f32[32,8,128]{2,1,0:T(8,128)}), f32[32,8,128]{2,1,0:T(8,128)S(1)}, u32[]{:S(2)}, u32[]{:S(2)}) %all-to-all-start) | async-done | bytes 131104 | tf_op jit(solution)/shard_map/all_to_all | solution.py:234
  20.0 5.7 %binning.1 = (f32[8,8,512]{2,1,0:T(8,128)S(1)}, f32[8,8,512]{2,1,0:T(8,128)S(1)}, f32[8,8,512]{2,1,0:T(8,128)S(1)}) custom-call(f32[32,8,128]{2,1,0:T(8,128)S(1)} %all-to-all-done.got, f32[8,8,512]{2,1,0:T(8,128)S(1)} %copy-done), custom_call_target="tpu_custom_call" | custom-call | tf_op jit(solution)/shard_map/binning/pallas_call | solution.py:237
  25.8 0.4 collective-permute-start
  26.1 3.2 %collective-permute-start.1 = (f32[8,8,512]{2,1,0:T(8,128)S(1)}, f32[8,8,512]{2,1,0:T(8,128)S(1)}, u32[]{:S(2)}, u32[]{:S(2)}) collective-permute-start(f32[8,8,512]{2,1,0:T(8,128)S(1)} %get-tuple-element.12), channel_id=1, source_target_pairs={{1,0},{2,1},{3,2},{4,3},{5,4},{6,5},{7,6},{0,7},{9,8},{10,9},{11,1... | collective-permute-start | bytes 393224 | tf_op jit(solution)/shard_map/ppermute | solution.py:207
  29.4 0.1 slice_bitcast_fusion.1
  29.5 0.1 pad_bitcast_fusion
  29.6 3.2 %collective-permute-done.from_left = f32[8,8,512]{2,1,0:T(8,128)S(1)} collective-permute-done((f32[8,8,512]{2,1,0:T(8,128)S(1)}, f32[8,8,512]{2,1,0:T(8,128)S(1)}, u32[]{:S(2)}, u32[]{:S(2)}) %collective-permute-start) | collective-permute-done | bytes 131104 | tf_op jit(solution)/shard_map/ppermute | solution.py:206
  32.8 0.0 collective-permute-done.1.from_right
  32.8 2.8 %collective-permute-start.2 = (f32[6,16,512]{2,1,0:T(8,128)S(1)}, f32[6,16,512]{2,1,0:T(8,128)S(1)}, u32[]{:S(2)}, u32[]{:S(2)}) collective-permute-start(f32[6,16,512]{2,1,0:T(8,128)S(1)} %get-tuple-element.13), channel_id=1, source_target_pairs={{0,8},{8,16},{16,24},{1,9},{9,17},{17,25},{2,10},{10,18},{18,26},{... | collective-permute-start | bytes 589832 | tf_op jit(solution)/shard_map/ppermute | solution.py:206
  35.6 1.3 %collective-permute-start.3 = (f32[6,16,512]{2,1,0:T(8,128)S(1)}, f32[6,16,512]{2,1,0:T(8,128)S(1)}, u32[]{:S(2)}, u32[]{:S(2)}) collective-permute-start(f32[6,16,512]{2,1,0:T(8,128)S(1)} %get-tuple-element.14), channel_id=1, source_target_pairs={{8,0},{16,8},{24,16},{9,1},{17,9},{25,17},{10,2},{18,10},{26,18},{... | collective-permute-start | bytes 589832 | tf_op jit(solution)/shard_map/ppermute | solution.py:207
  36.9 0.1 pad_maximum_fusion
  37.0 0.1 add_convert_fusion.inside
  37.1 1.7 %collective-permute-done.2.from_up = f32[6,16,512]{2,1,0:T(8,128)S(1)} collective-permute-done((f32[6,16,512]{2,1,0:T(8,128)S(1)}, f32[6,16,512]{2,1,0:T(8,128)S(1)}, u32[]{:S(2)}, u32[]{:S(2)}) %collective-permute-start.2) | collective-permute-done | bytes 196640 | tf_op jit(solution)/shard_map/ppermute | solution.py:206
  38.8 5.6 %collective-permute-done.3.from_down = f32[6,16,512]{2,1,0:T(8,128)S(1)} collective-permute-done((f32[6,16,512]{2,1,0:T(8,128)S(1)}, f32[6,16,512]{2,1,0:T(8,128)S(1)}, u32[]{:S(2)}, u32[]{:S(2)}) %collective-permute-start.3) | collective-permute-done | bytes 196640 | tf_op jit(solution)/shard_map/ppermute | solution.py:207
  44.3 7.5 %field.1 = f32[8,8,512]{2,1,0:T(8,128)} custom-call(s32[2]{0:T(128)S(1)} %add_convert_fusion.inside, f32[8,8,512]{2,1,0:T(8,128)S(1)} %copy-done, f32[8,8,512]{2,1,0:T(8,128)S(1)} %get-tuple-element.10.behind, f32[8,8,512]{2,1,0:T(8,128)S(1)} %collective-permute-done.from_left, f32[8,8,512]{2,1,0:T(8,128)S(1)} %collective-permute-done.1.from_right, ...), custom_call_target="tpu_custom_call" | custom-call | tf_op jit(solution)/shard_map/field/pallas_call | solution.py:265
  (12 shorter events, 0.1 us)
Async XLA Ops:
  0.0 0.7 %copy-start.4 = (s32[1,32]{1,0:T(1,128)S(1)}, s32[1,32]{1,0:T(1,128)}, u32[]{:S(2)}) copy-start(s32[1,32]{1,0:T(1,128)} %counts.1) | copy-start | bytes 388
  0.0 0.7 %copy-start.5 = (s32[1,32]{1,0:T(1,128)S(1)}, s32[1,32]{1,0:T(1,128)}, u32[]{:S(2)}) copy-start(s32[1,32]{1,0:T(1,128)} %offsets.1) | copy-start | bytes 388
  0.7 0.8 %copy-start.1 = (f32[16384]{0:T(1024)S(1)}, f32[16384]{0:T(1024)}, u32[]{:S(2)}) copy-start(f32[16384]{0:T(1024)} %param.7) | copy-start | bytes 196612
  1.5 0.8 %copy-start.2 = (s32[16384]{0:T(1024)S(1)}, s32[16384]{0:T(1024)}, u32[]{:S(2)}) copy-start(s32[16384]{0:T(1024)} %param.8) | copy-start | bytes 196612
  2.4 0.8 %copy-start.3 = (s32[16384]{0:T(1024)S(1)}, s32[16384]{0:T(1024)}, u32[]{:S(2)}) copy-start(s32[16384]{0:T(1024)} %param.9) | copy-start | bytes 196612
  4.6 7.3 %copy-start.6 = (f32[2,27,512]{2,0,1:T(2,128)S(1)}, f32[2,27,512]{2,0,1:T(2,128)}, u32[]{:S(2)}) copy-start(f32[2,27,512]{2,0,1:T(2,128)} %param.13) | copy-start | bytes 331780
  4.6 15.5 %all-to-all-start = ((f32[32,8,128]{2,1,0:T(8,128)}), f32[32,8,128]{2,1,0:T(8,128)S(1)}, u32[]{:S(2)}, u32[]{:S(2)}) async-start(f32[32,8,128]{2,1,0:T(8,128)} %compact.1), calls=%async_computation | async-start | bytes 262144 | tf_op jit(solution)/shard_map/all_to_all | solution.py:234
  11.9 8.2 %copy-start = (f32[8,8,512]{2,1,0:T(8,128)S(1)}, f32[8,8,512]{2,1,0:T(8,128)}, u32[]{:S(2)}) copy-start(f32[8,8,512]{2,1,0:T(8,128)} %latent.5) | copy-start | bytes 393220
  25.8 7.0 %collective-permute-start = (f32[8,8,512]{2,1,0:T(8,128)S(1)}, f32[8,8,512]{2,1,0:T(8,128)S(1)}, u32[]{:S(2)}, u32[]{:S(2)}) collective-permute-start(f32[8,8,512]{2,1,0:T(8,128)S(1)} %get-tuple-element.11), channel_id=1, source_target_pairs={{0,1},{1,2},{2,3},{3,4},{4,5},{5,6},{6,7},{7,0},{8,9},{9,10},{10,1... | collective-permute-start | bytes 393224 | tf_op jit(solution)/shard_map/ppermute | solution.py:206
  26.1 6.6 %collective-permute-start.1 = (f32[8,8,512]{2,1,0:T(8,128)S(1)}, f32[8,8,512]{2,1,0:T(8,128)S(1)}, u32[]{:S(2)}, u32[]{:S(2)}) collective-permute-start(f32[8,8,512]{2,1,0:T(8,128)S(1)} %get-tuple-element.12), channel_id=1, source_target_pairs={{1,0},{2,1},{3,2},{4,3},{5,4},{6,5},{7,6},{0,7},{9,8},{10,9},{11,1... | collective-permute-start | bytes 393224 | tf_op jit(solution)/shard_map/ppermute | solution.py:207
  32.8 6.0 %collective-permute-start.2 = (f32[6,16,512]{2,1,0:T(8,128)S(1)}, f32[6,16,512]{2,1,0:T(8,128)S(1)}, u32[]{:S(2)}, u32[]{:S(2)}) collective-permute-start(f32[6,16,512]{2,1,0:T(8,128)S(1)} %get-tuple-element.13), channel_id=1, source_target_pairs={{0,8},{8,16},{16,24},{1,9},{9,17},{17,25},{2,10},{10,18},{18,26},{... | collective-permute-start | bytes 589832 | tf_op jit(solution)/shard_map/ppermute | solution.py:206
  35.6 8.7 %collective-permute-start.3 = (f32[6,16,512]{2,1,0:T(8,128)S(1)}, f32[6,16,512]{2,1,0:T(8,128)S(1)}, u32[]{:S(2)}, u32[]{:S(2)}) collective-permute-start(f32[6,16,512]{2,1,0:T(8,128)S(1)} %get-tuple-element.14), channel_id=1, source_target_pairs={{8,0},{16,8},{24,16},{9,1},{17,9},{25,17},{10,2},{18,10},{26,18},{... | collective-permute-start | bytes 589832 | tf_op jit(solution)/shard_map/ppermute | solution.py:207

commit v2 on v0

v2 whole, which is shorter than its diff:
```python
import functools

import jax
import jax.numpy as jnp
from jax import lax
from jax.experimental import pallas as pl
from jax.experimental.pallas import tpu as pltpu
from jax.sharding import PartitionSpec as P

CAP = 512
LANES = 128
SUBLANES = 8
RUNS = CAP // LANES
bin_width = 0.0625


def position(axis):
    index = lax.axis_index(axis)
    return index, lax.bitwise_and(index, 1)


def either(flag, if_set, if_clear):
    return jnp.where(jnp.full(if_set.shape, flag, jnp.int32) > 0, if_set, if_clear)


def sublane(radial):
    return lax.broadcasted_iota(jnp.int32, (SUBLANES, radial), 0)


def pack_sides(rows, to_partner, to_outer):
    _, odd = position("lon")
    sub = sublane(rows[0].shape[1])
    for group in range(len(rows) // 4):
        before, after = rows[4 * group], rows[4 * group]
        for k in range(1, 4):
            row = rows[4 * group + k]
            pair = lax.shift_right_logical(sub, 1)
            before = jnp.where(pair == k, pltpu.roll(row, 2 * k, 0), before)
            after = jnp.where(pair == 3 - k, pltpu.roll(row, SUBLANES - 2 * k, 0), after)
        to_partner[group] = either(odd, before, after)
        to_outer[group] = either(odd, after, before)


def unpack_sides(from_partner, from_outer, height):
    _, odd = position("lon")
    sub = sublane(from_partner.shape[2])
    tiles = []
    for group in range(height // 4):
        partner, outer = from_partner[group], from_outer[group]
        before, after = either(odd, partner, outer), either(odd, outer, partner)
        for k in range(4):
            if k:
                tiles.append(jnp.where(sub < 4, pltpu.roll(after, SUBLANES - 2 * k, 0), pltpu.roll(before, 2 * k, 0)))
            else:
                tiles.append(jnp.where(sub < 4, after, before))
    return tiles


def pack_ends_kernel(field, from_partner, from_outer, to_partner, to_outer):
    height, _, radial = field.shape
    _, odd = position("lat")
    sub = sublane(radial)
    outside = (sub < 2) | (sub >= 6)
    tiles = unpack_sides(from_partner, from_outer, height)

    def ends(first):
        return (
            field[first],
            field[first + 1],
            jnp.where(outside, tiles[first], pltpu.roll(tiles[first + 1], 4, 0)),
        )

    for place, (top, bottom) in enumerate(zip(ends(0), ends(height - 2))):
        to_partner[place] = either(odd, top, bottom)
        to_outer[place] = either(odd, bottom, top)


def fill_wide(wide, rows, sides, ends):
    height = len(rows)
    tiles = unpack_sides(*sides, height)
    for row in range(height):
        wide[row + 2, :SUBLANES] = rows[row]
        wide[row + 2, SUBLANES:] = tiles[row]
    _, odd = position("lat")
    from_partner, from_outer = ends
    packs = [(from_partner[place], from_outer[place]) for place in range(3)]
    above = [either(odd, partner, outer) for partner, outer in packs]
    below = [either(odd, outer, partner) for partner, outer in packs]
    for first, (one, two, corners) in ((0, above), (height + 2, below)):
        wide[first, :SUBLANES] = one
        wide[first + 1, :SUBLANES] = two
        wide[first, SUBLANES:] = corners
        wide[first + 1, SUBLANES:] = pltpu.roll(corners, 4, 0)


def radial_shifts(field):
    radial = field.shape[-1]
    lane = lax.broadcasted_iota(jnp.int32, field.shape, field.ndim - 1)
    return (
        jnp.where(lane == 0, 0.0, pltpu.roll(field, 1, field.ndim - 1)),
        jnp.where(lane == radial - 1, 0.0, pltpu.roll(field, radial - 1, field.ndim - 1)),
    )


def two_levels(wide, first_coef, second_coef, shifted, middle, write):
    reach, cols, radial = wide.shape
    height = reach - 4
    lat, _ = position("lat")
    bounds = (lat > 0).astype(jnp.int32), (lat < lax.axis_size("lat") - 1).astype(jnp.int32)

    for row in range(reach):
        for place, moved in enumerate(radial_shifts(wide[row])):
            shifted[place, row] = moved

    def taps_of(coef, at):
        return [jnp.broadcast_to(coef[k:k + 1, at], (SUBLANES, LANES)) for k in range(27)]

    def first_level(tile, _):
        at = pl.ds(pl.multiple_of(tile * LANES, LANES), LANES)
        taps = taps_of(first_coef, at)
        for row in range(1, reach - 1):
            parts = []
            for side in (slice(0, SUBLANES), slice(SUBLANES, cols)):
                sums = [None, None, None]
                for above in (-1, 0, 1):
                    window = (shifted[0, row + above, side, at], wide[row + above, side, at], shifted[1, row + above, side, at])
                    for beside in range(3):
                        for step in range(3):
                            term = taps[(above + 1) * 9 + beside * 3 + step] * window[step]
                            sums[beside] = term if sums[beside] is None else sums[beside] + term
                parts.append(sums)
            whole = [jnp.concatenate([parts[0][b], parts[1][b]], axis=0) for b in range(3)]
            value = whole[1] + pltpu.roll(whole[0], 1, 0) + pltpu.roll(whole[2], cols - 1, 0)
            if row in (1, reach - 2):
                value = either(bounds[row != 1], value, jnp.zeros_like(value))
            middle[0, 0, row - 1, :, at] = pltpu.roll(value, 1, 0)[:SUBLANES]
            middle[1, 0, row - 1, :, at] = value[:SUBLANES]
            middle[2, 0, row - 1, :, at] = pltpu.roll(value, cols - 1, 0)[:SUBLANES]
        return 0

    lax.fori_loop(0, radial // LANES, first_level, 0)

    for row in range(reach - 2):
        for beside in range(3):
            for place, moved in enumerate(radial_shifts(middle[beside, 0, row])):
                middle[beside, place + 1, row] = moved

    order = (1, 0, 2)

    def second_level(tile, _):
        at = pl.ds(pl.multiple_of(tile * LANES, LANES), LANES)
        taps = taps_of(second_coef, at)
        for row in range(height):
            total = None
            for above in range(3):
                for beside in range(3):
                    for step in range(3):
                        term = taps[above * 9 + beside * 3 + step] * middle[beside, order[step], row + above, :, at]
                        total = term if total is None else total + term
            write(row, at, total)
        return 0

    lax.fori_loop(0, radial // LANES, second_level, 0)


def open_kernel(
    counts_in, offsets_in, residual_in, pixel_in, bins_in, latent_in, out, to_partner, to_outer,
    counts, offsets, residual, pixel, bins, latent, arrived,
):
    pairs = (
        (latent_in, latent), (counts_in, counts), (offsets_in, offsets),
        (residual_in, residual), (pixel_in, pixel), (bins_in, bins),
    )
    copies = [pltpu.make_async_copy(source, target, arrived.at[i]) for i, (source, target) in enumerate(pairs)]
    for copy in copies:
        copy.start()
    copies[0].wait()
    height, _, radial = latent.shape
    pack_sides([latent[row] for row in range(height)], to_partner, to_outer)
    for copy in copies[1:]:
        copy.wait()

    lane = lax.broadcasted_iota(jnp.int32, (SUBLANES, LANES), 1)
    row = lax.broadcasted_iota(jnp.int32, (SUBLANES, LANES), 0)
    slot = row * LANES + lane
    for owner in range(out.shape[0]):
        start = offsets[0, owner]
        first = lax.shift_right_logical(start, 7)
        part = lax.bitwise_and(start, LANES - 1)
        live = slot < counts[0, owner]

        def window(values):
            turned = pltpu.roll(values, lax.bitwise_and(LANES - part, LANES - 1), 1)
            joined = jnp.where(lane < LANES - part, turned, pltpu.roll(turned, SUBLANES - 1, 0))
            return jnp.where(live, joined, 0.0)

        at = pl.ds(first, SUBLANES)
        cell = (pixel[at, :] * radial + bins[at, :]).astype(jnp.float32)
        out[owner] = jnp.where(row < RUNS, window(residual[at, :]), pltpu.roll(window(cell), RUNS, 0))


def behind_of(got, lefts, rights, *, radial, pixels):
    half = radial // 2
    classes = 2 * pixels
    shards = got.shape[0]
    group = lefts[0].shape[1] // CAP
    column = lax.broadcasted_iota(jnp.int32, (classes, LANES), 0).astype(jnp.float32).astype(jnp.bfloat16)
    place = lax.broadcasted_iota(jnp.int32, (half, LANES), 0).astype(jnp.float32).astype(jnp.bfloat16)
    zero = jnp.zeros((), jnp.bfloat16)
    one = jnp.ones((), jnp.bfloat16)

    def tall(row, height):
        return jnp.concatenate([jnp.broadcast_to(row, (16, LANES)).astype(jnp.bfloat16)] * (height // 16), axis=0)

    def build(turn, left, right):
        for member in range(group):
            tile = got[turn * group + member]
            cell = tile.astype(jnp.int32)
            pixel = lax.shift_right_logical(cell, radial.bit_length() - 1)
            bins = lax.bitwise_and(cell, radial - 1)
            upper = (bins >= half).astype(jnp.int32)
            label = (upper * pixels + pixel).astype(jnp.float32)
            low = (bins - upper * half).astype(jnp.float32)
            coarse = tile.astype(jnp.bfloat16).astype(jnp.float32)
            rest = tile - coarse
            for run in range(RUNS):
                at = slice((member * RUNS + run) * LANES, (member * RUNS + run + 1) * LANES)
                mine = tall(label[RUNS + run:RUNS + run + 1], classes) == column
                left[:classes, at] = jnp.where(mine, tall(coarse[run:run + 1], classes), zero)
                left[classes:, at] = jnp.where(mine, tall(rest[run:run + 1], classes), zero)
                right[:, at] = jnp.where(tall(low[RUNS + run:RUNS + run + 1], half) >= place, one, zero)

    def product(left, right):
        return lax.dot_general(left[...], right[...], (((1,), (1,)), ((), ())), preferred_element_type=jnp.float32)

    def step(pair, total):
        build(2 * pair + 1, lefts[1], rights[1])
        total = total + product(lefts[0], rights[0])
        build(jnp.minimum(2 * pair + 2, shards // group - 1), lefts[0], rights[0])
        return total + product(lefts[1], rights[1])

    build(0, lefts[0], rights[0])
    total = lax.fori_loop(0, shards // group // 2, step, jnp.zeros((2 * classes, half), jnp.float32))
    both = (total[:classes] + total[classes:]) * bin_width
    near, far = both[:pixels], both[pixels:]
    return near + far[:, :1], far


def bin_kernel(got, density, upstream, to_partner, to_outer, left_0, left_1, right_0, right_1):
    height, width, radial = density.shape
    near, far = behind_of(got, (left_0, left_1), (right_0, right_1), radial=radial, pixels=height * width)
    rows = []
    for row in range(height):
        at = slice(row * width, (row + 1) * width)
        rows.append(density[row] * jnp.concatenate([near[at], far[at]], axis=1))
        upstream[row] = rows[row]
    pack_sides(rows, to_partner, to_outer)


def density_kernel(latent, side_0, side_1, end_0, end_1, stencils, out, wide, shifted, middle):
    fill_wide(wide, [latent[row] for row in range(latent.shape[0])], (side_0, side_1), (end_0, end_1))

    def write(row, at, value):
        out[row, :, at] = jnp.exp(value)

    two_levels(wide, stencils.at[0], stencils.at[1], shifted, middle, write)


def back_kernel(latent, upstream, side_0, side_1, end_0, end_1, mirrored, out, wide, shifted, middle):
    fill_wide(wide, [upstream[row] for row in range(upstream.shape[0])], (side_0, side_1), (end_0, end_1))

    def write(row, at, value):
        out[row, :, at] = latent[row, :, at] + value

    two_levels(wide, mirrored.at[1], mirrored.at[0], shifted, middle, write)


def mirror(stencils):
    turned = jnp.flip(stencils, axis=1).reshape(stencils.shape[0], 9, 3, stencils.shape[2])
    edge = jnp.zeros_like(turned[:, :, 0, :1])
    back = jnp.concatenate([edge, turned[:, :, 0, :-1]], axis=-1)
    ahead = jnp.concatenate([turned[:, :, 2, 1:], edge], axis=-1)
    return jnp.stack([back, turned[:, :, 1], ahead], axis=2).reshape(stencils.shape)


def swap(to_partner, to_outer, axis, closed):
    count = lax.axis_size(axis)
    outer = [(i, (i + 1) % count) for i in range(1, count, 2) if closed or i + 1 < count]
    inner = [(i, i + 1) for i in range(0, count - 1, 2)]

    def both_ways(pairs):
        return pairs + [(j, i) for i, j in pairs]

    from_outer = lax.ppermute(to_outer, axis, both_ways(outer))
    return lax.ppermute(to_partner, axis, both_ways(inner)), from_outer


VMEM = pl.BlockSpec(memory_space=pltpu.VMEM)
HBM = pl.BlockSpec(memory_space=pl.ANY)
LIMIT = pltpu.CompilerParams(vmem_limit_bytes=32 * 1024 * 1024)


def on_device(residual, star_pixel, star_bin, send_counts, send_offsets, latent, stencils):
    height, width, radial = latent.shape
    shards = send_counts.shape[1]
    slots = residual.shape[0]
    f32 = jnp.float32
    i32 = jnp.int32
    tile = jax.ShapeDtypeStruct((height, width, radial), f32)
    sides = jax.ShapeDtypeStruct((height // 4, SUBLANES, radial), f32)
    ends = jax.ShapeDtypeStruct((3, SUBLANES, radial), f32)
    reach, cols = height + 4, 2 * width
    level_scratch = [
        pltpu.VMEM((reach, cols, radial), f32),
        pltpu.VMEM((2, reach, cols, radial), f32),
        pltpu.VMEM((3, 3, reach - 2, width, radial), f32),
    ]

    def table(values):
        return values.reshape(slots // LANES, LANES)

    packed, to_partner, to_outer = pl.pallas_call(
        open_kernel,
        out_shape=(jax.ShapeDtypeStruct((shards, 2 * RUNS, LANES), f32), sides, sides),
        in_specs=[HBM] * 6,
        out_specs=(VMEM, VMEM, VMEM),
        scratch_shapes=[pltpu.SMEM((1, shards), i32)] * 2
        + [pltpu.VMEM((slots // LANES, LANES), kind) for kind in (f32, i32, i32)]
        + [pltpu.VMEM((height, width, radial), f32), pltpu.SemaphoreType.DMA((6,))],
        compiler_params=LIMIT,
        name="opening",
    )(send_counts, send_offsets, table(residual), table(star_pixel), table(star_bin), latent)
    got = lax.all_to_all(packed, ("lat", "lon"), split_axis=0, concat_axis=0, tiled=True)

    def pack_ends(field, beside):
        return pl.pallas_call(
            pack_ends_kernel,
            out_shape=(ends, ends),
            in_specs=[VMEM] * 3,
            out_specs=(VMEM, VMEM),
            compiler_params=LIMIT,
            name="pack_ends",
        )(field, *beside)

    beside = swap(to_partner, to_outer, "lon", True)
    above = swap(*pack_ends(latent, beside), "lat", False)
    density = pl.pallas_call(
        density_kernel,
        out_shape=tile,
        in_specs=[VMEM] * 6,
        out_specs=VMEM,
        scratch_shapes=level_scratch,
        compiler_params=LIMIT,
        name="density",
    )(latent, *beside, *above, stencils)

    pieces = 2 * CAP
    upstream, to_partner, to_outer = pl.pallas_call(
        bin_kernel,
        out_shape=(tile, sides, sides),
        in_specs=[VMEM, VMEM],
        out_specs=(VMEM, VMEM, VMEM),
        scratch_shapes=[pltpu.VMEM((4 * height * width, pieces), jnp.bfloat16)] * 2
        + [pltpu.VMEM((radial // 2, pieces), jnp.bfloat16)] * 2,
        compiler_params=LIMIT,
        name="binning",
    )(got, density)
    beside = swap(to_partner, to_outer, "lon", True)
    above = swap(*pack_ends(upstream, beside), "lat", False)
    return pl.pallas_call(
        back_kernel,
        out_shape=tile,
        in_specs=[VMEM] * 7,
        out_specs=VMEM,
        scratch_shapes=level_scratch,
        compiler_params=LIMIT,
        name="back",
    )(latent, upstream, *beside, *above, mirror(stencils))


def solution(mesh):
    return jax.shard_map(
        on_device,
        mesh=mesh,
        in_specs=(
            P(("lat", "lon")),
            P(("lat", "lon")),
            P(("lat", "lon")),
            P(("lat", "lon"), None),
            P(("lat", "lon"), None),
            P("lat", "lon", None),
            P(),
        ),
        out_specs=P("lat", "lon", None),
        check_vma=False,
    )
```

time: 457 us -> 44.3 us (0.10)
  the two profiles are of different devices: /device:TPU:2 before, /device:TPU:4 now
where the time goes in v2:
time: 44.3 us; the launch traced here: 43.9 us
  starting transfers between devices  16.4 us (37%)
  Pallas kernels  11.3 us (26%)
  waiting for transfers between devices  10.7 us (24%)
  local copies, waits for them, and re-layouts  5.2 us (12%)
    ppermute x4, starting transfers between devices, swap(): from_outer = lax.ppermute(to_outer, axis, both_ways(outer))  11.6 us
    ppermute x4, waiting for transfers between devices, swap(): from_outer = lax.ppermute(to_outer, axis, both_ways(outer))  8.65 us
    pallas_call x1, Pallas kernels, on_device(): pl.pallas_call(bin_kernel, out_shape=(tile, sides, sides), in_specs=[VMEM...  5.77 us
    unnamed x17, local copies, waits for them, and re-layouts  4.98 us
    all_to_all x1, starting transfers between devices, on_device(): lax.all_to_all(packed, ('lat', 'lon'), split_axis=0, concat_axis=0, tiled...  3.06 us
    pallas_call x1, Pallas kernels, on_device(): pl.pallas_call(back_kernel, out_shape=tile, in_specs=[VMEM] * 7, out_spec...  2.26 us
    ppermute x4, waiting for transfers between devices, swap(): return (lax.ppermute(to_partner, axis, both_ways(inner)), from_outer)  2.08 us
    ppermute x4, starting transfers between devices, swap(): return (lax.ppermute(to_partner, axis, both_ways(inner)), from_outer)  1.74 us
  transfers between devices with their start and end apart: 9, of which 5 were waited for; matrix products, arithmetic and copies ran while one was open for 1% of the time, Pallas kernels for 4%

profile of v2, /device:TPU:4, one launch (start us, length us, event | category | flops | bytes accessed | tf_op | source)
XLA Modules:
  0.0 43.9 jit_solution(3404826519191642292)
XLA Ops:
  0.0 0.7 %copy-done.5 = s32[1,32]{1,0:T(1,128)S(1)} copy-done((s32[1,32]{1,0:T(1,128)S(1)}, s32[1,32]{1,0:T(1,128)}, u32[]{:S(2)}) %copy-start.5) | copy-done | bytes 152
  0.7 0.9 %copy-done = f32[8,8,512]{2,1,0:T(8,128)S(1)} copy-done((f32[8,8,512]{2,1,0:T(8,128)S(1)}, f32[8,8,512]{2,1,0:T(8,128)}, u32[]{:S(2)}) %copy-start) | copy-done | bytes 131096
  1.6 0.8 %copy-done.2 = f32[16384]{0:T(1024)S(1)} copy-done((f32[16384]{0:T(1024)S(1)}, f32[16384]{0:T(1024)}, u32[]{:S(2)}) %copy-start.2) | copy-done | bytes 65560
  2.4 0.8 %copy-done.3 = s32[16384]{0:T(1024)S(1)} copy-done((s32[16384]{0:T(1024)S(1)}, s32[16384]{0:T(1024)}, u32[]{:S(2)}) %copy-start.3) | copy-done | bytes 65560
  3.3 0.8 %copy-done.4 = s32[16384]{0:T(1024)S(1)} copy-done((s32[16384]{0:T(1024)S(1)}, s32[16384]{0:T(1024)}, u32[]{:S(2)}) %copy-start.4) | copy-done | bytes 65560
  4.1 1.6 %opening.1 = (f32[32,8,128]{2,1,0:T(8,128)}, f32[2,8,512]{2,1,0:T(8,128)S(1)}, f32[2,8,512]{2,1,0:T(8,128)S(1)}) custom-call(s32[1,32]{1,0:T(1,128)S(1)} %copy-done.5, s32[1,32]{1,0:T(1,128)S(1)} %copy-done.6, f32[128,128]{1,0:T(8,128)S(1)} %bitcast.17, s32[128,128]{1,0:T(8,128)S(1)} %bitcast.18, s32[128,128]{1,0:T(8,128)S(1)} %bitcast.19, ...), custom_call_target="tpu_custom_call" | custom-call | tf_op jit(solution)/shard_map/opening/pallas_call | solution.py:322
  5.7 0.1 collective-permute-start
  5.8 3.7 %collective-permute-start.1 = (f32[2,8,512]{2,1,0:T(8,128)S(1)}, f32[2,8,512]{2,1,0:T(8,128)S(1)}, u32[]{:S(2)}, u32[]{:S(2)}) collective-permute-start(f32[2,8,512]{2,1,0:T(8,128)S(1)} %get-tuple-element.17), channel_id=1, source_target_pairs={{1,2},{3,4},{5,6},{7,0},{2,1},{4,3},{6,5},{0,7},{9,10},{11,12},{13... | collective-permute-start | bytes 98312 | tf_op jit(solution)/shard_map/ppermute | solution.py:294
  9.5 3.1 %all-to-all-start = ((f32[32,8,128]{2,1,0:T(8,128)}), f32[32,8,128]{2,1,0:T(8,128)S(1)}, u32[]{:S(2)}, u32[]{:S(2)}) async-start(f32[32,8,128]{2,1,0:T(8,128)} %get-tuple-element.15), calls=%async_computation | async-start | bytes 262144 | tf_op jit(solution)/shard_map/all_to_all | solution.py:333
  12.6 0.9 %copy-done.1 = f32[8,8,512]{2,1,0:T(8,128)S(1)} copy-done((f32[8,8,512]{2,1,0:T(8,128)S(1)}, f32[8,8,512]{2,1,0:T(8,128)}, u32[]{:S(2)}) %copy-start.1) | copy-done | bytes 131096
  13.5 1.5 %collective-permute-start.2 = (f32[3,8,512]{2,1,0:T(8,128)S(1)}, f32[3,8,512]{2,1,0:T(8,128)S(1)}, u32[]{:S(2)}, u32[]{:S(2)}) collective-permute-start(f32[3,8,512]{2,1,0:T(8,128)S(1)} %get-tuple-element.18), channel_id=1, source_target_pairs={{0,8},{16,24},{8,0},{24,16},{1,9},{17,25},{9,1},{25,17},{2,10},{18... | collective-permute-start | bytes 147464 | tf_op jit(solution)/shard_map/ppermute | solution.py:295
  15.0 2.2 %collective-permute-start.3 = (f32[3,8,512]{2,1,0:T(8,128)S(1)}, f32[3,8,512]{2,1,0:T(8,128)S(1)}, u32[]{:S(2)}, u32[]{:S(2)}) collective-permute-start(f32[3,8,512]{2,1,0:T(8,128)S(1)} %get-tuple-element.19), channel_id=1, source_target_pairs={{8,16},{16,8},{9,17},{17,9},{10,18},{18,10},{11,19},{19,11},{12,20... | collective-permute-start | bytes 147464 | tf_op jit(solution)/shard_map/ppermute | solution.py:294
  17.2 0.1 slice_bitcast_fusion.1
  17.3 0.4 collective-permute-done.2.end_0
  17.7 4.2 %collective-permute-done.3.end_1 = f32[3,8,512]{2,1,0:T(8,128)S(1)} collective-permute-done((f32[3,8,512]{2,1,0:T(8,128)S(1)}, f32[3,8,512]{2,1,0:T(8,128)S(1)}, u32[]{:S(2)}, u32[]{:S(2)}) %collective-permute-start.3) | collective-permute-done | bytes 49184 | tf_op jit(solution)/shard_map/ppermute | solution.py:294
  21.9 1.6 %density.1 = f32[8,8,512]{2,1,0:T(8,128)S(1)} custom-call(f32[8,8,512]{2,1,0:T(8,128)S(1)} %copy-done.1, f32[2,8,512]{2,1,0:T(8,128)S(1)} %collective-permute-done.from_partner.side_0, f32[2,8,512]{2,1,0:T(8,128)S(1)} %collective-permute-done.1.from_outer.side_1, f32[3,8,512]{2,1,0:T(8,128)S(1)} %collective-permute-done.2.end_0, ...), custom_call_target="tpu_custom_call" | custom-call | tf_op jit(solution)/shard_map/density/pallas_call | solution.py:347
  23.5 5.8 %binning.1 = (f32[8,8,512]{2,1,0:T(8,128)S(1)}, f32[2,8,512]{2,1,0:T(8,128)S(1)}, f32[2,8,512]{2,1,0:T(8,128)S(1)}) custom-call(f32[32,8,128]{2,1,0:T(8,128)S(1)} %all-to-all-done.got, f32[8,8,512]{2,1,0:T(8,128)S(1)} %density.1), custom_call_target="tpu_custom_call" | custom-call | tf_op jit(solution)/shard_map/binning/pallas_call | solution.py:358
  29.4 3.5 %collective-permute-start.5 = (f32[2,8,512]{2,1,0:T(8,128)S(1)}, f32[2,8,512]{2,1,0:T(8,128)S(1)}, u32[]{:S(2)}, u32[]{:S(2)}) collective-permute-start(f32[2,8,512]{2,1,0:T(8,128)S(1)} %get-tuple-element.22), channel_id=1, source_target_pairs={{1,2},{3,4},{5,6},{7,0},{2,1},{4,3},{6,5},{0,7},{9,10},{11,12},{13... | collective-permute-start | bytes 98312 | tf_op jit(solution)/shard_map/ppermute | solution.py:294
  32.8 0.1 pad_bitcast_fusion
  33.0 1.7 %collective-permute-done.5.from_outer.side_1 = f32[2,8,512]{2,1,0:T(8,128)S(1)} collective-permute-done((f32[2,8,512]{2,1,0:T(8,128)S(1)}, f32[2,8,512]{2,1,0:T(8,128)S(1)}, u32[]{:S(2)}, u32[]{:S(2)}) %collective-permute-start.5) | collective-permute-done | bytes 32800 | tf_op jit(solution)/shard_map/ppermute | solution.py:294
  34.7 2.3 %collective-permute-start.7 = (f32[3,8,512]{2,1,0:T(8,128)S(1)}, f32[3,8,512]{2,1,0:T(8,128)S(1)}, u32[]{:S(2)}, u32[]{:S(2)}) collective-permute-start(f32[3,8,512]{2,1,0:T(8,128)S(1)} %get-tuple-element.24), channel_id=1, source_target_pairs={{8,16},{16,8},{9,17},{17,9},{10,18},{18,10},{11,19},{19,11},{12,20... | collective-permute-start | bytes 147464 | tf_op jit(solution)/shard_map/ppermute | solution.py:294
  37.2 1.7 %collective-permute-done.6.end_0 = f32[3,8,512]{2,1,0:T(8,128)S(1)} collective-permute-done((f32[3,8,512]{2,1,0:T(8,128)S(1)}, f32[3,8,512]{2,1,0:T(8,128)S(1)}, u32[]{:S(2)}, u32[]{:S(2)}) %collective-permute-start.6) | collective-permute-done | bytes 49184 | tf_op jit(solution)/shard_map/ppermute | solution.py:295
  38.8 2.8 %collective-permute-done.7.end_1 = f32[3,8,512]{2,1,0:T(8,128)S(1)} collective-permute-done((f32[3,8,512]{2,1,0:T(8,128)S(1)}, f32[3,8,512]{2,1,0:T(8,128)S(1)}, u32[]{:S(2)}, u32[]{:S(2)}) %collective-permute-start.7) | collective-permute-done | bytes 49184 | tf_op jit(solution)/shard_map/ppermute | solution.py:294
  41.6 2.3 %back.1 = f32[8,8,512]{2,1,0:T(8,128)} custom-call(f32[8,8,512]{2,1,0:T(8,128)S(1)} %copy-done.1, f32[8,8,512]{2,1,0:T(8,128)S(1)} %get-tuple-element.20.field.upstream, f32[2,8,512]{2,1,0:T(8,128)S(1)} %collective-permute-done.4.from_partner.side_0, f32[2,8,512]{2,1,0:T(8,128)S(1)} %collective-permute-done.5.from_outer.side_1, ...), custom_call_target="tpu_custom_call" | custom-call | tf_op jit(solution)/shard_map/back/pallas_call | solution.py:370
  (23 shorter events, 0.3 us)
Async XLA Ops:
  0.0 0.7 %copy-start.5 = (s32[1,32]{1,0:T(1,128)S(1)}, s32[1,32]{1,0:T(1,128)}, u32[]{:S(2)}) copy-start(s32[1,32]{1,0:T(1,128)} %counts_in.1) | copy-start | bytes 388
  0.0 0.7 %copy-start.6 = (s32[1,32]{1,0:T(1,128)S(1)}, s32[1,32]{1,0:T(1,128)}, u32[]{:S(2)}) copy-start(s32[1,32]{1,0:T(1,128)} %offsets_in.1) | copy-start | bytes 388
  0.7 0.9 %copy-start = (f32[8,8,512]{2,1,0:T(8,128)S(1)}, f32[8,8,512]{2,1,0:T(8,128)}, u32[]{:S(2)}) copy-start(f32[8,8,512]{2,1,0:T(8,128)} %latent.3) | copy-start | bytes 393220
  1.6 0.8 %copy-start.2 = (f32[16384]{0:T(1024)S(1)}, f32[16384]{0:T(1024)}, u32[]{:S(2)}) copy-start(f32[16384]{0:T(1024)} %param.7) | copy-start | bytes 196612
  2.4 0.8 %copy-start.3 = (s32[16384]{0:T(1024)S(1)}, s32[16384]{0:T(1024)}, u32[]{:S(2)}) copy-start(s32[16384]{0:T(1024)} %param.8) | copy-start | bytes 196612
  3.3 0.8 %copy-start.4 = (s32[16384]{0:T(1024)S(1)}, s32[16384]{0:T(1024)}, u32[]{:S(2)}) copy-start(s32[16384]{0:T(1024)} %param.9) | copy-start | bytes 196612
  5.7 6.9 %collective-permute-start = (f32[2,8,512]{2,1,0:T(8,128)S(1)}, f32[2,8,512]{2,1,0:T(8,128)S(1)}, u32[]{:S(2)}, u32[]{:S(2)}) collective-permute-start(f32[2,8,512]{2,1,0:T(8,128)S(1)} %get-tuple-element.16), channel_id=1, source_target_pairs={{0,1},{2,3},{4,5},{6,7},{1,0},{3,2},{5,4},{7,6},{8,9},{10,11},{12,... | collective-permute-start | bytes 98312 | tf_op jit(solution)/shard_map/ppermute | solution.py:295
  5.8 6.8 %collective-permute-start.1 = (f32[2,8,512]{2,1,0:T(8,128)S(1)}, f32[2,8,512]{2,1,0:T(8,128)S(1)}, u32[]{:S(2)}, u32[]{:S(2)}) collective-permute-start(f32[2,8,512]{2,1,0:T(8,128)S(1)} %get-tuple-element.17), channel_id=1, source_target_pairs={{1,2},{3,4},{5,6},{7,0},{2,1},{4,3},{6,5},{0,7},{9,10},{11,12},{13... | collective-permute-start | bytes 98312 | tf_op jit(solution)/shard_map/ppermute | solution.py:294
  9.5 3.1 %copy-start.7 = (f32[2,27,512]{2,0,1:T(2,128)S(1)}, f32[2,27,512]{2,0,1:T(2,128)}, u32[]{:S(2)}) copy-start(f32[2,27,512]{2,0,1:T(2,128)} %param.13) | copy-start | bytes 331780
  9.5 14.0 %all-to-all-start = ((f32[32,8,128]{2,1,0:T(8,128)}), f32[32,8,128]{2,1,0:T(8,128)S(1)}, u32[]{:S(2)}, u32[]{:S(2)}) async-start(f32[32,8,128]{2,1,0:T(8,128)} %get-tuple-element.15), calls=%async_computation | async-start | bytes 262144 | tf_op jit(solution)/shard_map/all_to_all | solution.py:333
  12.5 0.9 %copy-start.1 = (f32[8,8,512]{2,1,0:T(8,128)S(1)}, f32[8,8,512]{2,1,0:T(8,128)}, u32[]{:S(2)}) copy-start(f32[8,8,512]{2,1,0:T(8,128)} %latent.3) | copy-start | bytes 393220
  13.5 4.2 %collective-permute-start.2 = (f32[3,8,512]{2,1,0:T(8,128)S(1)}, f32[3,8,512]{2,1,0:T(8,128)S(1)}, u32[]{:S(2)}, u32[]{:S(2)}) collective-permute-start(f32[3,8,512]{2,1,0:T(8,128)S(1)} %get-tuple-element.18), channel_id=1, source_target_pairs={{0,8},{16,24},{8,0},{24,16},{1,9},{17,25},{9,1},{25,17},{2,10},{18... | collective-permute-start | bytes 147464 | tf_op jit(solution)/shard_map/ppermute | solution.py:295
  15.0 6.9 %collective-permute-start.3 = (f32[3,8,512]{2,1,0:T(8,128)S(1)}, f32[3,8,512]{2,1,0:T(8,128)S(1)}, u32[]{:S(2)}, u32[]{:S(2)}) collective-permute-start(f32[3,8,512]{2,1,0:T(8,128)S(1)} %get-tuple-element.19), channel_id=1, source_target_pairs={{8,16},{16,8},{9,17},{17,9},{10,18},{18,10},{11,19},{19,11},{12,20... | collective-permute-start | bytes 147464 | tf_op jit(solution)/shard_map/ppermute | solution.py:294
  29.3 3.7 %collective-permute-start.4 = (f32[2,8,512]{2,1,0:T(8,128)S(1)}, f32[2,8,512]{2,1,0:T(8,128)S(1)}, u32[]{:S(2)}, u32[]{:S(2)}) collective-permute-start(f32[2,8,512]{2,1,0:T(8,128)S(1)} %get-tuple-element.21), channel_id=1, source_target_pairs={{0,1},{2,3},{4,5},{6,7},{1,0},{3,2},{5,4},{7,6},{8,9},{10,11},{12,... | collective-permute-start | bytes 98312 | tf_op jit(solution)/shard_map/ppermute | solution.py:295
  29.4 5.3 %collective-permute-start.5 = (f32[2,8,512]{2,1,0:T(8,128)S(1)}, f32[2,8,512]{2,1,0:T(8,128)S(1)}, u32[]{:S(2)}, u32[]{:S(2)}) collective-permute-start(f32[2,8,512]{2,1,0:T(8,128)S(1)} %get-tuple-element.22), channel_id=1, source_target_pairs={{1,2},{3,4},{5,6},{7,0},{2,1},{4,3},{6,5},{0,7},{9,10},{11,12},{13... | collective-permute-start | bytes 98312 | tf_op jit(solution)/shard_map/ppermute | solution.py:294
  34.7 4.2 %collective-permute-start.6 = (f32[3,8,512]{2,1,0:T(8,128)S(1)}, f32[3,8,512]{2,1,0:T(8,128)S(1)}, u32[]{:S(2)}, u32[]{:S(2)}) collective-permute-start(f32[3,8,512]{2,1,0:T(8,128)S(1)} %get-tuple-element.23), channel_id=1, source_target_pairs={{0,8},{16,24},{8,0},{24,16},{1,9},{17,25},{9,1},{25,17},{2,10},{18... | collective-permute-start | bytes 147464 | tf_op jit(solution)/shard_map/ppermute | solution.py:295
  34.7 6.9 %collective-permute-start.7 = (f32[3,8,512]{2,1,0:T(8,128)S(1)}, f32[3,8,512]{2,1,0:T(8,128)S(1)}, u32[]{:S(2)}, u32[]{:S(2)}) collective-permute-start(f32[3,8,512]{2,1,0:T(8,128)S(1)} %get-tuple-element.24), channel_id=1, source_target_pairs={{8,16},{16,8},{9,17},{17,9},{10,18},{18,10},{11,19},{19,11},{12,20... | collective-permute-start | bytes 147464 | tf_op jit(solution)/shard_map/ppermute | solution.py:294

commit v3 on v2

--- a/solution.py
+++ b/solution.py
@@ -164,8 +164,8 @@
 
 
 def open_kernel(
-    counts_in, offsets_in, residual_in, pixel_in, bins_in, latent_in, out, to_partner, to_outer,
-    counts, offsets, residual, pixel, bins, latent, arrived,
+    counts_in, offsets_in, residual_in, pixel_in, bins_in, latent_in, out, latent, to_partner, to_outer,
+    counts, offsets, residual, pixel, bins, arrived,
 ):
     pairs = (
         (latent_in, latent), (counts_in, counts), (offsets_in, offsets),
@@ -199,11 +199,10 @@
         out[owner] = jnp.where(row < RUNS, window(residual[at, :]), pltpu.roll(window(cell), RUNS, 0))
 
 
-def behind_of(got, lefts, rights, *, radial, pixels):
+def behind_of(got, *, radial, pixels):
     half = radial // 2
     classes = 2 * pixels
     shards = got.shape[0]
-    group = lefts[0].shape[1] // CAP
     column = lax.broadcasted_iota(jnp.int32, (classes, LANES), 0).astype(jnp.float32).astype(jnp.bfloat16)
     place = lax.broadcasted_iota(jnp.int32, (half, LANES), 0).astype(jnp.float32).astype(jnp.bfloat16)
     zero = jnp.zeros((), jnp.bfloat16)
@@ -212,43 +211,43 @@
     def tall(row, height):
         return jnp.concatenate([jnp.broadcast_to(row, (16, LANES)).astype(jnp.bfloat16)] * (height // 16), axis=0)
 
-    def build(turn, left, right):
-        for member in range(group):
-            tile = got[turn * group + member]
-            cell = tile.astype(jnp.int32)
-            pixel = lax.shift_right_logical(cell, radial.bit_length() - 1)
-            bins = lax.bitwise_and(cell, radial - 1)
-            upper = (bins >= half).astype(jnp.int32)
-            label = (upper * pixels + pixel).astype(jnp.float32)
-            low = (bins - upper * half).astype(jnp.float32)
-            coarse = tile.astype(jnp.bfloat16).astype(jnp.float32)
-            rest = tile - coarse
-            for run in range(RUNS):
-                at = slice((member * RUNS + run) * LANES, (member * RUNS + run + 1) * LANES)
-                mine = tall(label[RUNS + run:RUNS + run + 1], classes) == column
-                left[:classes, at] = jnp.where(mine, tall(coarse[run:run + 1], classes), zero)
-                left[classes:, at] = jnp.where(mine, tall(rest[run:run + 1], classes), zero)
-                right[:, at] = jnp.where(tall(low[RUNS + run:RUNS + run + 1], half) >= place, one, zero)
-
-    def product(left, right):
-        return lax.dot_general(left[...], right[...], (((1,), (1,)), ((), ())), preferred_element_type=jnp.float32)
-
-    def step(pair, total):
-        build(2 * pair + 1, lefts[1], rights[1])
-        total = total + product(lefts[0], rights[0])
-        build(jnp.minimum(2 * pair + 2, shards // group - 1), lefts[0], rights[0])
-        return total + product(lefts[1], rights[1])
-
-    build(0, lefts[0], rights[0])
-    total = lax.fori_loop(0, shards // group // 2, step, jnp.zeros((2 * classes, half), jnp.float32))
+    def product(shard):
+        tile = got[shard]
+        cell = tile.astype(jnp.int32)
+        pixel = lax.shift_right_logical(cell, radial.bit_length() - 1)
+        bins = lax.bitwise_and(cell, radial - 1)
+        upper = (bins >= half).astype(jnp.int32)
+        label = (upper * pixels + pixel).astype(jnp.float32)
+        low = (bins - upper * half).astype(jnp.float32)
+        coarse = tile.astype(jnp.bfloat16).astype(jnp.float32)
+        rest = tile - coarse
+        left, right = [], []
+        for run in range(RUNS):
+            mine = tall(label[RUNS + run:RUNS + run + 1], classes) == column
+            left.append(jnp.concatenate([
+                jnp.where(mine, tall(coarse[run:run + 1], classes), zero),
+                jnp.where(mine, tall(rest[run:run + 1], classes), zero),
+            ], axis=0))
+            right.append(jnp.where(tall(low[RUNS + run:RUNS + run + 1], half) >= place, one, zero))
+        return lax.dot_general(
+            jnp.concatenate(left, axis=1), jnp.concatenate(right, axis=1),
+            (((1,), (1,)), ((), ())), preferred_element_type=jnp.float32,
+        )
+
+    def step(turn, total):
+        for member in range(4):
+            total = total + product(4 * turn + member)
+        return total
+
+    total = lax.fori_loop(0, shards // 4, step, jnp.zeros((2 * classes, half), jnp.float32))
     both = (total[:classes] + total[classes:]) * bin_width
     near, far = both[:pixels], both[pixels:]
     return near + far[:, :1], far
 
 
-def bin_kernel(got, density, upstream, to_partner, to_outer, left_0, left_1, right_0, right_1):
+def bin_kernel(got, density, upstream, to_partner, to_outer):
     height, width, radial = density.shape
-    near, far = behind_of(got, (left_0, left_1), (right_0, right_1), radial=radial, pixels=height * width)
+    near, far = behind_of(got, radial=radial, pixels=height * width)
     rows = []
     for row in range(height):
         at = slice(row * width, (row + 1) * width)
@@ -296,7 +295,7 @@
 
 
 VMEM = pl.BlockSpec(memory_space=pltpu.VMEM)
-HBM = pl.BlockSpec(memory_space=pl.ANY)
+HBM = pl.BlockSpec(memory_space=pltpu.HBM)
 LIMIT = pltpu.CompilerParams(vmem_limit_bytes=32 * 1024 * 1024)
 
 
@@ -319,17 +318,20 @@
     def table(values):
         return values.reshape(slots // LANES, LANES)
 
-    packed, to_partner, to_outer = pl.pallas_call(
+    packed, latent, to_partner, to_outer = pl.pallas_call(
         open_kernel,
-        out_shape=(jax.ShapeDtypeStruct((shards, 2 * RUNS, LANES), f32), sides, sides),
+        out_shape=(jax.ShapeDtypeStruct((shards, 2 * RUNS, LANES), f32), tile, sides, sides),
         in_specs=[HBM] * 6,
-        out_specs=(VMEM, VMEM, VMEM),
+        out_specs=(VMEM, VMEM, VMEM, VMEM),
         scratch_shapes=[pltpu.SMEM((1, shards), i32)] * 2
         + [pltpu.VMEM((slots // LANES, LANES), kind) for kind in (f32, i32, i32)]
-        + [pltpu.VMEM((height, width, radial), f32), pltpu.SemaphoreType.DMA((6,))],
+        + [pltpu.SemaphoreType.DMA((6,))],
         compiler_params=LIMIT,
         name="opening",
-    )(send_counts, send_offsets, table(residual), table(star_pixel), table(star_bin), latent)
+    )(*[
+        pltpu.with_memory_space_constraint(values, pltpu.HBM)
+        for values in (send_counts, send_offsets, table(residual), table(star_pixel), table(star_bin), latent)
+    ])
     got = lax.all_to_all(packed, ("lat", "lon"), split_axis=0, concat_axis=0, tiled=True)
 
     def pack_ends(field, beside):
@@ -354,14 +356,11 @@
         name="density",
     )(latent, *beside, *above, stencils)
 
-    pieces = 2 * CAP
     upstream, to_partner, to_outer = pl.pallas_call(
         bin_kernel,
         out_shape=(tile, sides, sides),
         in_specs=[VMEM, VMEM],
         out_specs=(VMEM, VMEM, VMEM),
-        scratch_shapes=[pltpu.VMEM((4 * height * width, pieces), jnp.bfloat16)] * 2
-        + [pltpu.VMEM((radial // 2, pieces), jnp.bfloat16)] * 2,
         compiler_params=LIMIT,
         name="binning",
     )(got, density)

time: 44.3 us -> 37.7 us (0.85)
  local copies, waits for them, and re-layouts: 5.2 us -> 0.25 us
  Pallas kernels: 11.3 us -> 9.81 us
    unnamed x17 -> x3, local copies, waits for them, and re-layouts: 4.98 us -> 0.03 us
    pallas_call x1, Pallas kernels: 5.77 us -> 4.04 us  [on_device(): pl.pallas_call(bin_kernel, out_shape=(tile, sides, sides), in_specs=[VMEM...]
where the time goes in v3:
time: 37.7 us; the launch traced here: 37.5 us
  starting transfers between devices  16.5 us (44%)
  waiting for transfers between devices  10.7 us (28%)
  Pallas kernels  9.81 us (26%)
    ppermute x4, starting transfers between devices, swap(): from_outer = lax.ppermute(to_outer, axis, both_ways(outer))  11.7 us
    ppermute x4, waiting for transfers between devices, swap(): from_outer = lax.ppermute(to_outer, axis, both_ways(outer))  8.49 us
    pallas_call x1, Pallas kernels, on_device(): pl.pallas_call(bin_kernel, out_shape=(tile, sides, sides), in_specs=[VMEM...  4.04 us
    all_to_all x1, starting transfers between devices, on_device(): lax.all_to_all(packed, ('lat', 'lon'), split_axis=0, concat_axis=0, tiled...  3.06 us
    pallas_call x1, Pallas kernels, on_device(): pl.pallas_call(back_kernel, out_shape=tile, in_specs=[VMEM] * 7, out_spec...  2.26 us
    ppermute x4, waiting for transfers between devices, swap(): return (lax.ppermute(to_partner, axis, both_ways(inner)), from_outer)  2.21 us
    pallas_call x1, Pallas kernels, on_device(): pl.pallas_call(open_kernel, out_shape=(jax.ShapeDtypeStruct((shards, 2 *...  1.84 us
    ppermute x4, starting transfers between devices, swap(): return (lax.ppermute(to_partner, axis, both_ways(inner)), from_outer)  1.74 us
  transfers between devices with their start and end apart: 9, of which 5 were waited for; matrix products, arithmetic and copies ran while one was open for 1% of the time, Pallas kernels for 4%

profile of v3, /device:TPU:4, one launch (start us, length us, event | category | flops | bytes accessed | tf_op | source)
XLA Modules:
  0.0 37.5 jit_solution(7484724874678596490)
XLA Ops:
  0.0 1.8 %opening.1 = (f32[32,8,128]{2,1,0:T(8,128)}, f32[8,8,512]{2,1,0:T(8,128)S(1)}, f32[2,8,512]{2,1,0:T(8,128)S(1)}, f32[2,8,512]{2,1,0:T(8,128)S(1)}) custom-call(s32[1,32]{1,0:T(1,128)} %counts_in.1, s32[1,32]{1,0:T(1,128)} %offsets_in.1, f32[128,128]{1,0:T(8,128)} %bitcast.20, s32[128,128]{1,0:T(8,128)} %bitcast.21, s32[128,128]{1,0:T(8,128)} %bitcast.22, ...), custom_call_target="tpu_custom_call" | custom-call | tf_op jit(solution)/shard_map/opening/pallas_call | solution.py:321
  1.9 0.1 collective-permute-start
  1.9 3.7 %collective-permute-start.1 = (f32[2,8,512]{2,1,0:T(8,128)S(1)}, f32[2,8,512]{2,1,0:T(8,128)S(1)}, u32[]{:S(2)}, u32[]{:S(2)}) collective-permute-start(f32[2,8,512]{2,1,0:T(8,128)S(1)} %get-tuple-element.19), channel_id=1, source_target_pairs={{1,2},{3,4},{5,6},{7,0},{2,1},{4,3},{6,5},{0,7},{9,10},{11,12},{13... | collective-permute-start | bytes 98312 | tf_op jit(solution)/shard_map/ppermute | solution.py:293
  5.6 3.1 %all-to-all-start = ((f32[32,8,128]{2,1,0:T(8,128)}), f32[32,8,128]{2,1,0:T(8,128)S(1)}, u32[]{:S(2)}, u32[]{:S(2)}) async-start(f32[32,8,128]{2,1,0:T(8,128)} %get-tuple-element.17), calls=%async_computation | async-start | bytes 262144 | tf_op jit(solution)/shard_map/all_to_all | solution.py:335
  8.7 0.0 collective-permute-done.from_partner.side_0
  8.7 0.0 collective-permute-done.1.from_outer.side_1
  8.8 1.5 %collective-permute-start.2 = (f32[3,8,512]{2,1,0:T(8,128)S(1)}, f32[3,8,512]{2,1,0:T(8,128)S(1)}, u32[]{:S(2)}, u32[]{:S(2)}) collective-permute-start(f32[3,8,512]{2,1,0:T(8,128)S(1)} %get-tuple-element.20), channel_id=1, source_target_pairs={{0,8},{16,24},{8,0},{24,16},{1,9},{17,25},{9,1},{25,17},{2,10},{18... | collective-permute-start | bytes 147464 | tf_op jit(solution)/shard_map/ppermute | solution.py:294
  10.3 2.2 %collective-permute-start.3 = (f32[3,8,512]{2,1,0:T(8,128)S(1)}, f32[3,8,512]{2,1,0:T(8,128)S(1)}, u32[]{:S(2)}, u32[]{:S(2)}) collective-permute-start(f32[3,8,512]{2,1,0:T(8,128)S(1)} %get-tuple-element.21), channel_id=1, source_target_pairs={{8,16},{16,8},{9,17},{17,9},{10,18},{18,10},{11,19},{19,11},{12,20... | collective-permute-start | bytes 147464 | tf_op jit(solution)/shard_map/ppermute | solution.py:293
  12.5 0.1 slice_bitcast_fusion.1
  12.6 0.6 %collective-permute-done.2.end_0 = f32[3,8,512]{2,1,0:T(8,128)S(1)} collective-permute-done((f32[3,8,512]{2,1,0:T(8,128)S(1)}, f32[3,8,512]{2,1,0:T(8,128)S(1)}, u32[]{:S(2)}, u32[]{:S(2)}) %collective-permute-start.2) | collective-permute-done | bytes 49184 | tf_op jit(solution)/shard_map/ppermute | solution.py:294
  13.2 4.0 %collective-permute-done.3.end_1 = f32[3,8,512]{2,1,0:T(8,128)S(1)} collective-permute-done((f32[3,8,512]{2,1,0:T(8,128)S(1)}, f32[3,8,512]{2,1,0:T(8,128)S(1)}, u32[]{:S(2)}, u32[]{:S(2)}) %collective-permute-start.3) | collective-permute-done | bytes 49184 | tf_op jit(solution)/shard_map/ppermute | solution.py:293
  17.2 1.6 %density.1 = f32[8,8,512]{2,1,0:T(8,128)S(1)} custom-call(f32[8,8,512]{2,1,0:T(8,128)S(1)} %get-tuple-element.16.field.latent, f32[2,8,512]{2,1,0:T(8,128)S(1)} %collective-permute-done.from_partner.side_0, f32[2,8,512]{2,1,0:T(8,128)S(1)} %collective-permute-done.1.from_outer.side_1, f32[3,8,512]{2,1,0:T(8,128)S(1)} %collective-permute-done.2.end_0, ...), custom_call_target="tpu_custom_call" | custom-call | tf_op jit(solution)/shard_map/density/pallas_call | solution.py:349
  18.8 0.0 all-to-all-done.got
  18.8 4.0 %binning.1 = (f32[8,8,512]{2,1,0:T(8,128)S(1)}, f32[2,8,512]{2,1,0:T(8,128)S(1)}, f32[2,8,512]{2,1,0:T(8,128)S(1)}) custom-call(f32[32,8,128]{2,1,0:T(8,128)S(1)} %all-to-all-done.got, f32[8,8,512]{2,1,0:T(8,128)S(1)} %density.1), custom_call_target="tpu_custom_call" | custom-call | tf_op jit(solution)/shard_map/binning/pallas_call | solution.py:359
  22.9 0.1 collective-permute-start.4
  23.0 3.5 %collective-permute-start.5 = (f32[2,8,512]{2,1,0:T(8,128)S(1)}, f32[2,8,512]{2,1,0:T(8,128)S(1)}, u32[]{:S(2)}, u32[]{:S(2)}) collective-permute-start(f32[2,8,512]{2,1,0:T(8,128)S(1)} %get-tuple-element.24), channel_id=1, source_target_pairs={{1,2},{3,4},{5,6},{7,0},{2,1},{4,3},{6,5},{0,7},{9,10},{11,12},{13... | collective-permute-start | bytes 98312 | tf_op jit(solution)/shard_map/ppermute | solution.py:293
  26.4 0.1 pad_bitcast_fusion
  26.5 1.7 %collective-permute-done.5.from_outer.side_1 = f32[2,8,512]{2,1,0:T(8,128)S(1)} collective-permute-done((f32[2,8,512]{2,1,0:T(8,128)S(1)}, f32[2,8,512]{2,1,0:T(8,128)S(1)}, u32[]{:S(2)}, u32[]{:S(2)}) %collective-permute-start.5) | collective-permute-done | bytes 32800 | tf_op jit(solution)/shard_map/ppermute | solution.py:293
  28.2 0.1 collective-permute-start.6
  28.3 2.3 %collective-permute-start.7 = (f32[3,8,512]{2,1,0:T(8,128)S(1)}, f32[3,8,512]{2,1,0:T(8,128)S(1)}, u32[]{:S(2)}, u32[]{:S(2)}) collective-permute-start(f32[3,8,512]{2,1,0:T(8,128)S(1)} %get-tuple-element.26), channel_id=1, source_target_pairs={{8,16},{16,8},{9,17},{17,9},{10,18},{18,10},{11,19},{19,11},{12,20... | collective-permute-start | bytes 147464 | tf_op jit(solution)/shard_map/ppermute | solution.py:293
  30.7 0.1 pad_maximum_fusion
  30.8 1.6 %collective-permute-done.6.end_0 = f32[3,8,512]{2,1,0:T(8,128)S(1)} collective-permute-done((f32[3,8,512]{2,1,0:T(8,128)S(1)}, f32[3,8,512]{2,1,0:T(8,128)S(1)}, u32[]{:S(2)}, u32[]{:S(2)}) %collective-permute-start.6) | collective-permute-done | bytes 49184 | tf_op jit(solution)/shard_map/ppermute | solution.py:294
  32.4 2.8 %collective-permute-done.7.end_1 = f32[3,8,512]{2,1,0:T(8,128)S(1)} collective-permute-done((f32[3,8,512]{2,1,0:T(8,128)S(1)}, f32[3,8,512]{2,1,0:T(8,128)S(1)}, u32[]{:S(2)}, u32[]{:S(2)}) %collective-permute-start.7) | collective-permute-done | bytes 49184 | tf_op jit(solution)/shard_map/ppermute | solution.py:293
  35.2 2.3 %back.1 = f32[8,8,512]{2,1,0:T(8,128)} custom-call(f32[8,8,512]{2,1,0:T(8,128)S(1)} %get-tuple-element.16.field.latent, f32[8,8,512]{2,1,0:T(8,128)S(1)} %get-tuple-element.22.field.upstream, f32[2,8,512]{2,1,0:T(8,128)S(1)} %collective-permute-done.4.from_partner.side_0, f32[2,8,512]{2,1,0:T(8,128)S(1)} %collective-permute-done.5.from_outer.side_1, ...), custom_call_target="tpu_custom_call" | custom-call | tf_op jit(solution)/shard_map/back/pallas_call | solution.py:369
  (9 shorter events, 0.1 us)
Async XLA Ops:
  1.9 6.9 %collective-permute-start = (f32[2,8,512]{2,1,0:T(8,128)S(1)}, f32[2,8,512]{2,1,0:T(8,128)S(1)}, u32[]{:S(2)}, u32[]{:S(2)}) collective-permute-start(f32[2,8,512]{2,1,0:T(8,128)S(1)} %get-tuple-element.18), channel_id=1, source_target_pairs={{0,1},{2,3},{4,5},{6,7},{1,0},{3,2},{5,4},{7,6},{8,9},{10,11},{12,... | collective-permute-start | bytes 98312 | tf_op jit(solution)/shard_map/ppermute | solution.py:294
  1.9 6.8 %collective-permute-start.1 = (f32[2,8,512]{2,1,0:T(8,128)S(1)}, f32[2,8,512]{2,1,0:T(8,128)S(1)}, u32[]{:S(2)}, u32[]{:S(2)}) collective-permute-start(f32[2,8,512]{2,1,0:T(8,128)S(1)} %get-tuple-element.19), channel_id=1, source_target_pairs={{1,2},{3,4},{5,6},{7,0},{2,1},{4,3},{6,5},{0,7},{9,10},{11,12},{13... | collective-permute-start | bytes 98312 | tf_op jit(solution)/shard_map/ppermute | solution.py:293
  5.6 3.1 %copy-start = (f32[2,27,512]{2,0,1:T(2,128)S(1)}, f32[2,27,512]{2,0,1:T(2,128)}, u32[]{:S(2)}) copy-start(f32[2,27,512]{2,0,1:T(2,128)} %param.13) | copy-start | bytes 331780
  5.6 13.2 %all-to-all-start = ((f32[32,8,128]{2,1,0:T(8,128)}), f32[32,8,128]{2,1,0:T(8,128)S(1)}, u32[]{:S(2)}, u32[]{:S(2)}) async-start(f32[32,8,128]{2,1,0:T(8,128)} %get-tuple-element.17), calls=%async_computation | async-start | bytes 262144 | tf_op jit(solution)/shard_map/all_to_all | solution.py:335
  8.8 4.4 %collective-permute-start.2 = (f32[3,8,512]{2,1,0:T(8,128)S(1)}, f32[3,8,512]{2,1,0:T(8,128)S(1)}, u32[]{:S(2)}, u32[]{:S(2)}) collective-permute-start(f32[3,8,512]{2,1,0:T(8,128)S(1)} %get-tuple-element.20), channel_id=1, source_target_pairs={{0,8},{16,24},{8,0},{24,16},{1,9},{17,25},{9,1},{25,17},{2,10},{18... | collective-permute-start | bytes 147464 | tf_op jit(solution)/shard_map/ppermute | solution.py:294
  10.3 6.9 %collective-permute-start.3 = (f32[3,8,512]{2,1,0:T(8,128)S(1)}, f32[3,8,512]{2,1,0:T(8,128)S(1)}, u32[]{:S(2)}, u32[]{:S(2)}) collective-permute-start(f32[3,8,512]{2,1,0:T(8,128)S(1)} %get-tuple-element.21), channel_id=1, source_target_pairs={{8,16},{16,8},{9,17},{17,9},{10,18},{18,10},{11,19},{19,11},{12,20... | collective-permute-start | bytes 147464 | tf_op jit(solution)/shard_map/ppermute | solution.py:293
  22.9 3.7 %collective-permute-start.4 = (f32[2,8,512]{2,1,0:T(8,128)S(1)}, f32[2,8,512]{2,1,0:T(8,128)S(1)}, u32[]{:S(2)}, u32[]{:S(2)}) collective-permute-start(f32[2,8,512]{2,1,0:T(8,128)S(1)} %get-tuple-element.23), channel_id=1, source_target_pairs={{0,1},{2,3},{4,5},{6,7},{1,0},{3,2},{5,4},{7,6},{8,9},{10,11},{12,... | collective-permute-start | bytes 98312 | tf_op jit(solution)/shard_map/ppermute | solution.py:294
  23.0 5.3 %collective-permute-start.5 = (f32[2,8,512]{2,1,0:T(8,128)S(1)}, f32[2,8,512]{2,1,0:T(8,128)S(1)}, u32[]{:S(2)}, u32[]{:S(2)}) collective-permute-start(f32[2,8,512]{2,1,0:T(8,128)S(1)} %get-tuple-element.24), channel_id=1, source_target_pairs={{1,2},{3,4},{5,6},{7,0},{2,1},{4,3},{6,5},{0,7},{9,10},{11,12},{13... | collective-permute-start | bytes 98312 | tf_op jit(solution)/shard_map/ppermute | solution.py:293
  28.2 4.2 %collective-permute-start.6 = (f32[3,8,512]{2,1,0:T(8,128)S(1)}, f32[3,8,512]{2,1,0:T(8,128)S(1)}, u32[]{:S(2)}, u32[]{:S(2)}) collective-permute-start(f32[3,8,512]{2,1,0:T(8,128)S(1)} %get-tuple-element.25), channel_id=1, source_target_pairs={{0,8},{16,24},{8,0},{24,16},{1,9},{17,25},{9,1},{25,17},{2,10},{18... | collective-permute-start | bytes 147464 | tf_op jit(solution)/shard_map/ppermute | solution.py:294
  28.3 6.9 %collective-permute-start.7 = (f32[3,8,512]{2,1,0:T(8,128)S(1)}, f32[3,8,512]{2,1,0:T(8,128)S(1)}, u32[]{:S(2)}, u32[]{:S(2)}) collective-permute-start(f32[3,8,512]{2,1,0:T(8,128)S(1)} %get-tuple-element.26), channel_id=1, source_target_pairs={{8,16},{16,8},{9,17},{17,9},{10,18},{18,10},{11,19},{19,11},{12,20... | collective-permute-start | bytes 147464 | tf_op jit(solution)/shard_map/ppermute | solution.py:293

commit v4 on v3

--- a/solution.py
+++ b/solution.py
@@ -75,24 +75,6 @@
         to_outer[place] = either(odd, bottom, top)
 
 
-def fill_wide(wide, rows, sides, ends):
-    height = len(rows)
-    tiles = unpack_sides(*sides, height)
-    for row in range(height):
-        wide[row + 2, :SUBLANES] = rows[row]
-        wide[row + 2, SUBLANES:] = tiles[row]
-    _, odd = position("lat")
-    from_partner, from_outer = ends
-    packs = [(from_partner[place], from_outer[place]) for place in range(3)]
-    above = [either(odd, partner, outer) for partner, outer in packs]
-    below = [either(odd, outer, partner) for partner, outer in packs]
-    for first, (one, two, corners) in ((0, above), (height + 2, below)):
-        wide[first, :SUBLANES] = one
-        wide[first + 1, :SUBLANES] = two
-        wide[first, SUBLANES:] = corners
-        wide[first + 1, SUBLANES:] = pltpu.roll(corners, 4, 0)
-
-
 def radial_shifts(field):
     radial = field.shape[-1]
     lane = lax.broadcasted_iota(jnp.int32, field.shape, field.ndim - 1)
@@ -102,23 +84,27 @@
     )
 
 
-def two_levels(wide, first_coef, second_coef, shifted, middle, write):
+def taps_of(coef, at):
+    return [jnp.broadcast_to(coef[k:k + 1, at], (SUBLANES, LANES)) for k in range(27)]
+
+
+def tiles_of_bins(radial, body):
+    def step(tile, _):
+        body(pl.ds(pl.multiple_of(tile * LANES, LANES), LANES))
+        return 0
+
+    lax.fori_loop(0, radial // LANES, step, 0)
+
+
+def first_level(wide, shifted, coef, centers, middle, real):
     reach, cols, radial = wide.shape
-    height = reach - 4
-    lat, _ = position("lat")
-    bounds = (lat > 0).astype(jnp.int32), (lat < lax.axis_size("lat") - 1).astype(jnp.int32)
-
     for row in range(reach):
         for place, moved in enumerate(radial_shifts(wide[row])):
             shifted[place, row] = moved
 
-    def taps_of(coef, at):
-        return [jnp.broadcast_to(coef[k:k + 1, at], (SUBLANES, LANES)) for k in range(27)]
-
-    def first_level(tile, _):
-        at = pl.ds(pl.multiple_of(tile * LANES, LANES), LANES)
-        taps = taps_of(first_coef, at)
-        for row in range(1, reach - 1):
+    def body(at):
+        taps = taps_of(coef, at)
+        for place, row in enumerate(centers):
             parts = []
             for side in (slice(0, SUBLANES), slice(SUBLANES, cols)):
                 sums = [None, None, None]
@@ -131,36 +117,80 @@
                 parts.append(sums)
             whole = [jnp.concatenate([parts[0][b], parts[1][b]], axis=0) for b in range(3)]
             value = whole[1] + pltpu.roll(whole[0], 1, 0) + pltpu.roll(whole[2], cols - 1, 0)
-            if row in (1, reach - 2):
-                value = either(bounds[row != 1], value, jnp.zeros_like(value))
-            middle[0, 0, row - 1, :, at] = pltpu.roll(value, 1, 0)[:SUBLANES]
-            middle[1, 0, row - 1, :, at] = value[:SUBLANES]
-            middle[2, 0, row - 1, :, at] = pltpu.roll(value, cols - 1, 0)[:SUBLANES]
-        return 0
-
-    lax.fori_loop(0, radial // LANES, first_level, 0)
-
-    for row in range(reach - 2):
+            if real[place] is not None:
+                value = either(real[place], value, jnp.zeros_like(value))
+            middle[0, 1, place, :, at] = pltpu.roll(value, 1, 0)[:SUBLANES]
+            middle[1, 1, place, :, at] = value[:SUBLANES]
+            middle[2, 1, place, :, at] = pltpu.roll(value, cols - 1, 0)[:SUBLANES]
+
+    tiles_of_bins(radial, body)
+    for place in range(len(centers)):
         for beside in range(3):
-            for place, moved in enumerate(radial_shifts(middle[beside, 0, row])):
-                middle[beside, place + 1, row] = moved
-
-    order = (1, 0, 2)
-
-    def second_level(tile, _):
-        at = pl.ds(pl.multiple_of(tile * LANES, LANES), LANES)
-        taps = taps_of(second_coef, at)
-        for row in range(height):
+            for step, moved in zip((0, 2), radial_shifts(middle[beside, 1, place])):
+                middle[beside, step, place] = moved
+
+
+def second_level(coef, windows, radial, write):
+    def body(at):
+        taps = taps_of(coef, at)
+        for row, around in windows.items():
             total = None
-            for above in range(3):
+            for above, (buffer, place) in enumerate(around):
                 for beside in range(3):
                     for step in range(3):
-                        term = taps[above * 9 + beside * 3 + step] * middle[beside, order[step], row + above, :, at]
+                        term = taps[above * 9 + beside * 3 + step] * buffer[beside, step, place, :, at]
                         total = term if total is None else total + term
             write(row, at, total)
-        return 0
-
-    lax.fori_loop(0, radial // LANES, second_level, 0)
+
+    tiles_of_bins(radial, body)
+
+
+def refine_inside_kernel(coefs, finish, field, side_0, side_1, stencils, extra, out, middle, wide, shifted):
+    height, width, radial = field.shape
+    tiles = unpack_sides(side_0, side_1, height)
+    for row in range(height):
+        wide[row, :width] = field[row]
+        wide[row, width:] = tiles[row]
+    first_level(wide, shifted, stencils.at[coefs[0]], range(1, height - 1), middle, [None] * (height - 2))
+
+    def write(row, at, value):
+        out[row - 2, :, at] = finish(value, extra[row, :, at])
+
+    windows = {row: [(middle, row - 2 + k) for k in range(3)] for row in range(2, height - 2)}
+    second_level(stencils.at[coefs[1]], windows, radial, write)
+
+
+def refine_ends_kernel(
+    coefs, finish, field, side_0, side_1, end_0, end_1, stencils, extra, inside, inner, out, middle, wide, shifted
+):
+    height, width, radial = field.shape
+    tiles = unpack_sides(side_0, side_1, height)
+    lat, odd = position("lat")
+    for place in range(3):
+        partner, outer = end_0[place], end_1[place]
+        for first, pack in ((0, either(odd, partner, outer)), (6, either(odd, outer, partner))):
+            if place < 2:
+                wide[first + place, :width] = pack
+            else:
+                wide[first, width:] = pack
+                wide[first + 1, width:] = pltpu.roll(pack, 4, 0)
+    for place, row in ((2, 0), (3, 1), (4, height - 2), (5, height - 1)):
+        wide[place, :width] = field[row]
+        wide[place, width:] = tiles[row]
+    above = (lat > 0).astype(jnp.int32)
+    below = (lat < lax.axis_size("lat") - 1).astype(jnp.int32)
+    first_level(wide, shifted, stencils.at[coefs[0]], (1, 2, 5, 6), middle, [above, None, None, below])
+
+    def write(row, at, value):
+        out[row, :, at] = finish(value, extra[row, :, at])
+
+    last = height - 3
+    top = [(middle, 0), (middle, 1), (inside, 0), (inside, 1)]
+    bottom = [(inside, last - 1), (inside, last), (middle, 2), (middle, 3)]
+    windows = {0: top[:3], 1: top[1:], height - 2: bottom[:3], height - 1: bottom[1:]}
+    second_level(stencils.at[coefs[1]], windows, radial, write)
+    for row in range(2, height - 2):
+        out[row] = inner[row - 2]
 
 
 def open_kernel(
@@ -203,13 +233,14 @@
     half = radial // 2
     classes = 2 * pixels
     shards = got.shape[0]
-    column = lax.broadcasted_iota(jnp.int32, (classes, LANES), 0).astype(jnp.float32).astype(jnp.bfloat16)
-    place = lax.broadcasted_iota(jnp.int32, (half, LANES), 0).astype(jnp.float32).astype(jnp.bfloat16)
-    zero = jnp.zeros((), jnp.bfloat16)
-    one = jnp.ones((), jnp.bfloat16)
+    bf16 = jnp.bfloat16
+    column = lax.broadcasted_iota(jnp.int32, (classes, LANES), 0).astype(jnp.float32).astype(bf16)
+    place = (lax.broadcasted_iota(jnp.int32, (half, LANES), 0) + 1).astype(jnp.float32).astype(bf16)
+    zero = jnp.zeros((), bf16)
+    one = jnp.ones((), bf16)
 
     def tall(row, height):
-        return jnp.concatenate([jnp.broadcast_to(row, (16, LANES)).astype(jnp.bfloat16)] * (height // 16), axis=0)
+        return jnp.concatenate([jnp.broadcast_to(row, (16, LANES)).astype(bf16)] * (height // 16), axis=0)
 
     def product(shard):
         tile = got[shard]
@@ -218,17 +249,18 @@
         bins = lax.bitwise_and(cell, radial - 1)
         upper = (bins >= half).astype(jnp.int32)
         label = (upper * pixels + pixel).astype(jnp.float32)
-        low = (bins - upper * half).astype(jnp.float32)
-        coarse = tile.astype(jnp.bfloat16).astype(jnp.float32)
+        low = (bins - upper * half + 1).astype(jnp.float32)
+        coarse = tile.astype(bf16).astype(jnp.float32)
         rest = tile - coarse
         left, right = [], []
         for run in range(RUNS):
-            mine = tall(label[RUNS + run:RUNS + run + 1], classes) == column
+            away = tall(label[RUNS + run:RUNS + run + 1], classes) - column
+            mine = jnp.maximum(one - away * away, zero)
             left.append(jnp.concatenate([
-                jnp.where(mine, tall(coarse[run:run + 1], classes), zero),
-                jnp.where(mine, tall(rest[run:run + 1], classes), zero),
+                mine * tall(coarse[run:run + 1], classes),
+                mine * tall(rest[run:run + 1], classes),
             ], axis=0))
-            right.append(jnp.where(tall(low[RUNS + run:RUNS + run + 1], half) >= place, one, zero))
+            right.append(jnp.maximum(tall(low[RUNS + run:RUNS + run + 1], half), place))
         return lax.dot_general(
             jnp.concatenate(left, axis=1), jnp.concatenate(right, axis=1),
             (((1,), (1,)), ((), ())), preferred_element_type=jnp.float32,
@@ -241,7 +273,10 @@
 
     total = lax.fori_loop(0, shards // 4, step, jnp.zeros((2 * classes, half), jnp.float32))
     both = (total[:classes] + total[classes:]) * bin_width
-    near, far = both[:pixels], both[pixels:]
+    every = both[:, half - 1:] * (1.0 / half)
+    lane = lax.broadcasted_iota(jnp.int32, both.shape, 1)
+    at_least = jnp.where(lane == 0, every, pltpu.roll(both, 1, 1) - both + every)
+    near, far = at_least[:pixels], at_least[pixels:]
     return near + far[:, :1], far
 
 
@@ -256,24 +291,6 @@
     pack_sides(rows, to_partner, to_outer)
 
 
-def density_kernel(latent, side_0, side_1, end_0, end_1, stencils, out, wide, shifted, middle):
-    fill_wide(wide, [latent[row] for row in range(latent.shape[0])], (side_0, side_1), (end_0, end_1))
-
-    def write(row, at, value):
-        out[row, :, at] = jnp.exp(value)
-
-    two_levels(wide, stencils.at[0], stencils.at[1], shifted, middle, write)
-
-
-def back_kernel(latent, upstream, side_0, side_1, end_0, end_1, mirrored, out, wide, shifted, middle):
-    fill_wide(wide, [upstream[row] for row in range(upstream.shape[0])], (side_0, side_1), (end_0, end_1))
-
-    def write(row, at, value):
-        out[row, :, at] = latent[row, :, at] + value
-
-    two_levels(wide, mirrored.at[1], mirrored.at[0], shifted, middle, write)
-
-
 def mirror(stencils):
     turned = jnp.flip(stencils, axis=1).reshape(stencils.shape[0], 9, 3, stencils.shape[2])
     edge = jnp.zeros_like(turned[:, :, 0, :1])
@@ -308,17 +325,11 @@
     tile = jax.ShapeDtypeStruct((height, width, radial), f32)
     sides = jax.ShapeDtypeStruct((height // 4, SUBLANES, radial), f32)
     ends = jax.ShapeDtypeStruct((3, SUBLANES, radial), f32)
-    reach, cols = height + 4, 2 * width
-    level_scratch = [
-        pltpu.VMEM((reach, cols, radial), f32),
-        pltpu.VMEM((2, reach, cols, radial), f32),
-        pltpu.VMEM((3, 3, reach - 2, width, radial), f32),
-    ]
 
     def table(values):
         return values.reshape(slots // LANES, LANES)
 
-    packed, latent, to_partner, to_outer = pl.pallas_call(
+    packed, latent, *to_sides = pl.pallas_call(
         open_kernel,
         out_shape=(jax.ShapeDtypeStruct((shards, 2 * RUNS, LANES), f32), tile, sides, sides),
         in_specs=[HBM] * 6,
@@ -334,29 +345,43 @@
     ])
     got = lax.all_to_all(packed, ("lat", "lon"), split_axis=0, concat_axis=0, tiled=True)
 
-    def pack_ends(field, beside):
-        return pl.pallas_call(
+    def refined(field, to_sides, coefs, table, extra, finish, name):
+        beside = swap(*to_sides, "lon", True)
+        to_ends = pl.pallas_call(
             pack_ends_kernel,
             out_shape=(ends, ends),
             in_specs=[VMEM] * 3,
             out_specs=(VMEM, VMEM),
             compiler_params=LIMIT,
-            name="pack_ends",
+            name=name + "_pack",
         )(field, *beside)
-
-    beside = swap(to_partner, to_outer, "lon", True)
-    above = swap(*pack_ends(latent, beside), "lat", False)
-    density = pl.pallas_call(
-        density_kernel,
-        out_shape=tile,
-        in_specs=[VMEM] * 6,
-        out_specs=VMEM,
-        scratch_shapes=level_scratch,
-        compiler_params=LIMIT,
-        name="density",
-    )(latent, *beside, *above, stencils)
-
-    upstream, to_partner, to_outer = pl.pallas_call(
+        above = swap(*to_ends, "lat", False)
+        rows = pltpu.VMEM((height, 2 * width, radial), f32)
+        moved = pltpu.VMEM((2, height, 2 * width, radial), f32)
+        inner, middle = pl.pallas_call(
+            functools.partial(refine_inside_kernel, coefs, finish),
+            out_shape=(
+                jax.ShapeDtypeStruct((height - 4, width, radial), f32),
+                jax.ShapeDtypeStruct((3, 3, height - 2, width, radial), f32),
+            ),
+            in_specs=[VMEM] * 5,
+            out_specs=(VMEM, VMEM),
+            scratch_shapes=[rows, moved],
+            compiler_params=LIMIT,
+            name=name + "_inside",
+        )(field, *beside, table, extra)
+        return pl.pallas_call(
+            functools.partial(refine_ends_kernel, coefs, finish),
+            out_shape=tile,
+            in_specs=[VMEM] * 9,
+            out_specs=VMEM,
+            scratch_shapes=[pltpu.VMEM((3, 3, 4, width, radial), f32), rows, moved],
+            compiler_params=LIMIT,
+            name=name + "_ends",
+        )(field, *beside, *above, table, extra, middle, inner)
+
+    density = refined(latent, to_sides, (0, 1), stencils, latent, lambda value, _: jnp.exp(value), "density")
+    upstream, *to_sides = pl.pallas_call(
         bin_kernel,
         out_shape=(tile, sides, sides),
         in_specs=[VMEM, VMEM],
@@ -364,17 +389,7 @@
         compiler_params=LIMIT,
         name="binning",
     )(got, density)
-    beside = swap(to_partner, to_outer, "lon", True)
-    above = swap(*pack_ends(upstream, beside), "lat", False)
-    return pl.pallas_call(
-        back_kernel,
-        out_shape=tile,
-        in_specs=[VMEM] * 7,
-        out_specs=VMEM,
-        scratch_shapes=level_scratch,
-        compiler_params=LIMIT,
-        name="back",
-    )(latent, upstream, *beside, *above, mirror(stencils))
+    return refined(upstream, to_sides, (1, 0), mirror(stencils), latent, lambda value, field: field + value, "back")
 
 
 def solution(mesh):

time: 37.7 us -> 36.4 us (0.966)
  waiting for transfers between devices: 10.7 us -> 8.38 us
  Pallas kernels: 9.81 us -> 10.7 us
    ppermute x4, waiting for transfers between devices: 2.21 us -> 0.4 us  [swap(): return (lax.ppermute(to_partner, axis, both_ways(inner)), from_outer)]
    pallas_call x4 -> x6, Pallas kernels: 3.93 us -> 4.64 us  [the longest x2 2.48 us: refined(): pl.pallas_call(functools.partial(refine_ends_kernel, coefs, finish), out_...]
    ppermute x4, waiting for transfers between devices: 8.49 us -> 7.97 us  [swap(): from_outer = lax.ppermute(to_outer, axis, both_ways(outer))]
  transfers between devices with their start and end apart: 9 -> 9, of which waited for: 5 -> 4; matrix products, arithmetic and copies ran while one was open for 1% -> 1% of each run, Pallas kernels for 4% -> 8%
where the time goes in v4:
time: 36.4 us; the launch traced here: 36.2 us
  starting transfers between devices  16.7 us (46%)
  Pallas kernels  10.7 us (29%)
  waiting for transfers between devices  8.38 us (23%)
    ppermute x4, starting transfers between devices, swap(): from_outer = lax.ppermute(to_outer, axis, both_ways(outer))  11.9 us
    ppermute x4, waiting for transfers between devices, swap(): from_outer = lax.ppermute(to_outer, axis, both_ways(outer))  7.97 us
    pallas_call x1, Pallas kernels, on_device(): pl.pallas_call(bin_kernel, out_shape=(tile, sides, sides), in_specs=[VMEM...  4.18 us
    all_to_all x1, starting transfers between devices, on_device(): lax.all_to_all(packed, ('lat', 'lon'), split_axis=0, concat_axis=0, tiled...  3.06 us
    pallas_call x2, Pallas kernels, refined(): pl.pallas_call(functools.partial(refine_ends_kernel, coefs, finish), out_...  2.48 us
    pallas_call x2, Pallas kernels, refined(): pl.pallas_call(functools.partial(refine_inside_kernel, coefs, finish), ou...  2.12 us
    pallas_call x1, Pallas kernels, on_device(): pl.pallas_call(open_kernel, out_shape=(jax.ShapeDtypeStruct((shards, 2 *...  1.84 us
    ppermute x4, starting transfers between devices, swap(): return (lax.ppermute(to_partner, axis, both_ways(inner)), from_outer)  1.74 us
  transfers between devices with their start and end apart: 9, of which 4 were waited for; matrix products, arithmetic and copies ran while one was open for 1% of the time, Pallas kernels for 8%

profile of v4, /device:TPU:4, one launch (start us, length us, event | category | flops | bytes accessed | tf_op | source)
XLA Modules:
  0.0 36.2 jit_solution(5986300204355549945)
XLA Ops:
  0.0 1.8 %opening.1 = (f32[32,8,128]{2,1,0:T(8,128)}, f32[8,8,512]{2,1,0:T(8,128)S(1)}, f32[2,8,512]{2,1,0:T(8,128)S(1)}, f32[2,8,512]{2,1,0:T(8,128)S(1)}) custom-call(s32[1,32]{1,0:T(1,128)} %counts_in.1, s32[1,32]{1,0:T(1,128)} %offsets_in.1, f32[128,128]{1,0:T(8,128)} %bitcast.20, s32[128,128]{1,0:T(8,128)} %bitcast.21, s32[128,128]{1,0:T(8,128)} %bitcast.22, ...), custom_call_target="tpu_custom_call" | custom-call | tf_op jit(solution)/shard_map/opening/pallas_call | solution.py:332
  1.9 0.1 collective-permute-start
  1.9 3.7 %collective-permute-start.1 = (f32[2,8,512]{2,1,0:T(8,128)S(1)}, f32[2,8,512]{2,1,0:T(8,128)S(1)}, u32[]{:S(2)}, u32[]{:S(2)}) collective-permute-start(f32[2,8,512]{2,1,0:T(8,128)S(1)} %get-tuple-element.23), channel_id=1, source_target_pairs={{1,2},{3,4},{5,6},{7,0},{2,1},{4,3},{6,5},{0,7},{9,10},{11,12},{13... | collective-permute-start | bytes 98312 | tf_op jit(solution)/shard_map/ppermute | solution.py:310
  5.6 3.1 %all-to-all-start = ((f32[32,8,128]{2,1,0:T(8,128)}), f32[32,8,128]{2,1,0:T(8,128)S(1)}, u32[]{:S(2)}, u32[]{:S(2)}) async-start(f32[32,8,128]{2,1,0:T(8,128)} %get-tuple-element.20), calls=%async_computation | async-start | bytes 262144 | tf_op jit(solution)/shard_map/all_to_all | solution.py:346
  8.7 0.0 collective-permute-done.from_partner.side_0
  8.7 0.0 collective-permute-done.1.from_outer.side_1
  8.8 1.5 %collective-permute-start.2 = (f32[3,8,512]{2,1,0:T(8,128)S(1)}, f32[3,8,512]{2,1,0:T(8,128)S(1)}, u32[]{:S(2)}, u32[]{:S(2)}) collective-permute-start(f32[3,8,512]{2,1,0:T(8,128)S(1)} %get-tuple-element.24), channel_id=1, source_target_pairs={{0,8},{16,24},{8,0},{24,16},{1,9},{17,25},{9,1},{25,17},{2,10},{18... | collective-permute-start | bytes 147464 | tf_op jit(solution)/shard_map/ppermute | solution.py:311
  10.3 2.2 %collective-permute-start.3 = (f32[3,8,512]{2,1,0:T(8,128)S(1)}, f32[3,8,512]{2,1,0:T(8,128)S(1)}, u32[]{:S(2)}, u32[]{:S(2)}) collective-permute-start(f32[3,8,512]{2,1,0:T(8,128)S(1)} %get-tuple-element.25), channel_id=1, source_target_pairs={{8,16},{16,8},{9,17},{17,9},{10,18},{18,10},{11,19},{19,11},{12,20... | collective-permute-start | bytes 147464 | tf_op jit(solution)/shard_map/ppermute | solution.py:310
  12.5 0.1 slice_bitcast_fusion.1
  12.6 1.1 %density_inside.1 = (f32[4,8,512]{2,1,0:T(8,128)S(1)}, f32[3,3,6,8,512]{4,3,2,1,0:T(8,128)S(1)}) custom-call(f32[8,8,512]{2,1,0:T(8,128)S(1)} %get-tuple-element.21.field.extra, f32[2,8,512]{2,1,0:T(8,128)S(1)} %collective-permute-done.from_partner.side_0, f32[2,8,512]{2,1,0:T(8,128)S(1)} %collective-permute-done.1.from_outer.side_1, ...), custom_call_target="tpu_custom_call" | custom-call | tf_op jit(solution)/shard_map/density_inside/pallas_call | solution.py:361
  13.7 3.5 %collective-permute-done.3.end_1 = f32[3,8,512]{2,1,0:T(8,128)S(1)} collective-permute-done((f32[3,8,512]{2,1,0:T(8,128)S(1)}, f32[3,8,512]{2,1,0:T(8,128)S(1)}, u32[]{:S(2)}, u32[]{:S(2)}) %collective-permute-start.3) | collective-permute-done | bytes 49184 | tf_op jit(solution)/shard_map/ppermute | solution.py:310
  17.2 0.9 %density_ends.1.density = f32[8,8,512]{2,1,0:T(8,128)S(1)} custom-call(f32[8,8,512]{2,1,0:T(8,128)S(1)} %get-tuple-element.21.field.extra, f32[2,8,512]{2,1,0:T(8,128)S(1)} %collective-permute-done.from_partner.side_0, f32[2,8,512]{2,1,0:T(8,128)S(1)} %collective-permute-done.1.from_outer.side_1, f32[3,8,512]{2,1,0:T(8,128)S(1)} %collective-permute-done.2.end_0, ...), custom_call_target="tpu_custom_call" | custom-call | tf_op jit(solution)/shard_map/density_ends/pallas_call | solution.py:373
  18.1 4.2 %binning.1 = (f32[8,8,512]{2,1,0:T(8,128)S(1)}, f32[2,8,512]{2,1,0:T(8,128)S(1)}, f32[2,8,512]{2,1,0:T(8,128)S(1)}) custom-call(f32[32,8,128]{2,1,0:T(8,128)S(1)} %all-to-all-done.got, f32[8,8,512]{2,1,0:T(8,128)S(1)} %density_ends.1.density), custom_call_target="tpu_custom_call" | custom-call | tf_op jit(solution)/shard_map/binning/pallas_call | solution.py:384
  22.3 0.1 collective-permute-start.4
  22.4 3.5 %collective-permute-start.5 = (f32[2,8,512]{2,1,0:T(8,128)S(1)}, f32[2,8,512]{2,1,0:T(8,128)S(1)}, u32[]{:S(2)}, u32[]{:S(2)}) collective-permute-start(f32[2,8,512]{2,1,0:T(8,128)S(1)} %get-tuple-element.30), channel_id=1, source_target_pairs={{1,2},{3,4},{5,6},{7,0},{2,1},{4,3},{6,5},{0,7},{9,10},{11,12},{13... | collective-permute-start | bytes 98312 | tf_op jit(solution)/shard_map/ppermute | solution.py:310
  25.9 0.1 pad_bitcast_fusion
  26.0 1.7 %collective-permute-done.5.from_outer.side_1 = f32[2,8,512]{2,1,0:T(8,128)S(1)} collective-permute-done((f32[2,8,512]{2,1,0:T(8,128)S(1)}, f32[2,8,512]{2,1,0:T(8,128)S(1)}, u32[]{:S(2)}, u32[]{:S(2)}) %collective-permute-start.5) | collective-permute-done | bytes 32800 | tf_op jit(solution)/shard_map/ppermute | solution.py:310
  27.7 0.1 collective-permute-start.6
  27.8 2.5 %collective-permute-start.7 = (f32[3,8,512]{2,1,0:T(8,128)S(1)}, f32[3,8,512]{2,1,0:T(8,128)S(1)}, u32[]{:S(2)}, u32[]{:S(2)}) collective-permute-start(f32[3,8,512]{2,1,0:T(8,128)S(1)} %get-tuple-element.32), channel_id=1, source_target_pairs={{8,16},{16,8},{9,17},{17,9},{10,18},{18,10},{11,19},{19,11},{12,20... | collective-permute-start | bytes 147464 | tf_op jit(solution)/shard_map/ppermute | solution.py:310
  30.3 0.1 pad_maximum_fusion
  30.4 1.1 %back_inside.1 = (f32[4,8,512]{2,1,0:T(8,128)S(1)}, f32[3,3,6,8,512]{4,3,2,1,0:T(8,128)S(1)}) custom-call(f32[8,8,512]{2,1,0:T(8,128)S(1)} %get-tuple-element.28.field, f32[2,8,512]{2,1,0:T(8,128)S(1)} %collective-permute-done.4.from_partner.side_0, f32[2,8,512]{2,1,0:T(8,128)S(1)} %collective-permute-done.5.from_outer.side_1, ...), custom_call_target="tpu_custom_call" | custom-call | tf_op jit(solution)/shard_map/back_inside/pallas_call | solution.py:361
  31.4 0.4 %collective-permute-done.6.end_0 = f32[3,8,512]{2,1,0:T(8,128)S(1)} collective-permute-done((f32[3,8,512]{2,1,0:T(8,128)S(1)}, f32[3,8,512]{2,1,0:T(8,128)S(1)}, u32[]{:S(2)}, u32[]{:S(2)}) %collective-permute-start.6) | collective-permute-done | bytes 49184 | tf_op jit(solution)/shard_map/ppermute | solution.py:311
  31.8 2.8 %collective-permute-done.7.end_1 = f32[3,8,512]{2,1,0:T(8,128)S(1)} collective-permute-done((f32[3,8,512]{2,1,0:T(8,128)S(1)}, f32[3,8,512]{2,1,0:T(8,128)S(1)}, u32[]{:S(2)}, u32[]{:S(2)}) %collective-permute-start.7) | collective-permute-done | bytes 49184 | tf_op jit(solution)/shard_map/ppermute | solution.py:310
  34.6 1.6 %back_ends.1 = f32[8,8,512]{2,1,0:T(8,128)} custom-call(f32[8,8,512]{2,1,0:T(8,128)S(1)} %get-tuple-element.28.field, f32[2,8,512]{2,1,0:T(8,128)S(1)} %collective-permute-done.4.from_partner.side_0, f32[2,8,512]{2,1,0:T(8,128)S(1)} %collective-permute-done.5.from_outer.side_1, f32[3,8,512]{2,1,0:T(8,128)S(1)} %collective-permute-done.6.end_0, ...), custom_call_target="tpu_custom_call" | custom-call | tf_op jit(solution)/shard_map/back_ends/pallas_call | solution.py:373
  (11 shorter events, 0.1 us)
Async XLA Ops:
  1.9 6.9 %collective-permute-start = (f32[2,8,512]{2,1,0:T(8,128)S(1)}, f32[2,8,512]{2,1,0:T(8,128)S(1)}, u32[]{:S(2)}, u32[]{:S(2)}) collective-permute-start(f32[2,8,512]{2,1,0:T(8,128)S(1)} %get-tuple-element.22), channel_id=1, source_target_pairs={{0,1},{2,3},{4,5},{6,7},{1,0},{3,2},{5,4},{7,6},{8,9},{10,11},{12,... | collective-permute-start | bytes 98312 | tf_op jit(solution)/shard_map/ppermute | solution.py:311
  1.9 6.8 %collective-permute-start.1 = (f32[2,8,512]{2,1,0:T(8,128)S(1)}, f32[2,8,512]{2,1,0:T(8,128)S(1)}, u32[]{:S(2)}, u32[]{:S(2)}) collective-permute-start(f32[2,8,512]{2,1,0:T(8,128)S(1)} %get-tuple-element.23), channel_id=1, source_target_pairs={{1,2},{3,4},{5,6},{7,0},{2,1},{4,3},{6,5},{0,7},{9,10},{11,12},{13... | collective-permute-start | bytes 98312 | tf_op jit(solution)/shard_map/ppermute | solution.py:310
  5.6 3.1 %copy-start = (f32[2,27,512]{2,0,1:T(2,128)S(1)}, f32[2,27,512]{2,0,1:T(2,128)}, u32[]{:S(2)}) copy-start(f32[2,27,512]{2,0,1:T(2,128)} %param.13) | copy-start | bytes 331780
  5.6 12.5 %all-to-all-start = ((f32[32,8,128]{2,1,0:T(8,128)}), f32[32,8,128]{2,1,0:T(8,128)S(1)}, u32[]{:S(2)}, u32[]{:S(2)}) async-start(f32[32,8,128]{2,1,0:T(8,128)} %get-tuple-element.20), calls=%async_computation | async-start | bytes 262144 | tf_op jit(solution)/shard_map/all_to_all | solution.py:346
  8.8 4.9 %collective-permute-start.2 = (f32[3,8,512]{2,1,0:T(8,128)S(1)}, f32[3,8,512]{2,1,0:T(8,128)S(1)}, u32[]{:S(2)}, u32[]{:S(2)}) collective-permute-start(f32[3,8,512]{2,1,0:T(8,128)S(1)} %get-tuple-element.24), channel_id=1, source_target_pairs={{0,8},{16,24},{8,0},{24,16},{1,9},{17,25},{9,1},{25,17},{2,10},{18... | collective-permute-start | bytes 147464 | tf_op jit(solution)/shard_map/ppermute | solution.py:311
  10.3 6.9 %collective-permute-start.3 = (f32[3,8,512]{2,1,0:T(8,128)S(1)}, f32[3,8,512]{2,1,0:T(8,128)S(1)}, u32[]{:S(2)}, u32[]{:S(2)}) collective-permute-start(f32[3,8,512]{2,1,0:T(8,128)S(1)} %get-tuple-element.25), channel_id=1, source_target_pairs={{8,16},{16,8},{9,17},{17,9},{10,18},{18,10},{11,19},{19,11},{12,20... | collective-permute-start | bytes 147464 | tf_op jit(solution)/shard_map/ppermute | solution.py:310
  22.3 3.7 %collective-permute-start.4 = (f32[2,8,512]{2,1,0:T(8,128)S(1)}, f32[2,8,512]{2,1,0:T(8,128)S(1)}, u32[]{:S(2)}, u32[]{:S(2)}) collective-permute-start(f32[2,8,512]{2,1,0:T(8,128)S(1)} %get-tuple-element.29), channel_id=1, source_target_pairs={{0,1},{2,3},{4,5},{6,7},{1,0},{3,2},{5,4},{7,6},{8,9},{10,11},{12,... | collective-permute-start | bytes 98312 | tf_op jit(solution)/shard_map/ppermute | solution.py:311
  22.4 5.3 %collective-permute-start.5 = (f32[2,8,512]{2,1,0:T(8,128)S(1)}, f32[2,8,512]{2,1,0:T(8,128)S(1)}, u32[]{:S(2)}, u32[]{:S(2)}) collective-permute-start(f32[2,8,512]{2,1,0:T(8,128)S(1)} %get-tuple-element.30), channel_id=1, source_target_pairs={{1,2},{3,4},{5,6},{7,0},{2,1},{4,3},{6,5},{0,7},{9,10},{11,12},{13... | collective-permute-start | bytes 98312 | tf_op jit(solution)/shard_map/ppermute | solution.py:310
  27.7 4.2 %collective-permute-start.6 = (f32[3,8,512]{2,1,0:T(8,128)S(1)}, f32[3,8,512]{2,1,0:T(8,128)S(1)}, u32[]{:S(2)}, u32[]{:S(2)}) collective-permute-start(f32[3,8,512]{2,1,0:T(8,128)S(1)} %get-tuple-element.31), channel_id=1, source_target_pairs={{0,8},{16,24},{8,0},{24,16},{1,9},{17,25},{9,1},{25,17},{2,10},{18... | collective-permute-start | bytes 147464 | tf_op jit(solution)/shard_map/ppermute | solution.py:311
  27.8 6.9 %collective-permute-start.7 = (f32[3,8,512]{2,1,0:T(8,128)S(1)}, f32[3,8,512]{2,1,0:T(8,128)S(1)}, u32[]{:S(2)}, u32[]{:S(2)}) collective-permute-start(f32[3,8,512]{2,1,0:T(8,128)S(1)} %get-tuple-element.32), channel_id=1, source_target_pairs={{8,16},{16,8},{9,17},{17,9},{10,18},{18,10},{11,19},{19,11},{12,20... | collective-permute-start | bytes 147464 | tf_op jit(solution)/shard_map/ppermute | solution.py:310

commit v5 on v4

--- a/solution.py
+++ b/solution.py
@@ -161,8 +161,9 @@
 
 
 def refine_ends_kernel(
-    coefs, finish, field, side_0, side_1, end_0, end_1, stencils, extra, inside, inner, out, middle, wide, shifted
+    coefs, finish, finish_inner, packs, field, side_0, side_1, end_0, end_1, stencils, extra, inside, inner, *rest
 ):
+    out, *to_sides, middle, wide, shifted = rest
     height, width, radial = field.shape
     tiles = unpack_sides(side_0, side_1, height)
     lat, odd = position("lat")
@@ -190,7 +191,9 @@
     windows = {0: top[:3], 1: top[1:], height - 2: bottom[:3], height - 1: bottom[1:]}
     second_level(stencils.at[coefs[1]], windows, radial, write)
     for row in range(2, height - 2):
-        out[row] = inner[row - 2]
+        out[row] = finish_inner(inner[row - 2], extra[row])
+    if packs:
+        pack_sides([out[row] for row in range(height)], *to_sides)
 
 
 def open_kernel(
@@ -232,46 +235,42 @@
 def behind_of(got, *, radial, pixels):
     half = radial // 2
     classes = 2 * pixels
-    shards = got.shape[0]
+    shards, rows, _ = got.shape
     bf16 = jnp.bfloat16
     column = lax.broadcasted_iota(jnp.int32, (classes, LANES), 0).astype(jnp.float32).astype(bf16)
-    place = (lax.broadcasted_iota(jnp.int32, (half, LANES), 0) + 1).astype(jnp.float32).astype(bf16)
+    places = [
+        (lax.broadcasted_iota(jnp.int32, (LANES, LANES), 1) + (first + 1)).astype(jnp.float32).astype(bf16)
+        for first in range(0, half, LANES)
+    ]
     zero = jnp.zeros((), bf16)
     one = jnp.ones((), bf16)
 
-    def tall(row, height):
-        return jnp.concatenate([jnp.broadcast_to(row, (16, LANES)).astype(bf16)] * (height // 16), axis=0)
-
-    def product(shard):
-        tile = got[shard]
-        cell = tile.astype(jnp.int32)
-        pixel = lax.shift_right_logical(cell, radial.bit_length() - 1)
-        bins = lax.bitwise_and(cell, radial - 1)
-        upper = (bins >= half).astype(jnp.int32)
-        label = (upper * pixels + pixel).astype(jnp.float32)
-        low = (bins - upper * half + 1).astype(jnp.float32)
-        coarse = tile.astype(bf16).astype(jnp.float32)
-        rest = tile - coarse
+    def tall(row):
+        return jnp.concatenate([jnp.broadcast_to(row, (16, LANES)).astype(bf16)] * (classes // 16), axis=0)
+
+    tiles = got[...].reshape(shards * rows, LANES)
+    cell = tiles.astype(jnp.int32)
+    pixel = lax.shift_right_logical(cell, radial.bit_length() - 1)
+    bins = lax.bitwise_and(cell, radial - 1)
+    upper = (bins >= half).astype(jnp.int32)
+    label = (upper * pixels + pixel).astype(jnp.float32)
+    lows = jnp.transpose((bins - upper * half + 1).astype(jnp.float32))
+    coarse = tiles.astype(bf16).astype(jnp.float32)
+    rest = tiles - coarse
+
+    total = jnp.zeros((2 * classes, half), jnp.float32)
+    for first in range(0, shards, 2):
         left, right = [], []
-        for run in range(RUNS):
-            away = tall(label[RUNS + run:RUNS + run + 1], classes) - column
+        for run in range(2 * RUNS):
+            row = (first + run // RUNS) * rows + run % RUNS
+            away = tall(label[row + RUNS:row + RUNS + 1]) - column
             mine = jnp.maximum(one - away * away, zero)
-            left.append(jnp.concatenate([
-                mine * tall(coarse[run:run + 1], classes),
-                mine * tall(rest[run:run + 1], classes),
-            ], axis=0))
-            right.append(jnp.maximum(tall(low[RUNS + run:RUNS + run + 1], half), place))
-        return lax.dot_general(
-            jnp.concatenate(left, axis=1), jnp.concatenate(right, axis=1),
-            (((1,), (1,)), ((), ())), preferred_element_type=jnp.float32,
+            left.append(jnp.concatenate([mine * tall(coarse[row:row + 1]), mine * tall(rest[row:row + 1])], axis=0))
+            low = jnp.broadcast_to(lows[:, row + RUNS:row + RUNS + 1], (LANES, LANES)).astype(bf16)
+            right.append(jnp.concatenate([jnp.maximum(low, place) for place in places], axis=1))
+        total = total + jnp.dot(
+            jnp.concatenate(left, axis=1), jnp.concatenate(right, axis=0), preferred_element_type=jnp.float32
         )
-
-    def step(turn, total):
-        for member in range(4):
-            total = total + product(4 * turn + member)
-        return total
-
-    total = lax.fori_loop(0, shards // 4, step, jnp.zeros((2 * classes, half), jnp.float32))
     both = (total[:classes] + total[classes:]) * bin_width
     every = both[:, half - 1:] * (1.0 / half)
     lane = lax.broadcasted_iota(jnp.int32, both.shape, 1)
@@ -280,15 +279,12 @@
     return near + far[:, :1], far
 
 
-def bin_kernel(got, density, upstream, to_partner, to_outer):
-    height, width, radial = density.shape
+def bin_kernel(got, _, behind):
+    height, width, radial = behind.shape
     near, far = behind_of(got, radial=radial, pixels=height * width)
-    rows = []
     for row in range(height):
         at = slice(row * width, (row + 1) * width)
-        rows.append(density[row] * jnp.concatenate([near[at], far[at]], axis=1))
-        upstream[row] = rows[row]
-    pack_sides(rows, to_partner, to_outer)
+        behind[row] = jnp.concatenate([near[at], far[at]], axis=1)
 
 
 def mirror(stencils):
@@ -307,8 +303,8 @@
     def both_ways(pairs):
         return pairs + [(j, i) for i, j in pairs]
 
-    from_outer = lax.ppermute(to_outer, axis, both_ways(outer))
-    return lax.ppermute(to_partner, axis, both_ways(inner)), from_outer
+    from_partner = lax.ppermute(to_partner, axis, both_ways(inner))
+    return from_partner, lax.ppermute(to_outer, axis, both_ways(outer))
 
 
 VMEM = pl.BlockSpec(memory_space=pltpu.VMEM)
@@ -345,7 +341,7 @@
     ])
     got = lax.all_to_all(packed, ("lat", "lon"), split_axis=0, concat_axis=0, tiled=True)
 
-    def refined(field, to_sides, coefs, table, extra, finish, name):
+    def spread(field, to_sides, name):
         beside = swap(*to_sides, "lon", True)
         to_ends = pl.pallas_call(
             pack_ends_kernel,
@@ -355,10 +351,13 @@
             compiler_params=LIMIT,
             name=name + "_pack",
         )(field, *beside)
-        above = swap(*to_ends, "lat", False)
-        rows = pltpu.VMEM((height, 2 * width, radial), f32)
-        moved = pltpu.VMEM((2, height, 2 * width, radial), f32)
-        inner, middle = pl.pallas_call(
+        return beside, swap(*to_ends, "lat", False)
+
+    rows = pltpu.VMEM((height, 2 * width, radial), f32)
+    moved = pltpu.VMEM((2, height, 2 * width, radial), f32)
+
+    def refined_inside(coefs, finish, field, beside, table, extra, name):
+        return pl.pallas_call(
             functools.partial(refine_inside_kernel, coefs, finish),
             out_shape=(
                 jax.ShapeDtypeStruct((height - 4, width, radial), f32),
@@ -370,26 +369,44 @@
             compiler_params=LIMIT,
             name=name + "_inside",
         )(field, *beside, table, extra)
+
+    def refined_ends(coefs, finish, finish_inner, field, beside, above, table, extra, inner, middle, name, packs):
         return pl.pallas_call(
-            functools.partial(refine_ends_kernel, coefs, finish),
-            out_shape=tile,
+            functools.partial(refine_ends_kernel, coefs, finish, finish_inner, packs),
+            out_shape=(tile, sides, sides) if packs else tile,
             in_specs=[VMEM] * 9,
-            out_specs=VMEM,
+            out_specs=(VMEM,) * 3 if packs else VMEM,
             scratch_shapes=[pltpu.VMEM((3, 3, 4, width, radial), f32), rows, moved],
             compiler_params=LIMIT,
             name=name + "_ends",
         )(field, *beside, *above, table, extra, middle, inner)
 
-    density = refined(latent, to_sides, (0, 1), stencils, latent, lambda value, _: jnp.exp(value), "density")
-    upstream, *to_sides = pl.pallas_call(
+    beside, above = spread(latent, to_sides, "density")
+    inner, middle = refined_inside(
+        (0, 1), lambda value, _: jnp.exp(value), latent, beside, stencils, latent, "density"
+    )
+    behind = pl.pallas_call(
         bin_kernel,
-        out_shape=(tile, sides, sides),
+        out_shape=tile,
         in_specs=[VMEM, VMEM],
-        out_specs=(VMEM, VMEM, VMEM),
+        out_specs=VMEM,
         compiler_params=LIMIT,
         name="binning",
-    )(got, density)
-    return refined(upstream, to_sides, (1, 0), mirror(stencils), latent, lambda value, field: field + value, "back")
+    )(got, inner)
+    upstream, *to_sides = refined_ends(
+        (0, 1), lambda value, mass: jnp.exp(value) * mass, lambda value, mass: value * mass,
+        latent, beside, above, stencils, behind, inner, middle, "density", True,
+    )
+
+    mirrored = mirror(stencils)
+    beside, above = spread(upstream, to_sides, "back")
+    inner, middle = refined_inside(
+        (1, 0), lambda value, field: field + value, upstream, beside, mirrored, latent, "back"
+    )
+    return refined_ends(
+        (1, 0), lambda value, field: field + value, lambda value, _: value,
+        upstream, beside, above, mirrored, latent, inner, middle, "back", False,
+    )
 
 
 def solution(mesh):

time: 36.4 us -> 35.7 us (0.981)
  the two profiles are of different devices: /device:TPU:4 before, /device:TPU:2 now
where the time goes in v5:
time: 35.7 us; the launch traced here: 35.5 us
  starting transfers between devices  18.3 us (51%)
  Pallas kernels  9.8 us (27%)
  waiting for transfers between devices  6.86 us (19%)
    ppermute x4, starting transfers between devices, swap(): return (from_partner, lax.ppermute(to_outer, axis, both_ways(outer)))  13.3 us
    ppermute x4, waiting for transfers between devices, swap(): return (from_partner, lax.ppermute(to_outer, axis, both_ways(outer)))  5.76 us
    pallas_call x1, Pallas kernels, on_device(): pl.pallas_call(bin_kernel, out_shape=tile, in_specs=[VMEM, VMEM], out_spe...  3.29 us
    all_to_all x1, starting transfers between devices, on_device(): lax.all_to_all(packed, ('lat', 'lon'), split_axis=0, concat_axis=0, tiled...  3.09 us
    pallas_call x2, Pallas kernels, refined_ends(): pl.pallas_call(functools.partial(refine_ends_kernel, coefs, finish, finis...  2.5 us
    pallas_call x2, Pallas kernels, refined_inside(): pl.pallas_call(functools.partial(refine_inside_kernel, coefs, finish), ou...  2.12 us
    ppermute x4, starting transfers between devices, swap(): from_partner = lax.ppermute(to_partner, axis, both_ways(inner))  1.93 us
    pallas_call x1, Pallas kernels, on_device(): pl.pallas_call(open_kernel, out_shape=(jax.ShapeDtypeStruct((shards, 2 *...  1.84 us
  transfers between devices with their start and end apart: 9, of which 3 were waited for; matrix products, arithmetic and copies ran while one was open for 1% of the time, Pallas kernels for 15%

profile of v5, /device:TPU:2, one launch (start us, length us, event | category | flops | bytes accessed | tf_op | source)
XLA Modules:
  0.0 35.5 jit_solution(38262684935589754)
XLA Ops:
  0.0 1.8 %opening.1 = (f32[32,8,128]{2,1,0:T(8,128)}, f32[8,8,512]{2,1,0:T(8,128)S(1)}, f32[2,8,512]{2,1,0:T(8,128)S(1)}, f32[2,8,512]{2,1,0:T(8,128)S(1)}) custom-call(s32[1,32]{1,0:T(1,128)} %counts_in.1, s32[1,32]{1,0:T(1,128)} %offsets_in.1, f32[128,128]{1,0:T(8,128)} %bitcast.20, s32[128,128]{1,0:T(8,128)} %bitcast.21, s32[128,128]{1,0:T(8,128)} %bitcast.22, ...), custom_call_target="tpu_custom_call" | custom-call | tf_op jit(solution)/shard_map/opening/pallas_call | solution.py:328
  1.9 0.1 collective-permute-start
  1.9 3.7 %collective-permute-start.1 = (f32[2,8,512]{2,1,0:T(8,128)S(1)}, f32[2,8,512]{2,1,0:T(8,128)S(1)}, u32[]{:S(2)}, u32[]{:S(2)}) collective-permute-start(f32[2,8,512]{2,1,0:T(8,128)S(1)} %get-tuple-element.22), channel_id=1, source_target_pairs={{1,2},{3,4},{5,6},{7,0},{2,1},{4,3},{6,5},{0,7},{9,10},{11,12},{13... | collective-permute-start | bytes 98312 | tf_op jit(solution)/shard_map/ppermute | solution.py:307
  5.6 3.1 %all-to-all-start = ((f32[32,8,128]{2,1,0:T(8,128)}), f32[32,8,128]{2,1,0:T(8,128)S(1)}, u32[]{:S(2)}, u32[]{:S(2)}) async-start(f32[32,8,128]{2,1,0:T(8,128)} %get-tuple-element.25), calls=%async_computation | async-start | bytes 262144 | tf_op jit(solution)/shard_map/all_to_all | solution.py:342
  8.8 0.0 collective-permute-done.from_partner.side_0
  8.8 0.0 collective-permute-done.1.from_outer.side_1
  8.8 0.3 collective-permute-start.2
  9.1 4.6 %collective-permute-start.3 = (f32[3,8,512]{2,1,0:T(8,128)S(1)}, f32[3,8,512]{2,1,0:T(8,128)S(1)}, u32[]{:S(2)}, u32[]{:S(2)}) collective-permute-start(f32[3,8,512]{2,1,0:T(8,128)S(1)} %get-tuple-element.24), channel_id=1, source_target_pairs={{8,16},{16,8},{9,17},{17,9},{10,18},{18,10},{11,19},{19,11},{12,20... | collective-permute-start | bytes 147464 | tf_op jit(solution)/shard_map/ppermute | solution.py:307
  13.7 0.1 slice_bitcast_fusion.1
  13.8 1.1 %density_inside.1 = (f32[4,8,512]{2,1,0:T(8,128)S(1)}, f32[3,3,6,8,512]{4,3,2,1,0:T(8,128)S(1)}) custom-call(f32[8,8,512]{2,1,0:T(8,128)S(1)} %get-tuple-element.20.field.extra, f32[2,8,512]{2,1,0:T(8,128)S(1)} %collective-permute-done.from_partner.side_0, f32[2,8,512]{2,1,0:T(8,128)S(1)} %collective-permute-done.1.from_outer.side_1, ...), custom_call_target="tpu_custom_call" | custom-call | tf_op jit(solution)/shard_map/density_inside/pallas_call | solution.py:360
  14.9 1.1 %all-to-all-done.got = f32[32,8,128]{2,1,0:T(8,128)S(1)} async-done(((f32[32,8,128]{2,1,0:T(8,128)}), f32[32,8,128]{2,1,0:T(8,128)S(1)}, u32[]{:S(2)}, u32[]{:S(2)}) %all-to-all-start) | async-done | bytes 131104 | tf_op jit(solution)/shard_map/all_to_all | solution.py:342
  16.0 3.3 %binning.1.extra = f32[8,8,512]{2,1,0:T(8,128)S(1)} custom-call(f32[32,8,128]{2,1,0:T(8,128)S(1)} %all-to-all-done.got, f32[4,8,512]{2,1,0:T(8,128)S(1)} %get-tuple-element.26._.inner), custom_call_target="tpu_custom_call" | custom-call | tf_op jit(solution)/shard_map/binning/pallas_call | solution.py:388
  19.3 0.0 collective-permute-done.2.end_0
  19.3 0.9 %density_ends.1 = (f32[8,8,512]{2,1,0:T(8,128)S(1)}, f32[2,8,512]{2,1,0:T(8,128)S(1)}, f32[2,8,512]{2,1,0:T(8,128)S(1)}) custom-call(f32[8,8,512]{2,1,0:T(8,128)S(1)} %get-tuple-element.20.field.extra, f32[2,8,512]{2,1,0:T(8,128)S(1)} %collective-permute-done.from_partner.side_0, f32[2,8,512]{2,1,0:T(8,128)S(1)} %collective-permute-done.1.from_outer.side_1, ...), custom_call_target="tpu_custom_call" | custom-call | tf_op jit(solution)/shard_map/density_ends/pallas_call | solution.py:374
  20.3 0.1 collective-permute-start.4
  20.3 2.4 %collective-permute-start.5 = (f32[2,8,512]{2,1,0:T(8,128)S(1)}, f32[2,8,512]{2,1,0:T(8,128)S(1)}, u32[]{:S(2)}, u32[]{:S(2)}) collective-permute-start(f32[2,8,512]{2,1,0:T(8,128)S(1)} %get-tuple-element.30), channel_id=1, source_target_pairs={{1,2},{3,4},{5,6},{7,0},{2,1},{4,3},{6,5},{0,7},{9,10},{11,12},{13... | collective-permute-start | bytes 98312 | tf_op jit(solution)/shard_map/ppermute | solution.py:307
  22.7 0.1 pad_bitcast_fusion
  22.9 2.7 %collective-permute-done.5.from_outer.side_1 = f32[2,8,512]{2,1,0:T(8,128)S(1)} collective-permute-done((f32[2,8,512]{2,1,0:T(8,128)S(1)}, f32[2,8,512]{2,1,0:T(8,128)S(1)}, u32[]{:S(2)}, u32[]{:S(2)}) %collective-permute-start.5) | collective-permute-done | bytes 32800 | tf_op jit(solution)/shard_map/ppermute | solution.py:307
  25.6 1.5 %collective-permute-start.6 = (f32[3,8,512]{2,1,0:T(8,128)S(1)}, f32[3,8,512]{2,1,0:T(8,128)S(1)}, u32[]{:S(2)}, u32[]{:S(2)}) collective-permute-start(f32[3,8,512]{2,1,0:T(8,128)S(1)} %get-tuple-element.31), channel_id=1, source_target_pairs={{0,8},{16,24},{8,0},{24,16},{1,9},{17,25},{9,1},{25,17},{2,10},{18... | collective-permute-start | bytes 147464 | tf_op jit(solution)/shard_map/ppermute | solution.py:306
  27.0 2.6 %collective-permute-start.7 = (f32[3,8,512]{2,1,0:T(8,128)S(1)}, f32[3,8,512]{2,1,0:T(8,128)S(1)}, u32[]{:S(2)}, u32[]{:S(2)}) collective-permute-start(f32[3,8,512]{2,1,0:T(8,128)S(1)} %get-tuple-element.32), channel_id=1, source_target_pairs={{8,16},{16,8},{9,17},{17,9},{10,18},{18,10},{11,19},{19,11},{12,20... | collective-permute-start | bytes 147464 | tf_op jit(solution)/shard_map/ppermute | solution.py:307
  29.7 0.1 pad_maximum_fusion
  29.8 1.1 %back_inside.1 = (f32[4,8,512]{2,1,0:T(8,128)S(1)}, f32[3,3,6,8,512]{4,3,2,1,0:T(8,128)S(1)}) custom-call(f32[8,8,512]{2,1,0:T(8,128)S(1)} %get-tuple-element.28.field, f32[2,8,512]{2,1,0:T(8,128)S(1)} %collective-permute-done.4.from_partner.side_0, f32[2,8,512]{2,1,0:T(8,128)S(1)} %collective-permute-done.5.from_outer.side_1, ...), custom_call_target="tpu_custom_call" | custom-call | tf_op jit(solution)/shard_map/back_inside/pallas_call | solution.py:360
  30.8 3.1 %collective-permute-done.7.end_1 = f32[3,8,512]{2,1,0:T(8,128)S(1)} collective-permute-done((f32[3,8,512]{2,1,0:T(8,128)S(1)}, f32[3,8,512]{2,1,0:T(8,128)S(1)}, u32[]{:S(2)}, u32[]{:S(2)}) %collective-permute-start.7) | collective-permute-done | bytes 49184 | tf_op jit(solution)/shard_map/ppermute | solution.py:307
  33.9 1.6 %back_ends.1 = f32[8,8,512]{2,1,0:T(8,128)} custom-call(f32[8,8,512]{2,1,0:T(8,128)S(1)} %get-tuple-element.28.field, f32[2,8,512]{2,1,0:T(8,128)S(1)} %collective-permute-done.4.from_partner.side_0, f32[2,8,512]{2,1,0:T(8,128)S(1)} %collective-permute-done.5.from_outer.side_1, f32[3,8,512]{2,1,0:T(8,128)S(1)} %collective-permute-done.6.end_0, ...), custom_call_target="tpu_custom_call" | custom-call | tf_op jit(solution)/shard_map/back_ends/pallas_call | solution.py:374
  (11 shorter events, 0.1 us)
Async XLA Ops:
  1.9 6.9 %collective-permute-start = (f32[2,8,512]{2,1,0:T(8,128)S(1)}, f32[2,8,512]{2,1,0:T(8,128)S(1)}, u32[]{:S(2)}, u32[]{:S(2)}) collective-permute-start(f32[2,8,512]{2,1,0:T(8,128)S(1)} %get-tuple-element.21), channel_id=1, source_target_pairs={{0,1},{2,3},{4,5},{6,7},{1,0},{3,2},{5,4},{7,6},{8,9},{10,11},{12,... | collective-permute-start | bytes 98312 | tf_op jit(solution)/shard_map/ppermute | solution.py:306
  1.9 6.8 %collective-permute-start.1 = (f32[2,8,512]{2,1,0:T(8,128)S(1)}, f32[2,8,512]{2,1,0:T(8,128)S(1)}, u32[]{:S(2)}, u32[]{:S(2)}) collective-permute-start(f32[2,8,512]{2,1,0:T(8,128)S(1)} %get-tuple-element.22), channel_id=1, source_target_pairs={{1,2},{3,4},{5,6},{7,0},{2,1},{4,3},{6,5},{0,7},{9,10},{11,12},{13... | collective-permute-start | bytes 98312 | tf_op jit(solution)/shard_map/ppermute | solution.py:307
  5.6 3.1 %copy-start = (f32[2,27,512]{2,0,1:T(2,128)S(1)}, f32[2,27,512]{2,0,1:T(2,128)}, u32[]{:S(2)}) copy-start(f32[2,27,512]{2,0,1:T(2,128)} %param.13) | copy-start | bytes 331780
  5.6 10.4 %all-to-all-start = ((f32[32,8,128]{2,1,0:T(8,128)}), f32[32,8,128]{2,1,0:T(8,128)S(1)}, u32[]{:S(2)}, u32[]{:S(2)}) async-start(f32[32,8,128]{2,1,0:T(8,128)} %get-tuple-element.25), calls=%async_computation | async-start | bytes 262144 | tf_op jit(solution)/shard_map/all_to_all | solution.py:342
  8.8 10.5 %collective-permute-start.2 = (f32[3,8,512]{2,1,0:T(8,128)S(1)}, f32[3,8,512]{2,1,0:T(8,128)S(1)}, u32[]{:S(2)}, u32[]{:S(2)}) collective-permute-start(f32[3,8,512]{2,1,0:T(8,128)S(1)} %get-tuple-element.23), channel_id=1, source_target_pairs={{0,8},{16,24},{8,0},{24,16},{1,9},{17,25},{9,1},{25,17},{2,10},{18... | collective-permute-start | bytes 147464 | tf_op jit(solution)/shard_map/ppermute | solution.py:306
  9.1 10.2 %collective-permute-start.3 = (f32[3,8,512]{2,1,0:T(8,128)S(1)}, f32[3,8,512]{2,1,0:T(8,128)S(1)}, u32[]{:S(2)}, u32[]{:S(2)}) collective-permute-start(f32[3,8,512]{2,1,0:T(8,128)S(1)} %get-tuple-element.24), channel_id=1, source_target_pairs={{8,16},{16,8},{9,17},{17,9},{10,18},{18,10},{11,19},{19,11},{12,20... | collective-permute-start | bytes 147464 | tf_op jit(solution)/shard_map/ppermute | solution.py:307
  20.3 2.6 %collective-permute-start.4 = (f32[2,8,512]{2,1,0:T(8,128)S(1)}, f32[2,8,512]{2,1,0:T(8,128)S(1)}, u32[]{:S(2)}, u32[]{:S(2)}) collective-permute-start(f32[2,8,512]{2,1,0:T(8,128)S(1)} %get-tuple-element.29), channel_id=1, source_target_pairs={{0,1},{2,3},{4,5},{6,7},{1,0},{3,2},{5,4},{7,6},{8,9},{10,11},{12,... | collective-permute-start | bytes 98312 | tf_op jit(solution)/shard_map/ppermute | solution.py:306
  20.3 5.2 %collective-permute-start.5 = (f32[2,8,512]{2,1,0:T(8,128)S(1)}, f32[2,8,512]{2,1,0:T(8,128)S(1)}, u32[]{:S(2)}, u32[]{:S(2)}) collective-permute-start(f32[2,8,512]{2,1,0:T(8,128)S(1)} %get-tuple-element.30), channel_id=1, source_target_pairs={{1,2},{3,4},{5,6},{7,0},{2,1},{4,3},{6,5},{0,7},{9,10},{11,12},{13... | collective-permute-start | bytes 98312 | tf_op jit(solution)/shard_map/ppermute | solution.py:307
  25.6 5.3 %collective-permute-start.6 = (f32[3,8,512]{2,1,0:T(8,128)S(1)}, f32[3,8,512]{2,1,0:T(8,128)S(1)}, u32[]{:S(2)}, u32[]{:S(2)}) collective-permute-start(f32[3,8,512]{2,1,0:T(8,128)S(1)} %get-tuple-element.31), channel_id=1, source_target_pairs={{0,8},{16,24},{8,0},{24,16},{1,9},{17,25},{9,1},{25,17},{2,10},{18... | collective-permute-start | bytes 147464 | tf_op jit(solution)/shard_map/ppermute | solution.py:306
  27.0 6.9 %collective-permute-start.7 = (f32[3,8,512]{2,1,0:T(8,128)S(1)}, f32[3,8,512]{2,1,0:T(8,128)S(1)}, u32[]{:S(2)}, u32[]{:S(2)}) collective-permute-start(f32[3,8,512]{2,1,0:T(8,128)S(1)} %get-tuple-element.32), channel_id=1, source_target_pairs={{8,16},{16,8},{9,17},{17,9},{10,18},{18,10},{11,19},{19,11},{12,20... | collective-permute-start | bytes 147464 | tf_op jit(solution)/shard_map/ppermute | solution.py:307

commit v6 on v5

--- a/solution.py
+++ b/solution.py
@@ -243,7 +243,6 @@
         for first in range(0, half, LANES)
     ]
     zero = jnp.zeros((), bf16)
-    one = jnp.ones((), bf16)
 
     def tall(row):
         return jnp.concatenate([jnp.broadcast_to(row, (16, LANES)).astype(bf16)] * (classes // 16), axis=0)
@@ -263,9 +262,10 @@
         left, right = [], []
         for run in range(2 * RUNS):
             row = (first + run // RUNS) * rows + run % RUNS
-            away = tall(label[row + RUNS:row + RUNS + 1]) - column
-            mine = jnp.maximum(one - away * away, zero)
-            left.append(jnp.concatenate([mine * tall(coarse[row:row + 1]), mine * tall(rest[row:row + 1])], axis=0))
+            mine = tall(label[row + RUNS:row + RUNS + 1]) == column
+            left.append(jnp.concatenate([
+                jnp.where(mine, tall(coarse[row:row + 1]), zero), jnp.where(mine, tall(rest[row:row + 1]), zero)
+            ], axis=0))
             low = jnp.broadcast_to(lows[:, row + RUNS:row + RUNS + 1], (LANES, LANES)).astype(bf16)
             right.append(jnp.concatenate([jnp.maximum(low, place) for place in places], axis=1))
         total = total + jnp.dot(
@@ -293,6 +293,16 @@
     back = jnp.concatenate([edge, turned[:, :, 0, :-1]], axis=-1)
     ahead = jnp.concatenate([turned[:, :, 2, 1:], edge], axis=-1)
     return jnp.stack([back, turned[:, :, 1], ahead], axis=2).reshape(stencils.shape)
+
+
+def gathered_ends(to_partner, to_outer):
+    every = lax.all_gather(jnp.stack([to_partner, to_outer]), "lat")
+    lat = lax.axis_index("lat")
+    outer = lat + 2 * lax.rem(lat, 2) - 1
+    inside = (outer >= 0) & (outer < lax.axis_size("lat"))
+    from_partner = lax.dynamic_index_in_dim(every, lat + 1 - 2 * lax.rem(lat, 2), keepdims=False)[0]
+    from_outer = lax.dynamic_index_in_dim(every, jnp.clip(outer, 0, lax.axis_size("lat") - 1), keepdims=False)[1]
+    return from_partner, jnp.where(inside, from_outer, 0.0)
 
 
 def swap(to_partner, to_outer, axis, closed):
@@ -341,7 +351,7 @@
     ])
     got = lax.all_to_all(packed, ("lat", "lon"), split_axis=0, concat_axis=0, tiled=True)
 
-    def spread(field, to_sides, name):
+    def spread(field, to_sides, name, gathers):
         beside = swap(*to_sides, "lon", True)
         to_ends = pl.pallas_call(
             pack_ends_kernel,
@@ -351,7 +361,7 @@
             compiler_params=LIMIT,
             name=name + "_pack",
         )(field, *beside)
-        return beside, swap(*to_ends, "lat", False)
+        return beside, gathered_ends(*to_ends) if gathers else swap(*to_ends, "lat", False)
 
     rows = pltpu.VMEM((height, 2 * width, radial), f32)
     moved = pltpu.VMEM((2, height, 2 * width, radial), f32)
@@ -381,7 +391,7 @@
             name=name + "_ends",
         )(field, *beside, *above, table, extra, middle, inner)
 
-    beside, above = spread(latent, to_sides, "density")
+    beside, above = spread(latent, to_sides, "density", False)
     inner, middle = refined_inside(
         (0, 1), lambda value, _: jnp.exp(value), latent, beside, stencils, latent, "density"
     )
@@ -399,7 +409,7 @@
     )
 
     mirrored = mirror(stencils)
-    beside, above = spread(upstream, to_sides, "back")
+    beside, above = spread(upstream, to_sides, "back", True)
     inner, middle = refined_inside(
         (1, 0), lambda value, field: field + value, upstream, beside, mirrored, latent, "back"
     )

time: 35.7 us -> 39.9 us (1.12)
  the two profiles are of different devices: /device:TPU:2 before, /device:TPU:0 now
where the time goes in v6:
time: 39.9 us; the launch traced here: 39.7 us
  starting transfers between devices  11.6 us (29%)
  Pallas kernels  9.8 us (25%)
  blocking collectives  9.2 us (23%)
  waiting for transfers between devices  8.59 us (22%)
    all_gather x1, blocking collectives, gathered_ends(): every = lax.all_gather(jnp.stack([to_partner, to_outer]), 'lat')  9.2 us
    ppermute x3, starting transfers between devices, swap(): return (from_partner, lax.ppermute(to_outer, axis, both_ways(outer)))  6.07 us
    all_to_all x1, waiting for transfers between devices, on_device(): lax.all_to_all(packed, ('lat', 'lon'), split_axis=0, concat_axis=0, tiled...  4.27 us
    ppermute x3, waiting for transfers between devices, swap(): return (from_partner, lax.ppermute(to_outer, axis, both_ways(outer)))  4.25 us
    pallas_call x1, Pallas kernels, on_device(): pl.pallas_call(bin_kernel, out_shape=tile, in_specs=[VMEM, VMEM], out_spe...  3.28 us
    all_to_all x1, starting transfers between devices, on_device(): lax.all_to_all(packed, ('lat', 'lon'), split_axis=0, concat_axis=0, tiled...  2.81 us
    ppermute x3, starting transfers between devices, swap(): from_partner = lax.ppermute(to_partner, axis, both_ways(inner))  2.73 us
    pallas_call x2, Pallas kernels, refined_ends(): pl.pallas_call(functools.partial(refine_ends_kernel, coefs, finish, finis...  2.51 us
  transfers between devices with their start and end apart: 7, of which 3 were waited for; matrix products, arithmetic and copies ran while one was open for 1% of the time, Pallas kernels for 11%

profile of v6, /device:TPU:0, one launch (start us, length us, event | category | flops | bytes accessed | tf_op | source)
XLA Modules:
  0.0 39.7 jit_solution(14654565549942986130)
XLA Ops:
  0.0 1.8 %opening.1 = (f32[32,8,128]{2,1,0:T(8,128)}, f32[8,8,512]{2,1,0:T(8,128)S(1)}, f32[2,8,512]{2,1,0:T(8,128)S(1)}, f32[2,8,512]{2,1,0:T(8,128)S(1)}) custom-call(s32[1,32]{1,0:T(1,128)} %counts_in.1, s32[1,32]{1,0:T(1,128)} %offsets_in.1, f32[128,128]{1,0:T(8,128)} %bitcast.30, s32[128,128]{1,0:T(8,128)} %bitcast.31, s32[128,128]{1,0:T(8,128)} %bitcast.32, ...), custom_call_target="tpu_custom_call" | custom-call | tf_op jit(solution)/shard_map/opening/pallas_call | solution.py:338
  1.9 0.5 %collective-permute-start = (f32[2,8,512]{2,1,0:T(8,128)S(1)}, f32[2,8,512]{2,1,0:T(8,128)S(1)}, u32[]{:S(2)}, u32[]{:S(2)}) collective-permute-start(f32[2,8,512]{2,1,0:T(8,128)S(1)} %get-tuple-element.21), channel_id=1, source_target_pairs={{0,1},{2,3},{4,5},{6,7},{1,0},{3,2},{5,4},{7,6},{8,9},{10,11},{12,... | collective-permute-start | bytes 98312 | tf_op jit(solution)/shard_map/ppermute | solution.py:316
  2.4 4.7 %collective-permute-start.1 = (f32[2,8,512]{2,1,0:T(8,128)S(1)}, f32[2,8,512]{2,1,0:T(8,128)S(1)}, u32[]{:S(2)}, u32[]{:S(2)}) collective-permute-start(f32[2,8,512]{2,1,0:T(8,128)S(1)} %get-tuple-element.22), channel_id=1, source_target_pairs={{1,2},{3,4},{5,6},{7,0},{2,1},{4,3},{6,5},{0,7},{9,10},{11,12},{13... | collective-permute-start | bytes 98312 | tf_op jit(solution)/shard_map/ppermute | solution.py:317
  7.1 2.8 %all-to-all-start = ((f32[32,8,128]{2,1,0:T(8,128)}), f32[32,8,128]{2,1,0:T(8,128)S(1)}, u32[]{:S(2)}, u32[]{:S(2)}) async-start(f32[32,8,128]{2,1,0:T(8,128)} %get-tuple-element.25), calls=%async_computation | async-start | bytes 262144 | tf_op jit(solution)/shard_map/all_to_all | solution.py:352
  9.9 0.1 slice_bitcast_fusion.1
  10.0 0.0 collective-permute-done.from_partner.side_0
  10.0 0.0 collective-permute-done.1.from_outer.side_1
  10.1 1.8 %collective-permute-start.2 = (f32[3,8,512]{2,1,0:T(8,128)S(1)}, f32[3,8,512]{2,1,0:T(8,128)S(1)}, u32[]{:S(2)}, u32[]{:S(2)}) collective-permute-start(f32[3,8,512]{2,1,0:T(8,128)S(1)} %get-tuple-element.23), channel_id=1, source_target_pairs={{0,8},{16,24},{8,0},{24,16},{1,9},{17,25},{9,1},{25,17},{2,10},{18... | collective-permute-start | bytes 147464 | tf_op jit(solution)/shard_map/ppermute | solution.py:316
  11.9 0.7 %collective-permute-start.3 = (f32[3,8,512]{2,1,0:T(8,128)S(1)}, f32[3,8,512]{2,1,0:T(8,128)S(1)}, u32[]{:S(2)}, u32[]{:S(2)}) collective-permute-start(f32[3,8,512]{2,1,0:T(8,128)S(1)} %get-tuple-element.24), channel_id=1, source_target_pairs={{8,16},{16,8},{9,17},{17,9},{10,18},{18,10},{11,19},{19,11},{12,20... | collective-permute-start | bytes 147464 | tf_op jit(solution)/shard_map/ppermute | solution.py:317
  12.6 0.1 pad_bitcast_fusion
  12.7 1.1 %density_inside.1 = (f32[4,8,512]{2,1,0:T(8,128)S(1)}, f32[3,3,6,8,512]{4,3,2,1,0:T(8,128)S(1)}) custom-call(f32[8,8,512]{2,1,0:T(8,128)S(1)} %get-tuple-element.20.field.extra, f32[2,8,512]{2,1,0:T(8,128)S(1)} %collective-permute-done.from_partner.side_0, f32[2,8,512]{2,1,0:T(8,128)S(1)} %collective-permute-done.1.from_outer.side_1, ...), custom_call_target="tpu_custom_call" | custom-call | tf_op jit(solution)/shard_map/density_inside/pallas_call | solution.py:370
  13.8 4.3 %all-to-all-done.got = f32[32,8,128]{2,1,0:T(8,128)S(1)} async-done(((f32[32,8,128]{2,1,0:T(8,128)}), f32[32,8,128]{2,1,0:T(8,128)S(1)}, u32[]{:S(2)}, u32[]{:S(2)}) %all-to-all-start) | async-done | bytes 131104 | tf_op jit(solution)/shard_map/all_to_all | solution.py:352
  18.1 3.3 %binning.1.extra = f32[8,8,512]{2,1,0:T(8,128)S(1)} custom-call(f32[32,8,128]{2,1,0:T(8,128)S(1)} %all-to-all-done.got, f32[4,8,512]{2,1,0:T(8,128)S(1)} %get-tuple-element.26._.inner), custom_call_target="tpu_custom_call" | custom-call | tf_op jit(solution)/shard_map/binning/pallas_call | solution.py:398
  21.4 0.0 collective-permute-done.2.end_0
  21.4 0.0 collective-permute-done.3.end_1
  21.4 0.9 %density_ends.1 = (f32[8,8,512]{2,1,0:T(8,128)S(1)}, f32[2,8,512]{2,1,0:T(8,128)S(1)}, f32[2,8,512]{2,1,0:T(8,128)S(1)}) custom-call(f32[8,8,512]{2,1,0:T(8,128)S(1)} %get-tuple-element.20.field.extra, f32[2,8,512]{2,1,0:T(8,128)S(1)} %collective-permute-done.from_partner.side_0, f32[2,8,512]{2,1,0:T(8,128)S(1)} %collective-permute-done.1.from_outer.side_1, ...), custom_call_target="tpu_custom_call" | custom-call | tf_op jit(solution)/shard_map/density_ends/pallas_call | solution.py:384
  22.3 0.4 collective-permute-start.4
  22.7 0.7 %collective-permute-start.5 = (f32[2,8,512]{2,1,0:T(8,128)S(1)}, f32[2,8,512]{2,1,0:T(8,128)S(1)}, u32[]{:S(2)}, u32[]{:S(2)}) collective-permute-start(f32[2,8,512]{2,1,0:T(8,128)S(1)} %get-tuple-element.30), channel_id=1, source_target_pairs={{1,2},{3,4},{5,6},{7,0},{2,1},{4,3},{6,5},{0,7},{9,10},{11,12},{13... | collective-permute-start | bytes 98312 | tf_op jit(solution)/shard_map/ppermute | solution.py:317
  23.4 0.1 pad_maximum_fusion
  23.5 0.1 collective-permute-done.4.from_partner.side_0
  23.6 4.2 %collective-permute-done.5.from_outer.side_1 = f32[2,8,512]{2,1,0:T(8,128)S(1)} collective-permute-done((f32[2,8,512]{2,1,0:T(8,128)S(1)}, f32[2,8,512]{2,1,0:T(8,128)S(1)}, u32[]{:S(2)}, u32[]{:S(2)}) %collective-permute-start.5) | collective-permute-done | bytes 32800 | tf_op jit(solution)/shard_map/ppermute | solution.py:317
  27.9 9.2 %all-gather = f32[8,3,8,512]{3,2,1,0:T(8,128)S(1)} all-gather(f32[2,3,8,512]{3,2,1,0:T(8,128)S(1)} %pad_maximum_fusion.1), channel_id=2, replica_groups=mesh['lat'=4,'lon'=8] {'lat'}, dimensions={0}, use_global_device_ids=true | all-gather | bytes 491520 | tf_op jit(solution)/shard_map/all_gather | solution.py:299
  37.1 1.1 %back_inside.1 = (f32[4,8,512]{2,1,0:T(8,128)S(1)}, f32[3,3,6,8,512]{4,3,2,1,0:T(8,128)S(1)}) custom-call(f32[8,8,512]{2,1,0:T(8,128)S(1)} %get-tuple-element.28.field, f32[2,8,512]{2,1,0:T(8,128)S(1)} %collective-permute-done.4.from_partner.side_0, f32[2,8,512]{2,1,0:T(8,128)S(1)} %collective-permute-done.5.from_outer.side_1, ...), custom_call_target="tpu_custom_call" | custom-call | tf_op jit(solution)/shard_map/back_inside/pallas_call | solution.py:370
  38.2 1.6 %back_ends.1 = f32[8,8,512]{2,1,0:T(8,128)} custom-call(f32[8,8,512]{2,1,0:T(8,128)S(1)} %get-tuple-element.28.field, f32[2,8,512]{2,1,0:T(8,128)S(1)} %collective-permute-done.4.from_partner.side_0, f32[2,8,512]{2,1,0:T(8,128)S(1)} %collective-permute-done.5.from_outer.side_1, f32[3,8,512]{2,1,0:T(8,128)S(1)} %get-tuple-element.36.end_0, ...), custom_call_target="tpu_custom_call" | custom-call | tf_op jit(solution)/shard_map/back_ends/pallas_call | solution.py:384
  (10 shorter events, 0.1 us)
Async XLA Ops:
  1.9 8.2 %collective-permute-start = (f32[2,8,512]{2,1,0:T(8,128)S(1)}, f32[2,8,512]{2,1,0:T(8,128)S(1)}, u32[]{:S(2)}, u32[]{:S(2)}) collective-permute-start(f32[2,8,512]{2,1,0:T(8,128)S(1)} %get-tuple-element.21), channel_id=1, source_target_pairs={{0,1},{2,3},{4,5},{6,7},{1,0},{3,2},{5,4},{7,6},{8,9},{10,11},{12,... | collective-permute-start | bytes 98312 | tf_op jit(solution)/shard_map/ppermute | solution.py:316
  2.4 7.7 %collective-permute-start.1 = (f32[2,8,512]{2,1,0:T(8,128)S(1)}, f32[2,8,512]{2,1,0:T(8,128)S(1)}, u32[]{:S(2)}, u32[]{:S(2)}) collective-permute-start(f32[2,8,512]{2,1,0:T(8,128)S(1)} %get-tuple-element.22), channel_id=1, source_target_pairs={{1,2},{3,4},{5,6},{7,0},{2,1},{4,3},{6,5},{0,7},{9,10},{11,12},{13... | collective-permute-start | bytes 98312 | tf_op jit(solution)/shard_map/ppermute | solution.py:317
  7.1 2.8 %copy-start = (f32[2,27,512]{2,0,1:T(2,128)S(1)}, f32[2,27,512]{2,0,1:T(2,128)}, u32[]{:S(2)}) copy-start(f32[2,27,512]{2,0,1:T(2,128)} %param.13) | copy-start | bytes 331780
  7.1 11.0 %all-to-all-start = ((f32[32,8,128]{2,1,0:T(8,128)}), f32[32,8,128]{2,1,0:T(8,128)S(1)}, u32[]{:S(2)}, u32[]{:S(2)}) async-start(f32[32,8,128]{2,1,0:T(8,128)} %get-tuple-element.25), calls=%async_computation | async-start | bytes 262144 | tf_op jit(solution)/shard_map/all_to_all | solution.py:352
  10.1 11.3 %collective-permute-start.2 = (f32[3,8,512]{2,1,0:T(8,128)S(1)}, f32[3,8,512]{2,1,0:T(8,128)S(1)}, u32[]{:S(2)}, u32[]{:S(2)}) collective-permute-start(f32[3,8,512]{2,1,0:T(8,128)S(1)} %get-tuple-element.23), channel_id=1, source_target_pairs={{0,8},{16,24},{8,0},{24,16},{1,9},{17,25},{9,1},{25,17},{2,10},{18... | collective-permute-start | bytes 147464 | tf_op jit(solution)/shard_map/ppermute | solution.py:316
  11.9 9.4 %collective-permute-start.3 = (f32[3,8,512]{2,1,0:T(8,128)S(1)}, f32[3,8,512]{2,1,0:T(8,128)S(1)}, u32[]{:S(2)}, u32[]{:S(2)}) collective-permute-start(f32[3,8,512]{2,1,0:T(8,128)S(1)} %get-tuple-element.24), channel_id=1, source_target_pairs={{8,16},{16,8},{9,17},{17,9},{10,18},{18,10},{11,19},{19,11},{12,20... | collective-permute-start | bytes 147464 | tf_op jit(solution)/shard_map/ppermute | solution.py:317
  22.3 1.3 %collective-permute-start.4 = (f32[2,8,512]{2,1,0:T(8,128)S(1)}, f32[2,8,512]{2,1,0:T(8,128)S(1)}, u32[]{:S(2)}, u32[]{:S(2)}) collective-permute-start(f32[2,8,512]{2,1,0:T(8,128)S(1)} %get-tuple-element.29), channel_id=1, source_target_pairs={{0,1},{2,3},{4,5},{6,7},{1,0},{3,2},{5,4},{7,6},{8,9},{10,11},{12,... | collective-permute-start | bytes 98312 | tf_op jit(solution)/shard_map/ppermute | solution.py:316
  22.7 5.1 %collective-permute-start.5 = (f32[2,8,512]{2,1,0:T(8,128)S(1)}, f32[2,8,512]{2,1,0:T(8,128)S(1)}, u32[]{:S(2)}, u32[]{:S(2)}) collective-permute-start(f32[2,8,512]{2,1,0:T(8,128)S(1)} %get-tuple-element.30), channel_id=1, source_target_pairs={{1,2},{3,4},{5,6},{7,0},{2,1},{4,3},{6,5},{0,7},{9,10},{11,12},{13... | collective-permute-start | bytes 98312 | tf_op jit(solution)/shard_map/ppermute | solution.py:317

commit v7 on v5

--- a/solution.py
+++ b/solution.py
@@ -161,7 +161,7 @@
 
 
 def refine_ends_kernel(
-    coefs, finish, finish_inner, packs, field, side_0, side_1, end_0, end_1, stencils, extra, inside, inner, *rest
+    coefs, finish, finish_inner, packs, field, side_0, side_1, end_1, end_0, stencils, extra, inside, inner, *rest
 ):
     out, *to_sides, middle, wide, shifted = rest
     height, width, radial = field.shape
@@ -236,6 +236,7 @@
     half = radial // 2
     classes = 2 * pixels
     shards, rows, _ = got.shape
+    group = 4
     bf16 = jnp.bfloat16
     column = lax.broadcasted_iota(jnp.int32, (classes, LANES), 0).astype(jnp.float32).astype(bf16)
     places = [
@@ -243,34 +244,34 @@
         for first in range(0, half, LANES)
     ]
     zero = jnp.zeros((), bf16)
-    one = jnp.ones((), bf16)
 
     def tall(row):
         return jnp.concatenate([jnp.broadcast_to(row, (16, LANES)).astype(bf16)] * (classes // 16), axis=0)
 
-    tiles = got[...].reshape(shards * rows, LANES)
-    cell = tiles.astype(jnp.int32)
-    pixel = lax.shift_right_logical(cell, radial.bit_length() - 1)
-    bins = lax.bitwise_and(cell, radial - 1)
-    upper = (bins >= half).astype(jnp.int32)
-    label = (upper * pixels + pixel).astype(jnp.float32)
-    lows = jnp.transpose((bins - upper * half + 1).astype(jnp.float32))
-    coarse = tiles.astype(bf16).astype(jnp.float32)
-    rest = tiles - coarse
-
-    total = jnp.zeros((2 * classes, half), jnp.float32)
-    for first in range(0, shards, 2):
+    def step(turn, total):
+        tiles = got[pl.ds(group * turn, group)].reshape(group * rows, LANES)
+        cell = tiles.astype(jnp.int32)
+        pixel = lax.shift_right_logical(cell, radial.bit_length() - 1)
+        bins = lax.bitwise_and(cell, radial - 1)
+        upper = (bins >= half).astype(jnp.int32)
+        label = (upper * pixels + pixel).astype(jnp.float32)
+        lows = jnp.transpose((bins - upper * half + 1).astype(jnp.float32))
+        coarse = tiles.astype(bf16).astype(jnp.float32)
+        rest = tiles - coarse
         left, right = [], []
-        for run in range(2 * RUNS):
-            row = (first + run // RUNS) * rows + run % RUNS
-            away = tall(label[row + RUNS:row + RUNS + 1]) - column
-            mine = jnp.maximum(one - away * away, zero)
-            left.append(jnp.concatenate([mine * tall(coarse[row:row + 1]), mine * tall(rest[row:row + 1])], axis=0))
+        for run in range(group * RUNS):
+            row = run // RUNS * rows + run % RUNS
+            mine = tall(label[row + RUNS:row + RUNS + 1]) == column
+            left.append(jnp.concatenate([
+                jnp.where(mine, tall(coarse[row:row + 1]), zero), jnp.where(mine, tall(rest[row:row + 1]), zero)
+            ], axis=0))
             low = jnp.broadcast_to(lows[:, row + RUNS:row + RUNS + 1], (LANES, LANES)).astype(bf16)
             right.append(jnp.concatenate([jnp.maximum(low, place) for place in places], axis=1))
-        total = total + jnp.dot(
+        return total + jnp.dot(
             jnp.concatenate(left, axis=1), jnp.concatenate(right, axis=0), preferred_element_type=jnp.float32
         )
+
+    total = lax.fori_loop(0, shards // group, step, jnp.zeros((2 * classes, half), jnp.float32))
     both = (total[:classes] + total[classes:]) * bin_width
     every = both[:, half - 1:] * (1.0 / half)
     lane = lax.broadcasted_iota(jnp.int32, both.shape, 1)
@@ -295,7 +296,7 @@
     return jnp.stack([back, turned[:, :, 1], ahead], axis=2).reshape(stencils.shape)
 
 
-def swap(to_partner, to_outer, axis, closed):
+def swap(to_partner, to_outer, axis, closed, outer_first=False):
     count = lax.axis_size(axis)
     outer = [(i, (i + 1) % count) for i in range(1, count, 2) if closed or i + 1 < count]
     inner = [(i, i + 1) for i in range(0, count - 1, 2)]
@@ -303,8 +304,8 @@
     def both_ways(pairs):
         return pairs + [(j, i) for i, j in pairs]
 
-    from_partner = lax.ppermute(to_partner, axis, both_ways(inner))
-    return from_partner, lax.ppermute(to_outer, axis, both_ways(outer))
+    moves = [(to_partner, inner), (to_outer, outer)]
+    return tuple(lax.ppermute(values, axis, both_ways(pairs)) for values, pairs in moves[::-1 if outer_first else 1])
 
 
 VMEM = pl.BlockSpec(memory_space=pltpu.VMEM)
@@ -351,7 +352,7 @@
             compiler_params=LIMIT,
             name=name + "_pack",
         )(field, *beside)
-        return beside, swap(*to_ends, "lat", False)
+        return beside, swap(*to_ends, "lat", False, outer_first=True)
 
     rows = pltpu.VMEM((height, 2 * width, radial), f32)
     moved = pltpu.VMEM((2, height, 2 * width, radial), f32)

time: 35.7 us -> 38.5 us (1.078)
  the two profiles are of different devices: /device:TPU:2 before, /device:TPU:0 now
where the time goes in v7:
time: 38.5 us; the launch traced here: 38.3 us
  starting transfers between devices  19.2 us (50%)
  Pallas kernels  12.1 us (31%)
  waiting for transfers between devices  6.56 us (17%)
    ppermute x8, starting transfers between devices, swap(): lax.ppermute(values, axis, both_ways(pairs))  16.3 us
    pallas_call x1, Pallas kernels, on_device(): pl.pallas_call(bin_kernel, out_shape=tile, in_specs=[VMEM, VMEM], out_spe...  5.54 us
    ppermute x8, waiting for transfers between devices, swap(): lax.ppermute(values, axis, both_ways(pairs))  4.89 us
    all_to_all x1, starting transfers between devices, on_device(): lax.all_to_all(packed, ('lat', 'lon'), split_axis=0, concat_axis=0, tiled...  2.81 us
    pallas_call x2, Pallas kernels, refined_ends(): pl.pallas_call(functools.partial(refine_ends_kernel, coefs, finish, finis...  2.5 us
    pallas_call x2, Pallas kernels, refined_inside(): pl.pallas_call(functools.partial(refine_inside_kernel, coefs, finish), ou...  2.12 us
    pallas_call x1, Pallas kernels, on_device(): pl.pallas_call(open_kernel, out_shape=(jax.ShapeDtypeStruct((shards, 2 *...  1.84 us
    all_to_all x1, waiting for transfers between devices, on_device(): lax.all_to_all(packed, ('lat', 'lon'), split_axis=0, concat_axis=0, tiled...  1.67 us
  transfers between devices with their start and end apart: 9, of which 3 were waited for; matrix products, arithmetic and copies ran while one was open for 1% of the time, Pallas kernels for 20%

profile of v7, /device:TPU:0, one launch (start us, length us, event | category | flops | bytes accessed | tf_op | source)
XLA Modules:
  0.0 38.3 jit_solution(15153646022074382871)
XLA Ops:
  0.0 1.8 %opening.1 = (f32[32,8,128]{2,1,0:T(8,128)}, f32[8,8,512]{2,1,0:T(8,128)S(1)}, f32[2,8,512]{2,1,0:T(8,128)S(1)}, f32[2,8,512]{2,1,0:T(8,128)S(1)}) custom-call(s32[1,32]{1,0:T(1,128)} %counts_in.1, s32[1,32]{1,0:T(1,128)} %offsets_in.1, f32[128,128]{1,0:T(8,128)} %bitcast.20, s32[128,128]{1,0:T(8,128)} %bitcast.21, s32[128,128]{1,0:T(8,128)} %bitcast.22, ...), custom_call_target="tpu_custom_call" | custom-call | tf_op jit(solution)/shard_map/opening/pallas_call | solution.py:329
  1.9 0.5 %collective-permute-start = (f32[2,8,512]{2,1,0:T(8,128)S(1)}, f32[2,8,512]{2,1,0:T(8,128)S(1)}, u32[]{:S(2)}, u32[]{:S(2)}) collective-permute-start(f32[2,8,512]{2,1,0:T(8,128)S(1)} %get-tuple-element.21), channel_id=1, source_target_pairs={{0,1},{2,3},{4,5},{6,7},{1,0},{3,2},{5,4},{7,6},{8,9},{10,11},{12,... | collective-permute-start | bytes 98312 | tf_op jit(solution)/shard_map/ppermute | solution.py:308
  2.4 4.7 %collective-permute-start.1 = (f32[2,8,512]{2,1,0:T(8,128)S(1)}, f32[2,8,512]{2,1,0:T(8,128)S(1)}, u32[]{:S(2)}, u32[]{:S(2)}) collective-permute-start(f32[2,8,512]{2,1,0:T(8,128)S(1)} %get-tuple-element.22), channel_id=1, source_target_pairs={{1,2},{3,4},{5,6},{7,0},{2,1},{4,3},{6,5},{0,7},{9,10},{11,12},{13... | collective-permute-start | bytes 98312 | tf_op jit(solution)/shard_map/ppermute | solution.py:308
  7.1 2.8 %all-to-all-start = ((f32[32,8,128]{2,1,0:T(8,128)}), f32[32,8,128]{2,1,0:T(8,128)S(1)}, u32[]{:S(2)}, u32[]{:S(2)}) async-start(f32[32,8,128]{2,1,0:T(8,128)} %get-tuple-element.25), calls=%async_computation | async-start | bytes 262144 | tf_op jit(solution)/shard_map/all_to_all | solution.py:343
  9.9 0.0 collective-permute-done.from_partner.side_0
  9.9 0.0 collective-permute-done.1.from_outer.side_1
  10.0 0.7 %collective-permute-start.2 = (f32[3,8,512]{2,1,0:T(8,128)S(1)}, f32[3,8,512]{2,1,0:T(8,128)S(1)}, u32[]{:S(2)}, u32[]{:S(2)}) collective-permute-start(f32[3,8,512]{2,1,0:T(8,128)S(1)} %get-tuple-element.23), channel_id=1, source_target_pairs={{8,16},{16,8},{9,17},{17,9},{10,18},{18,10},{11,19},{19,11},{12,20... | collective-permute-start | bytes 147464 | tf_op jit(solution)/shard_map/ppermute | solution.py:308
  10.7 4.5 %collective-permute-start.3 = (f32[3,8,512]{2,1,0:T(8,128)S(1)}, f32[3,8,512]{2,1,0:T(8,128)S(1)}, u32[]{:S(2)}, u32[]{:S(2)}) collective-permute-start(f32[3,8,512]{2,1,0:T(8,128)S(1)} %get-tuple-element.24), channel_id=1, source_target_pairs={{0,8},{16,24},{8,0},{24,16},{1,9},{17,25},{9,1},{25,17},{2,10},{18... | collective-permute-start | bytes 147464 | tf_op jit(solution)/shard_map/ppermute | solution.py:308
  15.2 0.1 slice_bitcast_fusion.1
  15.3 1.1 %density_inside.1 = (f32[4,8,512]{2,1,0:T(8,128)S(1)}, f32[3,3,6,8,512]{4,3,2,1,0:T(8,128)S(1)}) custom-call(f32[8,8,512]{2,1,0:T(8,128)S(1)} %get-tuple-element.20.field.extra, f32[2,8,512]{2,1,0:T(8,128)S(1)} %collective-permute-done.from_partner.side_0, f32[2,8,512]{2,1,0:T(8,128)S(1)} %collective-permute-done.1.from_outer.side_1, ...), custom_call_target="tpu_custom_call" | custom-call | tf_op jit(solution)/shard_map/density_inside/pallas_call | solution.py:361
  16.4 1.7 %all-to-all-done.got = f32[32,8,128]{2,1,0:T(8,128)S(1)} async-done(((f32[32,8,128]{2,1,0:T(8,128)}), f32[32,8,128]{2,1,0:T(8,128)S(1)}, u32[]{:S(2)}, u32[]{:S(2)}) %all-to-all-start) | async-done | bytes 131104 | tf_op jit(solution)/shard_map/all_to_all | solution.py:343
  18.1 5.5 %binning.1.extra = f32[8,8,512]{2,1,0:T(8,128)S(1)} custom-call(f32[32,8,128]{2,1,0:T(8,128)S(1)} %all-to-all-done.got, f32[4,8,512]{2,1,0:T(8,128)S(1)} %get-tuple-element.26._.inner), custom_call_target="tpu_custom_call" | custom-call | tf_op jit(solution)/shard_map/binning/pallas_call | solution.py:389
  23.6 0.0 collective-permute-done.2.end_1
  23.6 0.9 %density_ends.1 = (f32[8,8,512]{2,1,0:T(8,128)S(1)}, f32[2,8,512]{2,1,0:T(8,128)S(1)}, f32[2,8,512]{2,1,0:T(8,128)S(1)}) custom-call(f32[8,8,512]{2,1,0:T(8,128)S(1)} %get-tuple-element.20.field.extra, f32[2,8,512]{2,1,0:T(8,128)S(1)} %collective-permute-done.from_partner.side_0, f32[2,8,512]{2,1,0:T(8,128)S(1)} %collective-permute-done.1.from_outer.side_1, ...), custom_call_target="tpu_custom_call" | custom-call | tf_op jit(solution)/shard_map/density_ends/pallas_call | solution.py:375
  24.6 0.4 %collective-permute-start.4 = (f32[2,8,512]{2,1,0:T(8,128)S(1)}, f32[2,8,512]{2,1,0:T(8,128)S(1)}, u32[]{:S(2)}, u32[]{:S(2)}) collective-permute-start(f32[2,8,512]{2,1,0:T(8,128)S(1)} %get-tuple-element.29), channel_id=1, source_target_pairs={{0,1},{2,3},{4,5},{6,7},{1,0},{3,2},{5,4},{7,6},{8,9},{10,11},{12,... | collective-permute-start | bytes 98312 | tf_op jit(solution)/shard_map/ppermute | solution.py:308
  25.0 1.5 %collective-permute-start.5 = (f32[2,8,512]{2,1,0:T(8,128)S(1)}, f32[2,8,512]{2,1,0:T(8,128)S(1)}, u32[]{:S(2)}, u32[]{:S(2)}) collective-permute-start(f32[2,8,512]{2,1,0:T(8,128)S(1)} %get-tuple-element.30), channel_id=1, source_target_pairs={{1,2},{3,4},{5,6},{7,0},{2,1},{4,3},{6,5},{0,7},{9,10},{11,12},{13... | collective-permute-start | bytes 98312 | tf_op jit(solution)/shard_map/ppermute | solution.py:308
  26.5 0.1 pad_bitcast_fusion
  26.6 3.5 %collective-permute-done.5.from_outer.side_1 = f32[2,8,512]{2,1,0:T(8,128)S(1)} collective-permute-done((f32[2,8,512]{2,1,0:T(8,128)S(1)}, f32[2,8,512]{2,1,0:T(8,128)S(1)}, u32[]{:S(2)}, u32[]{:S(2)}) %collective-permute-start.5) | collective-permute-done | bytes 32800 | tf_op jit(solution)/shard_map/ppermute | solution.py:308
  30.1 0.7 %collective-permute-start.6 = (f32[3,8,512]{2,1,0:T(8,128)S(1)}, f32[3,8,512]{2,1,0:T(8,128)S(1)}, u32[]{:S(2)}, u32[]{:S(2)}) collective-permute-start(f32[3,8,512]{2,1,0:T(8,128)S(1)} %get-tuple-element.31), channel_id=1, source_target_pairs={{8,16},{16,8},{9,17},{17,9},{10,18},{18,10},{11,19},{19,11},{12,20... | collective-permute-start | bytes 147464 | tf_op jit(solution)/shard_map/ppermute | solution.py:308
  30.8 3.4 %collective-permute-start.7 = (f32[3,8,512]{2,1,0:T(8,128)S(1)}, f32[3,8,512]{2,1,0:T(8,128)S(1)}, u32[]{:S(2)}, u32[]{:S(2)}) collective-permute-start(f32[3,8,512]{2,1,0:T(8,128)S(1)} %get-tuple-element.32), channel_id=1, source_target_pairs={{0,8},{16,24},{8,0},{24,16},{1,9},{17,25},{9,1},{25,17},{2,10},{18... | collective-permute-start | bytes 147464 | tf_op jit(solution)/shard_map/ppermute | solution.py:308
  34.2 0.1 pad_maximum_fusion
  34.3 1.1 %back_inside.1 = (f32[4,8,512]{2,1,0:T(8,128)S(1)}, f32[3,3,6,8,512]{4,3,2,1,0:T(8,128)S(1)}) custom-call(f32[8,8,512]{2,1,0:T(8,128)S(1)} %get-tuple-element.28.field, f32[2,8,512]{2,1,0:T(8,128)S(1)} %collective-permute-done.4.from_partner.side_0, f32[2,8,512]{2,1,0:T(8,128)S(1)} %collective-permute-done.5.from_outer.side_1, ...), custom_call_target="tpu_custom_call" | custom-call | tf_op jit(solution)/shard_map/back_inside/pallas_call | solution.py:361
  35.3 1.3 %collective-permute-done.7.end_0 = f32[3,8,512]{2,1,0:T(8,128)S(1)} collective-permute-done((f32[3,8,512]{2,1,0:T(8,128)S(1)}, f32[3,8,512]{2,1,0:T(8,128)S(1)}, u32[]{:S(2)}, u32[]{:S(2)}) %collective-permute-start.7) | collective-permute-done | bytes 49184 | tf_op jit(solution)/shard_map/ppermute | solution.py:308
  36.7 1.6 %back_ends.1 = f32[8,8,512]{2,1,0:T(8,128)} custom-call(f32[8,8,512]{2,1,0:T(8,128)S(1)} %get-tuple-element.28.field, f32[2,8,512]{2,1,0:T(8,128)S(1)} %collective-permute-done.4.from_partner.side_0, f32[2,8,512]{2,1,0:T(8,128)S(1)} %collective-permute-done.5.from_outer.side_1, f32[3,8,512]{2,1,0:T(8,128)S(1)} %collective-permute-done.6.end_1, ...), custom_call_target="tpu_custom_call" | custom-call | tf_op jit(solution)/shard_map/back_ends/pallas_call | solution.py:375
  (11 shorter events, 0.1 us)
Async XLA Ops:
  1.9 8.1 %collective-permute-start = (f32[2,8,512]{2,1,0:T(8,128)S(1)}, f32[2,8,512]{2,1,0:T(8,128)S(1)}, u32[]{:S(2)}, u32[]{:S(2)}) collective-permute-start(f32[2,8,512]{2,1,0:T(8,128)S(1)} %get-tuple-element.21), channel_id=1, source_target_pairs={{0,1},{2,3},{4,5},{6,7},{1,0},{3,2},{5,4},{7,6},{8,9},{10,11},{12,... | collective-permute-start | bytes 98312 | tf_op jit(solution)/shard_map/ppermute | solution.py:308
  2.4 7.6 %collective-permute-start.1 = (f32[2,8,512]{2,1,0:T(8,128)S(1)}, f32[2,8,512]{2,1,0:T(8,128)S(1)}, u32[]{:S(2)}, u32[]{:S(2)}) collective-permute-start(f32[2,8,512]{2,1,0:T(8,128)S(1)} %get-tuple-element.22), channel_id=1, source_target_pairs={{1,2},{3,4},{5,6},{7,0},{2,1},{4,3},{6,5},{0,7},{9,10},{11,12},{13... | collective-permute-start | bytes 98312 | tf_op jit(solution)/shard_map/ppermute | solution.py:308
  7.1 2.8 %copy-start = (f32[2,27,512]{2,0,1:T(2,128)S(1)}, f32[2,27,512]{2,0,1:T(2,128)}, u32[]{:S(2)}) copy-start(f32[2,27,512]{2,0,1:T(2,128)} %param.13) | copy-start | bytes 331780
  7.1 11.0 %all-to-all-start = ((f32[32,8,128]{2,1,0:T(8,128)}), f32[32,8,128]{2,1,0:T(8,128)S(1)}, u32[]{:S(2)}, u32[]{:S(2)}) async-start(f32[32,8,128]{2,1,0:T(8,128)} %get-tuple-element.25), calls=%async_computation | async-start | bytes 262144 | tf_op jit(solution)/shard_map/all_to_all | solution.py:343
  10.0 13.6 %collective-permute-start.2 = (f32[3,8,512]{2,1,0:T(8,128)S(1)}, f32[3,8,512]{2,1,0:T(8,128)S(1)}, u32[]{:S(2)}, u32[]{:S(2)}) collective-permute-start(f32[3,8,512]{2,1,0:T(8,128)S(1)} %get-tuple-element.23), channel_id=1, source_target_pairs={{8,16},{16,8},{9,17},{17,9},{10,18},{18,10},{11,19},{19,11},{12,20... | collective-permute-start | bytes 147464 | tf_op jit(solution)/shard_map/ppermute | solution.py:308
  10.7 13.0 %collective-permute-start.3 = (f32[3,8,512]{2,1,0:T(8,128)S(1)}, f32[3,8,512]{2,1,0:T(8,128)S(1)}, u32[]{:S(2)}, u32[]{:S(2)}) collective-permute-start(f32[3,8,512]{2,1,0:T(8,128)S(1)} %get-tuple-element.24), channel_id=1, source_target_pairs={{0,8},{16,24},{8,0},{24,16},{1,9},{17,25},{9,1},{25,17},{2,10},{18... | collective-permute-start | bytes 147464 | tf_op jit(solution)/shard_map/ppermute | solution.py:308
  24.6 2.0 %collective-permute-start.4 = (f32[2,8,512]{2,1,0:T(8,128)S(1)}, f32[2,8,512]{2,1,0:T(8,128)S(1)}, u32[]{:S(2)}, u32[]{:S(2)}) collective-permute-start(f32[2,8,512]{2,1,0:T(8,128)S(1)} %get-tuple-element.29), channel_id=1, source_target_pairs={{0,1},{2,3},{4,5},{6,7},{1,0},{3,2},{5,4},{7,6},{8,9},{10,11},{12,... | collective-permute-start | bytes 98312 | tf_op jit(solution)/shard_map/ppermute | solution.py:308
  25.0 5.1 %collective-permute-start.5 = (f32[2,8,512]{2,1,0:T(8,128)S(1)}, f32[2,8,512]{2,1,0:T(8,128)S(1)}, u32[]{:S(2)}, u32[]{:S(2)}) collective-permute-start(f32[2,8,512]{2,1,0:T(8,128)S(1)} %get-tuple-element.30), channel_id=1, source_target_pairs={{1,2},{3,4},{5,6},{7,0},{2,1},{4,3},{6,5},{0,7},{9,10},{11,12},{13... | collective-permute-start | bytes 98312 | tf_op jit(solution)/shard_map/ppermute | solution.py:308
  30.1 5.2 %collective-permute-start.6 = (f32[3,8,512]{2,1,0:T(8,128)S(1)}, f32[3,8,512]{2,1,0:T(8,128)S(1)}, u32[]{:S(2)}, u32[]{:S(2)}) collective-permute-start(f32[3,8,512]{2,1,0:T(8,128)S(1)} %get-tuple-element.31), channel_id=1, source_target_pairs={{8,16},{16,8},{9,17},{17,9},{10,18},{18,10},{11,19},{19,11},{12,20... | collective-permute-start | bytes 147464 | tf_op jit(solution)/shard_map/ppermute | solution.py:308
  30.8 5.9 %collective-permute-start.7 = (f32[3,8,512]{2,1,0:T(8,128)S(1)}, f32[3,8,512]{2,1,0:T(8,128)S(1)}, u32[]{:S(2)}, u32[]{:S(2)}) collective-permute-start(f32[3,8,512]{2,1,0:T(8,128)S(1)} %get-tuple-element.32), channel_id=1, source_target_pairs={{0,8},{16,24},{8,0},{24,16},{1,9},{17,25},{9,1},{25,17},{2,10},{18... | collective-permute-start | bytes 147464 | tf_op jit(solution)/shard_map/ppermute | solution.py:308

commit v8 on v5

--- a/solution.py
+++ b/solution.py
@@ -161,7 +161,7 @@
 
 
 def refine_ends_kernel(
-    coefs, finish, finish_inner, packs, field, side_0, side_1, end_0, end_1, stencils, extra, inside, inner, *rest
+    coefs, finish, packs, field, side_0, side_1, end_1, end_0, stencils, extra, inside, inner, *rest
 ):
     out, *to_sides, middle, wide, shifted = rest
     height, width, radial = field.shape
@@ -191,9 +191,9 @@
     windows = {0: top[:3], 1: top[1:], height - 2: bottom[:3], height - 1: bottom[1:]}
     second_level(stencils.at[coefs[1]], windows, radial, write)
     for row in range(2, height - 2):
-        out[row] = finish_inner(inner[row - 2], extra[row])
+        out[row] = inner[row - 2]
     if packs:
-        pack_sides([out[row] for row in range(height)], *to_sides)
+        pack_sides([out[row] * extra[row] for row in range(height)], *to_sides)
 
 
 def open_kernel(
@@ -232,8 +232,9 @@
         out[owner] = jnp.where(row < RUNS, window(residual[at, :]), pltpu.roll(window(cell), RUNS, 0))
 
 
-def behind_of(got, *, radial, pixels):
+def behind_of(got, part, *, height, width, radial):
     half = radial // 2
+    pixels = height * width // 2
     classes = 2 * pixels
     shards, rows, _ = got.shape
     bf16 = jnp.bfloat16
@@ -243,7 +244,6 @@
         for first in range(0, half, LANES)
     ]
     zero = jnp.zeros((), bf16)
-    one = jnp.ones((), bf16)
 
     def tall(row):
         return jnp.concatenate([jnp.broadcast_to(row, (16, LANES)).astype(bf16)] * (classes // 16), axis=0)
@@ -253,7 +253,9 @@
     pixel = lax.shift_right_logical(cell, radial.bit_length() - 1)
     bins = lax.bitwise_and(cell, radial - 1)
     upper = (bins >= half).astype(jnp.int32)
-    label = (upper * pixels + pixel).astype(jnp.float32)
+    place = lax.bitwise_and(pixel + 2, width - 1)
+    own = upper * pixels + lax.shift_right_logical(pixel, 3) * 4 + lax.bitwise_and(place, 3)
+    label = jnp.where(lax.shift_right_logical(place, 2) == part, own, classes).astype(jnp.float32)
     lows = jnp.transpose((bins - upper * half + 1).astype(jnp.float32))
     coarse = tiles.astype(bf16).astype(jnp.float32)
     rest = tiles - coarse
@@ -263,9 +265,10 @@
         left, right = [], []
         for run in range(2 * RUNS):
             row = (first + run // RUNS) * rows + run % RUNS
-            away = tall(label[row + RUNS:row + RUNS + 1]) - column
-            mine = jnp.maximum(one - away * away, zero)
-            left.append(jnp.concatenate([mine * tall(coarse[row:row + 1]), mine * tall(rest[row:row + 1])], axis=0))
+            mine = tall(label[row + RUNS:row + RUNS + 1]) == column
+            left.append(jnp.concatenate([
+                jnp.where(mine, tall(coarse[row:row + 1]), zero), jnp.where(mine, tall(rest[row:row + 1]), zero)
+            ], axis=0))
             low = jnp.broadcast_to(lows[:, row + RUNS:row + RUNS + 1], (LANES, LANES)).astype(bf16)
             right.append(jnp.concatenate([jnp.maximum(low, place) for place in places], axis=1))
         total = total + jnp.dot(
@@ -276,15 +279,31 @@
     lane = lax.broadcasted_iota(jnp.int32, both.shape, 1)
     at_least = jnp.where(lane == 0, every, pltpu.roll(both, 1, 1) - both + every)
     near, far = at_least[:pixels], at_least[pixels:]
-    return near + far[:, :1], far
-
-
-def bin_kernel(got, _, behind):
+    return jnp.concatenate([near + far[:, :1], far], axis=1)
+
+
+def column_rows(packed, part, height):
+    rows = []
+    for row in range(height):
+        tile = packed[row // 2 * SUBLANES:(row // 2 + 1) * SUBLANES]
+        turn = row % 2 * 4 + (2 if part == 0 else SUBLANES - 2)
+        rows.append(pltpu.roll(tile, (SUBLANES - turn) % SUBLANES, 0))
+    return rows
+
+
+def bin_sides_kernel(got, _, behind):
     height, width, radial = behind.shape
-    near, far = behind_of(got, radial=radial, pixels=height * width)
-    for row in range(height):
-        at = slice(row * width, (row + 1) * width)
-        behind[row] = jnp.concatenate([near[at], far[at]], axis=1)
+    packed = behind_of(got, 0, height=height, width=width, radial=radial)
+    for row, values in enumerate(column_rows(packed, 0, height)):
+        behind[row] = values
+
+
+def bin_rest_kernel(got, density, behind, upstream):
+    height, width, radial = behind.shape
+    sub = sublane(radial)
+    packed = behind_of(got, 1, height=height, width=width, radial=radial)
+    for row, values in enumerate(column_rows(packed, 1, height)):
+        upstream[row] = density[row] * jnp.where((sub < 2) | (sub >= 6), behind[row], values)
 
 
 def mirror(stencils):
@@ -295,7 +314,7 @@
     return jnp.stack([back, turned[:, :, 1], ahead], axis=2).reshape(stencils.shape)
 
 
-def swap(to_partner, to_outer, axis, closed):
+def swap(to_partner, to_outer, axis, closed, outer_first=False):
     count = lax.axis_size(axis)
     outer = [(i, (i + 1) % count) for i in range(1, count, 2) if closed or i + 1 < count]
     inner = [(i, i + 1) for i in range(0, count - 1, 2)]
@@ -303,8 +322,8 @@
     def both_ways(pairs):
         return pairs + [(j, i) for i, j in pairs]
 
-    from_partner = lax.ppermute(to_partner, axis, both_ways(inner))
-    return from_partner, lax.ppermute(to_outer, axis, both_ways(outer))
+    moves = [(to_partner, inner), (to_outer, outer)]
+    return tuple(lax.ppermute(values, axis, both_ways(pairs)) for values, pairs in moves[::-1 if outer_first else 1])
 
 
 VMEM = pl.BlockSpec(memory_space=pltpu.VMEM)
@@ -351,7 +370,7 @@
             compiler_params=LIMIT,
             name=name + "_pack",
         )(field, *beside)
-        return beside, swap(*to_ends, "lat", False)
+        return beside, swap(*to_ends, "lat", False, outer_first=True)
 
     rows = pltpu.VMEM((height, 2 * width, radial), f32)
     moved = pltpu.VMEM((2, height, 2 * width, radial), f32)
@@ -370,9 +389,9 @@
             name=name + "_inside",
         )(field, *beside, table, extra)
 
-    def refined_ends(coefs, finish, finish_inner, field, beside, above, table, extra, inner, middle, name, packs):
+    def refined_ends(coefs, finish, field, beside, above, table, extra, inner, middle, name, packs):
         return pl.pallas_call(
-            functools.partial(refine_ends_kernel, coefs, finish, finish_inner, packs),
+            functools.partial(refine_ends_kernel, coefs, finish, packs),
             out_shape=(tile, sides, sides) if packs else tile,
             in_specs=[VMEM] * 9,
             out_specs=(VMEM,) * 3 if packs else VMEM,
@@ -386,17 +405,24 @@
         (0, 1), lambda value, _: jnp.exp(value), latent, beside, stencils, latent, "density"
     )
     behind = pl.pallas_call(
-        bin_kernel,
+        bin_sides_kernel,
         out_shape=tile,
         in_specs=[VMEM, VMEM],
         out_specs=VMEM,
         compiler_params=LIMIT,
-        name="binning",
+        name="bin_sides",
     )(got, inner)
-    upstream, *to_sides = refined_ends(
-        (0, 1), lambda value, mass: jnp.exp(value) * mass, lambda value, mass: value * mass,
-        latent, beside, above, stencils, behind, inner, middle, "density", True,
-    )
+    density, *to_sides = refined_ends(
+        (0, 1), lambda value, _: jnp.exp(value), latent, beside, above, stencils, behind, inner, middle, "density", True,
+    )
+    upstream = pl.pallas_call(
+        bin_rest_kernel,
+        out_shape=tile,
+        in_specs=[VMEM] * 3,
+        out_specs=VMEM,
+        compiler_params=LIMIT,
+        name="bin_rest",
+    )(got, density, behind)
 
     mirrored = mirror(stencils)
     beside, above = spread(upstream, to_sides, "back")
@@ -404,8 +430,7 @@
         (1, 0), lambda value, field: field + value, upstream, beside, mirrored, latent, "back"
     )
     return refined_ends(
-        (1, 0), lambda value, field: field + value, lambda value, _: value,
-        upstream, beside, above, mirrored, latent, inner, middle, "back", False,
+        (1, 0), lambda value, field: field + value, upstream, beside, above, mirrored, latent, inner, middle, "back", False,
     )
 
 

time: 35.7 us -> 35.2 us (0.986)
  the two profiles are of different devices: /device:TPU:2 before, /device:TPU:0 now
where the time goes in v8:
time: 35.2 us; the launch traced here: 35 us
  starting transfers between devices  19.2 us (55%)
  Pallas kernels  11.1 us (32%)
  waiting for transfers between devices  4.27 us (12%)
    ppermute x8, starting transfers between devices, swap(): lax.ppermute(values, axis, both_ways(pairs))  16.3 us
    all_to_all x1, starting transfers between devices, on_device(): lax.all_to_all(packed, ('lat', 'lon'), split_axis=0, concat_axis=0, tiled...  2.81 us
    ppermute x8, waiting for transfers between devices, swap(): lax.ppermute(values, axis, both_ways(pairs))  2.6 us
    pallas_call x2, Pallas kernels, refined_ends(): pl.pallas_call(functools.partial(refine_ends_kernel, coefs, finish, packs...  2.5 us
    pallas_call x1, Pallas kernels, on_device(): pl.pallas_call(bin_rest_kernel, out_shape=tile, in_specs=[VMEM] * 3, out_...  2.28 us
    pallas_call x1, Pallas kernels, on_device(): pl.pallas_call(bin_sides_kernel, out_shape=tile, in_specs=[VMEM, VMEM], o...  2.28 us
    pallas_call x2, Pallas kernels, refined_inside(): pl.pallas_call(functools.partial(refine_inside_kernel, coefs, finish), ou...  2.12 us
    pallas_call x1, Pallas kernels, on_device(): pl.pallas_call(open_kernel, out_shape=(jax.ShapeDtypeStruct((shards, 2 *...  1.84 us
  transfers between devices with their start and end apart: 9, of which 3 were waited for; matrix products, arithmetic and copies ran while one was open for 1% of the time, Pallas kernels for 19%

profile of v8, /device:TPU:0, one launch (start us, length us, event | category | flops | bytes accessed | tf_op | source)
XLA Modules:
  0.0 35.0 jit_solution(9151001355105580690)
XLA Ops:
  0.0 1.8 %opening.1 = (f32[32,8,128]{2,1,0:T(8,128)}, f32[8,8,512]{2,1,0:T(8,128)S(1)}, f32[2,8,512]{2,1,0:T(8,128)S(1)}, f32[2,8,512]{2,1,0:T(8,128)S(1)}) custom-call(s32[1,32]{1,0:T(1,128)} %counts_in.1, s32[1,32]{1,0:T(1,128)} %offsets_in.1, f32[128,128]{1,0:T(8,128)} %bitcast.20, s32[128,128]{1,0:T(8,128)} %bitcast.21, s32[128,128]{1,0:T(8,128)} %bitcast.22, ...), custom_call_target="tpu_custom_call" | custom-call | tf_op jit(solution)/shard_map/opening/pallas_call | solution.py:347
  1.9 0.5 %collective-permute-start = (f32[2,8,512]{2,1,0:T(8,128)S(1)}, f32[2,8,512]{2,1,0:T(8,128)S(1)}, u32[]{:S(2)}, u32[]{:S(2)}) collective-permute-start(f32[2,8,512]{2,1,0:T(8,128)S(1)} %get-tuple-element.22), channel_id=1, source_target_pairs={{0,1},{2,3},{4,5},{6,7},{1,0},{3,2},{5,4},{7,6},{8,9},{10,11},{12,... | collective-permute-start | bytes 98312 | tf_op jit(solution)/shard_map/ppermute | solution.py:326
  2.4 4.7 %collective-permute-start.1 = (f32[2,8,512]{2,1,0:T(8,128)S(1)}, f32[2,8,512]{2,1,0:T(8,128)S(1)}, u32[]{:S(2)}, u32[]{:S(2)}) collective-permute-start(f32[2,8,512]{2,1,0:T(8,128)S(1)} %get-tuple-element.23), channel_id=1, source_target_pairs={{1,2},{3,4},{5,6},{7,0},{2,1},{4,3},{6,5},{0,7},{9,10},{11,12},{13... | collective-permute-start | bytes 98312 | tf_op jit(solution)/shard_map/ppermute | solution.py:326
  7.1 2.8 %all-to-all-start = ((f32[32,8,128]{2,1,0:T(8,128)}), f32[32,8,128]{2,1,0:T(8,128)S(1)}, u32[]{:S(2)}, u32[]{:S(2)}) async-start(f32[32,8,128]{2,1,0:T(8,128)} %get-tuple-element.20), calls=%async_computation | async-start | bytes 262144 | tf_op jit(solution)/shard_map/all_to_all | solution.py:361
  9.9 0.0 collective-permute-done.1.from_outer.side_1
  10.0 0.7 %collective-permute-start.2 = (f32[3,8,512]{2,1,0:T(8,128)S(1)}, f32[3,8,512]{2,1,0:T(8,128)S(1)}, u32[]{:S(2)}, u32[]{:S(2)}) collective-permute-start(f32[3,8,512]{2,1,0:T(8,128)S(1)} %get-tuple-element.24), channel_id=1, source_target_pairs={{8,16},{16,8},{9,17},{17,9},{10,18},{18,10},{11,19},{19,11},{12,20... | collective-permute-start | bytes 147464 | tf_op jit(solution)/shard_map/ppermute | solution.py:326
  10.7 4.5 %collective-permute-start.3 = (f32[3,8,512]{2,1,0:T(8,128)S(1)}, f32[3,8,512]{2,1,0:T(8,128)S(1)}, u32[]{:S(2)}, u32[]{:S(2)}) collective-permute-start(f32[3,8,512]{2,1,0:T(8,128)S(1)} %get-tuple-element.25), channel_id=1, source_target_pairs={{0,8},{16,24},{8,0},{24,16},{1,9},{17,25},{9,1},{25,17},{2,10},{18... | collective-permute-start | bytes 147464 | tf_op jit(solution)/shard_map/ppermute | solution.py:326
  15.2 0.1 slice_bitcast_fusion.1
  15.3 1.1 %density_inside.1 = (f32[4,8,512]{2,1,0:T(8,128)S(1)}, f32[3,3,6,8,512]{4,3,2,1,0:T(8,128)S(1)}) custom-call(f32[8,8,512]{2,1,0:T(8,128)S(1)} %get-tuple-element.21.field.extra, f32[2,8,512]{2,1,0:T(8,128)S(1)} %collective-permute-done.from_partner.side_0, f32[2,8,512]{2,1,0:T(8,128)S(1)} %collective-permute-done.1.from_outer.side_1, ...), custom_call_target="tpu_custom_call" | custom-call | tf_op jit(solution)/shard_map/density_inside/pallas_call | solution.py:379
  16.4 1.7 %all-to-all-done.got = f32[32,8,128]{2,1,0:T(8,128)S(1)} async-done(((f32[32,8,128]{2,1,0:T(8,128)}), f32[32,8,128]{2,1,0:T(8,128)S(1)}, u32[]{:S(2)}, u32[]{:S(2)}) %all-to-all-start) | async-done | bytes 131104 | tf_op jit(solution)/shard_map/all_to_all | solution.py:361
  18.1 2.3 %bin_sides.1.extra.behind = f32[8,8,512]{2,1,0:T(8,128)S(1)} custom-call(f32[32,8,128]{2,1,0:T(8,128)S(1)} %all-to-all-done.got, f32[4,8,512]{2,1,0:T(8,128)S(1)} %get-tuple-element.26._.inner), custom_call_target="tpu_custom_call" | custom-call | tf_op jit(solution)/shard_map/bin_sides/pallas_call | solution.py:407
  20.4 0.9 %density_ends.1 = (f32[8,8,512]{2,1,0:T(8,128)S(1)}, f32[2,8,512]{2,1,0:T(8,128)S(1)}, f32[2,8,512]{2,1,0:T(8,128)S(1)}) custom-call(f32[8,8,512]{2,1,0:T(8,128)S(1)} %get-tuple-element.21.field.extra, f32[2,8,512]{2,1,0:T(8,128)S(1)} %collective-permute-done.from_partner.side_0, f32[2,8,512]{2,1,0:T(8,128)S(1)} %collective-permute-done.1.from_outer.side_1, ...), custom_call_target="tpu_custom_call" | custom-call | tf_op jit(solution)/shard_map/density_ends/pallas_call | solution.py:393
  21.3 0.4 %collective-permute-start.4 = (f32[2,8,512]{2,1,0:T(8,128)S(1)}, f32[2,8,512]{2,1,0:T(8,128)S(1)}, u32[]{:S(2)}, u32[]{:S(2)}) collective-permute-start(f32[2,8,512]{2,1,0:T(8,128)S(1)} %get-tuple-element.29), channel_id=1, source_target_pairs={{0,1},{2,3},{4,5},{6,7},{1,0},{3,2},{5,4},{7,6},{8,9},{10,11},{12,... | collective-permute-start | bytes 98312 | tf_op jit(solution)/shard_map/ppermute | solution.py:326
  21.7 1.5 %collective-permute-start.5 = (f32[2,8,512]{2,1,0:T(8,128)S(1)}, f32[2,8,512]{2,1,0:T(8,128)S(1)}, u32[]{:S(2)}, u32[]{:S(2)}) collective-permute-start(f32[2,8,512]{2,1,0:T(8,128)S(1)} %get-tuple-element.30), channel_id=1, source_target_pairs={{1,2},{3,4},{5,6},{7,0},{2,1},{4,3},{6,5},{0,7},{9,10},{11,12},{13... | collective-permute-start | bytes 98312 | tf_op jit(solution)/shard_map/ppermute | solution.py:326
  23.2 0.1 pad_bitcast_fusion
  23.3 2.3 %bin_rest.1.field = f32[8,8,512]{2,1,0:T(8,128)S(1)} custom-call(f32[32,8,128]{2,1,0:T(8,128)S(1)} %all-to-all-done.got, f32[8,8,512]{2,1,0:T(8,128)S(1)} %get-tuple-element.28.density, f32[8,8,512]{2,1,0:T(8,128)S(1)} %bin_sides.1.extra.behind), custom_call_target="tpu_custom_call" | custom-call | tf_op jit(solution)/shard_map/bin_rest/pallas_call | solution.py:418
  25.6 0.0 collective-permute-done.4.from_partner.side_0
  25.6 1.2 %collective-permute-done.5.from_outer.side_1 = f32[2,8,512]{2,1,0:T(8,128)S(1)} collective-permute-done((f32[2,8,512]{2,1,0:T(8,128)S(1)}, f32[2,8,512]{2,1,0:T(8,128)S(1)}, u32[]{:S(2)}, u32[]{:S(2)}) %collective-permute-start.5) | collective-permute-done | bytes 32800 | tf_op jit(solution)/shard_map/ppermute | solution.py:326
  26.9 0.7 %collective-permute-start.6 = (f32[3,8,512]{2,1,0:T(8,128)S(1)}, f32[3,8,512]{2,1,0:T(8,128)S(1)}, u32[]{:S(2)}, u32[]{:S(2)}) collective-permute-start(f32[3,8,512]{2,1,0:T(8,128)S(1)} %get-tuple-element.31), channel_id=1, source_target_pairs={{8,16},{16,8},{9,17},{17,9},{10,18},{18,10},{11,19},{19,11},{12,20... | collective-permute-start | bytes 147464 | tf_op jit(solution)/shard_map/ppermute | solution.py:326
  27.5 3.4 %collective-permute-start.7 = (f32[3,8,512]{2,1,0:T(8,128)S(1)}, f32[3,8,512]{2,1,0:T(8,128)S(1)}, u32[]{:S(2)}, u32[]{:S(2)}) collective-permute-start(f32[3,8,512]{2,1,0:T(8,128)S(1)} %get-tuple-element.32), channel_id=1, source_target_pairs={{0,8},{16,24},{8,0},{24,16},{1,9},{17,25},{9,1},{25,17},{2,10},{18... | collective-permute-start | bytes 147464 | tf_op jit(solution)/shard_map/ppermute | solution.py:326
  30.9 0.1 pad_maximum_fusion
  31.0 1.1 %back_inside.1 = (f32[4,8,512]{2,1,0:T(8,128)S(1)}, f32[3,3,6,8,512]{4,3,2,1,0:T(8,128)S(1)}) custom-call(f32[8,8,512]{2,1,0:T(8,128)S(1)} %bin_rest.1.field, f32[2,8,512]{2,1,0:T(8,128)S(1)} %collective-permute-done.4.from_partner.side_0, f32[2,8,512]{2,1,0:T(8,128)S(1)} %collective-permute-done.5.from_outer.side_1, f32[2,27,512]{2,1,0:T(8,128)S(1)} %copy.23.stencils, ...), custom_call_target="tpu_custom_call" | custom-call | tf_op jit(solution)/shard_map/back_inside/pallas_call | solution.py:379
  32.1 1.3 %collective-permute-done.7.end_0 = f32[3,8,512]{2,1,0:T(8,128)S(1)} collective-permute-done((f32[3,8,512]{2,1,0:T(8,128)S(1)}, f32[3,8,512]{2,1,0:T(8,128)S(1)}, u32[]{:S(2)}, u32[]{:S(2)}) %collective-permute-start.7) | collective-permute-done | bytes 49184 | tf_op jit(solution)/shard_map/ppermute | solution.py:326
  33.4 1.6 %back_ends.1 = f32[8,8,512]{2,1,0:T(8,128)} custom-call(f32[8,8,512]{2,1,0:T(8,128)S(1)} %bin_rest.1.field, f32[2,8,512]{2,1,0:T(8,128)S(1)} %collective-permute-done.4.from_partner.side_0, f32[2,8,512]{2,1,0:T(8,128)S(1)} %collective-permute-done.5.from_outer.side_1, f32[3,8,512]{2,1,0:T(8,128)S(1)} %collective-permute-done.6.end_1, ...), custom_call_target="tpu_custom_call" | custom-call | tf_op jit(solution)/shard_map/back_ends/pallas_call | solution.py:393
  (12 shorter events, 0.1 us)
Async XLA Ops:
  1.9 8.1 %collective-permute-start = (f32[2,8,512]{2,1,0:T(8,128)S(1)}, f32[2,8,512]{2,1,0:T(8,128)S(1)}, u32[]{:S(2)}, u32[]{:S(2)}) collective-permute-start(f32[2,8,512]{2,1,0:T(8,128)S(1)} %get-tuple-element.22), channel_id=1, source_target_pairs={{0,1},{2,3},{4,5},{6,7},{1,0},{3,2},{5,4},{7,6},{8,9},{10,11},{12,... | collective-permute-start | bytes 98312 | tf_op jit(solution)/shard_map/ppermute | solution.py:326
  2.4 7.6 %collective-permute-start.1 = (f32[2,8,512]{2,1,0:T(8,128)S(1)}, f32[2,8,512]{2,1,0:T(8,128)S(1)}, u32[]{:S(2)}, u32[]{:S(2)}) collective-permute-start(f32[2,8,512]{2,1,0:T(8,128)S(1)} %get-tuple-element.23), channel_id=1, source_target_pairs={{1,2},{3,4},{5,6},{7,0},{2,1},{4,3},{6,5},{0,7},{9,10},{11,12},{13... | collective-permute-start | bytes 98312 | tf_op jit(solution)/shard_map/ppermute | solution.py:326
  7.1 2.8 %copy-start = (f32[2,27,512]{2,0,1:T(2,128)S(1)}, f32[2,27,512]{2,0,1:T(2,128)}, u32[]{:S(2)}) copy-start(f32[2,27,512]{2,0,1:T(2,128)} %param.13) | copy-start | bytes 331780
  7.1 11.0 %all-to-all-start = ((f32[32,8,128]{2,1,0:T(8,128)}), f32[32,8,128]{2,1,0:T(8,128)S(1)}, u32[]{:S(2)}, u32[]{:S(2)}) async-start(f32[32,8,128]{2,1,0:T(8,128)} %get-tuple-element.20), calls=%async_computation | async-start | bytes 262144 | tf_op jit(solution)/shard_map/all_to_all | solution.py:361
  10.0 10.4 %collective-permute-start.2 = (f32[3,8,512]{2,1,0:T(8,128)S(1)}, f32[3,8,512]{2,1,0:T(8,128)S(1)}, u32[]{:S(2)}, u32[]{:S(2)}) collective-permute-start(f32[3,8,512]{2,1,0:T(8,128)S(1)} %get-tuple-element.24), channel_id=1, source_target_pairs={{8,16},{16,8},{9,17},{17,9},{10,18},{18,10},{11,19},{19,11},{12,20... | collective-permute-start | bytes 147464 | tf_op jit(solution)/shard_map/ppermute | solution.py:326
  10.7 9.7 %collective-permute-start.3 = (f32[3,8,512]{2,1,0:T(8,128)S(1)}, f32[3,8,512]{2,1,0:T(8,128)S(1)}, u32[]{:S(2)}, u32[]{:S(2)}) collective-permute-start(f32[3,8,512]{2,1,0:T(8,128)S(1)} %get-tuple-element.25), channel_id=1, source_target_pairs={{0,8},{16,24},{8,0},{24,16},{1,9},{17,25},{9,1},{25,17},{2,10},{18... | collective-permute-start | bytes 147464 | tf_op jit(solution)/shard_map/ppermute | solution.py:326
  21.3 4.3 %collective-permute-start.4 = (f32[2,8,512]{2,1,0:T(8,128)S(1)}, f32[2,8,512]{2,1,0:T(8,128)S(1)}, u32[]{:S(2)}, u32[]{:S(2)}) collective-permute-start(f32[2,8,512]{2,1,0:T(8,128)S(1)} %get-tuple-element.29), channel_id=1, source_target_pairs={{0,1},{2,3},{4,5},{6,7},{1,0},{3,2},{5,4},{7,6},{8,9},{10,11},{12,... | collective-permute-start | bytes 98312 | tf_op jit(solution)/shard_map/ppermute | solution.py:326
  21.7 5.1 %collective-permute-start.5 = (f32[2,8,512]{2,1,0:T(8,128)S(1)}, f32[2,8,512]{2,1,0:T(8,128)S(1)}, u32[]{:S(2)}, u32[]{:S(2)}) collective-permute-start(f32[2,8,512]{2,1,0:T(8,128)S(1)} %get-tuple-element.30), channel_id=1, source_target_pairs={{1,2},{3,4},{5,6},{7,0},{2,1},{4,3},{6,5},{0,7},{9,10},{11,12},{13... | collective-permute-start | bytes 98312 | tf_op jit(solution)/shard_map/ppermute | solution.py:326
  26.9 5.2 %collective-permute-start.6 = (f32[3,8,512]{2,1,0:T(8,128)S(1)}, f32[3,8,512]{2,1,0:T(8,128)S(1)}, u32[]{:S(2)}, u32[]{:S(2)}) collective-permute-start(f32[3,8,512]{2,1,0:T(8,128)S(1)} %get-tuple-element.31), channel_id=1, source_target_pairs={{8,16},{16,8},{9,17},{17,9},{10,18},{18,10},{11,19},{19,11},{12,20... | collective-permute-start | bytes 147464 | tf_op jit(solution)/shard_map/ppermute | solution.py:326
  27.5 5.9 %collective-permute-start.7 = (f32[3,8,512]{2,1,0:T(8,128)S(1)}, f32[3,8,512]{2,1,0:T(8,128)S(1)}, u32[]{:S(2)}, u32[]{:S(2)}) collective-permute-start(f32[3,8,512]{2,1,0:T(8,128)S(1)} %get-tuple-element.32), channel_id=1, source_target_pairs={{0,8},{16,24},{8,0},{24,16},{1,9},{17,25},{9,1},{25,17},{2,10},{18... | collective-permute-start | bytes 147464 | tf_op jit(solution)/shard_map/ppermute | solution.py:326

commit v9 on v8

--- a/solution.py
+++ b/solution.py
@@ -56,12 +56,16 @@
     return tiles
 
 
-def pack_ends_kernel(field, from_partner, from_outer, to_partner, to_outer):
+def in_order(turned, first, second):
+    return (second, first) if turned else (first, second)
+
+
+def pack_ends_kernel(turned, field, side_0, side_1, to_partner, to_outer):
     height, _, radial = field.shape
     _, odd = position("lat")
     sub = sublane(radial)
     outside = (sub < 2) | (sub >= 6)
-    tiles = unpack_sides(from_partner, from_outer, height)
+    tiles = unpack_sides(*in_order(turned, side_0, side_1), height)
 
     def ends(first):
         return (
@@ -145,9 +149,9 @@
     tiles_of_bins(radial, body)
 
 
-def refine_inside_kernel(coefs, finish, field, side_0, side_1, stencils, extra, out, middle, wide, shifted):
+def refine_inside_kernel(turned, coefs, finish, field, side_0, side_1, stencils, extra, out, middle, wide, shifted):
     height, width, radial = field.shape
-    tiles = unpack_sides(side_0, side_1, height)
+    tiles = unpack_sides(*in_order(turned, side_0, side_1), height)
     for row in range(height):
         wide[row, :width] = field[row]
         wide[row, width:] = tiles[row]
@@ -161,11 +165,12 @@
 
 
 def refine_ends_kernel(
-    coefs, finish, packs, field, side_0, side_1, end_1, end_0, stencils, extra, inside, inner, *rest
+    turned, coefs, finish, packs, field, side_0, side_1, end_0, end_1, stencils, extra, inside, inner, *rest
 ):
     out, *to_sides, middle, wide, shifted = rest
     height, width, radial = field.shape
-    tiles = unpack_sides(side_0, side_1, height)
+    tiles = unpack_sides(*in_order(turned[0], side_0, side_1), height)
+    end_0, end_1 = in_order(turned[1], end_0, end_1)
     lat, odd = position("lat")
     for place in range(3):
         partner, outer = end_0[place], end_1[place]
@@ -256,7 +261,7 @@
     place = lax.bitwise_and(pixel + 2, width - 1)
     own = upper * pixels + lax.shift_right_logical(pixel, 3) * 4 + lax.bitwise_and(place, 3)
     label = jnp.where(lax.shift_right_logical(place, 2) == part, own, classes).astype(jnp.float32)
-    lows = jnp.transpose((bins - upper * half + 1).astype(jnp.float32))
+    lows = jnp.transpose((bins - upper * half + 1).astype(jnp.float32)).astype(bf16)
     coarse = tiles.astype(bf16).astype(jnp.float32)
     rest = tiles - coarse
 
@@ -269,7 +274,7 @@
             left.append(jnp.concatenate([
                 jnp.where(mine, tall(coarse[row:row + 1]), zero), jnp.where(mine, tall(rest[row:row + 1]), zero)
             ], axis=0))
-            low = jnp.broadcast_to(lows[:, row + RUNS:row + RUNS + 1], (LANES, LANES)).astype(bf16)
+            low = jnp.broadcast_to(lows[:, row + RUNS:row + RUNS + 1], (LANES, LANES))
             right.append(jnp.concatenate([jnp.maximum(low, place) for place in places], axis=1))
         total = total + jnp.dot(
             jnp.concatenate(left, axis=1), jnp.concatenate(right, axis=0), preferred_element_type=jnp.float32
@@ -360,24 +365,24 @@
     ])
     got = lax.all_to_all(packed, ("lat", "lon"), split_axis=0, concat_axis=0, tiled=True)
 
-    def spread(field, to_sides, name):
-        beside = swap(*to_sides, "lon", True)
+    def spread(field, to_sides, name, turned):
+        beside = swap(*to_sides, "lon", True, turned[0])
         to_ends = pl.pallas_call(
-            pack_ends_kernel,
+            functools.partial(pack_ends_kernel, turned[0]),
             out_shape=(ends, ends),
             in_specs=[VMEM] * 3,
             out_specs=(VMEM, VMEM),
             compiler_params=LIMIT,
             name=name + "_pack",
         )(field, *beside)
-        return beside, swap(*to_ends, "lat", False, outer_first=True)
+        return beside, swap(*to_ends, "lat", False, turned[1])
 
     rows = pltpu.VMEM((height, 2 * width, radial), f32)
     moved = pltpu.VMEM((2, height, 2 * width, radial), f32)
 
-    def refined_inside(coefs, finish, field, beside, table, extra, name):
+    def refined_inside(turned, coefs, finish, field, beside, table, extra, name):
         return pl.pallas_call(
-            functools.partial(refine_inside_kernel, coefs, finish),
+            functools.partial(refine_inside_kernel, turned[0], coefs, finish),
             out_shape=(
                 jax.ShapeDtypeStruct((height - 4, width, radial), f32),
                 jax.ShapeDtypeStruct((3, 3, height - 2, width, radial), f32),
@@ -389,9 +394,9 @@
             name=name + "_inside",
         )(field, *beside, table, extra)
 
-    def refined_ends(coefs, finish, field, beside, above, table, extra, inner, middle, name, packs):
+    def refined_ends(turned, coefs, finish, field, beside, above, table, extra, inner, middle, name, packs):
         return pl.pallas_call(
-            functools.partial(refine_ends_kernel, coefs, finish, packs),
+            functools.partial(refine_ends_kernel, turned, coefs, finish, packs),
             out_shape=(tile, sides, sides) if packs else tile,
             in_specs=[VMEM] * 9,
             out_specs=(VMEM,) * 3 if packs else VMEM,
@@ -400,9 +405,10 @@
             name=name + "_ends",
         )(field, *beside, *above, table, extra, middle, inner)
 
-    beside, above = spread(latent, to_sides, "density")
+    first_turned, last_turned = (False, True), (True, False)
+    beside, above = spread(latent, to_sides, "density", first_turned)
     inner, middle = refined_inside(
-        (0, 1), lambda value, _: jnp.exp(value), latent, beside, stencils, latent, "density"
+        first_turned, (0, 1), lambda value, _: jnp.exp(value), latent, beside, stencils, latent, "density"
     )
     behind = pl.pallas_call(
         bin_sides_kernel,
@@ -413,7 +419,8 @@
         name="bin_sides",
     )(got, inner)
     density, *to_sides = refined_ends(
-        (0, 1), lambda value, _: jnp.exp(value), latent, beside, above, stencils, behind, inner, middle, "density", True,
+        first_turned, (0, 1), lambda value, _: jnp.exp(value), latent, beside, above, stencils, behind, inner, middle,
+        "density", True,
     )
     upstream = pl.pallas_call(
         bin_rest_kernel,
@@ -425,12 +432,13 @@
     )(got, density, behind)
 
     mirrored = mirror(stencils)
-    beside, above = spread(upstream, to_sides, "back")
+    beside, above = spread(upstream, to_sides, "back", last_turned)
     inner, middle = refined_inside(
-        (1, 0), lambda value, field: field + value, upstream, beside, mirrored, latent, "back"
+        last_turned, (1, 0), lambda value, field: field + value, upstream, beside, mirrored, latent, "back"
     )
     return refined_ends(
-        (1, 0), lambda value, field: field + value, upstream, beside, above, mirrored, latent, inner, middle, "back", False,
+        last_turned, (1, 0), lambda value, field: field + value, upstream, beside, above, mirrored, latent, inner, middle,
+        "back", False,
     )
 
 

time: 35.2 us -> 34.2 us (0.972)
  the two profiles are of different devices: /device:TPU:0 before, /device:TPU:2 now
where the time goes in v9:
time: 34.2 us; the launch traced here: 34 us
  starting transfers between devices  15.3 us (45%)
  Pallas kernels  10.8 us (32%)
  waiting for transfers between devices  7.41 us (22%)
    ppermute x8, starting transfers between devices, swap(): lax.ppermute(values, axis, both_ways(pairs))  12.2 us
    ppermute x8, waiting for transfers between devices, swap(): lax.ppermute(values, axis, both_ways(pairs))  4.93 us
    all_to_all x1, starting transfers between devices, on_device(): lax.all_to_all(packed, ('lat', 'lon'), split_axis=0, concat_axis=0, tiled...  3.09 us
    pallas_call x2, Pallas kernels, refined_ends(): pl.pallas_call(functools.partial(refine_ends_kernel, turned, coefs, finis...  2.5 us
    all_to_all x1, waiting for transfers between devices, on_device(): lax.all_to_all(packed, ('lat', 'lon'), split_axis=0, concat_axis=0, tiled...  2.48 us
    pallas_call x1, Pallas kernels, on_device(): pl.pallas_call(bin_sides_kernel, out_shape=tile, in_specs=[VMEM, VMEM], o...  2.16 us
    pallas_call x1, Pallas kernels, on_device(): pl.pallas_call(bin_rest_kernel, out_shape=tile, in_specs=[VMEM] * 3, out_...  2.16 us
    pallas_call x2, Pallas kernels, refined_inside(): pl.pallas_call(functools.partial(refine_inside_kernel, turned[0], coefs,...  2.12 us
  transfers between devices with their start and end apart: 9, of which 3 were waited for; matrix products, arithmetic and copies ran while one was open for 1% of the time, Pallas kernels for 19%

profile of v9, /device:TPU:2, one launch (start us, length us, event | category | flops | bytes accessed | tf_op | source)
XLA Modules:
  0.0 34.0 jit_solution(724931325280444455)
XLA Ops:
  0.0 1.8 %opening.1 = (f32[32,8,128]{2,1,0:T(8,128)}, f32[8,8,512]{2,1,0:T(8,128)S(1)}, f32[2,8,512]{2,1,0:T(8,128)S(1)}, f32[2,8,512]{2,1,0:T(8,128)S(1)}) custom-call(s32[1,32]{1,0:T(1,128)} %counts_in.1, s32[1,32]{1,0:T(1,128)} %offsets_in.1, f32[128,128]{1,0:T(8,128)} %bitcast.20, s32[128,128]{1,0:T(8,128)} %bitcast.21, s32[128,128]{1,0:T(8,128)} %bitcast.22, ...), custom_call_target="tpu_custom_call" | custom-call | tf_op jit(solution)/shard_map/opening/pallas_call | solution.py:352
  1.9 0.1 collective-permute-start
  1.9 3.7 %collective-permute-start.1 = (f32[2,8,512]{2,1,0:T(8,128)S(1)}, f32[2,8,512]{2,1,0:T(8,128)S(1)}, u32[]{:S(2)}, u32[]{:S(2)}) collective-permute-start(f32[2,8,512]{2,1,0:T(8,128)S(1)} %get-tuple-element.23), channel_id=1, source_target_pairs={{1,2},{3,4},{5,6},{7,0},{2,1},{4,3},{6,5},{0,7},{9,10},{11,12},{13... | collective-permute-start | bytes 98312 | tf_op jit(solution)/shard_map/ppermute | solution.py:331
  5.6 3.1 %all-to-all-start = ((f32[32,8,128]{2,1,0:T(8,128)}), f32[32,8,128]{2,1,0:T(8,128)S(1)}, u32[]{:S(2)}, u32[]{:S(2)}) async-start(f32[32,8,128]{2,1,0:T(8,128)} %get-tuple-element.20), calls=%async_computation | async-start | bytes 262144 | tf_op jit(solution)/shard_map/all_to_all | solution.py:366
  8.8 0.0 collective-permute-done.side_0
  8.8 0.0 collective-permute-done.1.side_1
  8.8 3.4 %collective-permute-start.2 = (f32[3,8,512]{2,1,0:T(8,128)S(1)}, f32[3,8,512]{2,1,0:T(8,128)S(1)}, u32[]{:S(2)}, u32[]{:S(2)}) collective-permute-start(f32[3,8,512]{2,1,0:T(8,128)S(1)} %get-tuple-element.24), channel_id=1, source_target_pairs={{8,16},{16,8},{9,17},{17,9},{10,18},{18,10},{11,19},{19,11},{12,20... | collective-permute-start | bytes 147464 | tf_op jit(solution)/shard_map/ppermute | solution.py:331
  12.2 0.1 collective-permute-start.3
  12.3 0.1 slice_bitcast_fusion.1
  12.4 1.1 %density_inside.1 = (f32[4,8,512]{2,1,0:T(8,128)S(1)}, f32[3,3,6,8,512]{4,3,2,1,0:T(8,128)S(1)}) custom-call(f32[8,8,512]{2,1,0:T(8,128)S(1)} %get-tuple-element.21.field.extra, f32[2,8,512]{2,1,0:T(8,128)S(1)} %collective-permute-done.side_0, f32[2,8,512]{2,1,0:T(8,128)S(1)} %collective-permute-done.1.side_1, f32[2,27,512]{2,1,0:T(8,128)S(1)} %copy.19.stencils, ...), custom_call_target="tpu_custom_call" | custom-call | tf_op jit(solution)/shard_map/density_inside/pallas_call | solution.py:384
  13.5 2.5 %all-to-all-done.got = f32[32,8,128]{2,1,0:T(8,128)S(1)} async-done(((f32[32,8,128]{2,1,0:T(8,128)}), f32[32,8,128]{2,1,0:T(8,128)S(1)}, u32[]{:S(2)}, u32[]{:S(2)}) %all-to-all-start) | async-done | bytes 131104 | tf_op jit(solution)/shard_map/all_to_all | solution.py:366
  16.0 2.2 %bin_sides.1.extra.behind = f32[8,8,512]{2,1,0:T(8,128)S(1)} custom-call(f32[32,8,128]{2,1,0:T(8,128)S(1)} %all-to-all-done.got, f32[4,8,512]{2,1,0:T(8,128)S(1)} %get-tuple-element.26._.inner), custom_call_target="tpu_custom_call" | custom-call | tf_op jit(solution)/shard_map/bin_sides/pallas_call | solution.py:413
  18.1 0.9 %density_ends.1 = (f32[8,8,512]{2,1,0:T(8,128)S(1)}, f32[2,8,512]{2,1,0:T(8,128)S(1)}, f32[2,8,512]{2,1,0:T(8,128)S(1)}) custom-call(f32[8,8,512]{2,1,0:T(8,128)S(1)} %get-tuple-element.21.field.extra, f32[2,8,512]{2,1,0:T(8,128)S(1)} %collective-permute-done.side_0, f32[2,8,512]{2,1,0:T(8,128)S(1)} %collective-permute-done.1.side_1, ...), custom_call_target="tpu_custom_call" | custom-call | tf_op jit(solution)/shard_map/density_ends/pallas_call | solution.py:398
  19.1 0.8 %collective-permute-start.4 = (f32[2,8,512]{2,1,0:T(8,128)S(1)}, f32[2,8,512]{2,1,0:T(8,128)S(1)}, u32[]{:S(2)}, u32[]{:S(2)}) collective-permute-start(f32[2,8,512]{2,1,0:T(8,128)S(1)} %get-tuple-element.29), channel_id=1, source_target_pairs={{1,2},{3,4},{5,6},{7,0},{2,1},{4,3},{6,5},{0,7},{9,10},{11,12},{13... | collective-permute-start | bytes 98312 | tf_op jit(solution)/shard_map/ppermute | solution.py:331
  19.9 0.0 collective-permute-start.5
  19.9 0.1 pad_bitcast_fusion
  20.1 2.2 %bin_rest.1.field = f32[8,8,512]{2,1,0:T(8,128)S(1)} custom-call(f32[32,8,128]{2,1,0:T(8,128)S(1)} %all-to-all-done.got, f32[8,8,512]{2,1,0:T(8,128)S(1)} %get-tuple-element.28.density, f32[8,8,512]{2,1,0:T(8,128)S(1)} %bin_sides.1.extra.behind), custom_call_target="tpu_custom_call" | custom-call | tf_op jit(solution)/shard_map/bin_rest/pallas_call | solution.py:425
  22.2 2.1 %collective-permute-done.4.side_0 = f32[2,8,512]{2,1,0:T(8,128)S(1)} collective-permute-done((f32[2,8,512]{2,1,0:T(8,128)S(1)}, f32[2,8,512]{2,1,0:T(8,128)S(1)}, u32[]{:S(2)}, u32[]{:S(2)}) %collective-permute-start.4) | collective-permute-done | bytes 32800 | tf_op jit(solution)/shard_map/ppermute | solution.py:331
  24.3 1.3 %collective-permute-start.6 = (f32[3,8,512]{2,1,0:T(8,128)S(1)}, f32[3,8,512]{2,1,0:T(8,128)S(1)}, u32[]{:S(2)}, u32[]{:S(2)}) collective-permute-start(f32[3,8,512]{2,1,0:T(8,128)S(1)} %get-tuple-element.31), channel_id=1, source_target_pairs={{0,8},{16,24},{8,0},{24,16},{1,9},{17,25},{9,1},{25,17},{2,10},{18... | collective-permute-start | bytes 147464 | tf_op jit(solution)/shard_map/ppermute | solution.py:331
  25.6 2.9 %collective-permute-start.7 = (f32[3,8,512]{2,1,0:T(8,128)S(1)}, f32[3,8,512]{2,1,0:T(8,128)S(1)}, u32[]{:S(2)}, u32[]{:S(2)}) collective-permute-start(f32[3,8,512]{2,1,0:T(8,128)S(1)} %get-tuple-element.32), channel_id=1, source_target_pairs={{8,16},{16,8},{9,17},{17,9},{10,18},{18,10},{11,19},{19,11},{12,20... | collective-permute-start | bytes 147464 | tf_op jit(solution)/shard_map/ppermute | solution.py:331
  28.5 0.1 pad_maximum_fusion
  28.6 1.1 %back_inside.1 = (f32[4,8,512]{2,1,0:T(8,128)S(1)}, f32[3,3,6,8,512]{4,3,2,1,0:T(8,128)S(1)}) custom-call(f32[8,8,512]{2,1,0:T(8,128)S(1)} %bin_rest.1.field, f32[2,8,512]{2,1,0:T(8,128)S(1)} %collective-permute-done.4.side_0, f32[2,8,512]{2,1,0:T(8,128)S(1)} %collective-permute-done.5.side_1, f32[2,27,512]{2,1,0:T(8,128)S(1)} %copy.23.stencils, ...), custom_call_target="tpu_custom_call" | custom-call | tf_op jit(solution)/shard_map/back_inside/pallas_call | solution.py:384
  29.6 2.8 %collective-permute-done.7.end_1 = f32[3,8,512]{2,1,0:T(8,128)S(1)} collective-permute-done((f32[3,8,512]{2,1,0:T(8,128)S(1)}, f32[3,8,512]{2,1,0:T(8,128)S(1)}, u32[]{:S(2)}, u32[]{:S(2)}) %collective-permute-start.7) | collective-permute-done | bytes 49184 | tf_op jit(solution)/shard_map/ppermute | solution.py:331
  32.5 1.6 %back_ends.1 = f32[8,8,512]{2,1,0:T(8,128)} custom-call(f32[8,8,512]{2,1,0:T(8,128)S(1)} %bin_rest.1.field, f32[2,8,512]{2,1,0:T(8,128)S(1)} %collective-permute-done.4.side_0, f32[2,8,512]{2,1,0:T(8,128)S(1)} %collective-permute-done.5.side_1, f32[3,8,512]{2,1,0:T(8,128)S(1)} %collective-permute-done.6.end_0, ...), custom_call_target="tpu_custom_call" | custom-call | tf_op jit(solution)/shard_map/back_ends/pallas_call | solution.py:398
  (12 shorter events, 0.1 us)
Async XLA Ops:
  1.9 6.9 %collective-permute-start = (f32[2,8,512]{2,1,0:T(8,128)S(1)}, f32[2,8,512]{2,1,0:T(8,128)S(1)}, u32[]{:S(2)}, u32[]{:S(2)}) collective-permute-start(f32[2,8,512]{2,1,0:T(8,128)S(1)} %get-tuple-element.22), channel_id=1, source_target_pairs={{0,1},{2,3},{4,5},{6,7},{1,0},{3,2},{5,4},{7,6},{8,9},{10,11},{12,... | collective-permute-start | bytes 98312 | tf_op jit(solution)/shard_map/ppermute | solution.py:331
  1.9 6.8 %collective-permute-start.1 = (f32[2,8,512]{2,1,0:T(8,128)S(1)}, f32[2,8,512]{2,1,0:T(8,128)S(1)}, u32[]{:S(2)}, u32[]{:S(2)}) collective-permute-start(f32[2,8,512]{2,1,0:T(8,128)S(1)} %get-tuple-element.23), channel_id=1, source_target_pairs={{1,2},{3,4},{5,6},{7,0},{2,1},{4,3},{6,5},{0,7},{9,10},{11,12},{13... | collective-permute-start | bytes 98312 | tf_op jit(solution)/shard_map/ppermute | solution.py:331
  5.6 3.1 %copy-start = (f32[2,27,512]{2,0,1:T(2,128)S(1)}, f32[2,27,512]{2,0,1:T(2,128)}, u32[]{:S(2)}) copy-start(f32[2,27,512]{2,0,1:T(2,128)} %param.13) | copy-start | bytes 331780
  5.6 10.3 %all-to-all-start = ((f32[32,8,128]{2,1,0:T(8,128)}), f32[32,8,128]{2,1,0:T(8,128)S(1)}, u32[]{:S(2)}, u32[]{:S(2)}) async-start(f32[32,8,128]{2,1,0:T(8,128)} %get-tuple-element.20), calls=%async_computation | async-start | bytes 262144 | tf_op jit(solution)/shard_map/all_to_all | solution.py:366
  8.8 9.3 %collective-permute-start.2 = (f32[3,8,512]{2,1,0:T(8,128)S(1)}, f32[3,8,512]{2,1,0:T(8,128)S(1)}, u32[]{:S(2)}, u32[]{:S(2)}) collective-permute-start(f32[3,8,512]{2,1,0:T(8,128)S(1)} %get-tuple-element.24), channel_id=1, source_target_pairs={{8,16},{16,8},{9,17},{17,9},{10,18},{18,10},{11,19},{19,11},{12,20... | collective-permute-start | bytes 147464 | tf_op jit(solution)/shard_map/ppermute | solution.py:331
  12.2 5.9 %collective-permute-start.3 = (f32[3,8,512]{2,1,0:T(8,128)S(1)}, f32[3,8,512]{2,1,0:T(8,128)S(1)}, u32[]{:S(2)}, u32[]{:S(2)}) collective-permute-start(f32[3,8,512]{2,1,0:T(8,128)S(1)} %get-tuple-element.25), channel_id=1, source_target_pairs={{0,8},{16,24},{8,0},{24,16},{1,9},{17,25},{9,1},{25,17},{2,10},{18... | collective-permute-start | bytes 147464 | tf_op jit(solution)/shard_map/ppermute | solution.py:331
  19.1 5.2 %collective-permute-start.4 = (f32[2,8,512]{2,1,0:T(8,128)S(1)}, f32[2,8,512]{2,1,0:T(8,128)S(1)}, u32[]{:S(2)}, u32[]{:S(2)}) collective-permute-start(f32[2,8,512]{2,1,0:T(8,128)S(1)} %get-tuple-element.29), channel_id=1, source_target_pairs={{1,2},{3,4},{5,6},{7,0},{2,1},{4,3},{6,5},{0,7},{9,10},{11,12},{13... | collective-permute-start | bytes 98312 | tf_op jit(solution)/shard_map/ppermute | solution.py:331
  19.9 4.4 %collective-permute-start.5 = (f32[2,8,512]{2,1,0:T(8,128)S(1)}, f32[2,8,512]{2,1,0:T(8,128)S(1)}, u32[]{:S(2)}, u32[]{:S(2)}) collective-permute-start(f32[2,8,512]{2,1,0:T(8,128)S(1)} %get-tuple-element.30), channel_id=1, source_target_pairs={{0,1},{2,3},{4,5},{6,7},{1,0},{3,2},{5,4},{7,6},{8,9},{10,11},{12,... | collective-permute-start | bytes 98312 | tf_op jit(solution)/shard_map/ppermute | solution.py:331
  24.3 5.3 %collective-permute-start.6 = (f32[3,8,512]{2,1,0:T(8,128)S(1)}, f32[3,8,512]{2,1,0:T(8,128)S(1)}, u32[]{:S(2)}, u32[]{:S(2)}) collective-permute-start(f32[3,8,512]{2,1,0:T(8,128)S(1)} %get-tuple-element.31), channel_id=1, source_target_pairs={{0,8},{16,24},{8,0},{24,16},{1,9},{17,25},{9,1},{25,17},{2,10},{18... | collective-permute-start | bytes 147464 | tf_op jit(solution)/shard_map/ppermute | solution.py:331
  25.6 6.9 %collective-permute-start.7 = (f32[3,8,512]{2,1,0:T(8,128)S(1)}, f32[3,8,512]{2,1,0:T(8,128)S(1)}, u32[]{:S(2)}, u32[]{:S(2)}) collective-permute-start(f32[3,8,512]{2,1,0:T(8,128)S(1)} %get-tuple-element.32), channel_id=1, source_target_pairs={{8,16},{16,8},{9,17},{17,9},{10,18},{18,10},{11,19},{19,11},{12,20... | collective-permute-start | bytes 147464 | tf_op jit(solution)/shard_map/ppermute | solution.py:331

commit v10 on v9

--- a/solution.py
+++ b/solution.py
@@ -149,7 +149,7 @@
     tiles_of_bins(radial, body)
 
 
-def refine_inside_kernel(turned, coefs, finish, field, side_0, side_1, stencils, extra, out, middle, wide, shifted):
+def refine_inside_kernel(turned, coefs, finish, field, side_0, side_1, stencils, extra, _, out, middle, wide, shifted):
     height, width, radial = field.shape
     tiles = unpack_sides(*in_order(turned, side_0, side_1), height)
     for row in range(height):
@@ -165,12 +165,11 @@
 
 
 def refine_ends_kernel(
-    turned, coefs, finish, packs, field, side_0, side_1, end_0, end_1, stencils, extra, inside, inner, *rest
+    turned, coefs, finish, field, side_0, side_1, end_0, end_1, stencils, extra, inside, inner,
+    out, middle, wide, shifted,
 ):
-    out, *to_sides, middle, wide, shifted = rest
     height, width, radial = field.shape
-    tiles = unpack_sides(*in_order(turned[0], side_0, side_1), height)
-    end_0, end_1 = in_order(turned[1], end_0, end_1)
+    tiles = unpack_sides(*in_order(turned, side_0, side_1), height)
     lat, odd = position("lat")
     for place in range(3):
         partner, outer = end_0[place], end_1[place]
@@ -197,8 +196,6 @@
     second_level(stencils.at[coefs[1]], windows, radial, write)
     for row in range(2, height - 2):
         out[row] = inner[row - 2]
-    if packs:
-        pack_sides([out[row] * extra[row] for row in range(height)], *to_sides)
 
 
 def open_kernel(
@@ -296,11 +293,13 @@
     return rows
 
 
-def bin_sides_kernel(got, _, behind):
+def bin_sides_kernel(got, density, behind, to_partner, to_outer):
     height, width, radial = behind.shape
     packed = behind_of(got, 0, height=height, width=width, radial=radial)
-    for row, values in enumerate(column_rows(packed, 0, height)):
+    rows = column_rows(packed, 0, height)
+    for row, values in enumerate(rows):
         behind[row] = values
+    pack_sides([density[row] * values for row, values in enumerate(rows)], to_partner, to_outer)
 
 
 def bin_rest_kernel(got, density, behind, upstream):
@@ -329,6 +328,15 @@
 
     moves = [(to_partner, inner), (to_outer, outer)]
     return tuple(lax.ppermute(values, axis, both_ways(pairs)) for values, pairs in moves[::-1 if outer_first else 1])
+
+
+def relay(to_partner, to_outer):
+    if lax.axis_size("lat") != 4:
+        ends = swap(to_partner, to_outer, "lat", False)
+        return *ends, ends[0]
+    passing = lax.ppermute(to_outer, "lat", [(1, 3), (2, 0)])
+    from_partner = lax.ppermute(to_partner, "lat", [(0, 1), (1, 0), (2, 3), (3, 2)])
+    return from_partner, lax.ppermute(passing, "lat", [(0, 1), (3, 2)]), passing
 
 
 VMEM = pl.BlockSpec(memory_space=pltpu.VMEM)
@@ -366,62 +374,53 @@
     got = lax.all_to_all(packed, ("lat", "lon"), split_axis=0, concat_axis=0, tiled=True)
 
     def spread(field, to_sides, name, turned):
-        beside = swap(*to_sides, "lon", True, turned[0])
+        beside = swap(*to_sides, "lon", True, turned)
         to_ends = pl.pallas_call(
-            functools.partial(pack_ends_kernel, turned[0]),
+            functools.partial(pack_ends_kernel, turned),
             out_shape=(ends, ends),
             in_specs=[VMEM] * 3,
             out_specs=(VMEM, VMEM),
             compiler_params=LIMIT,
             name=name + "_pack",
         )(field, *beside)
-        return beside, swap(*to_ends, "lat", False, turned[1])
+        return beside, relay(*to_ends)
 
     rows = pltpu.VMEM((height, 2 * width, radial), f32)
     moved = pltpu.VMEM((2, height, 2 * width, radial), f32)
 
-    def refined_inside(turned, coefs, finish, field, beside, table, extra, name):
-        return pl.pallas_call(
-            functools.partial(refine_inside_kernel, turned[0], coefs, finish),
+    def refined(field, to_sides, turned, coefs, table, extra, finish, name):
+        beside, (*above, passing) = spread(field, to_sides, name, turned)
+        inner, middle = pl.pallas_call(
+            functools.partial(refine_inside_kernel, turned, coefs, finish),
             out_shape=(
                 jax.ShapeDtypeStruct((height - 4, width, radial), f32),
                 jax.ShapeDtypeStruct((3, 3, height - 2, width, radial), f32),
             ),
-            in_specs=[VMEM] * 5,
+            in_specs=[VMEM] * 6,
             out_specs=(VMEM, VMEM),
             scratch_shapes=[rows, moved],
             compiler_params=LIMIT,
             name=name + "_inside",
-        )(field, *beside, table, extra)
-
-    def refined_ends(turned, coefs, finish, field, beside, above, table, extra, inner, middle, name, packs):
+        )(field, *beside, table, extra, passing)
         return pl.pallas_call(
-            functools.partial(refine_ends_kernel, turned, coefs, finish, packs),
-            out_shape=(tile, sides, sides) if packs else tile,
+            functools.partial(refine_ends_kernel, turned, coefs, finish),
+            out_shape=tile,
             in_specs=[VMEM] * 9,
-            out_specs=(VMEM,) * 3 if packs else VMEM,
+            out_specs=VMEM,
             scratch_shapes=[pltpu.VMEM((3, 3, 4, width, radial), f32), rows, moved],
             compiler_params=LIMIT,
             name=name + "_ends",
         )(field, *beside, *above, table, extra, middle, inner)
 
-    first_turned, last_turned = (False, True), (True, False)
-    beside, above = spread(latent, to_sides, "density", first_turned)
-    inner, middle = refined_inside(
-        first_turned, (0, 1), lambda value, _: jnp.exp(value), latent, beside, stencils, latent, "density"
-    )
-    behind = pl.pallas_call(
+    density = refined(latent, to_sides, False, (0, 1), stencils, latent, lambda value, _: jnp.exp(value), "density")
+    behind, *to_sides = pl.pallas_call(
         bin_sides_kernel,
-        out_shape=tile,
+        out_shape=(tile, sides, sides),
         in_specs=[VMEM, VMEM],
-        out_specs=VMEM,
+        out_specs=(VMEM,) * 3,
         compiler_params=LIMIT,
         name="bin_sides",
-    )(got, inner)
-    density, *to_sides = refined_ends(
-        first_turned, (0, 1), lambda value, _: jnp.exp(value), latent, beside, above, stencils, behind, inner, middle,
-        "density", True,
-    )
+    )(got, density)
     upstream = pl.pallas_call(
         bin_rest_kernel,
         out_shape=tile,
@@ -430,15 +429,8 @@
         compiler_params=LIMIT,
         name="bin_rest",
     )(got, density, behind)
-
-    mirrored = mirror(stencils)
-    beside, above = spread(upstream, to_sides, "back", last_turned)
-    inner, middle = refined_inside(
-        last_turned, (1, 0), lambda value, field: field + value, upstream, beside, mirrored, latent, "back"
-    )
-    return refined_ends(
-        last_turned, (1, 0), lambda value, field: field + value, upstream, beside, above, mirrored, latent, inner, middle,
-        "back", False,
+    return refined(
+        upstream, to_sides, True, (1, 0), mirror(stencils), latent, lambda value, field: field + value, "back"
     )
 
 

time: 34.2 us -> 45.7 us (1.34); the launches traced: 34 us -> 44.8 us
  waiting for transfers between devices: 7.41 us -> 15.7 us
  starting transfers between devices: 15.3 us -> 17.8 us
    ppermute x0 -> x6, waiting for transfers between devices: none -> 10.3 us  [the longest x2 6.7 us: relay(): lax.ppermute(passing, 'lat', [(0, 1), (3, 2)])]
    ppermute x8 -> x4, starting transfers between devices: 12.2 us -> 4.27 us  [swap(): lax.ppermute(values, axis, both_ways(pairs))]
    ppermute x0 -> x6, starting transfers between devices: none -> 7.4 us  [the longest x2 4.7 us: relay(): passing = lax.ppermute(to_outer, 'lat', [(1, 3), (2, 0)])]
    all_to_all x1, starting transfers between devices: 3.09 us -> 6.13 us  [on_device(): lax.all_to_all(packed, ('lat', 'lon'), split_axis=0, concat_axis=0, tiled...]
    all_to_all x1, waiting for transfers between devices: 2.48 us -> 0.01 us  [on_device(): lax.all_to_all(packed, ('lat', 'lon'), split_axis=0, concat_axis=0, tiled...]
    ppermute x8 -> x4, waiting for transfers between devices: 4.93 us -> 5.42 us  [swap(): lax.ppermute(values, axis, both_ways(pairs))]
  transfers between devices with their start and end apart: 9 -> 11, of which waited for: 3 -> 7; matrix products, arithmetic and copies ran while one was open for 1% -> 1% of each run, Pallas kernels for 19% -> 12%
where the time goes in v10:
time: 45.7 us; the launch traced here: 44.8 us
  starting transfers between devices  17.8 us (39%)
  waiting for transfers between devices  15.7 us (34%)
  Pallas kernels  10.8 us (24%)
    ppermute x2, waiting for transfers between devices, relay(): lax.ppermute(passing, 'lat', [(0, 1), (3, 2)])  6.7 us
    all_to_all x1, starting transfers between devices, on_device(): lax.all_to_all(packed, ('lat', 'lon'), split_axis=0, concat_axis=0, tiled...  6.13 us
    ppermute x4, waiting for transfers between devices, swap(): lax.ppermute(values, axis, both_ways(pairs))  5.42 us
    ppermute x2, starting transfers between devices, relay(): passing = lax.ppermute(to_outer, 'lat', [(1, 3), (2, 0)])  4.7 us
    ppermute x4, starting transfers between devices, swap(): lax.ppermute(values, axis, both_ways(pairs))  4.27 us
    ppermute x2, waiting for transfers between devices, relay(): passing = lax.ppermute(to_outer, 'lat', [(1, 3), (2, 0)])  3.19 us
    ppermute x2, starting transfers between devices, relay(): lax.ppermute(passing, 'lat', [(0, 1), (3, 2)])  2.56 us
    pallas_call x2, Pallas kernels, refined(): pl.pallas_call(functools.partial(refine_ends_kernel, turned, coefs, finis...  2.48 us
  transfers between devices with their start and end apart: 11, of which 7 were waited for; matrix products, arithmetic and copies ran while one was open for 1% of the time, Pallas kernels for 12%

profile of v10, /device:TPU:2, one launch (start us, length us, event | category | flops | bytes accessed | tf_op | source)
XLA Modules:
  0.0 44.8 jit_solution(1340255279169973012)
XLA Ops:
  0.0 1.8 %opening.1 = (f32[32,8,128]{2,1,0:T(8,128)}, f32[8,8,512]{2,1,0:T(8,128)S(1)}, f32[2,8,512]{2,1,0:T(8,128)S(1)}, f32[2,8,512]{2,1,0:T(8,128)S(1)}) custom-call(s32[1,32]{1,0:T(1,128)} %counts_in.1, s32[1,32]{1,0:T(1,128)} %offsets_in.1, f32[128,128]{1,0:T(8,128)} %bitcast.20, s32[128,128]{1,0:T(8,128)} %bitcast.21, s32[128,128]{1,0:T(8,128)} %bitcast.22, ...), custom_call_target="tpu_custom_call" | custom-call | tf_op jit(solution)/shard_map/opening/pallas_call | solution.py:360
  1.9 6.1 %all-to-all-start = ((f32[32,8,128]{2,1,0:T(8,128)}), f32[32,8,128]{2,1,0:T(8,128)S(1)}, u32[]{:S(2)}, u32[]{:S(2)}) async-start(f32[32,8,128]{2,1,0:T(8,128)} %get-tuple-element.20), calls=%async_computation | async-start | bytes 262144 | tf_op jit(solution)/shard_map/all_to_all | solution.py:374
  8.0 0.2 collective-permute-start
  8.2 3.3 %collective-permute-start.1 = (f32[2,8,512]{2,1,0:T(8,128)S(1)}, f32[2,8,512]{2,1,0:T(8,128)S(1)}, u32[]{:S(2)}, u32[]{:S(2)}) collective-permute-start(f32[2,8,512]{2,1,0:T(8,128)S(1)} %get-tuple-element.23), channel_id=1, source_target_pairs={{1,2},{3,4},{5,6},{7,0},{2,1},{4,3},{6,5},{0,7},{9,10},{11,12},{13... | collective-permute-start | bytes 98312 | tf_op jit(solution)/shard_map/ppermute | solution.py:330
  11.5 3.2 %collective-permute-done.1.side_1 = f32[2,8,512]{2,1,0:T(8,128)S(1)} collective-permute-done((f32[2,8,512]{2,1,0:T(8,128)S(1)}, f32[2,8,512]{2,1,0:T(8,128)S(1)}, u32[]{:S(2)}, u32[]{:S(2)}) %collective-permute-start.1) | collective-permute-done | bytes 32800 | tf_op jit(solution)/shard_map/ppermute | solution.py:330
  14.8 3.4 %collective-permute-start.3 = (f32[3,8,512]{2,1,0:T(8,128)S(1)}, f32[3,8,512]{2,1,0:T(8,128)S(1)}, u32[]{:S(2)}, u32[]{:S(2)}) collective-permute-start(f32[3,8,512]{2,1,0:T(8,128)S(1)} %get-tuple-element.25), channel_id=1, source_target_pairs={{8,24},{16,0},{9,25},{17,1},{10,26},{18,2},{11,27},{19,3},{12,28},... | collective-permute-start | bytes 147464 | tf_op jit(solution)/shard_map/ppermute | solution.py:337
  18.3 1.7 %collective-permute-done.3._ = f32[3,8,512]{2,1,0:T(8,128)S(1)} collective-permute-done((f32[3,8,512]{2,1,0:T(8,128)S(1)}, f32[3,8,512]{2,1,0:T(8,128)S(1)}, u32[]{:S(2)}, u32[]{:S(2)}) %collective-permute-start.3) | collective-permute-done | bytes 49184 | tf_op jit(solution)/shard_map/ppermute | solution.py:337
  19.9 1.3 %collective-permute-start.4 = (f32[3,8,512]{2,1,0:T(8,128)S(1)}, f32[3,8,512]{2,1,0:T(8,128)S(1)}, u32[]{:S(2)}, u32[]{:S(2)}) collective-permute-start(f32[3,8,512]{2,1,0:T(8,128)S(1)} %collective-permute-done.3._), channel_id=1, source_target_pairs={{0,8},{24,16},{1,9},{25,17},{2,10},{26,18},{3,11},{27,19},{4,12},{... | collective-permute-start | bytes 147464 | tf_op jit(solution)/shard_map/ppermute | solution.py:339
  21.3 1.1 %density_inside.1 = (f32[4,8,512]{2,1,0:T(8,128)S(1)}, f32[3,3,6,8,512]{4,3,2,1,0:T(8,128)S(1)}) custom-call(f32[8,8,512]{2,1,0:T(8,128)S(1)} %get-tuple-element.21.field.extra, f32[2,8,512]{2,1,0:T(8,128)S(1)} %collective-permute-done.side_0, f32[2,8,512]{2,1,0:T(8,128)S(1)} %collective-permute-done.1.side_1, f32[2,27,512]{2,1,0:T(8,128)S(1)} %copy.19.stencils, ...), custom_call_target="tpu_custom_call" | custom-call | tf_op jit(solution)/shard_map/density_inside/pallas_call | solution.py:393
  22.4 3.5 %collective-permute-done.4.end_1 = f32[3,8,512]{2,1,0:T(8,128)S(1)} collective-permute-done((f32[3,8,512]{2,1,0:T(8,128)S(1)}, f32[3,8,512]{2,1,0:T(8,128)S(1)}, u32[]{:S(2)}, u32[]{:S(2)}) %collective-permute-start.4) | collective-permute-done | bytes 49184 | tf_op jit(solution)/shard_map/ppermute | solution.py:339
  25.9 0.9 %density_ends.1.density = f32[8,8,512]{2,1,0:T(8,128)S(1)} custom-call(f32[8,8,512]{2,1,0:T(8,128)S(1)} %get-tuple-element.21.field.extra, f32[2,8,512]{2,1,0:T(8,128)S(1)} %collective-permute-done.side_0, f32[2,8,512]{2,1,0:T(8,128)S(1)} %collective-permute-done.1.side_1, f32[3,8,512]{2,1,0:T(8,128)S(1)} %collective-permute-done.2.end_0, ...), custom_call_target="tpu_custom_call" | custom-call | tf_op jit(solution)/shard_map/density_ends/pallas_call | solution.py:405
  26.8 2.2 %bin_sides.1 = (f32[8,8,512]{2,1,0:T(8,128)S(1)}, f32[2,8,512]{2,1,0:T(8,128)S(1)}, f32[2,8,512]{2,1,0:T(8,128)S(1)}) custom-call(f32[32,8,128]{2,1,0:T(8,128)S(1)} %all-to-all-done.got, f32[8,8,512]{2,1,0:T(8,128)S(1)} %density_ends.1.density), custom_call_target="tpu_custom_call" | custom-call | tf_op jit(solution)/shard_map/bin_sides/pallas_call | solution.py:416
  29.0 0.8 %collective-permute-start.5 = (f32[2,8,512]{2,1,0:T(8,128)S(1)}, f32[2,8,512]{2,1,0:T(8,128)S(1)}, u32[]{:S(2)}, u32[]{:S(2)}) collective-permute-start(f32[2,8,512]{2,1,0:T(8,128)S(1)} %get-tuple-element.29), channel_id=1, source_target_pairs={{1,2},{3,4},{5,6},{7,0},{2,1},{4,3},{6,5},{0,7},{9,10},{11,12},{13... | collective-permute-start | bytes 98312 | tf_op jit(solution)/shard_map/ppermute | solution.py:330
  29.8 0.1 slice_bitcast_fusion.1
  29.9 2.2 %bin_rest.1.field = f32[8,8,512]{2,1,0:T(8,128)S(1)} custom-call(f32[32,8,128]{2,1,0:T(8,128)S(1)} %all-to-all-done.got, f32[8,8,512]{2,1,0:T(8,128)S(1)} %density_ends.1.density, f32[8,8,512]{2,1,0:T(8,128)S(1)} %get-tuple-element.28.behind), custom_call_target="tpu_custom_call" | custom-call | tf_op jit(solution)/shard_map/bin_rest/pallas_call | solution.py:424
  32.1 2.2 %collective-permute-done.5.side_0 = f32[2,8,512]{2,1,0:T(8,128)S(1)} collective-permute-done((f32[2,8,512]{2,1,0:T(8,128)S(1)}, f32[2,8,512]{2,1,0:T(8,128)S(1)}, u32[]{:S(2)}, u32[]{:S(2)}) %collective-permute-start.5) | collective-permute-done | bytes 32800 | tf_op jit(solution)/shard_map/ppermute | solution.py:330
  34.3 1.3 %collective-permute-start.8 = (f32[3,8,512]{2,1,0:T(8,128)S(1)}, f32[3,8,512]{2,1,0:T(8,128)S(1)}, u32[]{:S(2)}, u32[]{:S(2)}) collective-permute-start(f32[3,8,512]{2,1,0:T(8,128)S(1)} %get-tuple-element.32), channel_id=1, source_target_pairs={{8,24},{16,0},{9,25},{17,1},{10,26},{18,2},{11,27},{19,3},{12,28},... | collective-permute-start | bytes 147464 | tf_op jit(solution)/shard_map/ppermute | solution.py:337
  35.6 0.1 pad_bitcast_fusion
  35.7 1.5 %collective-permute-done.8._ = f32[3,8,512]{2,1,0:T(8,128)S(1)} collective-permute-done((f32[3,8,512]{2,1,0:T(8,128)S(1)}, f32[3,8,512]{2,1,0:T(8,128)S(1)}, u32[]{:S(2)}, u32[]{:S(2)}) %collective-permute-start.8) | collective-permute-done | bytes 49184 | tf_op jit(solution)/shard_map/ppermute | solution.py:337
  37.3 1.3 %collective-permute-start.9 = (f32[3,8,512]{2,1,0:T(8,128)S(1)}, f32[3,8,512]{2,1,0:T(8,128)S(1)}, u32[]{:S(2)}, u32[]{:S(2)}) collective-permute-start(f32[3,8,512]{2,1,0:T(8,128)S(1)} %collective-permute-done.8._), channel_id=1, source_target_pairs={{0,8},{24,16},{1,9},{25,17},{2,10},{26,18},{3,11},{27,19},{4,12},{... | collective-permute-start | bytes 147464 | tf_op jit(solution)/shard_map/ppermute | solution.py:339
  38.7 1.1 %back_inside.1 = (f32[4,8,512]{2,1,0:T(8,128)S(1)}, f32[3,3,6,8,512]{4,3,2,1,0:T(8,128)S(1)}) custom-call(f32[8,8,512]{2,1,0:T(8,128)S(1)} %bin_rest.1.field, f32[2,8,512]{2,1,0:T(8,128)S(1)} %collective-permute-done.5.side_0, f32[2,8,512]{2,1,0:T(8,128)S(1)} %collective-permute-done.6.side_1, f32[2,27,512]{2,1,0:T(8,128)S(1)} %copy.23.stencils, ...), custom_call_target="tpu_custom_call" | custom-call | tf_op jit(solution)/shard_map/back_inside/pallas_call | solution.py:393
  39.7 0.4 collective-permute-done.7.end_0
  40.1 3.2 %collective-permute-done.9.end_1 = f32[3,8,512]{2,1,0:T(8,128)S(1)} collective-permute-done((f32[3,8,512]{2,1,0:T(8,128)S(1)}, f32[3,8,512]{2,1,0:T(8,128)S(1)}, u32[]{:S(2)}, u32[]{:S(2)}) %collective-permute-start.9) | collective-permute-done | bytes 49184 | tf_op jit(solution)/shard_map/ppermute | solution.py:339
  43.3 1.6 %back_ends.1 = f32[8,8,512]{2,1,0:T(8,128)} custom-call(f32[8,8,512]{2,1,0:T(8,128)S(1)} %bin_rest.1.field, f32[2,8,512]{2,1,0:T(8,128)S(1)} %collective-permute-done.5.side_0, f32[2,8,512]{2,1,0:T(8,128)S(1)} %collective-permute-done.6.side_1, f32[3,8,512]{2,1,0:T(8,128)S(1)} %collective-permute-done.7.end_0, ...), custom_call_target="tpu_custom_call" | custom-call | tf_op jit(solution)/shard_map/back_ends/pallas_call | solution.py:405
  (16 shorter events, 0.3 us)
Async XLA Ops:
  1.9 25.0 %all-to-all-start = ((f32[32,8,128]{2,1,0:T(8,128)}), f32[32,8,128]{2,1,0:T(8,128)S(1)}, u32[]{:S(2)}, u32[]{:S(2)}) async-start(f32[32,8,128]{2,1,0:T(8,128)} %get-tuple-element.20), calls=%async_computation | async-start | bytes 262144 | tf_op jit(solution)/shard_map/all_to_all | solution.py:374
  8.0 13.2 %copy-start = (f32[2,27,512]{2,0,1:T(2,128)S(1)}, f32[2,27,512]{2,0,1:T(2,128)}, u32[]{:S(2)}) copy-start(f32[2,27,512]{2,0,1:T(2,128)} %param.13) | copy-start | bytes 331780
  8.0 3.5 %collective-permute-start = (f32[2,8,512]{2,1,0:T(8,128)S(1)}, f32[2,8,512]{2,1,0:T(8,128)S(1)}, u32[]{:S(2)}, u32[]{:S(2)}) collective-permute-start(f32[2,8,512]{2,1,0:T(8,128)S(1)} %get-tuple-element.22), channel_id=1, source_target_pairs={{0,1},{2,3},{4,5},{6,7},{1,0},{3,2},{5,4},{7,6},{8,9},{10,11},{12,... | collective-permute-start | bytes 98312 | tf_op jit(solution)/shard_map/ppermute | solution.py:330
  8.2 6.5 %collective-permute-start.1 = (f32[2,8,512]{2,1,0:T(8,128)S(1)}, f32[2,8,512]{2,1,0:T(8,128)S(1)}, u32[]{:S(2)}, u32[]{:S(2)}) collective-permute-start(f32[2,8,512]{2,1,0:T(8,128)S(1)} %get-tuple-element.23), channel_id=1, source_target_pairs={{1,2},{3,4},{5,6},{7,0},{2,1},{4,3},{6,5},{0,7},{9,10},{11,12},{13... | collective-permute-start | bytes 98312 | tf_op jit(solution)/shard_map/ppermute | solution.py:330
  14.8 5.1 %collective-permute-start.3 = (f32[3,8,512]{2,1,0:T(8,128)S(1)}, f32[3,8,512]{2,1,0:T(8,128)S(1)}, u32[]{:S(2)}, u32[]{:S(2)}) collective-permute-start(f32[3,8,512]{2,1,0:T(8,128)S(1)} %get-tuple-element.25), channel_id=1, source_target_pairs={{8,24},{16,0},{9,25},{17,1},{10,26},{18,2},{11,27},{19,3},{12,28},... | collective-permute-start | bytes 147464 | tf_op jit(solution)/shard_map/ppermute | solution.py:337
  18.2 4.2 %collective-permute-start.2 = (f32[3,8,512]{2,1,0:T(8,128)S(1)}, f32[3,8,512]{2,1,0:T(8,128)S(1)}, u32[]{:S(2)}, u32[]{:S(2)}) collective-permute-start(f32[3,8,512]{2,1,0:T(8,128)S(1)} %get-tuple-element.24), channel_id=1, source_target_pairs={{0,8},{8,0},{16,24},{24,16},{1,9},{9,1},{17,25},{25,17},{2,10},{10... | collective-permute-start | bytes 147464 | tf_op jit(solution)/shard_map/ppermute | solution.py:338
  19.9 6.0 %collective-permute-start.4 = (f32[3,8,512]{2,1,0:T(8,128)S(1)}, f32[3,8,512]{2,1,0:T(8,128)S(1)}, u32[]{:S(2)}, u32[]{:S(2)}) collective-permute-start(f32[3,8,512]{2,1,0:T(8,128)S(1)} %collective-permute-done.3._), channel_id=1, source_target_pairs={{0,8},{24,16},{1,9},{25,17},{2,10},{26,18},{3,11},{27,19},{4,12},{... | collective-permute-start | bytes 147464 | tf_op jit(solution)/shard_map/ppermute | solution.py:339
  29.0 5.2 %collective-permute-start.5 = (f32[2,8,512]{2,1,0:T(8,128)S(1)}, f32[2,8,512]{2,1,0:T(8,128)S(1)}, u32[]{:S(2)}, u32[]{:S(2)}) collective-permute-start(f32[2,8,512]{2,1,0:T(8,128)S(1)} %get-tuple-element.29), channel_id=1, source_target_pairs={{1,2},{3,4},{5,6},{7,0},{2,1},{4,3},{6,5},{0,7},{9,10},{11,12},{13... | collective-permute-start | bytes 98312 | tf_op jit(solution)/shard_map/ppermute | solution.py:330
  29.8 4.5 %collective-permute-start.6 = (f32[2,8,512]{2,1,0:T(8,128)S(1)}, f32[2,8,512]{2,1,0:T(8,128)S(1)}, u32[]{:S(2)}, u32[]{:S(2)}) collective-permute-start(f32[2,8,512]{2,1,0:T(8,128)S(1)} %get-tuple-element.30), channel_id=1, source_target_pairs={{0,1},{2,3},{4,5},{6,7},{1,0},{3,2},{5,4},{7,6},{8,9},{10,11},{12,... | collective-permute-start | bytes 98312 | tf_op jit(solution)/shard_map/ppermute | solution.py:330
  34.3 3.0 %collective-permute-start.8 = (f32[3,8,512]{2,1,0:T(8,128)S(1)}, f32[3,8,512]{2,1,0:T(8,128)S(1)}, u32[]{:S(2)}, u32[]{:S(2)}) collective-permute-start(f32[3,8,512]{2,1,0:T(8,128)S(1)} %get-tuple-element.32), channel_id=1, source_target_pairs={{8,24},{16,0},{9,25},{17,1},{10,26},{18,2},{11,27},{19,3},{12,28},... | collective-permute-start | bytes 147464 | tf_op jit(solution)/shard_map/ppermute | solution.py:337
  35.7 4.4 %collective-permute-start.7 = (f32[3,8,512]{2,1,0:T(8,128)S(1)}, f32[3,8,512]{2,1,0:T(8,128)S(1)}, u32[]{:S(2)}, u32[]{:S(2)}) collective-permute-start(f32[3,8,512]{2,1,0:T(8,128)S(1)} %get-tuple-element.31), channel_id=1, source_target_pairs={{0,8},{8,0},{16,24},{24,16},{1,9},{9,1},{17,25},{25,17},{2,10},{10... | collective-permute-start | bytes 147464 | tf_op jit(solution)/shard_map/ppermute | solution.py:338
  37.3 6.0 %collective-permute-start.9 = (f32[3,8,512]{2,1,0:T(8,128)S(1)}, f32[3,8,512]{2,1,0:T(8,128)S(1)}, u32[]{:S(2)}, u32[]{:S(2)}) collective-permute-start(f32[3,8,512]{2,1,0:T(8,128)S(1)} %collective-permute-done.8._), channel_id=1, source_target_pairs={{0,8},{24,16},{1,9},{25,17},{2,10},{26,18},{3,11},{27,19},{4,12},{... | collective-permute-start | bytes 147464 | tf_op jit(solution)/shard_map/ppermute | solution.py:339

commit v11 on v8

--- a/solution.py
+++ b/solution.py
@@ -56,12 +56,12 @@
     return tiles
 
 
-def pack_ends_kernel(field, from_partner, from_outer, to_partner, to_outer):
+def pack_ends_kernel(field, side_0, side_1, to_partner, to_outer):
     height, _, radial = field.shape
     _, odd = position("lat")
     sub = sublane(radial)
     outside = (sub < 2) | (sub >= 6)
-    tiles = unpack_sides(from_partner, from_outer, height)
+    tiles = unpack_sides(side_0, side_1, height)
 
     def ends(first):
         return (
@@ -96,19 +96,22 @@
     lax.fori_loop(0, radial // LANES, step, 0)
 
 
+ALL = (-1, 0, 1)
+
+
 def first_level(wide, shifted, coef, centers, middle, real):
-    reach, cols, radial = wide.shape
-    for row in range(reach):
+    _, cols, radial = wide.shape
+    for row in sorted({row + above for row, around in centers for above in around}):
         for place, moved in enumerate(radial_shifts(wide[row])):
             shifted[place, row] = moved
 
     def body(at):
         taps = taps_of(coef, at)
-        for place, row in enumerate(centers):
+        for place, (row, around) in enumerate(centers):
             parts = []
             for side in (slice(0, SUBLANES), slice(SUBLANES, cols)):
                 sums = [None, None, None]
-                for above in (-1, 0, 1):
+                for above in around:
                     window = (shifted[0, row + above, side, at], wide[row + above, side, at], shifted[1, row + above, side, at])
                     for beside in range(3):
                         for step in range(3):
@@ -135,7 +138,10 @@
         taps = taps_of(coef, at)
         for row, around in windows.items():
             total = None
-            for above, (buffer, place) in enumerate(around):
+            for above, at_row in enumerate(around):
+                if at_row is None:
+                    continue
+                buffer, place = at_row
                 for beside in range(3):
                     for step in range(3):
                         term = taps[above * 9 + beside * 3 + step] * buffer[beside, step, place, :, at]
@@ -145,25 +151,30 @@
     tiles_of_bins(radial, body)
 
 
-def refine_inside_kernel(coefs, finish, field, side_0, side_1, stencils, extra, out, middle, wide, shifted):
-    height, width, radial = field.shape
+def fill_wide(wide, field, side_0, side_1, rows):
+    height, width, _ = field.shape
     tiles = unpack_sides(side_0, side_1, height)
-    for row in range(height):
+    for row in rows:
         wide[row, :width] = field[row]
         wide[row, width:] = tiles[row]
-    first_level(wide, shifted, stencils.at[coefs[0]], range(1, height - 1), middle, [None] * (height - 2))
+
+
+def density_inside_kernel(field, side_0, side_1, stencils, out, middle, wide, shifted):
+    height, width, radial = field.shape
+    fill_wide(wide, field, side_0, side_1, range(height))
+    centers = [(row, ALL) for row in range(1, height - 1)]
+    first_level(wide, shifted, stencils.at[0], centers, middle, [None] * len(centers))
 
     def write(row, at, value):
-        out[row - 2, :, at] = finish(value, extra[row, :, at])
+        out[row - 2, :, at] = jnp.exp(value)
 
     windows = {row: [(middle, row - 2 + k) for k in range(3)] for row in range(2, height - 2)}
-    second_level(stencils.at[coefs[1]], windows, radial, write)
-
-
-def refine_ends_kernel(
-    coefs, finish, packs, field, side_0, side_1, end_1, end_0, stencils, extra, inside, inner, *rest
+    second_level(stencils.at[1], windows, radial, write)
+
+
+def density_ends_kernel(
+    field, side_0, side_1, end_1, end_0, stencils, inside, inner, behind, out, to_partner, to_outer, middle, wide, shifted
 ):
-    out, *to_sides, middle, wide, shifted = rest
     height, width, radial = field.shape
     tiles = unpack_sides(side_0, side_1, height)
     lat, odd = position("lat")
@@ -180,20 +191,69 @@
         wide[place, width:] = tiles[row]
     above = (lat > 0).astype(jnp.int32)
     below = (lat < lax.axis_size("lat") - 1).astype(jnp.int32)
-    first_level(wide, shifted, stencils.at[coefs[0]], (1, 2, 5, 6), middle, [above, None, None, below])
+    centers = [(row, ALL) for row in (1, 2, 5, 6)]
+    first_level(wide, shifted, stencils.at[0], centers, middle, [above, None, None, below])
 
     def write(row, at, value):
-        out[row, :, at] = finish(value, extra[row, :, at])
+        out[row, :, at] = jnp.exp(value)
 
     last = height - 3
     top = [(middle, 0), (middle, 1), (inside, 0), (inside, 1)]
     bottom = [(inside, last - 1), (inside, last), (middle, 2), (middle, 3)]
     windows = {0: top[:3], 1: top[1:], height - 2: bottom[:3], height - 1: bottom[1:]}
-    second_level(stencils.at[coefs[1]], windows, radial, write)
+    second_level(stencils.at[1], windows, radial, write)
     for row in range(2, height - 2):
         out[row] = inner[row - 2]
-    if packs:
-        pack_sides([out[row] * extra[row] for row in range(height)], *to_sides)
+    pack_sides([out[row] * behind[row] for row in range(height)], to_partner, to_outer)
+
+
+def back_reach_kernel(field, side_1, side_0, stencils, to_partner, to_outer, middle, wide, shifted, reach):
+    height, _, radial = field.shape
+    last = height - 1
+    fill_wide(wide, field, side_0, side_1, (0, 1, last - 1, last))
+    lat, odd = position("lat")
+    above = (lat > 0).astype(jnp.int32)
+    below = (lat < lax.axis_size("lat") - 1).astype(jnp.int32)
+    centers = [(-1, (1,)), (0, (0, 1)), (last, (-1, 0)), (last + 1, (-1,))]
+    first_level(wide, shifted, stencils.at[0], centers, middle, [above, None, None, below])
+
+    def write(row, at, value):
+        reach[row, :, at] = value
+
+    windows = {
+        0: [None, None, (middle, 0)],
+        1: [None, (middle, 0), (middle, 1)],
+        2: [(middle, 2), (middle, 3), None],
+        3: [(middle, 3), None, None],
+    }
+    second_level(stencils.at[1], windows, radial, write)
+    for place in range(2):
+        to_partner[place] = either(odd, reach[place], reach[2 + place])
+        to_outer[place] = either(odd, reach[2 + place], reach[place])
+
+
+def back_own_kernel(field, side_1, side_0, stencils, latent, edge, out, wide, shifted, middle):
+    height, _, radial = field.shape
+    fill_wide(wide, field, side_0, side_1, range(height))
+    centers = [(row, ALL) for row in range(1, height - 1)]
+    first_level(wide, shifted, stencils.at[0], centers, middle, [None] * len(centers))
+
+    def write(row, at, value):
+        out[row, :, at] = latent[row, :, at] + value
+
+    line = [(edge, 0), (edge, 1)] + [(middle, place) for place in range(height - 2)] + [(edge, 2), (edge, 3)]
+    second_level(stencils.at[1], {row: line[row:row + 3] for row in range(height)}, radial, write)
+
+
+def close_kernel(own, end_0, end_1, out):
+    height = own.shape[0]
+    _, odd = position("lat")
+    for row in range(2, height - 2):
+        out[row] = own[row]
+    for place in range(2):
+        partner, outer = end_0[place], end_1[place]
+        out[place] = own[place] + either(odd, partner, outer)
+        out[height - 2 + place] = own[height - 2 + place] + either(odd, outer, partner)
 
 
 def open_kernel(
@@ -201,18 +261,15 @@
     counts, offsets, residual, pixel, bins, arrived,
 ):
     pairs = (
-        (latent_in, latent), (counts_in, counts), (offsets_in, offsets),
-        (residual_in, residual), (pixel_in, pixel), (bins_in, bins),
+        (counts_in, counts), (offsets_in, offsets), (residual_in, residual), (pixel_in, pixel), (bins_in, bins),
+        (latent_in, latent),
     )
     copies = [pltpu.make_async_copy(source, target, arrived.at[i]) for i, (source, target) in enumerate(pairs)]
     for copy in copies:
         copy.start()
-    copies[0].wait()
+    for copy in copies[:-1]:
+        copy.wait()
     height, _, radial = latent.shape
-    pack_sides([latent[row] for row in range(height)], to_partner, to_outer)
-    for copy in copies[1:]:
-        copy.wait()
-
     lane = lax.broadcasted_iota(jnp.int32, (SUBLANES, LANES), 1)
     row = lax.broadcasted_iota(jnp.int32, (SUBLANES, LANES), 0)
     slot = row * LANES + lane
@@ -230,6 +287,9 @@
         at = pl.ds(first, SUBLANES)
         cell = (pixel[at, :] * radial + bins[at, :]).astype(jnp.float32)
         out[owner] = jnp.where(row < RUNS, window(residual[at, :]), pltpu.roll(window(cell), RUNS, 0))
+
+    copies[-1].wait()
+    pack_sides([latent[row] for row in range(height)], to_partner, to_outer)
 
 
 def behind_of(got, part, *, height, width, radial):
@@ -256,7 +316,7 @@
     place = lax.bitwise_and(pixel + 2, width - 1)
     own = upper * pixels + lax.shift_right_logical(pixel, 3) * 4 + lax.bitwise_and(place, 3)
     label = jnp.where(lax.shift_right_logical(place, 2) == part, own, classes).astype(jnp.float32)
-    lows = jnp.transpose((bins - upper * half + 1).astype(jnp.float32))
+    lows = jnp.transpose((bins - upper * half + 1).astype(jnp.float32)).astype(bf16)
     coarse = tiles.astype(bf16).astype(jnp.float32)
     rest = tiles - coarse
 
@@ -269,7 +329,7 @@
             left.append(jnp.concatenate([
                 jnp.where(mine, tall(coarse[row:row + 1]), zero), jnp.where(mine, tall(rest[row:row + 1]), zero)
             ], axis=0))
-            low = jnp.broadcast_to(lows[:, row + RUNS:row + RUNS + 1], (LANES, LANES)).astype(bf16)
+            low = jnp.broadcast_to(lows[:, row + RUNS:row + RUNS + 1], (LANES, LANES))
             right.append(jnp.concatenate([jnp.maximum(low, place) for place in places], axis=1))
         total = total + jnp.dot(
             jnp.concatenate(left, axis=1), jnp.concatenate(right, axis=0), preferred_element_type=jnp.float32
@@ -323,7 +383,8 @@
         return pairs + [(j, i) for i, j in pairs]
 
     moves = [(to_partner, inner), (to_outer, outer)]
-    return tuple(lax.ppermute(values, axis, both_ways(pairs)) for values, pairs in moves[::-1 if outer_first else 1])
+    got = [lax.ppermute(values, axis, both_ways(pairs)) for values, pairs in moves[::-1 if outer_first else 1]]
+    return tuple(got[::-1 if outer_first else 1])
 
 
 VMEM = pl.BlockSpec(memory_space=pltpu.VMEM)
@@ -360,78 +421,51 @@
     ])
     got = lax.all_to_all(packed, ("lat", "lon"), split_axis=0, concat_axis=0, tiled=True)
 
-    def spread(field, to_sides, name):
-        beside = swap(*to_sides, "lon", True)
-        to_ends = pl.pallas_call(
-            pack_ends_kernel,
-            out_shape=(ends, ends),
-            in_specs=[VMEM] * 3,
-            out_specs=(VMEM, VMEM),
-            compiler_params=LIMIT,
-            name=name + "_pack",
-        )(field, *beside)
-        return beside, swap(*to_ends, "lat", False, outer_first=True)
-
     rows = pltpu.VMEM((height, 2 * width, radial), f32)
     moved = pltpu.VMEM((2, height, 2 * width, radial), f32)
-
-    def refined_inside(coefs, finish, field, beside, table, extra, name):
+    edge = (3, 3, 4, width, radial)
+    inner_rows = (3, 3, height - 2, width, radial)
+
+    def call(kernel, name, outs, scratch, *operands):
         return pl.pallas_call(
-            functools.partial(refine_inside_kernel, coefs, finish),
-            out_shape=(
-                jax.ShapeDtypeStruct((height - 4, width, radial), f32),
-                jax.ShapeDtypeStruct((3, 3, height - 2, width, radial), f32),
-            ),
-            in_specs=[VMEM] * 5,
-            out_specs=(VMEM, VMEM),
-            scratch_shapes=[rows, moved],
+            kernel,
+            out_shape=outs,
+            in_specs=[VMEM] * len(operands),
+            out_specs=jax.tree.map(lambda _: VMEM, outs),
+            scratch_shapes=scratch,
             compiler_params=LIMIT,
-            name=name + "_inside",
-        )(field, *beside, table, extra)
-
-    def refined_ends(coefs, finish, field, beside, above, table, extra, inner, middle, name, packs):
-        return pl.pallas_call(
-            functools.partial(refine_ends_kernel, coefs, finish, packs),
-            out_shape=(tile, sides, sides) if packs else tile,
-            in_specs=[VMEM] * 9,
-            out_specs=(VMEM,) * 3 if packs else VMEM,
-            scratch_shapes=[pltpu.VMEM((3, 3, 4, width, radial), f32), rows, moved],
-            compiler_params=LIMIT,
-            name=name + "_ends",
-        )(field, *beside, *above, table, extra, middle, inner)
-
-    beside, above = spread(latent, to_sides, "density")
-    inner, middle = refined_inside(
-        (0, 1), lambda value, _: jnp.exp(value), latent, beside, stencils, latent, "density"
-    )
-    behind = pl.pallas_call(
-        bin_sides_kernel,
-        out_shape=tile,
-        in_specs=[VMEM, VMEM],
-        out_specs=VMEM,
-        compiler_params=LIMIT,
-        name="bin_sides",
-    )(got, inner)
-    density, *to_sides = refined_ends(
-        (0, 1), lambda value, _: jnp.exp(value), latent, beside, above, stencils, behind, inner, middle, "density", True,
-    )
-    upstream = pl.pallas_call(
-        bin_rest_kernel,
-        out_shape=tile,
-        in_specs=[VMEM] * 3,
-        out_specs=VMEM,
-        compiler_params=LIMIT,
-        name="bin_rest",
-    )(got, density, behind)
-
-    mirrored = mirror(stencils)
-    beside, above = spread(upstream, to_sides, "back")
-    inner, middle = refined_inside(
-        (1, 0), lambda value, field: field + value, upstream, beside, mirrored, latent, "back"
-    )
-    return refined_ends(
-        (1, 0), lambda value, field: field + value, upstream, beside, above, mirrored, latent, inner, middle, "back", False,
-    )
+            name=name,
+        )(*operands)
+
+    def shape(*sizes):
+        return jax.ShapeDtypeStruct(sizes, f32)
+
+    beside = swap(*to_sides, "lon", True)
+    to_ends = call(pack_ends_kernel, "density_pack", (ends, ends), [], latent, *beside)
+    above = swap(*to_ends, "lat", False, outer_first=True)
+    inner, middle = call(
+        density_inside_kernel, "density_inside", (shape(height - 4, width, radial), shape(*inner_rows)), [rows, moved],
+        latent, *beside, stencils,
+    )
+    behind = call(bin_sides_kernel, "bin_sides", tile, [], got, inner)
+    density, *to_sides = call(
+        density_ends_kernel, "density_ends", (tile, sides, sides), [pltpu.VMEM(edge, f32), rows, moved],
+        latent, *beside, *above[::-1], stencils, middle, inner, behind,
+    )
+    upstream = call(bin_rest_kernel, "bin_rest", tile, [], got, density, behind)
+
+    mirrored = mirror(stencils)[::-1]
+    beside = swap(*to_sides, "lon", True, outer_first=True)
+    *to_ends, middle = call(
+        back_reach_kernel, "back_reach", (shape(2, width, radial), shape(2, width, radial), shape(*edge)),
+        [rows, moved, pltpu.VMEM((4, width, radial), f32)], upstream, *beside[::-1], mirrored,
+    )
+    above = swap(*to_ends, "lat", False)
+    own = call(
+        back_own_kernel, "back_own", tile, [rows, moved, pltpu.VMEM(inner_rows, f32)],
+        upstream, *beside[::-1], mirrored, latent, middle,
+    )
+    return call(close_kernel, "close", tile, [], own, *above)
 
 
 def solution(mesh):

time: 35.2 us -> 33.7 us (0.957)
  the two profiles are of different devices: /device:TPU:0 before, /device:TPU:2 now
where the time goes in v11:
time: 33.7 us; the launch traced here: 33.5 us
  starting transfers between devices  15.3 us (45%)
  Pallas kernels  10.6 us (31%)
  waiting for transfers between devices  7.09 us (21%)
    ppermute x8, starting transfers between devices, swap(): lax.ppermute(values, axis, both_ways(pairs))  12.2 us
    pallas_call x8, Pallas kernels, call(): pl.pallas_call(kernel, out_shape=outs, in_specs=[VMEM] * len(operands), o...  8.83 us
    ppermute x8, waiting for transfers between devices, swap(): lax.ppermute(values, axis, both_ways(pairs))  4.73 us
    all_to_all x1, starting transfers between devices, on_device(): lax.all_to_all(packed, ('lat', 'lon'), split_axis=0, concat_axis=0, tiled...  3.09 us
    all_to_all x1, waiting for transfers between devices, on_device(): lax.all_to_all(packed, ('lat', 'lon'), split_axis=0, concat_axis=0, tiled...  2.36 us
    pallas_call x1, Pallas kernels, on_device(): pl.pallas_call(open_kernel, out_shape=(jax.ShapeDtypeStruct((shards, 2 *...  1.78 us
  transfers between devices with their start and end apart: 9, of which 3 were waited for; matrix products, arithmetic and copies ran while one was open for 1% of the time, Pallas kernels for 20%

profile of v11, /device:TPU:2, one launch (start us, length us, event | category | flops | bytes accessed | tf_op | source)
XLA Modules:
  0.0 33.5 jit_solution(4010462413757652553)
XLA Ops:
  0.0 1.8 %opening.1 = (f32[32,8,128]{2,1,0:T(8,128)}, f32[8,8,512]{2,1,0:T(8,128)S(1)}, f32[2,8,512]{2,1,0:T(8,128)S(1)}, f32[2,8,512]{2,1,0:T(8,128)S(1)}) custom-call(s32[1,32]{1,0:T(1,128)} %counts_in.1, s32[1,32]{1,0:T(1,128)} %offsets_in.1, f32[128,128]{1,0:T(8,128)} %bitcast.20, s32[128,128]{1,0:T(8,128)} %bitcast.21, s32[128,128]{1,0:T(8,128)} %bitcast.22, ...), custom_call_target="tpu_custom_call" | custom-call | tf_op jit(solution)/shard_map/opening/pallas_call | solution.py:408
  1.8 0.1 collective-permute-start
  1.9 3.7 %collective-permute-start.1 = (f32[2,8,512]{2,1,0:T(8,128)S(1)}, f32[2,8,512]{2,1,0:T(8,128)S(1)}, u32[]{:S(2)}, u32[]{:S(2)}) collective-permute-start(f32[2,8,512]{2,1,0:T(8,128)S(1)} %get-tuple-element.22), channel_id=1, source_target_pairs={{1,2},{3,4},{5,6},{7,0},{2,1},{4,3},{6,5},{0,7},{9,10},{11,12},{13... | collective-permute-start | bytes 98312 | tf_op jit(solution)/shard_map/ppermute | solution.py:386
  5.6 3.1 %all-to-all-start = ((f32[32,8,128]{2,1,0:T(8,128)}), f32[32,8,128]{2,1,0:T(8,128)S(1)}, u32[]{:S(2)}, u32[]{:S(2)}) async-start(f32[32,8,128]{2,1,0:T(8,128)} %get-tuple-element.19), calls=%async_computation | async-start | bytes 262144 | tf_op jit(solution)/shard_map/all_to_all | solution.py:422
  8.7 0.1 slice_bitcast_fusion.1
  8.8 0.0 collective-permute-done.side_0
  8.8 0.0 collective-permute-done.1.side_1
  8.9 3.4 %collective-permute-start.2 = (f32[3,8,512]{2,1,0:T(8,128)S(1)}, f32[3,8,512]{2,1,0:T(8,128)S(1)}, u32[]{:S(2)}, u32[]{:S(2)}) collective-permute-start(f32[3,8,512]{2,1,0:T(8,128)S(1)} %get-tuple-element.23), channel_id=1, source_target_pairs={{8,16},{16,8},{9,17},{17,9},{10,18},{18,10},{11,19},{19,11},{12,20... | collective-permute-start | bytes 147464 | tf_op jit(solution)/shard_map/ppermute | solution.py:386
  12.2 0.1 collective-permute-start.3
  12.3 0.1 pad_bitcast_fusion
  12.5 1.1 %density_inside.1 = (f32[4,8,512]{2,1,0:T(8,128)S(1)}, f32[3,3,6,8,512]{4,3,2,1,0:T(8,128)S(1)}) custom-call(f32[8,8,512]{2,1,0:T(8,128)S(1)} %get-tuple-element.20.field.latent, f32[2,8,512]{2,1,0:T(8,128)S(1)} %collective-permute-done.side_0, f32[2,8,512]{2,1,0:T(8,128)S(1)} %collective-permute-done.1.side_1, f32[2,27,512]{2,1,0:T(8,128)S(1)} %copy.18.stencils), custom_call_target="tpu_custom_call" | custom-call | tf_op jit(solution)/shard_map/density_inside/pallas_call | solution.py:430
  13.5 2.4 %all-to-all-done.got = f32[32,8,128]{2,1,0:T(8,128)S(1)} async-done(((f32[32,8,128]{2,1,0:T(8,128)}), f32[32,8,128]{2,1,0:T(8,128)S(1)}, u32[]{:S(2)}, u32[]{:S(2)}) %all-to-all-start) | async-done | bytes 131104 | tf_op jit(solution)/shard_map/all_to_all | solution.py:422
  15.9 2.2 %bin_sides.1.behind = f32[8,8,512]{2,1,0:T(8,128)S(1)} custom-call(f32[32,8,128]{2,1,0:T(8,128)S(1)} %all-to-all-done.got, f32[4,8,512]{2,1,0:T(8,128)S(1)} %get-tuple-element.26._.inner), custom_call_target="tpu_custom_call" | custom-call | tf_op jit(solution)/shard_map/bin_sides/pallas_call | solution.py:430
  18.1 0.9 %density_ends.1 = (f32[8,8,512]{2,1,0:T(8,128)S(1)}, f32[2,8,512]{2,1,0:T(8,128)S(1)}, f32[2,8,512]{2,1,0:T(8,128)S(1)}) custom-call(f32[8,8,512]{2,1,0:T(8,128)S(1)} %get-tuple-element.20.field.latent, f32[2,8,512]{2,1,0:T(8,128)S(1)} %collective-permute-done.side_0, f32[2,8,512]{2,1,0:T(8,128)S(1)} %collective-permute-done.1.side_1, ...), custom_call_target="tpu_custom_call" | custom-call | tf_op jit(solution)/shard_map/density_ends/pallas_call | solution.py:430
  19.0 0.8 %collective-permute-start.4 = (f32[2,8,512]{2,1,0:T(8,128)S(1)}, f32[2,8,512]{2,1,0:T(8,128)S(1)}, u32[]{:S(2)}, u32[]{:S(2)}) collective-permute-start(f32[2,8,512]{2,1,0:T(8,128)S(1)} %get-tuple-element.28), channel_id=1, source_target_pairs={{1,2},{3,4},{5,6},{7,0},{2,1},{4,3},{6,5},{0,7},{9,10},{11,12},{13... | collective-permute-start | bytes 98312 | tf_op jit(solution)/shard_map/ppermute | solution.py:386
  19.9 0.1 pad_maximum_fusion
  20.0 2.2 %bin_rest.1.field = f32[8,8,512]{2,1,0:T(8,128)S(1)} custom-call(f32[32,8,128]{2,1,0:T(8,128)S(1)} %all-to-all-done.got, f32[8,8,512]{2,1,0:T(8,128)S(1)} %get-tuple-element.27.density, f32[8,8,512]{2,1,0:T(8,128)S(1)} %bin_sides.1.behind), custom_call_target="tpu_custom_call" | custom-call | tf_op jit(solution)/shard_map/bin_rest/pallas_call | solution.py:430
  22.2 2.1 %collective-permute-done.4.side_1 = f32[2,8,512]{2,1,0:T(8,128)S(1)} collective-permute-done((f32[2,8,512]{2,1,0:T(8,128)S(1)}, f32[2,8,512]{2,1,0:T(8,128)S(1)}, u32[]{:S(2)}, u32[]{:S(2)}) %collective-permute-start.4) | collective-permute-done | bytes 32800 | tf_op jit(solution)/shard_map/ppermute | solution.py:386
  24.2 0.6 %back_reach.1 = (f32[2,8,512]{2,1,0:T(8,128)S(1)}, f32[2,8,512]{2,1,0:T(8,128)S(1)}, f32[3,3,4,8,512]{4,3,2,1,0:T(8,128)S(1)}) custom-call(f32[8,8,512]{2,1,0:T(8,128)S(1)} %bin_rest.1.field, f32[2,8,512]{2,1,0:T(8,128)S(1)} %collective-permute-done.4.side_1, f32[2,8,512]{2,1,0:T(8,128)S(1)} %collective-permute-done.5.side_0, f32[2,27,512]{2,1,0:T(8,128)S(1)} %rev.8.stencils), custom_call_target="tpu_custom_call" | custom-call | tf_op jit(solution)/shard_map/back_reach/pallas_call | solution.py:430
  24.9 1.3 %collective-permute-start.6 = (f32[2,8,512]{2,1,0:T(8,128)S(1)}, f32[2,8,512]{2,1,0:T(8,128)S(1)}, u32[]{:S(2)}, u32[]{:S(2)}) collective-permute-start(f32[2,8,512]{2,1,0:T(8,128)S(1)} %get-tuple-element.31), channel_id=1, source_target_pairs={{0,8},{16,24},{8,0},{24,16},{1,9},{17,25},{9,1},{25,17},{2,10},{18... | collective-permute-start | bytes 98312 | tf_op jit(solution)/shard_map/ppermute | solution.py:386
  26.1 2.9 %collective-permute-start.7 = (f32[2,8,512]{2,1,0:T(8,128)S(1)}, f32[2,8,512]{2,1,0:T(8,128)S(1)}, u32[]{:S(2)}, u32[]{:S(2)}) collective-permute-start(f32[2,8,512]{2,1,0:T(8,128)S(1)} %get-tuple-element.32), channel_id=1, source_target_pairs={{8,16},{16,8},{9,17},{17,9},{10,18},{18,10},{11,19},{19,11},{12,20... | collective-permute-start | bytes 98312 | tf_op jit(solution)/shard_map/ppermute | solution.py:386
  29.0 1.2 %back_own.1.own = f32[8,8,512]{2,1,0:T(8,128)S(1)} custom-call(f32[8,8,512]{2,1,0:T(8,128)S(1)} %bin_rest.1.field, f32[2,8,512]{2,1,0:T(8,128)S(1)} %collective-permute-done.4.side_1, f32[2,8,512]{2,1,0:T(8,128)S(1)} %collective-permute-done.5.side_0, f32[2,27,512]{2,1,0:T(8,128)S(1)} %rev.8.stencils, f32[8,8,512]{2,1,0:T(8,128)S(1)} %get-tuple-element.20.field.latent, ...), custom_call_target="tpu_custom_call" | custom-call | tf_op jit(solution)/shard_map/back_own/pallas_call | solution.py:430
  30.2 2.6 %collective-permute-done.7.end_1 = f32[2,8,512]{2,1,0:T(8,128)S(1)} collective-permute-done((f32[2,8,512]{2,1,0:T(8,128)S(1)}, f32[2,8,512]{2,1,0:T(8,128)S(1)}, u32[]{:S(2)}, u32[]{:S(2)}) %collective-permute-start.7) | collective-permute-done | bytes 32800 | tf_op jit(solution)/shard_map/ppermute | solution.py:386
  32.8 0.7 %close.1 = f32[8,8,512]{2,1,0:T(8,128)} custom-call(f32[8,8,512]{2,1,0:T(8,128)S(1)} %back_own.1.own, f32[2,8,512]{2,1,0:T(8,128)S(1)} %collective-permute-done.6.end_0, f32[2,8,512]{2,1,0:T(8,128)S(1)} %collective-permute-done.7.end_1), custom_call_target="tpu_custom_call" | custom-call | tf_op jit(solution)/shard_map/close/pallas_call | solution.py:430
  (13 shorter events, 0.1 us)
Async XLA Ops:
  1.8 7.0 %collective-permute-start = (f32[2,8,512]{2,1,0:T(8,128)S(1)}, f32[2,8,512]{2,1,0:T(8,128)S(1)}, u32[]{:S(2)}, u32[]{:S(2)}) collective-permute-start(f32[2,8,512]{2,1,0:T(8,128)S(1)} %get-tuple-element.21), channel_id=1, source_target_pairs={{0,1},{2,3},{4,5},{6,7},{1,0},{3,2},{5,4},{7,6},{8,9},{10,11},{12,... | collective-permute-start | bytes 98312 | tf_op jit(solution)/shard_map/ppermute | solution.py:386
  1.9 6.9 %collective-permute-start.1 = (f32[2,8,512]{2,1,0:T(8,128)S(1)}, f32[2,8,512]{2,1,0:T(8,128)S(1)}, u32[]{:S(2)}, u32[]{:S(2)}) collective-permute-start(f32[2,8,512]{2,1,0:T(8,128)S(1)} %get-tuple-element.22), channel_id=1, source_target_pairs={{1,2},{3,4},{5,6},{7,0},{2,1},{4,3},{6,5},{0,7},{9,10},{11,12},{13... | collective-permute-start | bytes 98312 | tf_op jit(solution)/shard_map/ppermute | solution.py:386
  5.6 3.1 %copy-start = (f32[2,27,512]{2,0,1:T(2,128)S(1)}, f32[2,27,512]{2,0,1:T(2,128)}, u32[]{:S(2)}) copy-start(f32[2,27,512]{2,0,1:T(2,128)} %param.13) | copy-start | bytes 331780
  5.6 10.3 %all-to-all-start = ((f32[32,8,128]{2,1,0:T(8,128)}), f32[32,8,128]{2,1,0:T(8,128)S(1)}, u32[]{:S(2)}, u32[]{:S(2)}) async-start(f32[32,8,128]{2,1,0:T(8,128)} %get-tuple-element.19), calls=%async_computation | async-start | bytes 262144 | tf_op jit(solution)/shard_map/all_to_all | solution.py:422
  8.9 9.2 %collective-permute-start.2 = (f32[3,8,512]{2,1,0:T(8,128)S(1)}, f32[3,8,512]{2,1,0:T(8,128)S(1)}, u32[]{:S(2)}, u32[]{:S(2)}) collective-permute-start(f32[3,8,512]{2,1,0:T(8,128)S(1)} %get-tuple-element.23), channel_id=1, source_target_pairs={{8,16},{16,8},{9,17},{17,9},{10,18},{18,10},{11,19},{19,11},{12,20... | collective-permute-start | bytes 147464 | tf_op jit(solution)/shard_map/ppermute | solution.py:386
  12.2 5.8 %collective-permute-start.3 = (f32[3,8,512]{2,1,0:T(8,128)S(1)}, f32[3,8,512]{2,1,0:T(8,128)S(1)}, u32[]{:S(2)}, u32[]{:S(2)}) collective-permute-start(f32[3,8,512]{2,1,0:T(8,128)S(1)} %get-tuple-element.24), channel_id=1, source_target_pairs={{0,8},{16,24},{8,0},{24,16},{1,9},{17,25},{9,1},{25,17},{2,10},{18... | collective-permute-start | bytes 147464 | tf_op jit(solution)/shard_map/ppermute | solution.py:386
  19.0 5.2 %collective-permute-start.4 = (f32[2,8,512]{2,1,0:T(8,128)S(1)}, f32[2,8,512]{2,1,0:T(8,128)S(1)}, u32[]{:S(2)}, u32[]{:S(2)}) collective-permute-start(f32[2,8,512]{2,1,0:T(8,128)S(1)} %get-tuple-element.28), channel_id=1, source_target_pairs={{1,2},{3,4},{5,6},{7,0},{2,1},{4,3},{6,5},{0,7},{9,10},{11,12},{13... | collective-permute-start | bytes 98312 | tf_op jit(solution)/shard_map/ppermute | solution.py:386
  19.9 4.4 %collective-permute-start.5 = (f32[2,8,512]{2,1,0:T(8,128)S(1)}, f32[2,8,512]{2,1,0:T(8,128)S(1)}, u32[]{:S(2)}, u32[]{:S(2)}) collective-permute-start(f32[2,8,512]{2,1,0:T(8,128)S(1)} %get-tuple-element.29), channel_id=1, source_target_pairs={{0,1},{2,3},{4,5},{6,7},{1,0},{3,2},{5,4},{7,6},{8,9},{10,11},{12,... | collective-permute-start | bytes 98312 | tf_op jit(solution)/shard_map/ppermute | solution.py:386
  24.9 5.3 %collective-permute-start.6 = (f32[2,8,512]{2,1,0:T(8,128)S(1)}, f32[2,8,512]{2,1,0:T(8,128)S(1)}, u32[]{:S(2)}, u32[]{:S(2)}) collective-permute-start(f32[2,8,512]{2,1,0:T(8,128)S(1)} %get-tuple-element.31), channel_id=1, source_target_pairs={{0,8},{16,24},{8,0},{24,16},{1,9},{17,25},{9,1},{25,17},{2,10},{18... | collective-permute-start | bytes 98312 | tf_op jit(solution)/shard_map/ppermute | solution.py:386
  26.1 6.7 %collective-permute-start.7 = (f32[2,8,512]{2,1,0:T(8,128)S(1)}, f32[2,8,512]{2,1,0:T(8,128)S(1)}, u32[]{:S(2)}, u32[]{:S(2)}) collective-permute-start(f32[2,8,512]{2,1,0:T(8,128)S(1)} %get-tuple-element.32), channel_id=1, source_target_pairs={{8,16},{16,8},{9,17},{17,9},{10,18},{18,10},{11,19},{19,11},{12,20... | collective-permute-start | bytes 98312 | tf_op jit(solution)/shard_map/ppermute | solution.py:386

commit v12 on v11

--- a/solution.py
+++ b/solution.py
@@ -89,11 +89,8 @@
 
 
 def tiles_of_bins(radial, body):
-    def step(tile, _):
-        body(pl.ds(pl.multiple_of(tile * LANES, LANES), LANES))
-        return 0
-
-    lax.fori_loop(0, radial // LANES, step, 0)
+    for start in range(0, radial, LANES):
+        body(slice(start, start + LANES))
 
 
 ALL = (-1, 0, 1)
@@ -275,24 +272,27 @@
     slot = row * LANES + lane
     for owner in range(out.shape[0]):
         start = offsets[0, owner]
-        first = lax.shift_right_logical(start, 7)
+        tile = lax.shift_right_logical(start, 10)
+        first = lax.bitwise_and(lax.shift_right_logical(start, 7), SUBLANES - 1)
         part = lax.bitwise_and(start, LANES - 1)
         live = slot < counts[0, owner]
-
-        def window(values):
-            turned = pltpu.roll(values, lax.bitwise_and(LANES - part, LANES - 1), 1)
-            joined = jnp.where(lane < LANES - part, turned, pltpu.roll(turned, SUBLANES - 1, 0))
-            return jnp.where(live, joined, 0.0)
-
-        at = pl.ds(first, SUBLANES)
-        cell = (pixel[at, :] * radial + bins[at, :]).astype(jnp.float32)
-        out[owner] = jnp.where(row < RUNS, window(residual[at, :]), pltpu.roll(window(cell), RUNS, 0))
+        here = row < SUBLANES - first
+
+        def window(one, two):
+            up = lax.bitwise_and(SUBLANES - first, SUBLANES - 1)
+            rows = jnp.where(here, pltpu.roll(one, up, 0), pltpu.roll(two, up, 0))
+            turned = pltpu.roll(rows, lax.bitwise_and(LANES - part, LANES - 1), 1)
+            return jnp.where(lane < LANES - part, turned, pltpu.roll(turned, SUBLANES - 1, 0))
+
+        value = window(residual[tile], residual[tile + 1])
+        cell = window(*[(pixel[at] * radial + bins[at]).astype(jnp.float32) for at in (tile, tile + 1)])
+        out[owner] = jnp.where(row < RUNS, jnp.where(live, value, 0.0), pltpu.roll(jnp.where(live, cell, 0.0), RUNS, 0))
 
     copies[-1].wait()
     pack_sides([latent[row] for row in range(height)], to_partner, to_outer)
 
 
-def behind_of(got, part, *, height, width, radial):
+def behind_of(got, part, group, *, height, width, radial):
     half = radial // 2
     pixels = height * width // 2
     classes = 2 * pixels
@@ -321,9 +321,9 @@
     rest = tiles - coarse
 
     total = jnp.zeros((2 * classes, half), jnp.float32)
-    for first in range(0, shards, 2):
+    for first in range(0, shards, group):
         left, right = [], []
-        for run in range(2 * RUNS):
+        for run in range(group * RUNS):
             row = (first + run // RUNS) * rows + run % RUNS
             mine = tall(label[row + RUNS:row + RUNS + 1]) == column
             left.append(jnp.concatenate([
@@ -353,7 +353,7 @@
 
 def bin_sides_kernel(got, _, behind):
     height, width, radial = behind.shape
-    packed = behind_of(got, 0, height=height, width=width, radial=radial)
+    packed = behind_of(got, 0, 1, height=height, width=width, radial=radial)
     for row, values in enumerate(column_rows(packed, 0, height)):
         behind[row] = values
 
@@ -361,7 +361,7 @@
 def bin_rest_kernel(got, density, behind, upstream):
     height, width, radial = behind.shape
     sub = sublane(radial)
-    packed = behind_of(got, 1, height=height, width=width, radial=radial)
+    packed = behind_of(got, 1, 4, height=height, width=width, radial=radial)
     for row, values in enumerate(column_rows(packed, 1, height)):
         upstream[row] = density[row] * jnp.where((sub < 2) | (sub >= 6), behind[row], values)
 
@@ -403,7 +403,7 @@
     ends = jax.ShapeDtypeStruct((3, SUBLANES, radial), f32)
 
     def table(values):
-        return values.reshape(slots // LANES, LANES)
+        return values.reshape(slots // (SUBLANES * LANES), SUBLANES, LANES)
 
     packed, latent, *to_sides = pl.pallas_call(
         open_kernel,
@@ -411,7 +411,7 @@
         in_specs=[HBM] * 6,
         out_specs=(VMEM, VMEM, VMEM, VMEM),
         scratch_shapes=[pltpu.SMEM((1, shards), i32)] * 2
-        + [pltpu.VMEM((slots // LANES, LANES), kind) for kind in (f32, i32, i32)]
+        + [pltpu.VMEM((slots // (SUBLANES * LANES), SUBLANES, LANES), kind) for kind in (f32, i32, i32)]
         + [pltpu.SemaphoreType.DMA((6,))],
         compiler_params=LIMIT,
         name="opening",

time: 33.7 us -> 33.2 us (0.985)
  Pallas kernels: 10.6 us -> 9.3 us
  waiting for transfers between devices: 7.09 us -> 7.83 us
    pallas_call x8, Pallas kernels: 8.83 us -> 7.43 us  [call(): pl.pallas_call(kernel, out_shape=outs, in_specs=[VMEM] * len(operands), o...]
    ppermute x8, waiting for transfers between devices: 4.73 us -> 5.1 us  [swap(): lax.ppermute(values, axis, both_ways(pairs))]
    all_to_all x1, waiting for transfers between devices: 2.36 us -> 2.73 us  [on_device(): lax.all_to_all(packed, ('lat', 'lon'), split_axis=0, concat_axis=0, tiled...]
  transfers between devices with their start and end apart: 9 -> 9, of which waited for: 3 -> 3; matrix products, arithmetic and copies ran while one was open for 1% -> 1% of each run, Pallas kernels for 20% -> 18%
where the time goes in v12:
time: 33.2 us; the launch traced here: 32.9 us
  starting transfers between devices  15.3 us (46%)
  Pallas kernels  9.3 us (28%)
  waiting for transfers between devices  7.83 us (24%)
    ppermute x8, starting transfers between devices, swap(): lax.ppermute(values, axis, both_ways(pairs))  12.2 us
    pallas_call x8, Pallas kernels, call(): pl.pallas_call(kernel, out_shape=outs, in_specs=[VMEM] * len(operands), o...  7.43 us
    ppermute x8, waiting for transfers between devices, swap(): lax.ppermute(values, axis, both_ways(pairs))  5.1 us
    all_to_all x1, starting transfers between devices, on_device(): lax.all_to_all(packed, ('lat', 'lon'), split_axis=0, concat_axis=0, tiled...  3.09 us
    all_to_all x1, waiting for transfers between devices, on_device(): lax.all_to_all(packed, ('lat', 'lon'), split_axis=0, concat_axis=0, tiled...  2.73 us
    pallas_call x1, Pallas kernels, on_device(): pl.pallas_call(open_kernel, out_shape=(jax.ShapeDtypeStruct((shards, 2 *...  1.87 us
  transfers between devices with their start and end apart: 9, of which 3 were waited for; matrix products, arithmetic and copies ran while one was open for 1% of the time, Pallas kernels for 18%

profile of v12, /device:TPU:2, one launch (start us, length us, event | category | flops | bytes accessed | tf_op | source)
XLA Modules:
  0.0 32.9 jit_solution(5156731621376162083)
XLA Ops:
  0.0 1.9 %opening.1 = (f32[32,8,128]{2,1,0:T(8,128)}, f32[8,8,512]{2,1,0:T(8,128)S(1)}, f32[2,8,512]{2,1,0:T(8,128)S(1)}, f32[2,8,512]{2,1,0:T(8,128)S(1)}) custom-call(s32[1,32]{1,0:T(1,128)} %counts_in.1, s32[1,32]{1,0:T(1,128)} %offsets_in.1, f32[16,8,128]{2,1,0:T(8,128)} %bitcast.20, s32[16,8,128]{2,1,0:T(8,128)} %bitcast.21, s32[16,8,128]{2,1,0:T(8,128)} %bitcast.22, ...), custom_call_target="tpu_custom_call" | custom-call | tf_op jit(solution)/shard_map/opening/pallas_call | solution.py:408
  1.9 0.1 collective-permute-start
  2.0 3.7 %collective-permute-start.1 = (f32[2,8,512]{2,1,0:T(8,128)S(1)}, f32[2,8,512]{2,1,0:T(8,128)S(1)}, u32[]{:S(2)}, u32[]{:S(2)}) collective-permute-start(f32[2,8,512]{2,1,0:T(8,128)S(1)} %get-tuple-element.22), channel_id=1, source_target_pairs={{1,2},{3,4},{5,6},{7,0},{2,1},{4,3},{6,5},{0,7},{9,10},{11,12},{13... | collective-permute-start | bytes 98312 | tf_op jit(solution)/shard_map/ppermute | solution.py:386
  5.7 3.1 %all-to-all-start = ((f32[32,8,128]{2,1,0:T(8,128)}), f32[32,8,128]{2,1,0:T(8,128)S(1)}, u32[]{:S(2)}, u32[]{:S(2)}) async-start(f32[32,8,128]{2,1,0:T(8,128)} %get-tuple-element.19), calls=%async_computation | async-start | bytes 262144 | tf_op jit(solution)/shard_map/all_to_all | solution.py:422
  8.8 0.1 slice_bitcast_fusion.1
  8.9 0.0 collective-permute-done.side_0
  8.9 0.0 collective-permute-done.1.side_1
  8.9 3.4 %collective-permute-start.2 = (f32[3,8,512]{2,1,0:T(8,128)S(1)}, f32[3,8,512]{2,1,0:T(8,128)S(1)}, u32[]{:S(2)}, u32[]{:S(2)}) collective-permute-start(f32[3,8,512]{2,1,0:T(8,128)S(1)} %get-tuple-element.23), channel_id=1, source_target_pairs={{8,16},{16,8},{9,17},{17,9},{10,18},{18,10},{11,19},{19,11},{12,20... | collective-permute-start | bytes 147464 | tf_op jit(solution)/shard_map/ppermute | solution.py:386
  12.3 0.1 collective-permute-start.3
  12.4 0.1 pad_bitcast_fusion
  12.6 0.7 %density_inside.1 = (f32[4,8,512]{2,1,0:T(8,128)S(1)}, f32[3,3,6,8,512]{4,3,2,1,0:T(8,128)S(1)}) custom-call(f32[8,8,512]{2,1,0:T(8,128)S(1)} %get-tuple-element.20.field.latent, f32[2,8,512]{2,1,0:T(8,128)S(1)} %collective-permute-done.side_0, f32[2,8,512]{2,1,0:T(8,128)S(1)} %collective-permute-done.1.side_1, f32[2,27,512]{2,1,0:T(8,128)S(1)} %copy.18.stencils), custom_call_target="tpu_custom_call" | custom-call | tf_op jit(solution)/shard_map/density_inside/pallas_call | solution.py:430
  13.3 2.7 %all-to-all-done.got = f32[32,8,128]{2,1,0:T(8,128)S(1)} async-done(((f32[32,8,128]{2,1,0:T(8,128)}), f32[32,8,128]{2,1,0:T(8,128)S(1)}, u32[]{:S(2)}, u32[]{:S(2)}) %all-to-all-start) | async-done | bytes 131104 | tf_op jit(solution)/shard_map/all_to_all | solution.py:422
  16.0 2.2 %bin_sides.1.behind = f32[8,8,512]{2,1,0:T(8,128)S(1)} custom-call(f32[32,8,128]{2,1,0:T(8,128)S(1)} %all-to-all-done.got, f32[4,8,512]{2,1,0:T(8,128)S(1)} %get-tuple-element.26._.inner), custom_call_target="tpu_custom_call" | custom-call | tf_op jit(solution)/shard_map/bin_sides/pallas_call | solution.py:430
  18.2 0.5 %density_ends.1 = (f32[8,8,512]{2,1,0:T(8,128)S(1)}, f32[2,8,512]{2,1,0:T(8,128)S(1)}, f32[2,8,512]{2,1,0:T(8,128)S(1)}) custom-call(f32[8,8,512]{2,1,0:T(8,128)S(1)} %get-tuple-element.20.field.latent, f32[2,8,512]{2,1,0:T(8,128)S(1)} %collective-permute-done.side_0, f32[2,8,512]{2,1,0:T(8,128)S(1)} %collective-permute-done.1.side_1, ...), custom_call_target="tpu_custom_call" | custom-call | tf_op jit(solution)/shard_map/density_ends/pallas_call | solution.py:430
  18.7 0.8 %collective-permute-start.4 = (f32[2,8,512]{2,1,0:T(8,128)S(1)}, f32[2,8,512]{2,1,0:T(8,128)S(1)}, u32[]{:S(2)}, u32[]{:S(2)}) collective-permute-start(f32[2,8,512]{2,1,0:T(8,128)S(1)} %get-tuple-element.28), channel_id=1, source_target_pairs={{1,2},{3,4},{5,6},{7,0},{2,1},{4,3},{6,5},{0,7},{9,10},{11,12},{13... | collective-permute-start | bytes 98312 | tf_op jit(solution)/shard_map/ppermute | solution.py:386
  19.6 0.1 pad_maximum_fusion
  19.7 2.2 %bin_rest.1.field = f32[8,8,512]{2,1,0:T(8,128)S(1)} custom-call(f32[32,8,128]{2,1,0:T(8,128)S(1)} %all-to-all-done.got, f32[8,8,512]{2,1,0:T(8,128)S(1)} %get-tuple-element.27.density, f32[8,8,512]{2,1,0:T(8,128)S(1)} %bin_sides.1.behind), custom_call_target="tpu_custom_call" | custom-call | tf_op jit(solution)/shard_map/bin_rest/pallas_call | solution.py:430
  21.9 2.1 %collective-permute-done.4.side_1 = f32[2,8,512]{2,1,0:T(8,128)S(1)} collective-permute-done((f32[2,8,512]{2,1,0:T(8,128)S(1)}, f32[2,8,512]{2,1,0:T(8,128)S(1)}, u32[]{:S(2)}, u32[]{:S(2)}) %collective-permute-start.4) | collective-permute-done | bytes 32800 | tf_op jit(solution)/shard_map/ppermute | solution.py:386
  23.9 0.4 %back_reach.1 = (f32[2,8,512]{2,1,0:T(8,128)S(1)}, f32[2,8,512]{2,1,0:T(8,128)S(1)}, f32[3,3,4,8,512]{4,3,2,1,0:T(8,128)S(1)}) custom-call(f32[8,8,512]{2,1,0:T(8,128)S(1)} %bin_rest.1.field, f32[2,8,512]{2,1,0:T(8,128)S(1)} %collective-permute-done.4.side_1, f32[2,8,512]{2,1,0:T(8,128)S(1)} %collective-permute-done.5.side_0, f32[2,27,512]{2,1,0:T(8,128)S(1)} %rev.8.stencils), custom_call_target="tpu_custom_call" | custom-call | tf_op jit(solution)/shard_map/back_reach/pallas_call | solution.py:430
  24.3 1.3 %collective-permute-start.6 = (f32[2,8,512]{2,1,0:T(8,128)S(1)}, f32[2,8,512]{2,1,0:T(8,128)S(1)}, u32[]{:S(2)}, u32[]{:S(2)}) collective-permute-start(f32[2,8,512]{2,1,0:T(8,128)S(1)} %get-tuple-element.31), channel_id=1, source_target_pairs={{0,8},{16,24},{8,0},{24,16},{1,9},{17,25},{9,1},{25,17},{2,10},{18... | collective-permute-start | bytes 98312 | tf_op jit(solution)/shard_map/ppermute | solution.py:386
  25.6 2.9 %collective-permute-start.7 = (f32[2,8,512]{2,1,0:T(8,128)S(1)}, f32[2,8,512]{2,1,0:T(8,128)S(1)}, u32[]{:S(2)}, u32[]{:S(2)}) collective-permute-start(f32[2,8,512]{2,1,0:T(8,128)S(1)} %get-tuple-element.32), channel_id=1, source_target_pairs={{8,16},{16,8},{9,17},{17,9},{10,18},{18,10},{11,19},{19,11},{12,20... | collective-permute-start | bytes 98312 | tf_op jit(solution)/shard_map/ppermute | solution.py:386
  28.4 0.8 %back_own.1.own = f32[8,8,512]{2,1,0:T(8,128)S(1)} custom-call(f32[8,8,512]{2,1,0:T(8,128)S(1)} %bin_rest.1.field, f32[2,8,512]{2,1,0:T(8,128)S(1)} %collective-permute-done.4.side_1, f32[2,8,512]{2,1,0:T(8,128)S(1)} %collective-permute-done.5.side_0, f32[2,27,512]{2,1,0:T(8,128)S(1)} %rev.8.stencils, f32[8,8,512]{2,1,0:T(8,128)S(1)} %get-tuple-element.20.field.latent, ...), custom_call_target="tpu_custom_call" | custom-call | tf_op jit(solution)/shard_map/back_own/pallas_call | solution.py:430
  29.3 3.0 %collective-permute-done.7.end_1 = f32[2,8,512]{2,1,0:T(8,128)S(1)} collective-permute-done((f32[2,8,512]{2,1,0:T(8,128)S(1)}, f32[2,8,512]{2,1,0:T(8,128)S(1)}, u32[]{:S(2)}, u32[]{:S(2)}) %collective-permute-start.7) | collective-permute-done | bytes 32800 | tf_op jit(solution)/shard_map/ppermute | solution.py:386
  32.3 0.7 %close.1 = f32[8,8,512]{2,1,0:T(8,128)} custom-call(f32[8,8,512]{2,1,0:T(8,128)S(1)} %back_own.1.own, f32[2,8,512]{2,1,0:T(8,128)S(1)} %collective-permute-done.6.end_0, f32[2,8,512]{2,1,0:T(8,128)S(1)} %collective-permute-done.7.end_1), custom_call_target="tpu_custom_call" | custom-call | tf_op jit(solution)/shard_map/close/pallas_call | solution.py:430
  (13 shorter events, 0.1 us)
Async XLA Ops:
  1.9 7.0 %collective-permute-start = (f32[2,8,512]{2,1,0:T(8,128)S(1)}, f32[2,8,512]{2,1,0:T(8,128)S(1)}, u32[]{:S(2)}, u32[]{:S(2)}) collective-permute-start(f32[2,8,512]{2,1,0:T(8,128)S(1)} %get-tuple-element.21), channel_id=1, source_target_pairs={{0,1},{2,3},{4,5},{6,7},{1,0},{3,2},{5,4},{7,6},{8,9},{10,11},{12,... | collective-permute-start | bytes 98312 | tf_op jit(solution)/shard_map/ppermute | solution.py:386
  2.0 6.9 %collective-permute-start.1 = (f32[2,8,512]{2,1,0:T(8,128)S(1)}, f32[2,8,512]{2,1,0:T(8,128)S(1)}, u32[]{:S(2)}, u32[]{:S(2)}) collective-permute-start(f32[2,8,512]{2,1,0:T(8,128)S(1)} %get-tuple-element.22), channel_id=1, source_target_pairs={{1,2},{3,4},{5,6},{7,0},{2,1},{4,3},{6,5},{0,7},{9,10},{11,12},{13... | collective-permute-start | bytes 98312 | tf_op jit(solution)/shard_map/ppermute | solution.py:386
  5.7 3.1 %copy-start = (f32[2,27,512]{2,0,1:T(2,128)S(1)}, f32[2,27,512]{2,0,1:T(2,128)}, u32[]{:S(2)}) copy-start(f32[2,27,512]{2,0,1:T(2,128)} %param.13) | copy-start | bytes 331780
  5.7 10.3 %all-to-all-start = ((f32[32,8,128]{2,1,0:T(8,128)}), f32[32,8,128]{2,1,0:T(8,128)S(1)}, u32[]{:S(2)}, u32[]{:S(2)}) async-start(f32[32,8,128]{2,1,0:T(8,128)} %get-tuple-element.19), calls=%async_computation | async-start | bytes 262144 | tf_op jit(solution)/shard_map/all_to_all | solution.py:422
  8.9 9.2 %collective-permute-start.2 = (f32[3,8,512]{2,1,0:T(8,128)S(1)}, f32[3,8,512]{2,1,0:T(8,128)S(1)}, u32[]{:S(2)}, u32[]{:S(2)}) collective-permute-start(f32[3,8,512]{2,1,0:T(8,128)S(1)} %get-tuple-element.23), channel_id=1, source_target_pairs={{8,16},{16,8},{9,17},{17,9},{10,18},{18,10},{11,19},{19,11},{12,20... | collective-permute-start | bytes 147464 | tf_op jit(solution)/shard_map/ppermute | solution.py:386
  12.3 5.8 %collective-permute-start.3 = (f32[3,8,512]{2,1,0:T(8,128)S(1)}, f32[3,8,512]{2,1,0:T(8,128)S(1)}, u32[]{:S(2)}, u32[]{:S(2)}) collective-permute-start(f32[3,8,512]{2,1,0:T(8,128)S(1)} %get-tuple-element.24), channel_id=1, source_target_pairs={{0,8},{16,24},{8,0},{24,16},{1,9},{17,25},{9,1},{25,17},{2,10},{18... | collective-permute-start | bytes 147464 | tf_op jit(solution)/shard_map/ppermute | solution.py:386
  18.7 5.2 %collective-permute-start.4 = (f32[2,8,512]{2,1,0:T(8,128)S(1)}, f32[2,8,512]{2,1,0:T(8,128)S(1)}, u32[]{:S(2)}, u32[]{:S(2)}) collective-permute-start(f32[2,8,512]{2,1,0:T(8,128)S(1)} %get-tuple-element.28), channel_id=1, source_target_pairs={{1,2},{3,4},{5,6},{7,0},{2,1},{4,3},{6,5},{0,7},{9,10},{11,12},{13... | collective-permute-start | bytes 98312 | tf_op jit(solution)/shard_map/ppermute | solution.py:386
  19.6 4.4 %collective-permute-start.5 = (f32[2,8,512]{2,1,0:T(8,128)S(1)}, f32[2,8,512]{2,1,0:T(8,128)S(1)}, u32[]{:S(2)}, u32[]{:S(2)}) collective-permute-start(f32[2,8,512]{2,1,0:T(8,128)S(1)} %get-tuple-element.29), channel_id=1, source_target_pairs={{0,1},{2,3},{4,5},{6,7},{1,0},{3,2},{5,4},{7,6},{8,9},{10,11},{12,... | collective-permute-start | bytes 98312 | tf_op jit(solution)/shard_map/ppermute | solution.py:386
  24.3 5.0 %collective-permute-start.6 = (f32[2,8,512]{2,1,0:T(8,128)S(1)}, f32[2,8,512]{2,1,0:T(8,128)S(1)}, u32[]{:S(2)}, u32[]{:S(2)}) collective-permute-start(f32[2,8,512]{2,1,0:T(8,128)S(1)} %get-tuple-element.31), channel_id=1, source_target_pairs={{0,8},{16,24},{8,0},{24,16},{1,9},{17,25},{9,1},{25,17},{2,10},{18... | collective-permute-start | bytes 98312 | tf_op jit(solution)/shard_map/ppermute | solution.py:386
  25.6 6.7 %collective-permute-start.7 = (f32[2,8,512]{2,1,0:T(8,128)S(1)}, f32[2,8,512]{2,1,0:T(8,128)S(1)}, u32[]{:S(2)}, u32[]{:S(2)}) collective-permute-start(f32[2,8,512]{2,1,0:T(8,128)S(1)} %get-tuple-element.32), channel_id=1, source_target_pairs={{8,16},{16,8},{9,17},{17,9},{10,18},{18,10},{11,19},{19,11},{12,20... | collective-permute-start | bytes 98312 | tf_op jit(solution)/shard_map/ppermute | solution.py:386

commit v13 on v11

--- a/solution.py
+++ b/solution.py
@@ -89,11 +89,8 @@
 
 
 def tiles_of_bins(radial, body):
-    def step(tile, _):
-        body(pl.ds(pl.multiple_of(tile * LANES, LANES), LANES))
-        return 0
-
-    lax.fori_loop(0, radial // LANES, step, 0)
+    for start in range(0, radial, LANES):
+        body(slice(start, start + LANES))
 
 
 ALL = (-1, 0, 1)
@@ -245,20 +242,26 @@
     second_level(stencils.at[1], {row: line[row:row + 3] for row in range(height)}, radial, write)
 
 
-def close_kernel(own, end_0, end_1, out):
+def close_kernel(own, end_0, end_1, out, top, bottom, sent):
     height = own.shape[0]
+    last = height - 2
+    pairs = ((own.at[2:last], out.at[2:last]), (top, out.at[:2]), (bottom, out.at[last:]))
+    copies = [pltpu.make_async_copy(source, target, sent.at[i]) for i, (source, target) in enumerate(pairs)]
+    copies[0].start()
     _, odd = position("lat")
-    for row in range(2, height - 2):
-        out[row] = own[row]
     for place in range(2):
-        partner, outer = end_0[place], end_1[place]
-        out[place] = own[place] + either(odd, partner, outer)
-        out[height - 2 + place] = own[height - 2 + place] + either(odd, outer, partner)
+        top[place] = own[place] + either(odd, end_0[place], end_1[place])
+    copies[1].start()
+    for place in range(2):
+        bottom[place] = own[last + place] + either(odd, end_1[place], end_0[place])
+    copies[2].start()
+    for copy in copies:
+        copy.wait()
 
 
 def open_kernel(
     counts_in, offsets_in, residual_in, pixel_in, bins_in, latent_in, out, latent, to_partner, to_outer,
-    counts, offsets, residual, pixel, bins, arrived,
+    counts, offsets, residual, pixel, bins, table, arrived,
 ):
     pairs = (
         (counts_in, counts), (offsets_in, offsets), (residual_in, residual), (pixel_in, pixel), (bins_in, bins),
@@ -270,38 +273,37 @@
     for copy in copies[:-1]:
         copy.wait()
     height, _, radial = latent.shape
+    length = residual.shape[0]
+    table[pl.ds(0, length, stride=2), :] = residual[...]
+    table[pl.ds(1, length, stride=2), :] = (pixel[...] * radial + bins[...]).astype(jnp.float32)
+
     lane = lax.broadcasted_iota(jnp.int32, (SUBLANES, LANES), 1)
     row = lax.broadcasted_iota(jnp.int32, (SUBLANES, LANES), 0)
-    slot = row * LANES + lane
+    slot = lax.shift_right_logical(row, 1) * LANES + lane
     for owner in range(out.shape[0]):
         start = offsets[0, owner]
-        first = lax.shift_right_logical(start, 7)
+        first = lax.shift_right_logical(start, 7) * 2
         part = lax.bitwise_and(start, LANES - 1)
-        live = slot < counts[0, owner]
-
-        def window(values):
-            turned = pltpu.roll(values, lax.bitwise_and(LANES - part, LANES - 1), 1)
-            joined = jnp.where(lane < LANES - part, turned, pltpu.roll(turned, SUBLANES - 1, 0))
-            return jnp.where(live, joined, 0.0)
-
-        at = pl.ds(first, SUBLANES)
-        cell = (pixel[at, :] * radial + bins[at, :]).astype(jnp.float32)
-        out[owner] = jnp.where(row < RUNS, window(residual[at, :]), pltpu.roll(window(cell), RUNS, 0))
+        turn = lax.bitwise_and(LANES - part, LANES - 1)
+        here = pltpu.roll(table[pl.ds(first, SUBLANES), :], turn, 1)
+        after = pltpu.roll(table[pl.ds(first + 2, SUBLANES), :], turn, 1)
+        joined = jnp.where(lane < LANES - part, here, after)
+        out[owner] = jnp.where(slot < counts[0, owner], joined, 0.0)
 
     copies[-1].wait()
     pack_sides([latent[row] for row in range(height)], to_partner, to_outer)
 
 
-def behind_of(got, part, *, height, width, radial):
-    half = radial // 2
+def behind_of(got, part, cuts, *, height, width, radial):
+    span = radial // cuts
     pixels = height * width // 2
-    classes = 2 * pixels
+    classes = cuts * pixels
     shards, rows, _ = got.shape
     bf16 = jnp.bfloat16
     column = lax.broadcasted_iota(jnp.int32, (classes, LANES), 0).astype(jnp.float32).astype(bf16)
     places = [
         (lax.broadcasted_iota(jnp.int32, (LANES, LANES), 1) + (first + 1)).astype(jnp.float32).astype(bf16)
-        for first in range(0, half, LANES)
+        for first in range(0, span, LANES)
     ]
     zero = jnp.zeros((), bf16)
 
@@ -312,34 +314,36 @@
     cell = tiles.astype(jnp.int32)
     pixel = lax.shift_right_logical(cell, radial.bit_length() - 1)
     bins = lax.bitwise_and(cell, radial - 1)
-    upper = (bins >= half).astype(jnp.int32)
+    cut = lax.shift_right_logical(bins, span.bit_length() - 1)
     place = lax.bitwise_and(pixel + 2, width - 1)
-    own = upper * pixels + lax.shift_right_logical(pixel, 3) * 4 + lax.bitwise_and(place, 3)
+    own = cut * pixels + lax.shift_right_logical(pixel, 3) * 4 + lax.bitwise_and(place, 3)
     label = jnp.where(lax.shift_right_logical(place, 2) == part, own, classes).astype(jnp.float32)
-    lows = jnp.transpose((bins - upper * half + 1).astype(jnp.float32)).astype(bf16)
+    lows = jnp.transpose((lax.bitwise_and(bins, span - 1) + 1).astype(jnp.float32)).astype(bf16)
     coarse = tiles.astype(bf16).astype(jnp.float32)
     rest = tiles - coarse
 
-    total = jnp.zeros((2 * classes, half), jnp.float32)
+    total = jnp.zeros((2 * classes, span), jnp.float32)
     for first in range(0, shards, 2):
         left, right = [], []
         for run in range(2 * RUNS):
-            row = (first + run // RUNS) * rows + run % RUNS
-            mine = tall(label[row + RUNS:row + RUNS + 1]) == column
+            row = (first + run // RUNS) * rows + run % RUNS * 2
+            mine = tall(label[row + 1:row + 2]) == column
             left.append(jnp.concatenate([
                 jnp.where(mine, tall(coarse[row:row + 1]), zero), jnp.where(mine, tall(rest[row:row + 1]), zero)
             ], axis=0))
-            low = jnp.broadcast_to(lows[:, row + RUNS:row + RUNS + 1], (LANES, LANES))
+            low = jnp.broadcast_to(lows[:, row + 1:row + 2], (LANES, LANES))
             right.append(jnp.concatenate([jnp.maximum(low, place) for place in places], axis=1))
         total = total + jnp.dot(
             jnp.concatenate(left, axis=1), jnp.concatenate(right, axis=0), preferred_element_type=jnp.float32
         )
     both = (total[:classes] + total[classes:]) * bin_width
-    every = both[:, half - 1:] * (1.0 / half)
+    every = both[:, span - 1:] * (1.0 / span)
     lane = lax.broadcasted_iota(jnp.int32, both.shape, 1)
     at_least = jnp.where(lane == 0, every, pltpu.roll(both, 1, 1) - both + every)
-    near, far = at_least[:pixels], at_least[pixels:]
-    return jnp.concatenate([near + far[:, :1], far], axis=1)
+    ranges = [at_least[start:start + pixels] for start in range(0, classes, pixels)]
+    for k in reversed(range(cuts - 1)):
+        ranges[k] = ranges[k] + ranges[k + 1][:, :1]
+    return jnp.concatenate(ranges, axis=1)
 
 
 def column_rows(packed, part, height):
@@ -353,7 +357,7 @@
 
 def bin_sides_kernel(got, _, behind):
     height, width, radial = behind.shape
-    packed = behind_of(got, 0, height=height, width=width, radial=radial)
+    packed = behind_of(got, 0, 4, height=height, width=width, radial=radial)
     for row, values in enumerate(column_rows(packed, 0, height)):
         behind[row] = values
 
@@ -361,7 +365,7 @@
 def bin_rest_kernel(got, density, behind, upstream):
     height, width, radial = behind.shape
     sub = sublane(radial)
-    packed = behind_of(got, 1, height=height, width=width, radial=radial)
+    packed = behind_of(got, 1, 2, height=height, width=width, radial=radial)
     for row, values in enumerate(column_rows(packed, 1, height)):
         upstream[row] = density[row] * jnp.where((sub < 2) | (sub >= 6), behind[row], values)
 
@@ -412,6 +416,7 @@
         out_specs=(VMEM, VMEM, VMEM, VMEM),
         scratch_shapes=[pltpu.SMEM((1, shards), i32)] * 2
         + [pltpu.VMEM((slots // LANES, LANES), kind) for kind in (f32, i32, i32)]
+        + [pltpu.VMEM((2 * slots // LANES, LANES), f32)]
         + [pltpu.SemaphoreType.DMA((6,))],
         compiler_params=LIMIT,
         name="opening",
@@ -465,7 +470,15 @@
         back_own_kernel, "back_own", tile, [rows, moved, pltpu.VMEM(inner_rows, f32)],
         upstream, *beside[::-1], mirrored, latent, middle,
     )
-    return call(close_kernel, "close", tile, [], own, *above)
+    return pl.pallas_call(
+        close_kernel,
+        out_shape=tile,
+        in_specs=[VMEM] * 3,
+        out_specs=HBM,
+        scratch_shapes=[pltpu.VMEM((2, width, radial), f32)] * 2 + [pltpu.SemaphoreType.DMA((3,))],
+        compiler_params=LIMIT,
+        name="close",
+    )(own, *above)
 
 
 def solution(mesh):

time: 33.7 us -> 33.8 us (level)
  waiting for transfers between devices: 7.09 us -> 7.84 us
  Pallas kernels: 10.6 us -> 9.94 us
    pallas_call x8 -> x7, Pallas kernels: 8.83 us -> 7.5 us  [call(): pl.pallas_call(kernel, out_shape=outs, in_specs=[VMEM] * len(operands), o...]
    pallas_call x0 -> x1, Pallas kernels: none -> 0.67 us  [on_device(): pl.pallas_call(close_kernel, out_shape=tile, in_specs=[VMEM] * 3, out_spe...]
    ppermute x8, waiting for transfers between devices: 4.73 us -> 5.11 us  [swap(): lax.ppermute(values, axis, both_ways(pairs))]
    all_to_all x1, waiting for transfers between devices: 2.36 us -> 2.73 us  [on_device(): lax.all_to_all(packed, ('lat', 'lon'), split_axis=0, concat_axis=0, tiled...]
where the time goes in v13:
time: 33.8 us; the launch traced here: 33.6 us
  starting transfers between devices  15.3 us (45%)
  Pallas kernels  9.94 us (29%)
  waiting for transfers between devices  7.84 us (23%)
    ppermute x8, starting transfers between devices, swap(): lax.ppermute(values, axis, both_ways(pairs))  12.2 us
    pallas_call x7, Pallas kernels, call(): pl.pallas_call(kernel, out_shape=outs, in_specs=[VMEM] * len(operands), o...  7.5 us
    ppermute x8, waiting for transfers between devices, swap(): lax.ppermute(values, axis, both_ways(pairs))  5.11 us
    all_to_all x1, starting transfers between devices, on_device(): lax.all_to_all(packed, ('lat', 'lon'), split_axis=0, concat_axis=0, tiled...  3.09 us
    all_to_all x1, waiting for transfers between devices, on_device(): lax.all_to_all(packed, ('lat', 'lon'), split_axis=0, concat_axis=0, tiled...  2.73 us
    pallas_call x1, Pallas kernels, on_device(): pl.pallas_call(open_kernel, out_shape=(jax.ShapeDtypeStruct((shards, 2 *...  1.76 us
  transfers between devices with their start and end apart: 9, of which 3 were waited for; matrix products, arithmetic and copies ran while one was open for 1% of the time, Pallas kernels for 20%

profile of v13, /device:TPU:2, one launch (start us, length us, event | category | flops | bytes accessed | tf_op | source)
XLA Modules:
  0.0 33.6 jit_solution(13890508363694930110)
XLA Ops:
  0.0 1.8 %opening.1 = (f32[32,8,128]{2,1,0:T(8,128)}, f32[8,8,512]{2,1,0:T(8,128)S(1)}, f32[2,8,512]{2,1,0:T(8,128)S(1)}, f32[2,8,512]{2,1,0:T(8,128)S(1)}) custom-call(s32[1,32]{1,0:T(1,128)} %counts_in.1, s32[1,32]{1,0:T(1,128)} %offsets_in.1, f32[128,128]{1,0:T(8,128)} %bitcast.20, s32[128,128]{1,0:T(8,128)} %bitcast.21, s32[128,128]{1,0:T(8,128)} %bitcast.22, ...), custom_call_target="tpu_custom_call" | custom-call | tf_op jit(solution)/shard_map/opening/pallas_call | solution.py:412
  1.8 0.1 collective-permute-start
  1.9 3.7 %collective-permute-start.1 = (f32[2,8,512]{2,1,0:T(8,128)S(1)}, f32[2,8,512]{2,1,0:T(8,128)S(1)}, u32[]{:S(2)}, u32[]{:S(2)}) collective-permute-start(f32[2,8,512]{2,1,0:T(8,128)S(1)} %get-tuple-element.22), channel_id=1, source_target_pairs={{1,2},{3,4},{5,6},{7,0},{2,1},{4,3},{6,5},{0,7},{9,10},{11,12},{13... | collective-permute-start | bytes 98312 | tf_op jit(solution)/shard_map/ppermute | solution.py:390
  5.6 3.1 %all-to-all-start = ((f32[32,8,128]{2,1,0:T(8,128)}), f32[32,8,128]{2,1,0:T(8,128)S(1)}, u32[]{:S(2)}, u32[]{:S(2)}) async-start(f32[32,8,128]{2,1,0:T(8,128)} %get-tuple-element.19), calls=%async_computation | async-start | bytes 262144 | tf_op jit(solution)/shard_map/all_to_all | solution.py:427
  8.7 0.1 slice_bitcast_fusion.1
  8.8 0.0 collective-permute-done.side_0
  8.8 3.4 %collective-permute-start.2 = (f32[3,8,512]{2,1,0:T(8,128)S(1)}, f32[3,8,512]{2,1,0:T(8,128)S(1)}, u32[]{:S(2)}, u32[]{:S(2)}) collective-permute-start(f32[3,8,512]{2,1,0:T(8,128)S(1)} %get-tuple-element.23), channel_id=1, source_target_pairs={{8,16},{16,8},{9,17},{17,9},{10,18},{18,10},{11,19},{19,11},{12,20... | collective-permute-start | bytes 147464 | tf_op jit(solution)/shard_map/ppermute | solution.py:390
  12.2 0.1 collective-permute-start.3
  12.3 0.1 pad_bitcast_fusion
  12.4 0.7 %density_inside.1 = (f32[4,8,512]{2,1,0:T(8,128)S(1)}, f32[3,3,6,8,512]{4,3,2,1,0:T(8,128)S(1)}) custom-call(f32[8,8,512]{2,1,0:T(8,128)S(1)} %get-tuple-element.20.field.latent, f32[2,8,512]{2,1,0:T(8,128)S(1)} %collective-permute-done.side_0, f32[2,8,512]{2,1,0:T(8,128)S(1)} %collective-permute-done.1.side_1, f32[2,27,512]{2,1,0:T(8,128)S(1)} %copy.18.stencils), custom_call_target="tpu_custom_call" | custom-call | tf_op jit(solution)/shard_map/density_inside/pallas_call | solution.py:435
  13.1 2.7 %all-to-all-done.got = f32[32,8,128]{2,1,0:T(8,128)S(1)} async-done(((f32[32,8,128]{2,1,0:T(8,128)}), f32[32,8,128]{2,1,0:T(8,128)S(1)}, u32[]{:S(2)}, u32[]{:S(2)}) %all-to-all-start) | async-done | bytes 131104 | tf_op jit(solution)/shard_map/all_to_all | solution.py:427
  15.9 2.9 %bin_sides.1.behind = f32[8,8,512]{2,1,0:T(8,128)S(1)} custom-call(f32[32,8,128]{2,1,0:T(8,128)S(1)} %all-to-all-done.got, f32[4,8,512]{2,1,0:T(8,128)S(1)} %get-tuple-element.26._.inner), custom_call_target="tpu_custom_call" | custom-call | tf_op jit(solution)/shard_map/bin_sides/pallas_call | solution.py:435
  18.8 0.0 collective-permute-done.2.end_1
  18.8 0.5 %density_ends.1 = (f32[8,8,512]{2,1,0:T(8,128)S(1)}, f32[2,8,512]{2,1,0:T(8,128)S(1)}, f32[2,8,512]{2,1,0:T(8,128)S(1)}) custom-call(f32[8,8,512]{2,1,0:T(8,128)S(1)} %get-tuple-element.20.field.latent, f32[2,8,512]{2,1,0:T(8,128)S(1)} %collective-permute-done.side_0, f32[2,8,512]{2,1,0:T(8,128)S(1)} %collective-permute-done.1.side_1, ...), custom_call_target="tpu_custom_call" | custom-call | tf_op jit(solution)/shard_map/density_ends/pallas_call | solution.py:435
  19.4 0.8 %collective-permute-start.4 = (f32[2,8,512]{2,1,0:T(8,128)S(1)}, f32[2,8,512]{2,1,0:T(8,128)S(1)}, u32[]{:S(2)}, u32[]{:S(2)}) collective-permute-start(f32[2,8,512]{2,1,0:T(8,128)S(1)} %get-tuple-element.28), channel_id=1, source_target_pairs={{1,2},{3,4},{5,6},{7,0},{2,1},{4,3},{6,5},{0,7},{9,10},{11,12},{13... | collective-permute-start | bytes 98312 | tf_op jit(solution)/shard_map/ppermute | solution.py:390
  20.2 0.1 pad_maximum_fusion
  20.3 2.2 %bin_rest.1.field = f32[8,8,512]{2,1,0:T(8,128)S(1)} custom-call(f32[32,8,128]{2,1,0:T(8,128)S(1)} %all-to-all-done.got, f32[8,8,512]{2,1,0:T(8,128)S(1)} %get-tuple-element.27.density, f32[8,8,512]{2,1,0:T(8,128)S(1)} %bin_sides.1.behind), custom_call_target="tpu_custom_call" | custom-call | tf_op jit(solution)/shard_map/bin_rest/pallas_call | solution.py:435
  22.5 2.1 %collective-permute-done.4.side_1 = f32[2,8,512]{2,1,0:T(8,128)S(1)} collective-permute-done((f32[2,8,512]{2,1,0:T(8,128)S(1)}, f32[2,8,512]{2,1,0:T(8,128)S(1)}, u32[]{:S(2)}, u32[]{:S(2)}) %collective-permute-start.4) | collective-permute-done | bytes 32800 | tf_op jit(solution)/shard_map/ppermute | solution.py:390
  24.6 0.4 %back_reach.1 = (f32[2,8,512]{2,1,0:T(8,128)S(1)}, f32[2,8,512]{2,1,0:T(8,128)S(1)}, f32[3,3,4,8,512]{4,3,2,1,0:T(8,128)S(1)}) custom-call(f32[8,8,512]{2,1,0:T(8,128)S(1)} %bin_rest.1.field, f32[2,8,512]{2,1,0:T(8,128)S(1)} %collective-permute-done.4.side_1, f32[2,8,512]{2,1,0:T(8,128)S(1)} %collective-permute-done.5.side_0, f32[2,27,512]{2,1,0:T(8,128)S(1)} %rev.8.stencils), custom_call_target="tpu_custom_call" | custom-call | tf_op jit(solution)/shard_map/back_reach/pallas_call | solution.py:435
  25.0 1.3 %collective-permute-start.6 = (f32[2,8,512]{2,1,0:T(8,128)S(1)}, f32[2,8,512]{2,1,0:T(8,128)S(1)}, u32[]{:S(2)}, u32[]{:S(2)}) collective-permute-start(f32[2,8,512]{2,1,0:T(8,128)S(1)} %get-tuple-element.31), channel_id=1, source_target_pairs={{0,8},{16,24},{8,0},{24,16},{1,9},{17,25},{9,1},{25,17},{2,10},{18... | collective-permute-start | bytes 98312 | tf_op jit(solution)/shard_map/ppermute | solution.py:390
  26.2 2.9 %collective-permute-start.7 = (f32[2,8,512]{2,1,0:T(8,128)S(1)}, f32[2,8,512]{2,1,0:T(8,128)S(1)}, u32[]{:S(2)}, u32[]{:S(2)}) collective-permute-start(f32[2,8,512]{2,1,0:T(8,128)S(1)} %get-tuple-element.32), channel_id=1, source_target_pairs={{8,16},{16,8},{9,17},{17,9},{10,18},{18,10},{11,19},{19,11},{12,20... | collective-permute-start | bytes 98312 | tf_op jit(solution)/shard_map/ppermute | solution.py:390
  29.1 0.8 %back_own.1.own = f32[8,8,512]{2,1,0:T(8,128)S(1)} custom-call(f32[8,8,512]{2,1,0:T(8,128)S(1)} %bin_rest.1.field, f32[2,8,512]{2,1,0:T(8,128)S(1)} %collective-permute-done.4.side_1, f32[2,8,512]{2,1,0:T(8,128)S(1)} %collective-permute-done.5.side_0, f32[2,27,512]{2,1,0:T(8,128)S(1)} %rev.8.stencils, f32[8,8,512]{2,1,0:T(8,128)S(1)} %get-tuple-element.20.field.latent, ...), custom_call_target="tpu_custom_call" | custom-call | tf_op jit(solution)/shard_map/back_own/pallas_call | solution.py:435
  29.9 3.0 %collective-permute-done.7.end_1 = f32[2,8,512]{2,1,0:T(8,128)S(1)} collective-permute-done((f32[2,8,512]{2,1,0:T(8,128)S(1)}, f32[2,8,512]{2,1,0:T(8,128)S(1)}, u32[]{:S(2)}, u32[]{:S(2)}) %collective-permute-start.7) | collective-permute-done | bytes 32800 | tf_op jit(solution)/shard_map/ppermute | solution.py:390
  32.9 0.7 %close.1 = f32[8,8,512]{2,1,0:T(8,128)} custom-call(f32[8,8,512]{2,1,0:T(8,128)S(1)} %back_own.1.own, f32[2,8,512]{2,1,0:T(8,128)S(1)} %collective-permute-done.6.end_0, f32[2,8,512]{2,1,0:T(8,128)S(1)} %collective-permute-done.7.end_1), custom_call_target="tpu_custom_call" | custom-call | tf_op jit(solution)/shard_map/close/pallas_call | solution.py:473
  (13 shorter events, 0.1 us)
Async XLA Ops:
  1.8 7.0 %collective-permute-start = (f32[2,8,512]{2,1,0:T(8,128)S(1)}, f32[2,8,512]{2,1,0:T(8,128)S(1)}, u32[]{:S(2)}, u32[]{:S(2)}) collective-permute-start(f32[2,8,512]{2,1,0:T(8,128)S(1)} %get-tuple-element.21), channel_id=1, source_target_pairs={{0,1},{2,3},{4,5},{6,7},{1,0},{3,2},{5,4},{7,6},{8,9},{10,11},{12,... | collective-permute-start | bytes 98312 | tf_op jit(solution)/shard_map/ppermute | solution.py:390
  1.9 6.9 %collective-permute-start.1 = (f32[2,8,512]{2,1,0:T(8,128)S(1)}, f32[2,8,512]{2,1,0:T(8,128)S(1)}, u32[]{:S(2)}, u32[]{:S(2)}) collective-permute-start(f32[2,8,512]{2,1,0:T(8,128)S(1)} %get-tuple-element.22), channel_id=1, source_target_pairs={{1,2},{3,4},{5,6},{7,0},{2,1},{4,3},{6,5},{0,7},{9,10},{11,12},{13... | collective-permute-start | bytes 98312 | tf_op jit(solution)/shard_map/ppermute | solution.py:390
  5.6 3.1 %copy-start = (f32[2,27,512]{2,0,1:T(2,128)S(1)}, f32[2,27,512]{2,0,1:T(2,128)}, u32[]{:S(2)}) copy-start(f32[2,27,512]{2,0,1:T(2,128)} %param.13) | copy-start | bytes 331780
  5.6 10.3 %all-to-all-start = ((f32[32,8,128]{2,1,0:T(8,128)}), f32[32,8,128]{2,1,0:T(8,128)S(1)}, u32[]{:S(2)}, u32[]{:S(2)}) async-start(f32[32,8,128]{2,1,0:T(8,128)} %get-tuple-element.19), calls=%async_computation | async-start | bytes 262144 | tf_op jit(solution)/shard_map/all_to_all | solution.py:427
  8.8 10.0 %collective-permute-start.2 = (f32[3,8,512]{2,1,0:T(8,128)S(1)}, f32[3,8,512]{2,1,0:T(8,128)S(1)}, u32[]{:S(2)}, u32[]{:S(2)}) collective-permute-start(f32[3,8,512]{2,1,0:T(8,128)S(1)} %get-tuple-element.23), channel_id=1, source_target_pairs={{8,16},{16,8},{9,17},{17,9},{10,18},{18,10},{11,19},{19,11},{12,20... | collective-permute-start | bytes 147464 | tf_op jit(solution)/shard_map/ppermute | solution.py:390
  12.2 6.6 %collective-permute-start.3 = (f32[3,8,512]{2,1,0:T(8,128)S(1)}, f32[3,8,512]{2,1,0:T(8,128)S(1)}, u32[]{:S(2)}, u32[]{:S(2)}) collective-permute-start(f32[3,8,512]{2,1,0:T(8,128)S(1)} %get-tuple-element.24), channel_id=1, source_target_pairs={{0,8},{16,24},{8,0},{24,16},{1,9},{17,25},{9,1},{25,17},{2,10},{18... | collective-permute-start | bytes 147464 | tf_op jit(solution)/shard_map/ppermute | solution.py:390
  19.4 5.2 %collective-permute-start.4 = (f32[2,8,512]{2,1,0:T(8,128)S(1)}, f32[2,8,512]{2,1,0:T(8,128)S(1)}, u32[]{:S(2)}, u32[]{:S(2)}) collective-permute-start(f32[2,8,512]{2,1,0:T(8,128)S(1)} %get-tuple-element.28), channel_id=1, source_target_pairs={{1,2},{3,4},{5,6},{7,0},{2,1},{4,3},{6,5},{0,7},{9,10},{11,12},{13... | collective-permute-start | bytes 98312 | tf_op jit(solution)/shard_map/ppermute | solution.py:390
  20.2 4.4 %collective-permute-start.5 = (f32[2,8,512]{2,1,0:T(8,128)S(1)}, f32[2,8,512]{2,1,0:T(8,128)S(1)}, u32[]{:S(2)}, u32[]{:S(2)}) collective-permute-start(f32[2,8,512]{2,1,0:T(8,128)S(1)} %get-tuple-element.29), channel_id=1, source_target_pairs={{0,1},{2,3},{4,5},{6,7},{1,0},{3,2},{5,4},{7,6},{8,9},{10,11},{12,... | collective-permute-start | bytes 98312 | tf_op jit(solution)/shard_map/ppermute | solution.py:390
  25.0 5.0 %collective-permute-start.6 = (f32[2,8,512]{2,1,0:T(8,128)S(1)}, f32[2,8,512]{2,1,0:T(8,128)S(1)}, u32[]{:S(2)}, u32[]{:S(2)}) collective-permute-start(f32[2,8,512]{2,1,0:T(8,128)S(1)} %get-tuple-element.31), channel_id=1, source_target_pairs={{0,8},{16,24},{8,0},{24,16},{1,9},{17,25},{9,1},{25,17},{2,10},{18... | collective-permute-start | bytes 98312 | tf_op jit(solution)/shard_map/ppermute | solution.py:390
  26.2 6.7 %collective-permute-start.7 = (f32[2,8,512]{2,1,0:T(8,128)S(1)}, f32[2,8,512]{2,1,0:T(8,128)S(1)}, u32[]{:S(2)}, u32[]{:S(2)}) collective-permute-start(f32[2,8,512]{2,1,0:T(8,128)S(1)} %get-tuple-element.32), channel_id=1, source_target_pairs={{8,16},{16,8},{9,17},{17,9},{10,18},{18,10},{11,19},{19,11},{12,20... | collective-permute-start | bytes 98312 | tf_op jit(solution)/shard_map/ppermute | solution.py:390

commit v14 on v13

--- a/solution.py
+++ b/solution.py
@@ -294,7 +294,7 @@
     pack_sides([latent[row] for row in range(height)], to_partner, to_outer)
 
 
-def behind_of(got, part, cuts, *, height, width, radial):
+def behind_of(got, part, cuts, rows_of, *, height, width, radial):
     span = radial // cuts
     pixels = height * width // 2
     classes = cuts * pixels
@@ -307,8 +307,9 @@
     ]
     zero = jnp.zeros((), bf16)
 
-    def tall(row):
-        return jnp.concatenate([jnp.broadcast_to(row, (16, LANES)).astype(bf16)] * (classes // 16), axis=0)
+    def tall(kind, row):
+        line = jnp.broadcast_to(rows_of[kind, row:row + 1, :], (16, LANES))
+        return jnp.concatenate([line.astype(bf16)] * (classes // 16), axis=0)
 
     tiles = got[...].reshape(shards * rows, LANES)
     cell = tiles.astype(jnp.int32)
@@ -317,20 +318,19 @@
     cut = lax.shift_right_logical(bins, span.bit_length() - 1)
     place = lax.bitwise_and(pixel + 2, width - 1)
     own = cut * pixels + lax.shift_right_logical(pixel, 3) * 4 + lax.bitwise_and(place, 3)
-    label = jnp.where(lax.shift_right_logical(place, 2) == part, own, classes).astype(jnp.float32)
+    rows_of[0] = jnp.where(lax.shift_right_logical(place, 2) == part, own, classes).astype(jnp.float32)
     lows = jnp.transpose((lax.bitwise_and(bins, span - 1) + 1).astype(jnp.float32)).astype(bf16)
     coarse = tiles.astype(bf16).astype(jnp.float32)
-    rest = tiles - coarse
+    rows_of[1] = coarse
+    rows_of[2] = tiles - coarse
 
     total = jnp.zeros((2 * classes, span), jnp.float32)
     for first in range(0, shards, 2):
         left, right = [], []
         for run in range(2 * RUNS):
             row = (first + run // RUNS) * rows + run % RUNS * 2
-            mine = tall(label[row + 1:row + 2]) == column
-            left.append(jnp.concatenate([
-                jnp.where(mine, tall(coarse[row:row + 1]), zero), jnp.where(mine, tall(rest[row:row + 1]), zero)
-            ], axis=0))
+            mine = tall(0, row + 1) == column
+            left.append(jnp.concatenate([jnp.where(mine, tall(kind, row), zero) for kind in (1, 2)], axis=0))
             low = jnp.broadcast_to(lows[:, row + 1:row + 2], (LANES, LANES))
             right.append(jnp.concatenate([jnp.maximum(low, place) for place in places], axis=1))
         total = total + jnp.dot(
@@ -355,17 +355,17 @@
     return rows
 
 
-def bin_sides_kernel(got, _, behind):
+def bin_sides_kernel(got, _, behind, rows_of):
     height, width, radial = behind.shape
-    packed = behind_of(got, 0, 4, height=height, width=width, radial=radial)
+    packed = behind_of(got, 0, 2, rows_of, height=height, width=width, radial=radial)
     for row, values in enumerate(column_rows(packed, 0, height)):
         behind[row] = values
 
 
-def bin_rest_kernel(got, density, behind, upstream):
+def bin_rest_kernel(got, density, behind, upstream, rows_of):
     height, width, radial = behind.shape
     sub = sublane(radial)
-    packed = behind_of(got, 1, 2, height=height, width=width, radial=radial)
+    packed = behind_of(got, 1, 2, rows_of, height=height, width=width, radial=radial)
     for row, values in enumerate(column_rows(packed, 1, height)):
         upstream[row] = density[row] * jnp.where((sub < 2) | (sub >= 6), behind[row], values)
 
@@ -429,6 +429,7 @@
     rows = pltpu.VMEM((height, 2 * width, radial), f32)
     moved = pltpu.VMEM((2, height, 2 * width, radial), f32)
     edge = (3, 3, 4, width, radial)
+    star_rows = pltpu.VMEM((3, shards * 2 * RUNS, LANES), f32)
     inner_rows = (3, 3, height - 2, width, radial)
 
     def call(kernel, name, outs, scratch, *operands):
@@ -452,12 +453,12 @@
         density_inside_kernel, "density_inside", (shape(height - 4, width, radial), shape(*inner_rows)), [rows, moved],
         latent, *beside, stencils,
     )
-    behind = call(bin_sides_kernel, "bin_sides", tile, [], got, inner)
+    behind = call(bin_sides_kernel, "bin_sides", tile, [star_rows], got, inner)
     density, *to_sides = call(
         density_ends_kernel, "density_ends", (tile, sides, sides), [pltpu.VMEM(edge, f32), rows, moved],
         latent, *beside, *above[::-1], stencils, middle, inner, behind,
     )
-    upstream = call(bin_rest_kernel, "bin_rest", tile, [], got, density, behind)
+    upstream = call(bin_rest_kernel, "bin_rest", tile, [star_rows], got, density, behind)
 
     mirrored = mirror(stencils)[::-1]
     beside = swap(*to_sides, "lon", True, outer_first=True)

time: 33.8 us -> 33.1 us (0.979)
  Pallas kernels: 9.94 us -> 9.2 us
    pallas_call x7, Pallas kernels: 7.5 us -> 6.76 us  [call(): pl.pallas_call(kernel, out_shape=outs, in_specs=[VMEM] * len(operands), o...]
  transfers between devices with their start and end apart: 9 -> 9, of which waited for: 3 -> 3; matrix products, arithmetic and copies ran while one was open for 1% -> 1% of each run, Pallas kernels for 20% -> 18%
where the time goes in v14:
time: 33.1 us; the launch traced here: 32.8 us
  starting transfers between devices  15.3 us (46%)
  Pallas kernels  9.2 us (28%)
  waiting for transfers between devices  7.83 us (24%)
    ppermute x8, starting transfers between devices, swap(): lax.ppermute(values, axis, both_ways(pairs))  12.2 us
    pallas_call x7, Pallas kernels, call(): pl.pallas_call(kernel, out_shape=outs, in_specs=[VMEM] * len(operands), o...  6.76 us
    ppermute x8, waiting for transfers between devices, swap(): lax.ppermute(values, axis, both_ways(pairs))  5.1 us
    all_to_all x1, starting transfers between devices, on_device(): lax.all_to_all(packed, ('lat', 'lon'), split_axis=0, concat_axis=0, tiled...  3.09 us
    all_to_all x1, waiting for transfers between devices, on_device(): lax.all_to_all(packed, ('lat', 'lon'), split_axis=0, concat_axis=0, tiled...  2.73 us
    pallas_call x1, Pallas kernels, on_device(): pl.pallas_call(open_kernel, out_shape=(jax.ShapeDtypeStruct((shards, 2 *...  1.76 us
    pallas_call x1, Pallas kernels, on_device(): pl.pallas_call(close_kernel, out_shape=tile, in_specs=[VMEM] * 3, out_spe...  0.67 us
  transfers between devices with their start and end apart: 9, of which 3 were waited for; matrix products, arithmetic and copies ran while one was open for 1% of the time, Pallas kernels for 18%

profile of v14, /device:TPU:2, one launch (start us, length us, event | category | flops | bytes accessed | tf_op | source)
XLA Modules:
  0.0 32.8 jit_solution(13804822922097067301)
XLA Ops:
  0.0 1.8 %opening.1 = (f32[32,8,128]{2,1,0:T(8,128)}, f32[8,8,512]{2,1,0:T(8,128)S(1)}, f32[2,8,512]{2,1,0:T(8,128)S(1)}, f32[2,8,512]{2,1,0:T(8,128)S(1)}) custom-call(s32[1,32]{1,0:T(1,128)} %counts_in.1, s32[1,32]{1,0:T(1,128)} %offsets_in.1, f32[128,128]{1,0:T(8,128)} %bitcast.20, s32[128,128]{1,0:T(8,128)} %bitcast.21, s32[128,128]{1,0:T(8,128)} %bitcast.22, ...), custom_call_target="tpu_custom_call" | custom-call | tf_op jit(solution)/shard_map/opening/pallas_call | solution.py:412
  1.8 0.1 collective-permute-start
  1.9 3.7 %collective-permute-start.1 = (f32[2,8,512]{2,1,0:T(8,128)S(1)}, f32[2,8,512]{2,1,0:T(8,128)S(1)}, u32[]{:S(2)}, u32[]{:S(2)}) collective-permute-start(f32[2,8,512]{2,1,0:T(8,128)S(1)} %get-tuple-element.22), channel_id=1, source_target_pairs={{1,2},{3,4},{5,6},{7,0},{2,1},{4,3},{6,5},{0,7},{9,10},{11,12},{13... | collective-permute-start | bytes 98312 | tf_op jit(solution)/shard_map/ppermute | solution.py:390
  5.6 3.1 %all-to-all-start = ((f32[32,8,128]{2,1,0:T(8,128)}), f32[32,8,128]{2,1,0:T(8,128)S(1)}, u32[]{:S(2)}, u32[]{:S(2)}) async-start(f32[32,8,128]{2,1,0:T(8,128)} %get-tuple-element.19), calls=%async_computation | async-start | bytes 262144 | tf_op jit(solution)/shard_map/all_to_all | solution.py:427
  8.7 0.1 slice_bitcast_fusion.1
  8.8 0.0 collective-permute-done.side_0
  8.8 3.4 %collective-permute-start.2 = (f32[3,8,512]{2,1,0:T(8,128)S(1)}, f32[3,8,512]{2,1,0:T(8,128)S(1)}, u32[]{:S(2)}, u32[]{:S(2)}) collective-permute-start(f32[3,8,512]{2,1,0:T(8,128)S(1)} %get-tuple-element.23), channel_id=1, source_target_pairs={{8,16},{16,8},{9,17},{17,9},{10,18},{18,10},{11,19},{19,11},{12,20... | collective-permute-start | bytes 147464 | tf_op jit(solution)/shard_map/ppermute | solution.py:390
  12.2 0.1 collective-permute-start.3
  12.3 0.1 pad_bitcast_fusion
  12.4 0.7 %density_inside.1 = (f32[4,8,512]{2,1,0:T(8,128)S(1)}, f32[3,3,6,8,512]{4,3,2,1,0:T(8,128)S(1)}) custom-call(f32[8,8,512]{2,1,0:T(8,128)S(1)} %get-tuple-element.20.field.latent, f32[2,8,512]{2,1,0:T(8,128)S(1)} %collective-permute-done.side_0, f32[2,8,512]{2,1,0:T(8,128)S(1)} %collective-permute-done.1.side_1, f32[2,27,512]{2,1,0:T(8,128)S(1)} %copy.18.stencils), custom_call_target="tpu_custom_call" | custom-call | tf_op jit(solution)/shard_map/density_inside/pallas_call | solution.py:436
  13.1 2.7 %all-to-all-done.got = f32[32,8,128]{2,1,0:T(8,128)S(1)} async-done(((f32[32,8,128]{2,1,0:T(8,128)}), f32[32,8,128]{2,1,0:T(8,128)S(1)}, u32[]{:S(2)}, u32[]{:S(2)}) %all-to-all-start) | async-done | bytes 131104 | tf_op jit(solution)/shard_map/all_to_all | solution.py:427
  15.9 2.2 %bin_sides.1.behind = f32[8,8,512]{2,1,0:T(8,128)S(1)} custom-call(f32[32,8,128]{2,1,0:T(8,128)S(1)} %all-to-all-done.got, f32[4,8,512]{2,1,0:T(8,128)S(1)} %get-tuple-element.26._.inner), custom_call_target="tpu_custom_call" | custom-call | tf_op jit(solution)/shard_map/bin_sides/pallas_call | solution.py:436
  18.0 0.0 collective-permute-done.2.end_1
  18.1 0.5 %density_ends.1 = (f32[8,8,512]{2,1,0:T(8,128)S(1)}, f32[2,8,512]{2,1,0:T(8,128)S(1)}, f32[2,8,512]{2,1,0:T(8,128)S(1)}) custom-call(f32[8,8,512]{2,1,0:T(8,128)S(1)} %get-tuple-element.20.field.latent, f32[2,8,512]{2,1,0:T(8,128)S(1)} %collective-permute-done.side_0, f32[2,8,512]{2,1,0:T(8,128)S(1)} %collective-permute-done.1.side_1, ...), custom_call_target="tpu_custom_call" | custom-call | tf_op jit(solution)/shard_map/density_ends/pallas_call | solution.py:436
  18.6 0.8 %collective-permute-start.4 = (f32[2,8,512]{2,1,0:T(8,128)S(1)}, f32[2,8,512]{2,1,0:T(8,128)S(1)}, u32[]{:S(2)}, u32[]{:S(2)}) collective-permute-start(f32[2,8,512]{2,1,0:T(8,128)S(1)} %get-tuple-element.28), channel_id=1, source_target_pairs={{1,2},{3,4},{5,6},{7,0},{2,1},{4,3},{6,5},{0,7},{9,10},{11,12},{13... | collective-permute-start | bytes 98312 | tf_op jit(solution)/shard_map/ppermute | solution.py:390
  19.5 0.1 pad_maximum_fusion
  19.6 2.2 %bin_rest.1.field = f32[8,8,512]{2,1,0:T(8,128)S(1)} custom-call(f32[32,8,128]{2,1,0:T(8,128)S(1)} %all-to-all-done.got, f32[8,8,512]{2,1,0:T(8,128)S(1)} %get-tuple-element.27.density, f32[8,8,512]{2,1,0:T(8,128)S(1)} %bin_sides.1.behind), custom_call_target="tpu_custom_call" | custom-call | tf_op jit(solution)/shard_map/bin_rest/pallas_call | solution.py:436
  21.7 2.1 %collective-permute-done.4.side_1 = f32[2,8,512]{2,1,0:T(8,128)S(1)} collective-permute-done((f32[2,8,512]{2,1,0:T(8,128)S(1)}, f32[2,8,512]{2,1,0:T(8,128)S(1)}, u32[]{:S(2)}, u32[]{:S(2)}) %collective-permute-start.4) | collective-permute-done | bytes 32800 | tf_op jit(solution)/shard_map/ppermute | solution.py:390
  23.8 0.4 %back_reach.1 = (f32[2,8,512]{2,1,0:T(8,128)S(1)}, f32[2,8,512]{2,1,0:T(8,128)S(1)}, f32[3,3,4,8,512]{4,3,2,1,0:T(8,128)S(1)}) custom-call(f32[8,8,512]{2,1,0:T(8,128)S(1)} %bin_rest.1.field, f32[2,8,512]{2,1,0:T(8,128)S(1)} %collective-permute-done.4.side_1, f32[2,8,512]{2,1,0:T(8,128)S(1)} %collective-permute-done.5.side_0, f32[2,27,512]{2,1,0:T(8,128)S(1)} %rev.8.stencils), custom_call_target="tpu_custom_call" | custom-call | tf_op jit(solution)/shard_map/back_reach/pallas_call | solution.py:436
  24.2 1.3 %collective-permute-start.6 = (f32[2,8,512]{2,1,0:T(8,128)S(1)}, f32[2,8,512]{2,1,0:T(8,128)S(1)}, u32[]{:S(2)}, u32[]{:S(2)}) collective-permute-start(f32[2,8,512]{2,1,0:T(8,128)S(1)} %get-tuple-element.31), channel_id=1, source_target_pairs={{0,8},{16,24},{8,0},{24,16},{1,9},{17,25},{9,1},{25,17},{2,10},{18... | collective-permute-start | bytes 98312 | tf_op jit(solution)/shard_map/ppermute | solution.py:390
  25.5 2.9 %collective-permute-start.7 = (f32[2,8,512]{2,1,0:T(8,128)S(1)}, f32[2,8,512]{2,1,0:T(8,128)S(1)}, u32[]{:S(2)}, u32[]{:S(2)}) collective-permute-start(f32[2,8,512]{2,1,0:T(8,128)S(1)} %get-tuple-element.32), channel_id=1, source_target_pairs={{8,16},{16,8},{9,17},{17,9},{10,18},{18,10},{11,19},{19,11},{12,20... | collective-permute-start | bytes 98312 | tf_op jit(solution)/shard_map/ppermute | solution.py:390
  28.3 0.8 %back_own.1.own = f32[8,8,512]{2,1,0:T(8,128)S(1)} custom-call(f32[8,8,512]{2,1,0:T(8,128)S(1)} %bin_rest.1.field, f32[2,8,512]{2,1,0:T(8,128)S(1)} %collective-permute-done.4.side_1, f32[2,8,512]{2,1,0:T(8,128)S(1)} %collective-permute-done.5.side_0, f32[2,27,512]{2,1,0:T(8,128)S(1)} %rev.8.stencils, f32[8,8,512]{2,1,0:T(8,128)S(1)} %get-tuple-element.20.field.latent, ...), custom_call_target="tpu_custom_call" | custom-call | tf_op jit(solution)/shard_map/back_own/pallas_call | solution.py:436
  29.2 3.0 %collective-permute-done.7.end_1 = f32[2,8,512]{2,1,0:T(8,128)S(1)} collective-permute-done((f32[2,8,512]{2,1,0:T(8,128)S(1)}, f32[2,8,512]{2,1,0:T(8,128)S(1)}, u32[]{:S(2)}, u32[]{:S(2)}) %collective-permute-start.7) | collective-permute-done | bytes 32800 | tf_op jit(solution)/shard_map/ppermute | solution.py:390
  32.2 0.7 %close.1 = f32[8,8,512]{2,1,0:T(8,128)} custom-call(f32[8,8,512]{2,1,0:T(8,128)S(1)} %back_own.1.own, f32[2,8,512]{2,1,0:T(8,128)S(1)} %collective-permute-done.6.end_0, f32[2,8,512]{2,1,0:T(8,128)S(1)} %collective-permute-done.7.end_1), custom_call_target="tpu_custom_call" | custom-call | tf_op jit(solution)/shard_map/close/pallas_call | solution.py:474
  (13 shorter events, 0.1 us)
Async XLA Ops:
  1.8 7.0 %collective-permute-start = (f32[2,8,512]{2,1,0:T(8,128)S(1)}, f32[2,8,512]{2,1,0:T(8,128)S(1)}, u32[]{:S(2)}, u32[]{:S(2)}) collective-permute-start(f32[2,8,512]{2,1,0:T(8,128)S(1)} %get-tuple-element.21), channel_id=1, source_target_pairs={{0,1},{2,3},{4,5},{6,7},{1,0},{3,2},{5,4},{7,6},{8,9},{10,11},{12,... | collective-permute-start | bytes 98312 | tf_op jit(solution)/shard_map/ppermute | solution.py:390
  1.9 6.9 %collective-permute-start.1 = (f32[2,8,512]{2,1,0:T(8,128)S(1)}, f32[2,8,512]{2,1,0:T(8,128)S(1)}, u32[]{:S(2)}, u32[]{:S(2)}) collective-permute-start(f32[2,8,512]{2,1,0:T(8,128)S(1)} %get-tuple-element.22), channel_id=1, source_target_pairs={{1,2},{3,4},{5,6},{7,0},{2,1},{4,3},{6,5},{0,7},{9,10},{11,12},{13... | collective-permute-start | bytes 98312 | tf_op jit(solution)/shard_map/ppermute | solution.py:390
  5.6 3.1 %copy-start = (f32[2,27,512]{2,0,1:T(2,128)S(1)}, f32[2,27,512]{2,0,1:T(2,128)}, u32[]{:S(2)}) copy-start(f32[2,27,512]{2,0,1:T(2,128)} %param.13) | copy-start | bytes 331780
  5.6 10.3 %all-to-all-start = ((f32[32,8,128]{2,1,0:T(8,128)}), f32[32,8,128]{2,1,0:T(8,128)S(1)}, u32[]{:S(2)}, u32[]{:S(2)}) async-start(f32[32,8,128]{2,1,0:T(8,128)} %get-tuple-element.19), calls=%async_computation | async-start | bytes 262144 | tf_op jit(solution)/shard_map/all_to_all | solution.py:427
  8.8 9.2 %collective-permute-start.2 = (f32[3,8,512]{2,1,0:T(8,128)S(1)}, f32[3,8,512]{2,1,0:T(8,128)S(1)}, u32[]{:S(2)}, u32[]{:S(2)}) collective-permute-start(f32[3,8,512]{2,1,0:T(8,128)S(1)} %get-tuple-element.23), channel_id=1, source_target_pairs={{8,16},{16,8},{9,17},{17,9},{10,18},{18,10},{11,19},{19,11},{12,20... | collective-permute-start | bytes 147464 | tf_op jit(solution)/shard_map/ppermute | solution.py:390
  12.2 5.8 %collective-permute-start.3 = (f32[3,8,512]{2,1,0:T(8,128)S(1)}, f32[3,8,512]{2,1,0:T(8,128)S(1)}, u32[]{:S(2)}, u32[]{:S(2)}) collective-permute-start(f32[3,8,512]{2,1,0:T(8,128)S(1)} %get-tuple-element.24), channel_id=1, source_target_pairs={{0,8},{16,24},{8,0},{24,16},{1,9},{17,25},{9,1},{25,17},{2,10},{18... | collective-permute-start | bytes 147464 | tf_op jit(solution)/shard_map/ppermute | solution.py:390
  18.6 5.2 %collective-permute-start.4 = (f32[2,8,512]{2,1,0:T(8,128)S(1)}, f32[2,8,512]{2,1,0:T(8,128)S(1)}, u32[]{:S(2)}, u32[]{:S(2)}) collective-permute-start(f32[2,8,512]{2,1,0:T(8,128)S(1)} %get-tuple-element.28), channel_id=1, source_target_pairs={{1,2},{3,4},{5,6},{7,0},{2,1},{4,3},{6,5},{0,7},{9,10},{11,12},{13... | collective-permute-start | bytes 98312 | tf_op jit(solution)/shard_map/ppermute | solution.py:390
  19.5 4.4 %collective-permute-start.5 = (f32[2,8,512]{2,1,0:T(8,128)S(1)}, f32[2,8,512]{2,1,0:T(8,128)S(1)}, u32[]{:S(2)}, u32[]{:S(2)}) collective-permute-start(f32[2,8,512]{2,1,0:T(8,128)S(1)} %get-tuple-element.29), channel_id=1, source_target_pairs={{0,1},{2,3},{4,5},{6,7},{1,0},{3,2},{5,4},{7,6},{8,9},{10,11},{12,... | collective-permute-start | bytes 98312 | tf_op jit(solution)/shard_map/ppermute | solution.py:390
  24.2 5.0 %collective-permute-start.6 = (f32[2,8,512]{2,1,0:T(8,128)S(1)}, f32[2,8,512]{2,1,0:T(8,128)S(1)}, u32[]{:S(2)}, u32[]{:S(2)}) collective-permute-start(f32[2,8,512]{2,1,0:T(8,128)S(1)} %get-tuple-element.31), channel_id=1, source_target_pairs={{0,8},{16,24},{8,0},{24,16},{1,9},{17,25},{9,1},{25,17},{2,10},{18... | collective-permute-start | bytes 98312 | tf_op jit(solution)/shard_map/ppermute | solution.py:390
  25.5 6.7 %collective-permute-start.7 = (f32[2,8,512]{2,1,0:T(8,128)S(1)}, f32[2,8,512]{2,1,0:T(8,128)S(1)}, u32[]{:S(2)}, u32[]{:S(2)}) collective-permute-start(f32[2,8,512]{2,1,0:T(8,128)S(1)} %get-tuple-element.32), channel_id=1, source_target_pairs={{8,16},{16,8},{9,17},{17,9},{10,18},{18,10},{11,19},{19,11},{12,20... | collective-permute-start | bytes 98312 | tf_op jit(solution)/shard_map/ppermute | solution.py:390

commit v15 on v13

--- a/solution.py
+++ b/solution.py
@@ -294,7 +294,7 @@
     pack_sides([latent[row] for row in range(height)], to_partner, to_outer)
 
 
-def behind_of(got, part, cuts, *, height, width, radial):
+def behind_of(got, part, cuts, rows_of, lows, *, height, width, radial):
     span = radial // cuts
     pixels = height * width // 2
     classes = cuts * pixels
@@ -307,35 +307,39 @@
     ]
     zero = jnp.zeros((), bf16)
 
-    def tall(row):
-        return jnp.concatenate([jnp.broadcast_to(row, (16, LANES)).astype(bf16)] * (classes // 16), axis=0)
-
-    tiles = got[...].reshape(shards * rows, LANES)
-    cell = tiles.astype(jnp.int32)
-    pixel = lax.shift_right_logical(cell, radial.bit_length() - 1)
-    bins = lax.bitwise_and(cell, radial - 1)
-    cut = lax.shift_right_logical(bins, span.bit_length() - 1)
-    place = lax.bitwise_and(pixel + 2, width - 1)
-    own = cut * pixels + lax.shift_right_logical(pixel, 3) * 4 + lax.bitwise_and(place, 3)
-    label = jnp.where(lax.shift_right_logical(place, 2) == part, own, classes).astype(jnp.float32)
-    lows = jnp.transpose((lax.bitwise_and(bins, span - 1) + 1).astype(jnp.float32)).astype(bf16)
-    coarse = tiles.astype(bf16).astype(jnp.float32)
-    rest = tiles - coarse
-
-    total = jnp.zeros((2 * classes, span), jnp.float32)
-    for first in range(0, shards, 2):
-        left, right = [], []
-        for run in range(2 * RUNS):
-            row = (first + run // RUNS) * rows + run % RUNS * 2
-            mine = tall(label[row + 1:row + 2]) == column
-            left.append(jnp.concatenate([
-                jnp.where(mine, tall(coarse[row:row + 1]), zero), jnp.where(mine, tall(rest[row:row + 1]), zero)
-            ], axis=0))
-            low = jnp.broadcast_to(lows[:, row + 1:row + 2], (LANES, LANES))
-            right.append(jnp.concatenate([jnp.maximum(low, place) for place in places], axis=1))
-        total = total + jnp.dot(
-            jnp.concatenate(left, axis=1), jnp.concatenate(right, axis=0), preferred_element_type=jnp.float32
-        )
+    turns = lows.shape[0]
+    for turn in range(turns):
+        tiles = got[turn * LANES // rows:(turn + 1) * LANES // rows].reshape(LANES, LANES)
+        cell = tiles.astype(jnp.int32)
+        pixel = lax.shift_right_logical(cell, radial.bit_length() - 1)
+        bins = lax.bitwise_and(cell, radial - 1)
+        cut = lax.shift_right_logical(bins, span.bit_length() - 1)
+        place = lax.bitwise_and(pixel + 2, width - 1)
+        own = cut * pixels + lax.shift_right_logical(pixel, 3) * 4 + lax.bitwise_and(place, 3)
+        coarse = tiles.astype(bf16).astype(jnp.float32)
+        rows_of[turn, 0] = jnp.where(lax.shift_right_logical(place, 2) == part, own, classes).astype(jnp.float32)
+        rows_of[turn, 1] = coarse
+        rows_of[turn, 2] = tiles - coarse
+        lows[turn] = jnp.transpose((lax.bitwise_and(bins, span - 1) + 1).astype(jnp.float32)).astype(bf16)
+
+    def step(turn, total):
+        def tall(kind, row):
+            line = jnp.broadcast_to(rows_of[turn, kind, row:row + 1, :], (16, LANES))
+            return jnp.concatenate([line.astype(bf16)] * (classes // 16), axis=0)
+
+        for first in range(0, LANES, 2 * rows):
+            left, right = [], []
+            for row in range(first, first + 2 * rows, 2):
+                mine = tall(0, row + 1) == column
+                left.append(jnp.concatenate([jnp.where(mine, tall(kind, row), zero) for kind in (1, 2)], axis=0))
+                low = jnp.broadcast_to(lows[turn, :, row + 1:row + 2], (LANES, LANES))
+                right.append(jnp.concatenate([jnp.maximum(low, place) for place in places], axis=1))
+            total = total + jnp.dot(
+                jnp.concatenate(left, axis=1), jnp.concatenate(right, axis=0), preferred_element_type=jnp.float32
+            )
+        return total
+
+    total = lax.fori_loop(0, turns, step, jnp.zeros((2 * classes, span), jnp.float32))
     both = (total[:classes] + total[classes:]) * bin_width
     every = both[:, span - 1:] * (1.0 / span)
     lane = lax.broadcasted_iota(jnp.int32, both.shape, 1)
@@ -355,17 +359,17 @@
     return rows
 
 
-def bin_sides_kernel(got, _, behind):
+def bin_sides_kernel(got, _, behind, rows_of, lows):
     height, width, radial = behind.shape
-    packed = behind_of(got, 0, 4, height=height, width=width, radial=radial)
+    packed = behind_of(got, 0, 2, rows_of, lows, height=height, width=width, radial=radial)
     for row, values in enumerate(column_rows(packed, 0, height)):
         behind[row] = values
 
 
-def bin_rest_kernel(got, density, behind, upstream):
+def bin_rest_kernel(got, density, behind, upstream, rows_of, lows):
     height, width, radial = behind.shape
     sub = sublane(radial)
-    packed = behind_of(got, 1, 2, height=height, width=width, radial=radial)
+    packed = behind_of(got, 1, 2, rows_of, lows, height=height, width=width, radial=radial)
     for row, values in enumerate(column_rows(packed, 1, height)):
         upstream[row] = density[row] * jnp.where((sub < 2) | (sub >= 6), behind[row], values)
 
@@ -429,6 +433,8 @@
     rows = pltpu.VMEM((height, 2 * width, radial), f32)
     moved = pltpu.VMEM((2, height, 2 * width, radial), f32)
     edge = (3, 3, 4, width, radial)
+    turns = shards * 2 * RUNS // LANES
+    star_rows = [pltpu.VMEM((turns, 3, LANES, LANES), f32), pltpu.VMEM((turns, LANES, LANES), jnp.bfloat16)]
     inner_rows = (3, 3, height - 2, width, radial)
 
     def call(kernel, name, outs, scratch, *operands):
@@ -452,12 +458,12 @@
         density_inside_kernel, "density_inside", (shape(height - 4, width, radial), shape(*inner_rows)), [rows, moved],
         latent, *beside, stencils,
     )
-    behind = call(bin_sides_kernel, "bin_sides", tile, [], got, inner)
+    behind = call(bin_sides_kernel, "bin_sides", tile, star_rows, got, inner)
     density, *to_sides = call(
         density_ends_kernel, "density_ends", (tile, sides, sides), [pltpu.VMEM(edge, f32), rows, moved],
         latent, *beside, *above[::-1], stencils, middle, inner, behind,
     )
-    upstream = call(bin_rest_kernel, "bin_rest", tile, [], got, density, behind)
+    upstream = call(bin_rest_kernel, "bin_rest", tile, star_rows, got, density, behind)
 
     mirrored = mirror(stencils)[::-1]
     beside = swap(*to_sides, "lon", True, outer_first=True)

time: 33.8 us -> 34 us (level)
  Pallas kernels: 9.94 us -> 11.1 us
  waiting for transfers between devices: 7.84 us -> 6.86 us
    pallas_call x7, Pallas kernels: 7.5 us -> 8.69 us  [call(): pl.pallas_call(kernel, out_shape=outs, in_specs=[VMEM] * len(operands), o...]
    ppermute x8, waiting for transfers between devices: 5.11 us -> 4.13 us  [swap(): lax.ppermute(values, axis, both_ways(pairs))]
  transfers between devices with their start and end apart: 9 -> 9, of which waited for: 3 -> 3; matrix products, arithmetic and copies ran while one was open for 1% -> 1% of each run, Pallas kernels for 20% -> 23%
where the time goes in v15:
time: 34 us; the launch traced here: 33.8 us
  starting transfers between devices  15.3 us (45%)
  Pallas kernels  11.1 us (33%)
  waiting for transfers between devices  6.86 us (20%)
    ppermute x8, starting transfers between devices, swap(): lax.ppermute(values, axis, both_ways(pairs))  12.2 us
    pallas_call x7, Pallas kernels, call(): pl.pallas_call(kernel, out_shape=outs, in_specs=[VMEM] * len(operands), o...  8.69 us
    ppermute x8, waiting for transfers between devices, swap(): lax.ppermute(values, axis, both_ways(pairs))  4.13 us
    all_to_all x1, starting transfers between devices, on_device(): lax.all_to_all(packed, ('lat', 'lon'), split_axis=0, concat_axis=0, tiled...  3.09 us
    all_to_all x1, waiting for transfers between devices, on_device(): lax.all_to_all(packed, ('lat', 'lon'), split_axis=0, concat_axis=0, tiled...  2.73 us
    pallas_call x1, Pallas kernels, on_device(): pl.pallas_call(open_kernel, out_shape=(jax.ShapeDtypeStruct((shards, 2 *...  1.76 us
  transfers between devices with their start and end apart: 9, of which 3 were waited for; matrix products, arithmetic and copies ran while one was open for 1% of the time, Pallas kernels for 23%

profile of v15, /device:TPU:2, one launch (start us, length us, event | category | flops | bytes accessed | tf_op | source)
XLA Modules:
  0.0 33.8 jit_solution(5567247776544467562)
XLA Ops:
  0.0 1.8 %opening.1 = (f32[32,8,128]{2,1,0:T(8,128)}, f32[8,8,512]{2,1,0:T(8,128)S(1)}, f32[2,8,512]{2,1,0:T(8,128)S(1)}, f32[2,8,512]{2,1,0:T(8,128)S(1)}) custom-call(s32[1,32]{1,0:T(1,128)} %counts_in.1, s32[1,32]{1,0:T(1,128)} %offsets_in.1, f32[128,128]{1,0:T(8,128)} %bitcast.20, s32[128,128]{1,0:T(8,128)} %bitcast.21, s32[128,128]{1,0:T(8,128)} %bitcast.22, ...), custom_call_target="tpu_custom_call" | custom-call | tf_op jit(solution)/shard_map/opening/pallas_call | solution.py:416
  1.8 0.1 collective-permute-start
  1.9 3.7 %collective-permute-start.1 = (f32[2,8,512]{2,1,0:T(8,128)S(1)}, f32[2,8,512]{2,1,0:T(8,128)S(1)}, u32[]{:S(2)}, u32[]{:S(2)}) collective-permute-start(f32[2,8,512]{2,1,0:T(8,128)S(1)} %get-tuple-element.22), channel_id=1, source_target_pairs={{1,2},{3,4},{5,6},{7,0},{2,1},{4,3},{6,5},{0,7},{9,10},{11,12},{13... | collective-permute-start | bytes 98312 | tf_op jit(solution)/shard_map/ppermute | solution.py:394
  5.6 3.1 %all-to-all-start = ((f32[32,8,128]{2,1,0:T(8,128)}), f32[32,8,128]{2,1,0:T(8,128)S(1)}, u32[]{:S(2)}, u32[]{:S(2)}) async-start(f32[32,8,128]{2,1,0:T(8,128)} %get-tuple-element.19), calls=%async_computation | async-start | bytes 262144 | tf_op jit(solution)/shard_map/all_to_all | solution.py:431
  8.7 0.1 slice_bitcast_fusion.1
  8.8 0.0 collective-permute-done.1.side_1
  8.8 3.4 %collective-permute-start.2 = (f32[3,8,512]{2,1,0:T(8,128)S(1)}, f32[3,8,512]{2,1,0:T(8,128)S(1)}, u32[]{:S(2)}, u32[]{:S(2)}) collective-permute-start(f32[3,8,512]{2,1,0:T(8,128)S(1)} %get-tuple-element.23), channel_id=1, source_target_pairs={{8,16},{16,8},{9,17},{17,9},{10,18},{18,10},{11,19},{19,11},{12,20... | collective-permute-start | bytes 147464 | tf_op jit(solution)/shard_map/ppermute | solution.py:394
  12.2 0.1 collective-permute-start.3
  12.3 0.1 pad_bitcast_fusion
  12.4 0.7 %density_inside.1 = (f32[4,8,512]{2,1,0:T(8,128)S(1)}, f32[3,3,6,8,512]{4,3,2,1,0:T(8,128)S(1)}) custom-call(f32[8,8,512]{2,1,0:T(8,128)S(1)} %get-tuple-element.20.field.latent, f32[2,8,512]{2,1,0:T(8,128)S(1)} %collective-permute-done.side_0, f32[2,8,512]{2,1,0:T(8,128)S(1)} %collective-permute-done.1.side_1, f32[2,27,512]{2,1,0:T(8,128)S(1)} %copy.18.stencils), custom_call_target="tpu_custom_call" | custom-call | tf_op jit(solution)/shard_map/density_inside/pallas_call | solution.py:441
  13.1 2.7 %all-to-all-done.got = f32[32,8,128]{2,1,0:T(8,128)S(1)} async-done(((f32[32,8,128]{2,1,0:T(8,128)}), f32[32,8,128]{2,1,0:T(8,128)S(1)}, u32[]{:S(2)}, u32[]{:S(2)}) %all-to-all-start) | async-done | bytes 131104 | tf_op jit(solution)/shard_map/all_to_all | solution.py:431
  15.9 3.1 %bin_sides.1.behind = f32[8,8,512]{2,1,0:T(8,128)S(1)} custom-call(f32[32,8,128]{2,1,0:T(8,128)S(1)} %all-to-all-done.got, f32[4,8,512]{2,1,0:T(8,128)S(1)} %get-tuple-element.26._.inner), custom_call_target="tpu_custom_call" | custom-call | tf_op jit(solution)/shard_map/bin_sides/pallas_call | solution.py:441
  19.0 0.0 collective-permute-done.3.end_0
  19.0 0.5 %density_ends.1 = (f32[8,8,512]{2,1,0:T(8,128)S(1)}, f32[2,8,512]{2,1,0:T(8,128)S(1)}, f32[2,8,512]{2,1,0:T(8,128)S(1)}) custom-call(f32[8,8,512]{2,1,0:T(8,128)S(1)} %get-tuple-element.20.field.latent, f32[2,8,512]{2,1,0:T(8,128)S(1)} %collective-permute-done.side_0, f32[2,8,512]{2,1,0:T(8,128)S(1)} %collective-permute-done.1.side_1, ...), custom_call_target="tpu_custom_call" | custom-call | tf_op jit(solution)/shard_map/density_ends/pallas_call | solution.py:441
  19.6 0.8 %collective-permute-start.4 = (f32[2,8,512]{2,1,0:T(8,128)S(1)}, f32[2,8,512]{2,1,0:T(8,128)S(1)}, u32[]{:S(2)}, u32[]{:S(2)}) collective-permute-start(f32[2,8,512]{2,1,0:T(8,128)S(1)} %get-tuple-element.28), channel_id=1, source_target_pairs={{1,2},{3,4},{5,6},{7,0},{2,1},{4,3},{6,5},{0,7},{9,10},{11,12},{13... | collective-permute-start | bytes 98312 | tf_op jit(solution)/shard_map/ppermute | solution.py:394
  20.4 0.1 pad_maximum_fusion
  20.5 3.1 %bin_rest.1.field = f32[8,8,512]{2,1,0:T(8,128)S(1)} custom-call(f32[32,8,128]{2,1,0:T(8,128)S(1)} %all-to-all-done.got, f32[8,8,512]{2,1,0:T(8,128)S(1)} %get-tuple-element.27.density, f32[8,8,512]{2,1,0:T(8,128)S(1)} %bin_sides.1.behind), custom_call_target="tpu_custom_call" | custom-call | tf_op jit(solution)/shard_map/bin_rest/pallas_call | solution.py:441
  23.7 1.1 %collective-permute-done.4.side_1 = f32[2,8,512]{2,1,0:T(8,128)S(1)} collective-permute-done((f32[2,8,512]{2,1,0:T(8,128)S(1)}, f32[2,8,512]{2,1,0:T(8,128)S(1)}, u32[]{:S(2)}, u32[]{:S(2)}) %collective-permute-start.4) | collective-permute-done | bytes 32800 | tf_op jit(solution)/shard_map/ppermute | solution.py:394
  24.8 0.4 %back_reach.1 = (f32[2,8,512]{2,1,0:T(8,128)S(1)}, f32[2,8,512]{2,1,0:T(8,128)S(1)}, f32[3,3,4,8,512]{4,3,2,1,0:T(8,128)S(1)}) custom-call(f32[8,8,512]{2,1,0:T(8,128)S(1)} %bin_rest.1.field, f32[2,8,512]{2,1,0:T(8,128)S(1)} %collective-permute-done.4.side_1, f32[2,8,512]{2,1,0:T(8,128)S(1)} %collective-permute-done.5.side_0, f32[2,27,512]{2,1,0:T(8,128)S(1)} %rev.8.stencils), custom_call_target="tpu_custom_call" | custom-call | tf_op jit(solution)/shard_map/back_reach/pallas_call | solution.py:441
  25.2 1.3 %collective-permute-start.6 = (f32[2,8,512]{2,1,0:T(8,128)S(1)}, f32[2,8,512]{2,1,0:T(8,128)S(1)}, u32[]{:S(2)}, u32[]{:S(2)}) collective-permute-start(f32[2,8,512]{2,1,0:T(8,128)S(1)} %get-tuple-element.31), channel_id=1, source_target_pairs={{0,8},{16,24},{8,0},{24,16},{1,9},{17,25},{9,1},{25,17},{2,10},{18... | collective-permute-start | bytes 98312 | tf_op jit(solution)/shard_map/ppermute | solution.py:394
  26.4 2.9 %collective-permute-start.7 = (f32[2,8,512]{2,1,0:T(8,128)S(1)}, f32[2,8,512]{2,1,0:T(8,128)S(1)}, u32[]{:S(2)}, u32[]{:S(2)}) collective-permute-start(f32[2,8,512]{2,1,0:T(8,128)S(1)} %get-tuple-element.32), channel_id=1, source_target_pairs={{8,16},{16,8},{9,17},{17,9},{10,18},{18,10},{11,19},{19,11},{12,20... | collective-permute-start | bytes 98312 | tf_op jit(solution)/shard_map/ppermute | solution.py:394
  29.3 0.8 %back_own.1.own = f32[8,8,512]{2,1,0:T(8,128)S(1)} custom-call(f32[8,8,512]{2,1,0:T(8,128)S(1)} %bin_rest.1.field, f32[2,8,512]{2,1,0:T(8,128)S(1)} %collective-permute-done.4.side_1, f32[2,8,512]{2,1,0:T(8,128)S(1)} %collective-permute-done.5.side_0, f32[2,27,512]{2,1,0:T(8,128)S(1)} %rev.8.stencils, f32[8,8,512]{2,1,0:T(8,128)S(1)} %get-tuple-element.20.field.latent, ...), custom_call_target="tpu_custom_call" | custom-call | tf_op jit(solution)/shard_map/back_own/pallas_call | solution.py:441
  30.1 3.0 %collective-permute-done.7.end_1 = f32[2,8,512]{2,1,0:T(8,128)S(1)} collective-permute-done((f32[2,8,512]{2,1,0:T(8,128)S(1)}, f32[2,8,512]{2,1,0:T(8,128)S(1)}, u32[]{:S(2)}, u32[]{:S(2)}) %collective-permute-start.7) | collective-permute-done | bytes 32800 | tf_op jit(solution)/shard_map/ppermute | solution.py:394
  33.1 0.7 %close.1 = f32[8,8,512]{2,1,0:T(8,128)} custom-call(f32[8,8,512]{2,1,0:T(8,128)S(1)} %back_own.1.own, f32[2,8,512]{2,1,0:T(8,128)S(1)} %collective-permute-done.6.end_0, f32[2,8,512]{2,1,0:T(8,128)S(1)} %collective-permute-done.7.end_1), custom_call_target="tpu_custom_call" | custom-call | tf_op jit(solution)/shard_map/close/pallas_call | solution.py:479
  (13 shorter events, 0.1 us)
Async XLA Ops:
  1.8 7.0 %collective-permute-start = (f32[2,8,512]{2,1,0:T(8,128)S(1)}, f32[2,8,512]{2,1,0:T(8,128)S(1)}, u32[]{:S(2)}, u32[]{:S(2)}) collective-permute-start(f32[2,8,512]{2,1,0:T(8,128)S(1)} %get-tuple-element.21), channel_id=1, source_target_pairs={{0,1},{2,3},{4,5},{6,7},{1,0},{3,2},{5,4},{7,6},{8,9},{10,11},{12,... | collective-permute-start | bytes 98312 | tf_op jit(solution)/shard_map/ppermute | solution.py:394
  1.9 6.9 %collective-permute-start.1 = (f32[2,8,512]{2,1,0:T(8,128)S(1)}, f32[2,8,512]{2,1,0:T(8,128)S(1)}, u32[]{:S(2)}, u32[]{:S(2)}) collective-permute-start(f32[2,8,512]{2,1,0:T(8,128)S(1)} %get-tuple-element.22), channel_id=1, source_target_pairs={{1,2},{3,4},{5,6},{7,0},{2,1},{4,3},{6,5},{0,7},{9,10},{11,12},{13... | collective-permute-start | bytes 98312 | tf_op jit(solution)/shard_map/ppermute | solution.py:394
  5.6 3.1 %copy-start = (f32[2,27,512]{2,0,1:T(2,128)S(1)}, f32[2,27,512]{2,0,1:T(2,128)}, u32[]{:S(2)}) copy-start(f32[2,27,512]{2,0,1:T(2,128)} %param.13) | copy-start | bytes 331780
  5.6 10.3 %all-to-all-start = ((f32[32,8,128]{2,1,0:T(8,128)}), f32[32,8,128]{2,1,0:T(8,128)S(1)}, u32[]{:S(2)}, u32[]{:S(2)}) async-start(f32[32,8,128]{2,1,0:T(8,128)} %get-tuple-element.19), calls=%async_computation | async-start | bytes 262144 | tf_op jit(solution)/shard_map/all_to_all | solution.py:431
  8.8 10.2 %collective-permute-start.2 = (f32[3,8,512]{2,1,0:T(8,128)S(1)}, f32[3,8,512]{2,1,0:T(8,128)S(1)}, u32[]{:S(2)}, u32[]{:S(2)}) collective-permute-start(f32[3,8,512]{2,1,0:T(8,128)S(1)} %get-tuple-element.23), channel_id=1, source_target_pairs={{8,16},{16,8},{9,17},{17,9},{10,18},{18,10},{11,19},{19,11},{12,20... | collective-permute-start | bytes 147464 | tf_op jit(solution)/shard_map/ppermute | solution.py:394
  12.2 6.8 %collective-permute-start.3 = (f32[3,8,512]{2,1,0:T(8,128)S(1)}, f32[3,8,512]{2,1,0:T(8,128)S(1)}, u32[]{:S(2)}, u32[]{:S(2)}) collective-permute-start(f32[3,8,512]{2,1,0:T(8,128)S(1)} %get-tuple-element.24), channel_id=1, source_target_pairs={{0,8},{16,24},{8,0},{24,16},{1,9},{17,25},{9,1},{25,17},{2,10},{18... | collective-permute-start | bytes 147464 | tf_op jit(solution)/shard_map/ppermute | solution.py:394
  19.6 5.2 %collective-permute-start.4 = (f32[2,8,512]{2,1,0:T(8,128)S(1)}, f32[2,8,512]{2,1,0:T(8,128)S(1)}, u32[]{:S(2)}, u32[]{:S(2)}) collective-permute-start(f32[2,8,512]{2,1,0:T(8,128)S(1)} %get-tuple-element.28), channel_id=1, source_target_pairs={{1,2},{3,4},{5,6},{7,0},{2,1},{4,3},{6,5},{0,7},{9,10},{11,12},{13... | collective-permute-start | bytes 98312 | tf_op jit(solution)/shard_map/ppermute | solution.py:394
  20.4 4.4 %collective-permute-start.5 = (f32[2,8,512]{2,1,0:T(8,128)S(1)}, f32[2,8,512]{2,1,0:T(8,128)S(1)}, u32[]{:S(2)}, u32[]{:S(2)}) collective-permute-start(f32[2,8,512]{2,1,0:T(8,128)S(1)} %get-tuple-element.29), channel_id=1, source_target_pairs={{0,1},{2,3},{4,5},{6,7},{1,0},{3,2},{5,4},{7,6},{8,9},{10,11},{12,... | collective-permute-start | bytes 98312 | tf_op jit(solution)/shard_map/ppermute | solution.py:394
  25.2 5.0 %collective-permute-start.6 = (f32[2,8,512]{2,1,0:T(8,128)S(1)}, f32[2,8,512]{2,1,0:T(8,128)S(1)}, u32[]{:S(2)}, u32[]{:S(2)}) collective-permute-start(f32[2,8,512]{2,1,0:T(8,128)S(1)} %get-tuple-element.31), channel_id=1, source_target_pairs={{0,8},{16,24},{8,0},{24,16},{1,9},{17,25},{9,1},{25,17},{2,10},{18... | collective-permute-start | bytes 98312 | tf_op jit(solution)/shard_map/ppermute | solution.py:394
  26.4 6.7 %collective-permute-start.7 = (f32[2,8,512]{2,1,0:T(8,128)S(1)}, f32[2,8,512]{2,1,0:T(8,128)S(1)}, u32[]{:S(2)}, u32[]{:S(2)}) collective-permute-start(f32[2,8,512]{2,1,0:T(8,128)S(1)} %get-tuple-element.32), channel_id=1, source_target_pairs={{8,16},{16,8},{9,17},{17,9},{10,18},{18,10},{11,19},{19,11},{12,20... | collective-permute-start | bytes 98312 | tf_op jit(solution)/shard_map/ppermute | solution.py:394

commit v16 on v14

--- a/solution.py
+++ b/solution.py
@@ -41,19 +41,25 @@
         to_outer[group] = either(odd, after, before)
 
 
+def unpack_side(packed, before, height):
+    tiles = []
+    for group in range(height // 4):
+        for k in range(4):
+            ahead = pltpu.roll(packed[group], -2 * k % SUBLANES, 0)
+            tiles.append(either(before, pltpu.roll(packed[group], 2 * k, 0), ahead))
+    return tiles
+
+
+def outer_place(radial):
+    _, odd = position("lon")
+    return lax.shift_right_logical(sublane(radial), 2) == 1 - odd
+
+
 def unpack_sides(from_partner, from_outer, height):
     _, odd = position("lon")
-    sub = sublane(from_partner.shape[2])
-    tiles = []
-    for group in range(height // 4):
-        partner, outer = from_partner[group], from_outer[group]
-        before, after = either(odd, partner, outer), either(odd, outer, partner)
-        for k in range(4):
-            if k:
-                tiles.append(jnp.where(sub < 4, pltpu.roll(after, SUBLANES - 2 * k, 0), pltpu.roll(before, 2 * k, 0)))
-            else:
-                tiles.append(jnp.where(sub < 4, after, before))
-    return tiles
+    place = outer_place(from_partner.shape[2])
+    pairs = zip(unpack_side(from_partner, odd, height), unpack_side(from_outer, 1 - odd, height))
+    return [jnp.where(place, outer, partner) for partner, outer in pairs]
 
 
 def pack_ends_kernel(field, side_0, side_1, to_partner, to_outer):
@@ -148,9 +154,8 @@
     tiles_of_bins(radial, body)
 
 
-def fill_wide(wide, field, side_0, side_1, rows):
-    height, width, _ = field.shape
-    tiles = unpack_sides(side_0, side_1, height)
+def fill_wide(wide, field, tiles, rows):
+    width = field.shape[1]
     for row in rows:
         wide[row, :width] = field[row]
         wide[row, width:] = tiles[row]
@@ -158,7 +163,7 @@
 
 def density_inside_kernel(field, side_0, side_1, stencils, out, middle, wide, shifted):
     height, width, radial = field.shape
-    fill_wide(wide, field, side_0, side_1, range(height))
+    fill_wide(wide, field, unpack_sides(side_0, side_1, height), range(height))
     centers = [(row, ALL) for row in range(1, height - 1)]
     first_level(wide, shifted, stencils.at[0], centers, middle, [None] * len(centers))
 
@@ -204,13 +209,14 @@
     pack_sides([out[row] * behind[row] for row in range(height)], to_partner, to_outer)
 
 
-def back_reach_kernel(field, side_1, side_0, stencils, to_partner, to_outer, middle, wide, shifted, reach):
-    height, _, radial = field.shape
-    last = height - 1
-    fill_wide(wide, field, side_0, side_1, (0, 1, last - 1, last))
+def on_grid():
     lat, odd = position("lat")
-    above = (lat > 0).astype(jnp.int32)
-    below = (lat < lax.axis_size("lat") - 1).astype(jnp.int32)
+    return odd, (lat > 0).astype(jnp.int32), (lat < lax.axis_size("lat") - 1).astype(jnp.int32)
+
+
+def reach_of(wide, stencils, reach, middle, shifted):
+    last, radial = wide.shape[0] - 1, wide.shape[2]
+    _, above, below = on_grid()
     centers = [(-1, (1,)), (0, (0, 1)), (last, (-1, 0)), (last + 1, (-1,))]
     first_level(wide, shifted, stencils.at[0], centers, middle, [above, None, None, below])
 
@@ -224,25 +230,57 @@
         3: [(middle, 3), None, None],
     }
     second_level(stencils.at[1], windows, radial, write)
-    for place in range(2):
-        to_partner[place] = either(odd, reach[place], reach[2 + place])
-        to_outer[place] = either(odd, reach[2 + place], reach[place])
-
-
-def back_own_kernel(field, side_1, side_0, stencils, latent, edge, out, wide, shifted, middle):
+
+
+def reach_near_kernel(field, side_0, stencils, to_partner, reach, middle, wide, shifted):
     height, _, radial = field.shape
-    fill_wide(wide, field, side_0, side_1, range(height))
-    centers = [(row, ALL) for row in range(1, height - 1)]
-    first_level(wide, shifted, stencils.at[0], centers, middle, [None] * len(centers))
+    _, odd_lon = position("lon")
+    place = outer_place(radial)
+    tiles = [jnp.where(place, 0.0, tile) for tile in unpack_side(side_0, odd_lon, height)]
+    fill_wide(wide, field, tiles, (0, 1, height - 2, height - 1))
+    reach_of(wide, stencils, reach, middle, shifted)
+    odd, _, _ = on_grid()
+    for row in range(2):
+        to_partner[row] = either(odd, reach[row], reach[2 + row])
+
+
+def reach_far_kernel(side_1, near, stencils, to_partner, to_outer, middle, wide, shifted, reach):
+    height, cols, radial = wide.shape
+    _, odd_lon = position("lon")
+    place = outer_place(radial)
+    tiles = unpack_side(side_1, 1 - odd_lon, height)
+    for row in (0, 1, height - 2, height - 1):
+        wide[row, :cols // 2] = jnp.zeros((cols // 2, radial), jnp.float32)
+        wide[row, cols // 2:] = jnp.where(place, tiles[row], 0.0)
+    reach_of(wide, stencils, reach, middle, shifted)
+    odd, _, _ = on_grid()
+    for row in range(2):
+        to_partner[row] = either(odd, reach[row], reach[2 + row])
+        to_outer[row] = either(odd, reach[2 + row] + near[2 + row], reach[row] + near[row])
+
+
+def back_own_kernel(field, side_0, side_1, stencils, latent, end_0, out, wide, shifted, middle):
+    height, _, radial = field.shape
+    last = height - 1
+    fill_wide(wide, field, unpack_sides(side_0, side_1, height), range(height))
+    odd, above, below = on_grid()
+    inner = [(row, ALL) for row in range(1, last)]
+    centers = [(-1, (1,)), (0, (0, 1)), *inner, (last, (-1, 0)), (last + 1, (-1,))]
+    first_level(wide, shifted, stencils.at[0], centers, middle, [above, *[None] * height, below])
 
     def write(row, at, value):
         out[row, :, at] = latent[row, :, at] + value
 
-    line = [(edge, 0), (edge, 1)] + [(middle, place) for place in range(height - 2)] + [(edge, 2), (edge, 3)]
-    second_level(stencils.at[1], {row: line[row:row + 3] for row in range(height)}, radial, write)
-
-
-def close_kernel(own, end_0, end_1, out, top, bottom, sent):
+    windows = {row: [(middle, row + k) for k in range(3)] for row in range(height)}
+    second_level(stencils.at[1], windows, radial, write)
+    for row in range(2):
+        part = end_0[row]
+        none = jnp.zeros_like(part)
+        out[row] += either(odd, part, none)
+        out[last - 1 + row] += either(odd, none, part)
+
+
+def close_kernel(own, end_1, end_0, out, top, bottom, sent):
     height = own.shape[0]
     last = height - 2
     pairs = ((own.at[2:last], out.at[2:last]), (top, out.at[:2]), (bottom, out.at[last:]))
@@ -378,17 +416,18 @@
     return jnp.stack([back, turned[:, :, 1], ahead], axis=2).reshape(stencils.shape)
 
 
+def pairwise(values, axis, closed, outer):
+    count = lax.axis_size(axis)
+    pairs = [(i, (i + 1) % count) for i in range(int(outer), count, 2) if closed or i + 1 < count]
+    return lax.ppermute(values, axis, pairs + [(j, i) for i, j in pairs])
+
+
 def swap(to_partner, to_outer, axis, closed, outer_first=False):
-    count = lax.axis_size(axis)
-    outer = [(i, (i + 1) % count) for i in range(1, count, 2) if closed or i + 1 < count]
-    inner = [(i, i + 1) for i in range(0, count - 1, 2)]
-
-    def both_ways(pairs):
-        return pairs + [(j, i) for i, j in pairs]
-
-    moves = [(to_partner, inner), (to_outer, outer)]
-    got = [lax.ppermute(values, axis, both_ways(pairs)) for values, pairs in moves[::-1 if outer_first else 1]]
-    return tuple(got[::-1 if outer_first else 1])
+    if outer_first:
+        from_outer = pairwise(to_outer, axis, closed, True)
+        return pairwise(to_partner, axis, closed, False), from_outer
+    from_partner = pairwise(to_partner, axis, closed, False)
+    return from_partner, pairwise(to_outer, axis, closed, True)
 
 
 VMEM = pl.BlockSpec(memory_space=pltpu.VMEM)
@@ -461,15 +500,22 @@
     upstream = call(bin_rest_kernel, "bin_rest", tile, [star_rows], got, density, behind)
 
     mirrored = mirror(stencils)[::-1]
-    beside = swap(*to_sides, "lon", True, outer_first=True)
-    *to_ends, middle = call(
-        back_reach_kernel, "back_reach", (shape(2, width, radial), shape(2, width, radial), shape(*edge)),
-        [rows, moved, pltpu.VMEM((4, width, radial), f32)], upstream, *beside[::-1], mirrored,
-    )
-    above = swap(*to_ends, "lat", False)
+    from_partner, from_outer = swap(*to_sides, "lon", True, outer_first=True)
+    pair = shape(2, width, radial)
+    quad = (4, width, radial)
+    near_part, near = call(
+        reach_near_kernel, "reach_near", (pair, shape(*quad)), [pltpu.VMEM(edge, f32), rows, moved],
+        upstream, from_partner, mirrored,
+    )
+    first_end = pairwise(near_part, "lat", False, False)
+    far_part, to_outer = call(
+        reach_far_kernel, "reach_far", (pair, pair), [pltpu.VMEM(edge, f32), rows, moved, pltpu.VMEM(quad, f32)],
+        from_outer, near, mirrored,
+    )
+    last_ends = pairwise(to_outer, "lat", False, True), pairwise(far_part, "lat", False, False)
     own = call(
-        back_own_kernel, "back_own", tile, [rows, moved, pltpu.VMEM(inner_rows, f32)],
-        upstream, *beside[::-1], mirrored, latent, middle,
+        back_own_kernel, "back_own", tile, [rows, moved, pltpu.VMEM((3, 3, height + 2, width, radial), f32)],
+        upstream, from_partner, from_outer, mirrored, latent, first_end,
     )
     return pl.pallas_call(
         close_kernel,
@@ -479,7 +525,7 @@
         scratch_shapes=[pltpu.VMEM((2, width, radial), f32)] * 2 + [pltpu.SemaphoreType.DMA((3,))],
         compiler_params=LIMIT,
         name="close",
-    )(own, *above)
+    )(own, *last_ends)
 
 
 def solution(mesh):

time: 33.1 us -> 33.9 us (1.024)
  the two profiles are of different devices: /device:TPU:2 before, /device:TPU:0 now
where the time goes in v16:
time: 33.9 us; the launch traced here: 33.7 us
  starting transfers between devices  20.2 us (60%)
  Pallas kernels  9.71 us (29%)
  waiting for transfers between devices  3.26 us (10%)
    ppermute x9, starting transfers between devices, pairwise(): return lax.ppermute(values, axis, pairs + [(j, i) for i, j in pairs])  17.4 us
    pallas_call x8, Pallas kernels, call(): pl.pallas_call(kernel, out_shape=outs, in_specs=[VMEM] * len(operands), o...  7.27 us
    all_to_all x1, starting transfers between devices, on_device(): lax.all_to_all(packed, ('lat', 'lon'), split_axis=0, concat_axis=0, tiled...  2.81 us
    all_to_all x1, waiting for transfers between devices, on_device(): lax.all_to_all(packed, ('lat', 'lon'), split_axis=0, concat_axis=0, tiled...  1.92 us
    pallas_call x1, Pallas kernels, on_device(): pl.pallas_call(open_kernel, out_shape=(jax.ShapeDtypeStruct((shards, 2 *...  1.76 us
    ppermute x9, waiting for transfers between devices, pairwise(): return lax.ppermute(values, axis, pairs + [(j, i) for i, j in pairs])  1.33 us
  transfers between devices with their start and end apart: 10, of which 3 were waited for; matrix products, arithmetic and copies ran while one was open for 1% of the time, Pallas kernels for 20%

profile of v16, /device:TPU:0, one launch (start us, length us, event | category | flops | bytes accessed | tf_op | source)
XLA Modules:
  0.0 33.7 jit_solution(5615226945524024728)
XLA Ops:
  0.0 1.8 %opening.1 = (f32[32,8,128]{2,1,0:T(8,128)}, f32[8,8,512]{2,1,0:T(8,128)S(1)}, f32[2,8,512]{2,1,0:T(8,128)S(1)}, f32[2,8,512]{2,1,0:T(8,128)S(1)}) custom-call(s32[1,32]{1,0:T(1,128)} %counts_in.1, s32[1,32]{1,0:T(1,128)} %offsets_in.1, f32[128,128]{1,0:T(8,128)} %bitcast.20, s32[128,128]{1,0:T(8,128)} %bitcast.21, s32[128,128]{1,0:T(8,128)} %bitcast.22, ...), custom_call_target="tpu_custom_call" | custom-call | tf_op jit(solution)/shard_map/opening/pallas_call | solution.py:451
  1.8 0.5 %collective-permute-start = (f32[2,8,512]{2,1,0:T(8,128)S(1)}, f32[2,8,512]{2,1,0:T(8,128)S(1)}, u32[]{:S(2)}, u32[]{:S(2)}) collective-permute-start(f32[2,8,512]{2,1,0:T(8,128)S(1)} %get-tuple-element.22), channel_id=1, source_target_pairs={{0,1},{2,3},{4,5},{6,7},{1,0},{3,2},{5,4},{7,6},{8,9},{10,11},{12,... | collective-permute-start | bytes 98312 | tf_op jit(solution)/shard_map/ppermute | solution.py:422
  2.3 4.7 %collective-permute-start.1 = (f32[2,8,512]{2,1,0:T(8,128)S(1)}, f32[2,8,512]{2,1,0:T(8,128)S(1)}, u32[]{:S(2)}, u32[]{:S(2)}) collective-permute-start(f32[2,8,512]{2,1,0:T(8,128)S(1)} %get-tuple-element.23), channel_id=1, source_target_pairs={{1,2},{3,4},{5,6},{7,0},{2,1},{4,3},{6,5},{0,7},{9,10},{11,12},{13... | collective-permute-start | bytes 98312 | tf_op jit(solution)/shard_map/ppermute | solution.py:422
  7.0 2.8 %all-to-all-start = ((f32[32,8,128]{2,1,0:T(8,128)}), f32[32,8,128]{2,1,0:T(8,128)S(1)}, u32[]{:S(2)}, u32[]{:S(2)}) async-start(f32[32,8,128]{2,1,0:T(8,128)} %get-tuple-element.20), calls=%async_computation | async-start | bytes 262144 | tf_op jit(solution)/shard_map/all_to_all | solution.py:466
  9.9 0.1 slice_bitcast_fusion.1
  10.0 0.7 %collective-permute-start.2 = (f32[3,8,512]{2,1,0:T(8,128)S(1)}, f32[3,8,512]{2,1,0:T(8,128)S(1)}, u32[]{:S(2)}, u32[]{:S(2)}) collective-permute-start(f32[3,8,512]{2,1,0:T(8,128)S(1)} %get-tuple-element.24), channel_id=1, source_target_pairs={{8,16},{16,8},{9,17},{17,9},{10,18},{18,10},{11,19},{19,11},{12,20... | collective-permute-start | bytes 147464 | tf_op jit(solution)/shard_map/ppermute | solution.py:422
  10.7 4.5 %collective-permute-start.3 = (f32[3,8,512]{2,1,0:T(8,128)S(1)}, f32[3,8,512]{2,1,0:T(8,128)S(1)}, u32[]{:S(2)}, u32[]{:S(2)}) collective-permute-start(f32[3,8,512]{2,1,0:T(8,128)S(1)} %get-tuple-element.25), channel_id=1, source_target_pairs={{0,8},{16,24},{8,0},{24,16},{1,9},{17,25},{9,1},{25,17},{2,10},{18... | collective-permute-start | bytes 147464 | tf_op jit(solution)/shard_map/ppermute | solution.py:422
  15.2 0.1 pad_bitcast_fusion
  15.4 0.7 %density_inside.1 = (f32[4,8,512]{2,1,0:T(8,128)S(1)}, f32[3,3,6,8,512]{4,3,2,1,0:T(8,128)S(1)}) custom-call(f32[8,8,512]{2,1,0:T(8,128)S(1)} %get-tuple-element.21.field.latent, f32[2,8,512]{2,1,0:T(8,128)S(1)} %collective-permute-done.side_0, f32[2,8,512]{2,1,0:T(8,128)S(1)} %collective-permute-done.1.side_1, f32[2,27,512]{2,1,0:T(8,128)S(1)} %copy.18.stencils), custom_call_target="tpu_custom_call" | custom-call | tf_op jit(solution)/shard_map/density_inside/pallas_call | solution.py:475
  16.1 1.9 %all-to-all-done.got = f32[32,8,128]{2,1,0:T(8,128)S(1)} async-done(((f32[32,8,128]{2,1,0:T(8,128)}), f32[32,8,128]{2,1,0:T(8,128)S(1)}, u32[]{:S(2)}, u32[]{:S(2)}) %all-to-all-start) | async-done | bytes 131104 | tf_op jit(solution)/shard_map/all_to_all | solution.py:466
  18.0 2.2 %bin_sides.1.behind = f32[8,8,512]{2,1,0:T(8,128)S(1)} custom-call(f32[32,8,128]{2,1,0:T(8,128)S(1)} %all-to-all-done.got, f32[4,8,512]{2,1,0:T(8,128)S(1)} %get-tuple-element.27._.inner), custom_call_target="tpu_custom_call" | custom-call | tf_op jit(solution)/shard_map/bin_sides/pallas_call | solution.py:475
  20.2 0.5 %density_ends.1 = (f32[8,8,512]{2,1,0:T(8,128)S(1)}, f32[2,8,512]{2,1,0:T(8,128)S(1)}, f32[2,8,512]{2,1,0:T(8,128)S(1)}) custom-call(f32[8,8,512]{2,1,0:T(8,128)S(1)} %get-tuple-element.21.field.latent, f32[2,8,512]{2,1,0:T(8,128)S(1)} %collective-permute-done.side_0, f32[2,8,512]{2,1,0:T(8,128)S(1)} %collective-permute-done.1.side_1, ...), custom_call_target="tpu_custom_call" | custom-call | tf_op jit(solution)/shard_map/density_ends/pallas_call | solution.py:475
  20.7 0.4 %collective-permute-start.4 = (f32[2,8,512]{2,1,0:T(8,128)S(1)}, f32[2,8,512]{2,1,0:T(8,128)S(1)}, u32[]{:S(2)}, u32[]{:S(2)}) collective-permute-start(f32[2,8,512]{2,1,0:T(8,128)S(1)} %get-tuple-element.29), channel_id=1, source_target_pairs={{0,1},{2,3},{4,5},{6,7},{1,0},{3,2},{5,4},{7,6},{8,9},{10,11},{12,... | collective-permute-start | bytes 98312 | tf_op jit(solution)/shard_map/ppermute | solution.py:422
  21.1 1.2 %collective-permute-start.5 = (f32[2,8,512]{2,1,0:T(8,128)S(1)}, f32[2,8,512]{2,1,0:T(8,128)S(1)}, u32[]{:S(2)}, u32[]{:S(2)}) collective-permute-start(f32[2,8,512]{2,1,0:T(8,128)S(1)} %get-tuple-element.30), channel_id=1, source_target_pairs={{1,2},{3,4},{5,6},{7,0},{2,1},{4,3},{6,5},{0,7},{9,10},{11,12},{13... | collective-permute-start | bytes 98312 | tf_op jit(solution)/shard_map/ppermute | solution.py:422
  22.5 2.2 %bin_rest.1.field = f32[8,8,512]{2,1,0:T(8,128)S(1)} custom-call(f32[32,8,128]{2,1,0:T(8,128)S(1)} %all-to-all-done.got, f32[8,8,512]{2,1,0:T(8,128)S(1)} %get-tuple-element.28.density, f32[8,8,512]{2,1,0:T(8,128)S(1)} %bin_sides.1.behind), custom_call_target="tpu_custom_call" | custom-call | tf_op jit(solution)/shard_map/bin_rest/pallas_call | solution.py:475
  24.6 0.4 %reach_near.1 = (f32[2,8,512]{2,1,0:T(8,128)S(1)}, f32[4,8,512]{2,1,0:T(8,128)S(1)}) custom-call(f32[8,8,512]{2,1,0:T(8,128)S(1)} %bin_rest.1.field, f32[2,8,512]{2,1,0:T(8,128)S(1)} %collective-permute-done.4.side_0, f32[2,27,512]{2,1,0:T(8,128)S(1)} %rev.8.stencils), custom_call_target="tpu_custom_call" | custom-call | tf_op jit(solution)/shard_map/reach_near/pallas_call | solution.py:475
  25.0 1.1 %collective-permute-start.6 = (f32[2,8,512]{2,1,0:T(8,128)S(1)}, f32[2,8,512]{2,1,0:T(8,128)S(1)}, u32[]{:S(2)}, u32[]{:S(2)}) collective-permute-start(f32[2,8,512]{2,1,0:T(8,128)S(1)} %get-tuple-element.31), channel_id=1, source_target_pairs={{0,8},{16,24},{8,0},{24,16},{1,9},{17,25},{9,1},{25,17},{2,10},{18... | collective-permute-start | bytes 98312 | tf_op jit(solution)/shard_map/ppermute | solution.py:422
  26.1 0.2 collective-permute-done.5.side_1
  26.3 0.3 %reach_far.1 = (f32[2,8,512]{2,1,0:T(8,128)S(1)}, f32[2,8,512]{2,1,0:T(8,128)S(1)}) custom-call(f32[2,8,512]{2,1,0:T(8,128)S(1)} %collective-permute-done.5.side_1, f32[4,8,512]{2,1,0:T(8,128)S(1)} %get-tuple-element.32.near, f32[2,27,512]{2,1,0:T(8,128)S(1)} %rev.8.stencils), custom_call_target="tpu_custom_call" | custom-call | tf_op jit(solution)/shard_map/reach_far/pallas_call | solution.py:475
  26.6 0.7 %collective-permute-start.7 = (f32[2,8,512]{2,1,0:T(8,128)S(1)}, f32[2,8,512]{2,1,0:T(8,128)S(1)}, u32[]{:S(2)}, u32[]{:S(2)}) collective-permute-start(f32[2,8,512]{2,1,0:T(8,128)S(1)} %get-tuple-element.33), channel_id=1, source_target_pairs={{8,16},{16,8},{9,17},{17,9},{10,18},{18,10},{11,19},{19,11},{12,20... | collective-permute-start | bytes 98312 | tf_op jit(solution)/shard_map/ppermute | solution.py:422
  27.3 3.6 %collective-permute-start.8 = (f32[2,8,512]{2,1,0:T(8,128)S(1)}, f32[2,8,512]{2,1,0:T(8,128)S(1)}, u32[]{:S(2)}, u32[]{:S(2)}) collective-permute-start(f32[2,8,512]{2,1,0:T(8,128)S(1)} %get-tuple-element.34), channel_id=1, source_target_pairs={{0,8},{16,24},{8,0},{24,16},{1,9},{17,25},{9,1},{25,17},{2,10},{18... | collective-permute-start | bytes 98312 | tf_op jit(solution)/shard_map/ppermute | solution.py:422
  30.9 1.0 %back_own.1.own = f32[8,8,512]{2,1,0:T(8,128)S(1)} custom-call(f32[8,8,512]{2,1,0:T(8,128)S(1)} %bin_rest.1.field, f32[2,8,512]{2,1,0:T(8,128)S(1)} %collective-permute-done.4.side_0, f32[2,8,512]{2,1,0:T(8,128)S(1)} %collective-permute-done.5.side_1, f32[2,27,512]{2,1,0:T(8,128)S(1)} %rev.8.stencils, f32[8,8,512]{2,1,0:T(8,128)S(1)} %get-tuple-element.21.field.latent, ...), custom_call_target="tpu_custom_call" | custom-call | tf_op jit(solution)/shard_map/back_own/pallas_call | solution.py:475
  31.9 1.2 %collective-permute-done.8.end_0 = f32[2,8,512]{2,1,0:T(8,128)S(1)} collective-permute-done((f32[2,8,512]{2,1,0:T(8,128)S(1)}, f32[2,8,512]{2,1,0:T(8,128)S(1)}, u32[]{:S(2)}, u32[]{:S(2)}) %collective-permute-start.8) | collective-permute-done | bytes 32800 | tf_op jit(solution)/shard_map/ppermute | solution.py:422
  33.0 0.7 %close.1 = f32[8,8,512]{2,1,0:T(8,128)} custom-call(f32[8,8,512]{2,1,0:T(8,128)S(1)} %back_own.1.own, f32[2,8,512]{2,1,0:T(8,128)S(1)} %collective-permute-done.7.end_1, f32[2,8,512]{2,1,0:T(8,128)S(1)} %collective-permute-done.8.end_0), custom_call_target="tpu_custom_call" | custom-call | tf_op jit(solution)/shard_map/close/pallas_call | solution.py:520
  (16 shorter events, 0.2 us)
Async XLA Ops:
  1.8 8.2 %collective-permute-start = (f32[2,8,512]{2,1,0:T(8,128)S(1)}, f32[2,8,512]{2,1,0:T(8,128)S(1)}, u32[]{:S(2)}, u32[]{:S(2)}) collective-permute-start(f32[2,8,512]{2,1,0:T(8,128)S(1)} %get-tuple-element.22), channel_id=1, source_target_pairs={{0,1},{2,3},{4,5},{6,7},{1,0},{3,2},{5,4},{7,6},{8,9},{10,11},{12,... | collective-permute-start | bytes 98312 | tf_op jit(solution)/shard_map/ppermute | solution.py:422
  2.3 7.7 %collective-permute-start.1 = (f32[2,8,512]{2,1,0:T(8,128)S(1)}, f32[2,8,512]{2,1,0:T(8,128)S(1)}, u32[]{:S(2)}, u32[]{:S(2)}) collective-permute-start(f32[2,8,512]{2,1,0:T(8,128)S(1)} %get-tuple-element.23), channel_id=1, source_target_pairs={{1,2},{3,4},{5,6},{7,0},{2,1},{4,3},{6,5},{0,7},{9,10},{11,12},{13... | collective-permute-start | bytes 98312 | tf_op jit(solution)/shard_map/ppermute | solution.py:422
  7.0 2.8 %copy-start = (f32[2,27,512]{2,0,1:T(2,128)S(1)}, f32[2,27,512]{2,0,1:T(2,128)}, u32[]{:S(2)}) copy-start(f32[2,27,512]{2,0,1:T(2,128)} %param.13) | copy-start | bytes 331780
  7.0 11.0 %all-to-all-start = ((f32[32,8,128]{2,1,0:T(8,128)}), f32[32,8,128]{2,1,0:T(8,128)S(1)}, u32[]{:S(2)}, u32[]{:S(2)}) async-start(f32[32,8,128]{2,1,0:T(8,128)} %get-tuple-element.20), calls=%async_computation | async-start | bytes 262144 | tf_op jit(solution)/shard_map/all_to_all | solution.py:466
  10.0 10.2 %collective-permute-start.2 = (f32[3,8,512]{2,1,0:T(8,128)S(1)}, f32[3,8,512]{2,1,0:T(8,128)S(1)}, u32[]{:S(2)}, u32[]{:S(2)}) collective-permute-start(f32[3,8,512]{2,1,0:T(8,128)S(1)} %get-tuple-element.24), channel_id=1, source_target_pairs={{8,16},{16,8},{9,17},{17,9},{10,18},{18,10},{11,19},{19,11},{12,20... | collective-permute-start | bytes 147464 | tf_op jit(solution)/shard_map/ppermute | solution.py:422
  10.7 9.5 %collective-permute-start.3 = (f32[3,8,512]{2,1,0:T(8,128)S(1)}, f32[3,8,512]{2,1,0:T(8,128)S(1)}, u32[]{:S(2)}, u32[]{:S(2)}) collective-permute-start(f32[3,8,512]{2,1,0:T(8,128)S(1)} %get-tuple-element.25), channel_id=1, source_target_pairs={{0,8},{16,24},{8,0},{24,16},{1,9},{17,25},{9,1},{25,17},{2,10},{18... | collective-permute-start | bytes 147464 | tf_op jit(solution)/shard_map/ppermute | solution.py:422
  20.7 3.9 %collective-permute-start.4 = (f32[2,8,512]{2,1,0:T(8,128)S(1)}, f32[2,8,512]{2,1,0:T(8,128)S(1)}, u32[]{:S(2)}, u32[]{:S(2)}) collective-permute-start(f32[2,8,512]{2,1,0:T(8,128)S(1)} %get-tuple-element.29), channel_id=1, source_target_pairs={{0,1},{2,3},{4,5},{6,7},{1,0},{3,2},{5,4},{7,6},{8,9},{10,11},{12,... | collective-permute-start | bytes 98312 | tf_op jit(solution)/shard_map/ppermute | solution.py:422
  21.1 5.1 %collective-permute-start.5 = (f32[2,8,512]{2,1,0:T(8,128)S(1)}, f32[2,8,512]{2,1,0:T(8,128)S(1)}, u32[]{:S(2)}, u32[]{:S(2)}) collective-permute-start(f32[2,8,512]{2,1,0:T(8,128)S(1)} %get-tuple-element.30), channel_id=1, source_target_pairs={{1,2},{3,4},{5,6},{7,0},{2,1},{4,3},{6,5},{0,7},{9,10},{11,12},{13... | collective-permute-start | bytes 98312 | tf_op jit(solution)/shard_map/ppermute | solution.py:422
  25.0 5.9 %collective-permute-start.6 = (f32[2,8,512]{2,1,0:T(8,128)S(1)}, f32[2,8,512]{2,1,0:T(8,128)S(1)}, u32[]{:S(2)}, u32[]{:S(2)}) collective-permute-start(f32[2,8,512]{2,1,0:T(8,128)S(1)} %get-tuple-element.31), channel_id=1, source_target_pairs={{0,8},{16,24},{8,0},{24,16},{1,9},{17,25},{9,1},{25,17},{2,10},{18... | collective-permute-start | bytes 98312 | tf_op jit(solution)/shard_map/ppermute | solution.py:422
  26.6 5.3 %collective-permute-start.7 = (f32[2,8,512]{2,1,0:T(8,128)S(1)}, f32[2,8,512]{2,1,0:T(8,128)S(1)}, u32[]{:S(2)}, u32[]{:S(2)}) collective-permute-start(f32[2,8,512]{2,1,0:T(8,128)S(1)} %get-tuple-element.33), channel_id=1, source_target_pairs={{8,16},{16,8},{9,17},{17,9},{10,18},{18,10},{11,19},{19,11},{12,20... | collective-permute-start | bytes 98312 | tf_op jit(solution)/shard_map/ppermute | solution.py:422
  27.3 5.7 %collective-permute-start.8 = (f32[2,8,512]{2,1,0:T(8,128)S(1)}, f32[2,8,512]{2,1,0:T(8,128)S(1)}, u32[]{:S(2)}, u32[]{:S(2)}) collective-permute-start(f32[2,8,512]{2,1,0:T(8,128)S(1)} %get-tuple-element.34), channel_id=1, source_target_pairs={{0,8},{16,24},{8,0},{24,16},{1,9},{17,25},{9,1},{25,17},{2,10},{18... | collective-permute-start | bytes 98312 | tf_op jit(solution)/shard_map/ppermute | solution.py:422

commit v17 on v14

--- a/solution.py
+++ b/solution.py
@@ -8,6 +8,7 @@
 from jax.sharding import PartitionSpec as P
 
 CAP = 512
+LEAST = 128
 LANES = 128
 SUBLANES = 8
 RUNS = CAP // LANES
@@ -294,7 +295,7 @@
     pack_sides([latent[row] for row in range(height)], to_partner, to_outer)
 
 
-def behind_of(got, part, cuts, rows_of, *, height, width, radial):
+def behind_of(got, part, cuts, runs, rows_of, *, height, width, radial):
     span = radial // cuts
     pixels = height * width // 2
     classes = cuts * pixels
@@ -325,10 +326,11 @@
     rows_of[2] = tiles - coarse
 
     total = jnp.zeros((2 * classes, span), jnp.float32)
-    for first in range(0, shards, 2):
+    group = 2 * RUNS // runs
+    for first in range(0, shards, group):
         left, right = [], []
-        for run in range(2 * RUNS):
-            row = (first + run // RUNS) * rows + run % RUNS * 2
+        for run in range(group * runs):
+            row = (first + run // runs) * rows + run % runs * 2
             mine = tall(0, row + 1) == column
             left.append(jnp.concatenate([jnp.where(mine, tall(kind, row), zero) for kind in (1, 2)], axis=0))
             low = jnp.broadcast_to(lows[:, row + 1:row + 2], (LANES, LANES))
@@ -355,19 +357,34 @@
     return rows
 
 
+def for_load(body):
+    lat, count = lax.axis_index("lat"), lax.axis_size("lat")
+    middle = (lat >= count // 4) & (lat < count - count // 4)
+    pl.when(middle)(lambda: body(RUNS))
+    pl.when(jnp.logical_not(middle))(lambda: body(LEAST // LANES))
+
+
 def bin_sides_kernel(got, _, behind, rows_of):
     height, width, radial = behind.shape
-    packed = behind_of(got, 0, 2, rows_of, height=height, width=width, radial=radial)
-    for row, values in enumerate(column_rows(packed, 0, height)):
-        behind[row] = values
+
+    def body(runs):
+        packed = behind_of(got, 0, 2, runs, rows_of, height=height, width=width, radial=radial)
+        for row, values in enumerate(column_rows(packed, 0, height)):
+            behind[row] = values
+
+    for_load(body)
 
 
 def bin_rest_kernel(got, density, behind, upstream, rows_of):
     height, width, radial = behind.shape
     sub = sublane(radial)
-    packed = behind_of(got, 1, 2, rows_of, height=height, width=width, radial=radial)
-    for row, values in enumerate(column_rows(packed, 1, height)):
-        upstream[row] = density[row] * jnp.where((sub < 2) | (sub >= 6), behind[row], values)
+
+    def body(runs):
+        packed = behind_of(got, 1, 2, runs, rows_of, height=height, width=width, radial=radial)
+        for row, values in enumerate(column_rows(packed, 1, height)):
+            upstream[row] = density[row] * jnp.where((sub < 2) | (sub >= 6), behind[row], values)
+
+    for_load(body)
 
 
 def mirror(stencils):

time: 33.1 us -> 31.9 us (0.964)
  starting transfers between devices: 15.3 us -> 14.6 us
  waiting for transfers between devices: 7.83 us -> 7.3 us
    ppermute x8, starting transfers between devices: 12.2 us -> 11.5 us  [swap(): lax.ppermute(values, axis, both_ways(pairs))]
    ppermute x8, waiting for transfers between devices: 5.1 us -> 4.57 us  [swap(): lax.ppermute(values, axis, both_ways(pairs))]
  transfers between devices with their start and end apart: 9 -> 9, of which waited for: 3 -> 3; matrix products, arithmetic and copies ran while one was open for 1% -> 1% of each run, Pallas kernels for 18% -> 19%
where the time goes in v17:
time: 31.9 us; the launch traced here: 31.7 us
  starting transfers between devices  14.6 us (46%)
  Pallas kernels  9.21 us (29%)
  waiting for transfers between devices  7.3 us (23%)
    ppermute x8, starting transfers between devices, swap(): lax.ppermute(values, axis, both_ways(pairs))  11.5 us
    pallas_call x7, Pallas kernels, call(): pl.pallas_call(kernel, out_shape=outs, in_specs=[VMEM] * len(operands), o...  6.78 us
    ppermute x8, waiting for transfers between devices, swap(): lax.ppermute(values, axis, both_ways(pairs))  4.57 us
    all_to_all x1, starting transfers between devices, on_device(): lax.all_to_all(packed, ('lat', 'lon'), split_axis=0, concat_axis=0, tiled...  3.09 us
    all_to_all x1, waiting for transfers between devices, on_device(): lax.all_to_all(packed, ('lat', 'lon'), split_axis=0, concat_axis=0, tiled...  2.73 us
    pallas_call x1, Pallas kernels, on_device(): pl.pallas_call(open_kernel, out_shape=(jax.ShapeDtypeStruct((shards, 2 *...  1.76 us
    pallas_call x1, Pallas kernels, on_device(): pl.pallas_call(close_kernel, out_shape=tile, in_specs=[VMEM] * 3, out_spe...  0.67 us
  transfers between devices with their start and end apart: 9, of which 3 were waited for; matrix products, arithmetic and copies ran while one was open for 1% of the time, Pallas kernels for 19%

profile of v17, /device:TPU:2, one launch (start us, length us, event | category | flops | bytes accessed | tf_op | source)
XLA Modules:
  0.0 31.7 jit_solution(3917753679804487597)
XLA Ops:
  0.0 1.8 %opening.1 = (f32[32,8,128]{2,1,0:T(8,128)}, f32[8,8,512]{2,1,0:T(8,128)S(1)}, f32[2,8,512]{2,1,0:T(8,128)S(1)}, f32[2,8,512]{2,1,0:T(8,128)S(1)}) custom-call(s32[1,32]{1,0:T(1,128)} %counts_in.1, s32[1,32]{1,0:T(1,128)} %offsets_in.1, f32[128,128]{1,0:T(8,128)} %bitcast.20, s32[128,128]{1,0:T(8,128)} %bitcast.21, s32[128,128]{1,0:T(8,128)} %bitcast.22, ...), custom_call_target="tpu_custom_call" | custom-call | tf_op jit(solution)/shard_map/opening/pallas_call | solution.py:429
  1.8 0.1 collective-permute-start
  1.9 3.7 %collective-permute-start.1 = (f32[2,8,512]{2,1,0:T(8,128)S(1)}, f32[2,8,512]{2,1,0:T(8,128)S(1)}, u32[]{:S(2)}, u32[]{:S(2)}) collective-permute-start(f32[2,8,512]{2,1,0:T(8,128)S(1)} %get-tuple-element.22), channel_id=1, source_target_pairs={{1,2},{3,4},{5,6},{7,0},{2,1},{4,3},{6,5},{0,7},{9,10},{11,12},{13... | collective-permute-start | bytes 98312 | tf_op jit(solution)/shard_map/ppermute | solution.py:407
  5.6 3.1 %all-to-all-start = ((f32[32,8,128]{2,1,0:T(8,128)}), f32[32,8,128]{2,1,0:T(8,128)S(1)}, u32[]{:S(2)}, u32[]{:S(2)}) async-start(f32[32,8,128]{2,1,0:T(8,128)} %get-tuple-element.19), calls=%async_computation | async-start | bytes 262144 | tf_op jit(solution)/shard_map/all_to_all | solution.py:444
  8.7 0.1 slice_bitcast_fusion.1
  8.8 0.0 collective-permute-done.1.side_1
  8.8 3.4 %collective-permute-start.2 = (f32[3,8,512]{2,1,0:T(8,128)S(1)}, f32[3,8,512]{2,1,0:T(8,128)S(1)}, u32[]{:S(2)}, u32[]{:S(2)}) collective-permute-start(f32[3,8,512]{2,1,0:T(8,128)S(1)} %get-tuple-element.23), channel_id=1, source_target_pairs={{8,16},{16,8},{9,17},{17,9},{10,18},{18,10},{11,19},{19,11},{12,20... | collective-permute-start | bytes 147464 | tf_op jit(solution)/shard_map/ppermute | solution.py:407
  12.2 0.1 collective-permute-start.3
  12.3 0.1 pad_bitcast_fusion
  12.4 0.7 %density_inside.1 = (f32[4,8,512]{2,1,0:T(8,128)S(1)}, f32[3,3,6,8,512]{4,3,2,1,0:T(8,128)S(1)}) custom-call(f32[8,8,512]{2,1,0:T(8,128)S(1)} %get-tuple-element.20.field.latent, f32[2,8,512]{2,1,0:T(8,128)S(1)} %collective-permute-done.side_0, f32[2,8,512]{2,1,0:T(8,128)S(1)} %collective-permute-done.1.side_1, f32[2,27,512]{2,1,0:T(8,128)S(1)} %copy.18.stencils), custom_call_target="tpu_custom_call" | custom-call | tf_op jit(solution)/shard_map/density_inside/pallas_call | solution.py:453
  13.1 2.7 %all-to-all-done.got = f32[32,8,128]{2,1,0:T(8,128)S(1)} async-done(((f32[32,8,128]{2,1,0:T(8,128)}), f32[32,8,128]{2,1,0:T(8,128)S(1)}, u32[]{:S(2)}, u32[]{:S(2)}) %all-to-all-start) | async-done | bytes 131104 | tf_op jit(solution)/shard_map/all_to_all | solution.py:444
  15.9 2.2 %bin_sides.1.behind = f32[8,8,512]{2,1,0:T(8,128)S(1)} custom-call(f32[32,8,128]{2,1,0:T(8,128)S(1)} %all-to-all-done.got, f32[4,8,512]{2,1,0:T(8,128)S(1)} %get-tuple-element.26._.inner), custom_call_target="tpu_custom_call" | custom-call | tf_op jit(solution)/shard_map/bin_sides/pallas_call | solution.py:453
  18.0 0.0 collective-permute-done.2.end_1
  18.1 0.5 %density_ends.1 = (f32[8,8,512]{2,1,0:T(8,128)S(1)}, f32[2,8,512]{2,1,0:T(8,128)S(1)}, f32[2,8,512]{2,1,0:T(8,128)S(1)}) custom-call(f32[8,8,512]{2,1,0:T(8,128)S(1)} %get-tuple-element.20.field.latent, f32[2,8,512]{2,1,0:T(8,128)S(1)} %collective-permute-done.side_0, f32[2,8,512]{2,1,0:T(8,128)S(1)} %collective-permute-done.1.side_1, ...), custom_call_target="tpu_custom_call" | custom-call | tf_op jit(solution)/shard_map/density_ends/pallas_call | solution.py:453
  18.6 0.8 %collective-permute-start.4 = (f32[2,8,512]{2,1,0:T(8,128)S(1)}, f32[2,8,512]{2,1,0:T(8,128)S(1)}, u32[]{:S(2)}, u32[]{:S(2)}) collective-permute-start(f32[2,8,512]{2,1,0:T(8,128)S(1)} %get-tuple-element.28), channel_id=1, source_target_pairs={{1,2},{3,4},{5,6},{7,0},{2,1},{4,3},{6,5},{0,7},{9,10},{11,12},{13... | collective-permute-start | bytes 98312 | tf_op jit(solution)/shard_map/ppermute | solution.py:407
  19.5 0.1 pad_maximum_fusion
  19.6 2.2 %bin_rest.1.field = f32[8,8,512]{2,1,0:T(8,128)S(1)} custom-call(f32[32,8,128]{2,1,0:T(8,128)S(1)} %all-to-all-done.got, f32[8,8,512]{2,1,0:T(8,128)S(1)} %get-tuple-element.27.density, f32[8,8,512]{2,1,0:T(8,128)S(1)} %bin_sides.1.behind), custom_call_target="tpu_custom_call" | custom-call | tf_op jit(solution)/shard_map/bin_rest/pallas_call | solution.py:453
  21.8 2.1 %collective-permute-done.4.side_1 = f32[2,8,512]{2,1,0:T(8,128)S(1)} collective-permute-done((f32[2,8,512]{2,1,0:T(8,128)S(1)}, f32[2,8,512]{2,1,0:T(8,128)S(1)}, u32[]{:S(2)}, u32[]{:S(2)}) %collective-permute-start.4) | collective-permute-done | bytes 32800 | tf_op jit(solution)/shard_map/ppermute | solution.py:407
  23.8 0.4 %back_reach.1 = (f32[2,8,512]{2,1,0:T(8,128)S(1)}, f32[2,8,512]{2,1,0:T(8,128)S(1)}, f32[3,3,4,8,512]{4,3,2,1,0:T(8,128)S(1)}) custom-call(f32[8,8,512]{2,1,0:T(8,128)S(1)} %bin_rest.1.field, f32[2,8,512]{2,1,0:T(8,128)S(1)} %collective-permute-done.4.side_1, f32[2,8,512]{2,1,0:T(8,128)S(1)} %collective-permute-done.5.side_0, f32[2,27,512]{2,1,0:T(8,128)S(1)} %rev.8.stencils), custom_call_target="tpu_custom_call" | custom-call | tf_op jit(solution)/shard_map/back_reach/pallas_call | solution.py:453
  24.2 0.1 collective-permute-start.6
  24.3 3.4 %collective-permute-start.7 = (f32[2,8,512]{2,1,0:T(8,128)S(1)}, f32[2,8,512]{2,1,0:T(8,128)S(1)}, u32[]{:S(2)}, u32[]{:S(2)}) collective-permute-start(f32[2,8,512]{2,1,0:T(8,128)S(1)} %get-tuple-element.32), channel_id=1, source_target_pairs={{8,16},{16,8},{9,17},{17,9},{10,18},{18,10},{11,19},{19,11},{12,20... | collective-permute-start | bytes 98312 | tf_op jit(solution)/shard_map/ppermute | solution.py:407
  27.7 0.8 %back_own.1.own = f32[8,8,512]{2,1,0:T(8,128)S(1)} custom-call(f32[8,8,512]{2,1,0:T(8,128)S(1)} %bin_rest.1.field, f32[2,8,512]{2,1,0:T(8,128)S(1)} %collective-permute-done.4.side_1, f32[2,8,512]{2,1,0:T(8,128)S(1)} %collective-permute-done.5.side_0, f32[2,27,512]{2,1,0:T(8,128)S(1)} %rev.8.stencils, f32[8,8,512]{2,1,0:T(8,128)S(1)} %get-tuple-element.20.field.latent, ...), custom_call_target="tpu_custom_call" | custom-call | tf_op jit(solution)/shard_map/back_own/pallas_call | solution.py:453
  28.5 2.5 %collective-permute-done.7.end_1 = f32[2,8,512]{2,1,0:T(8,128)S(1)} collective-permute-done((f32[2,8,512]{2,1,0:T(8,128)S(1)}, f32[2,8,512]{2,1,0:T(8,128)S(1)}, u32[]{:S(2)}, u32[]{:S(2)}) %collective-permute-start.7) | collective-permute-done | bytes 32800 | tf_op jit(solution)/shard_map/ppermute | solution.py:407
  31.0 0.7 %close.1 = f32[8,8,512]{2,1,0:T(8,128)} custom-call(f32[8,8,512]{2,1,0:T(8,128)S(1)} %back_own.1.own, f32[2,8,512]{2,1,0:T(8,128)S(1)} %collective-permute-done.6.end_0, f32[2,8,512]{2,1,0:T(8,128)S(1)} %collective-permute-done.7.end_1), custom_call_target="tpu_custom_call" | custom-call | tf_op jit(solution)/shard_map/close/pallas_call | solution.py:491
  (13 shorter events, 0.1 us)
Async XLA Ops:
  1.8 7.0 %collective-permute-start = (f32[2,8,512]{2,1,0:T(8,128)S(1)}, f32[2,8,512]{2,1,0:T(8,128)S(1)}, u32[]{:S(2)}, u32[]{:S(2)}) collective-permute-start(f32[2,8,512]{2,1,0:T(8,128)S(1)} %get-tuple-element.21), channel_id=1, source_target_pairs={{0,1},{2,3},{4,5},{6,7},{1,0},{3,2},{5,4},{7,6},{8,9},{10,11},{12,... | collective-permute-start | bytes 98312 | tf_op jit(solution)/shard_map/ppermute | solution.py:407
  1.9 6.9 %collective-permute-start.1 = (f32[2,8,512]{2,1,0:T(8,128)S(1)}, f32[2,8,512]{2,1,0:T(8,128)S(1)}, u32[]{:S(2)}, u32[]{:S(2)}) collective-permute-start(f32[2,8,512]{2,1,0:T(8,128)S(1)} %get-tuple-element.22), channel_id=1, source_target_pairs={{1,2},{3,4},{5,6},{7,0},{2,1},{4,3},{6,5},{0,7},{9,10},{11,12},{13... | collective-permute-start | bytes 98312 | tf_op jit(solution)/shard_map/ppermute | solution.py:407
  5.6 3.1 %copy-start = (f32[2,27,512]{2,0,1:T(2,128)S(1)}, f32[2,27,512]{2,0,1:T(2,128)}, u32[]{:S(2)}) copy-start(f32[2,27,512]{2,0,1:T(2,128)} %param.13) | copy-start | bytes 331780
  5.6 10.3 %all-to-all-start = ((f32[32,8,128]{2,1,0:T(8,128)}), f32[32,8,128]{2,1,0:T(8,128)S(1)}, u32[]{:S(2)}, u32[]{:S(2)}) async-start(f32[32,8,128]{2,1,0:T(8,128)} %get-tuple-element.19), calls=%async_computation | async-start | bytes 262144 | tf_op jit(solution)/shard_map/all_to_all | solution.py:444
  8.8 9.2 %collective-permute-start.2 = (f32[3,8,512]{2,1,0:T(8,128)S(1)}, f32[3,8,512]{2,1,0:T(8,128)S(1)}, u32[]{:S(2)}, u32[]{:S(2)}) collective-permute-start(f32[3,8,512]{2,1,0:T(8,128)S(1)} %get-tuple-element.23), channel_id=1, source_target_pairs={{8,16},{16,8},{9,17},{17,9},{10,18},{18,10},{11,19},{19,11},{12,20... | collective-permute-start | bytes 147464 | tf_op jit(solution)/shard_map/ppermute | solution.py:407
  12.2 5.8 %collective-permute-start.3 = (f32[3,8,512]{2,1,0:T(8,128)S(1)}, f32[3,8,512]{2,1,0:T(8,128)S(1)}, u32[]{:S(2)}, u32[]{:S(2)}) collective-permute-start(f32[3,8,512]{2,1,0:T(8,128)S(1)} %get-tuple-element.24), channel_id=1, source_target_pairs={{0,8},{16,24},{8,0},{24,16},{1,9},{17,25},{9,1},{25,17},{2,10},{18... | collective-permute-start | bytes 147464 | tf_op jit(solution)/shard_map/ppermute | solution.py:407
  18.6 5.2 %collective-permute-start.4 = (f32[2,8,512]{2,1,0:T(8,128)S(1)}, f32[2,8,512]{2,1,0:T(8,128)S(1)}, u32[]{:S(2)}, u32[]{:S(2)}) collective-permute-start(f32[2,8,512]{2,1,0:T(8,128)S(1)} %get-tuple-element.28), channel_id=1, source_target_pairs={{1,2},{3,4},{5,6},{7,0},{2,1},{4,3},{6,5},{0,7},{9,10},{11,12},{13... | collective-permute-start | bytes 98312 | tf_op jit(solution)/shard_map/ppermute | solution.py:407
  19.5 4.4 %collective-permute-start.5 = (f32[2,8,512]{2,1,0:T(8,128)S(1)}, f32[2,8,512]{2,1,0:T(8,128)S(1)}, u32[]{:S(2)}, u32[]{:S(2)}) collective-permute-start(f32[2,8,512]{2,1,0:T(8,128)S(1)} %get-tuple-element.29), channel_id=1, source_target_pairs={{0,1},{2,3},{4,5},{6,7},{1,0},{3,2},{5,4},{7,6},{8,9},{10,11},{12,... | collective-permute-start | bytes 98312 | tf_op jit(solution)/shard_map/ppermute | solution.py:407
  24.2 4.3 %collective-permute-start.6 = (f32[2,8,512]{2,1,0:T(8,128)S(1)}, f32[2,8,512]{2,1,0:T(8,128)S(1)}, u32[]{:S(2)}, u32[]{:S(2)}) collective-permute-start(f32[2,8,512]{2,1,0:T(8,128)S(1)} %get-tuple-element.31), channel_id=1, source_target_pairs={{0,8},{16,24},{8,0},{24,16},{1,9},{17,25},{9,1},{25,17},{2,10},{18... | collective-permute-start | bytes 98312 | tf_op jit(solution)/shard_map/ppermute | solution.py:407
  24.3 6.7 %collective-permute-start.7 = (f32[2,8,512]{2,1,0:T(8,128)S(1)}, f32[2,8,512]{2,1,0:T(8,128)S(1)}, u32[]{:S(2)}, u32[]{:S(2)}) collective-permute-start(f32[2,8,512]{2,1,0:T(8,128)S(1)} %get-tuple-element.32), channel_id=1, source_target_pairs={{8,16},{16,8},{9,17},{17,9},{10,18},{18,10},{11,19},{19,11},{12,20... | collective-permute-start | bytes 98312 | tf_op jit(solution)/shard_map/ppermute | solution.py:407

commit v18 on v17

--- a/solution.py
+++ b/solution.py
@@ -57,23 +57,37 @@
     return tiles
 
 
+def pack_four(rows, to_partner, to_outer):
+    _, odd = position("lon")
+    sub = sublane(rows[0].shape[1])
+    for group in range(len(rows) // 2):
+        one, two = rows[2 * group], pltpu.roll(rows[2 * group + 1], 4, 0)
+        before, after = jnp.where(sub < 4, one, two), jnp.where(sub < 4, two, one)
+        to_partner[group] = either(odd, before, after)
+        to_outer[group] = either(odd, after, before)
+
+
+def unpack_four(from_partner, from_outer, height):
+    _, odd = position("lon")
+    sub = sublane(from_partner.shape[2])
+    tiles = []
+    for group in range(height // 2):
+        partner, outer = from_partner[group], from_outer[group]
+        before, after = either(odd, partner, outer), either(odd, outer, partner)
+        tiles.append(jnp.where(sub < 4, after, before))
+        tiles.append(pltpu.roll(jnp.where(sub < 4, before, after), 4, 0))
+    return tiles
+
+
 def pack_ends_kernel(field, side_0, side_1, to_partner, to_outer):
-    height, _, radial = field.shape
+    height = field.shape[0]
     _, odd = position("lat")
-    sub = sublane(radial)
-    outside = (sub < 2) | (sub >= 6)
-    tiles = unpack_sides(side_0, side_1, height)
-
-    def ends(first):
-        return (
-            field[first],
-            field[first + 1],
-            jnp.where(outside, tiles[first], pltpu.roll(tiles[first + 1], 4, 0)),
-        )
-
-    for place, (top, bottom) in enumerate(zip(ends(0), ends(height - 2))):
-        to_partner[place] = either(odd, top, bottom)
-        to_outer[place] = either(odd, bottom, top)
+    tiles = unpack_four(side_0, side_1, height)
+    top = [field[0], field[1], tiles[0], tiles[1]]
+    bottom = [field[height - 2], field[height - 1], tiles[height - 2], tiles[height - 1]]
+    for place, (one, two) in enumerate(zip(top, bottom)):
+        to_partner[place] = either(odd, one, two)
+        to_outer[place] = either(odd, two, one)
 
 
 def radial_shifts(field):
@@ -120,9 +134,10 @@
             value = whole[1] + pltpu.roll(whole[0], 1, 0) + pltpu.roll(whole[2], cols - 1, 0)
             if real[place] is not None:
                 value = either(real[place], value, jnp.zeros_like(value))
-            middle[0, 1, place, :, at] = pltpu.roll(value, 1, 0)[:SUBLANES]
-            middle[1, 1, place, :, at] = value[:SUBLANES]
-            middle[2, 1, place, :, at] = pltpu.roll(value, cols - 1, 0)[:SUBLANES]
+            kept = middle.shape[3]
+            middle[0, 1, place, :, at] = pltpu.roll(value, 1, 0)[:kept]
+            middle[1, 1, place, :, at] = value[:kept]
+            middle[2, 1, place, :, at] = pltpu.roll(value, cols - 1, 0)[:kept]
 
     tiles_of_bins(radial, body)
     for place in range(len(centers)):
@@ -131,59 +146,58 @@
                 middle[beside, step, place] = moved
 
 
-def second_level(coef, windows, radial, write):
+def second_level(coef, windows, radial, write, cols=SUBLANES):
     def body(at):
         taps = taps_of(coef, at)
         for row, around in windows.items():
-            total = None
-            for above, at_row in enumerate(around):
-                if at_row is None:
-                    continue
-                buffer, place = at_row
-                for beside in range(3):
-                    for step in range(3):
-                        term = taps[above * 9 + beside * 3 + step] * buffer[beside, step, place, :, at]
-                        total = term if total is None else total + term
-            write(row, at, total)
+            for start in range(0, cols, SUBLANES):
+                side = slice(start, start + SUBLANES)
+                total = None
+                for above, at_row in enumerate(around):
+                    if at_row is None:
+                        continue
+                    buffer, place = at_row
+                    for beside in range(3):
+                        for step in range(3):
+                            term = taps[above * 9 + beside * 3 + step] * buffer[beside, step, place, side, at]
+                            total = term if total is None else total + term
+                write(row, side, at, total)
 
     tiles_of_bins(radial, body)
 
 
-def fill_wide(wide, field, side_0, side_1, rows):
-    height, width, _ = field.shape
-    tiles = unpack_sides(side_0, side_1, height)
+def fill_wide(wide, field, tiles, rows):
+    width = field.shape[1]
     for row in rows:
         wide[row, :width] = field[row]
         wide[row, width:] = tiles[row]
 
 
 def density_inside_kernel(field, side_0, side_1, stencils, out, middle, wide, shifted):
-    height, width, radial = field.shape
-    fill_wide(wide, field, side_0, side_1, range(height))
+    height, _, radial = field.shape
+    fill_wide(wide, field, unpack_four(side_0, side_1, height), range(height))
     centers = [(row, ALL) for row in range(1, height - 1)]
     first_level(wide, shifted, stencils.at[0], centers, middle, [None] * len(centers))
 
-    def write(row, at, value):
-        out[row - 2, :, at] = jnp.exp(value)
+    def write(row, side, at, value):
+        out[row - 2, side, at] = jnp.exp(value)
 
     windows = {row: [(middle, row - 2 + k) for k in range(3)] for row in range(2, height - 2)}
-    second_level(stencils.at[1], windows, radial, write)
+    second_level(stencils.at[1], windows, radial, write, wide.shape[1])
 
 
 def density_ends_kernel(
-    field, side_0, side_1, end_1, end_0, stencils, inside, inner, behind, out, to_partner, to_outer, middle, wide, shifted
+    field, side_0, side_1, end_1, end_0, stencils, inside, inner, _, out, middle, wide, shifted
 ):
     height, width, radial = field.shape
-    tiles = unpack_sides(side_0, side_1, height)
+    tiles = unpack_four(side_0, side_1, height)
     lat, odd = position("lat")
-    for place in range(3):
-        partner, outer = end_0[place], end_1[place]
-        for first, pack in ((0, either(odd, partner, outer)), (6, either(odd, outer, partner))):
-            if place < 2:
-                wide[first + place, :width] = pack
-            else:
-                wide[first, width:] = pack
-                wide[first + 1, width:] = pltpu.roll(pack, 4, 0)
+    for place in range(2):
+        for half in range(2):
+            partner, outer = end_0[2 * half + place], end_1[2 * half + place]
+            at = slice(half * width, (half + 1) * width)
+            wide[place, at] = either(odd, partner, outer)
+            wide[6 + place, at] = either(odd, outer, partner)
     for place, row in ((2, 0), (3, 1), (4, height - 2), (5, height - 1)):
         wide[place, :width] = field[row]
         wide[place, width:] = tiles[row]
@@ -192,31 +206,35 @@
     centers = [(row, ALL) for row in (1, 2, 5, 6)]
     first_level(wide, shifted, stencils.at[0], centers, middle, [above, None, None, below])
 
-    def write(row, at, value):
-        out[row, :, at] = jnp.exp(value)
+    def write(row, side, at, value):
+        out[row, side, at] = jnp.exp(value)
 
     last = height - 3
     top = [(middle, 0), (middle, 1), (inside, 0), (inside, 1)]
     bottom = [(inside, last - 1), (inside, last), (middle, 2), (middle, 3)]
     windows = {0: top[:3], 1: top[1:], height - 2: bottom[:3], height - 1: bottom[1:]}
-    second_level(stencils.at[1], windows, radial, write)
+    second_level(stencils.at[1], windows, radial, write, wide.shape[1])
     for row in range(2, height - 2):
         out[row] = inner[row - 2]
-    pack_sides([out[row] * behind[row] for row in range(height)], to_partner, to_outer)
-
-
-def back_reach_kernel(field, side_1, side_0, stencils, to_partner, to_outer, middle, wide, shifted, reach):
+
+
+def beside_tiles(side_0, side_1, density):
+    tiles = unpack_sides(side_0, side_1, density.shape[0])
+    return [tile * density[row, SUBLANES:] for row, tile in enumerate(tiles)]
+
+
+def back_reach_kernel(field, side_1, side_0, density, stencils, to_partner, to_outer, middle, wide, shifted, reach):
     height, _, radial = field.shape
     last = height - 1
-    fill_wide(wide, field, side_0, side_1, (0, 1, last - 1, last))
+    fill_wide(wide, field, beside_tiles(side_0, side_1, density), (0, 1, last - 1, last))
     lat, odd = position("lat")
     above = (lat > 0).astype(jnp.int32)
     below = (lat < lax.axis_size("lat") - 1).astype(jnp.int32)
     centers = [(-1, (1,)), (0, (0, 1)), (last, (-1, 0)), (last + 1, (-1,))]
     first_level(wide, shifted, stencils.at[0], centers, middle, [above, None, None, below])
 
-    def write(row, at, value):
-        reach[row, :, at] = value
+    def write(row, side, at, value):
+        reach[row, side, at] = value
 
     windows = {
         0: [None, None, (middle, 0)],
@@ -230,14 +248,14 @@
         to_outer[place] = either(odd, reach[2 + place], reach[place])
 
 
-def back_own_kernel(field, side_1, side_0, stencils, latent, edge, out, wide, shifted, middle):
+def back_own_kernel(field, side_1, side_0, density, stencils, latent, edge, out, wide, shifted, middle):
     height, _, radial = field.shape
-    fill_wide(wide, field, side_0, side_1, range(height))
+    fill_wide(wide, field, beside_tiles(side_0, side_1, density), range(height))
     centers = [(row, ALL) for row in range(1, height - 1)]
     first_level(wide, shifted, stencils.at[0], centers, middle, [None] * len(centers))
 
-    def write(row, at, value):
-        out[row, :, at] = latent[row, :, at] + value
+    def write(row, side, at, value):
+        out[row, side, at] = latent[row, side, at] + value
 
     line = [(edge, 0), (edge, 1)] + [(middle, place) for place in range(height - 2)] + [(edge, 2), (edge, 3)]
     second_level(stencils.at[1], {row: line[row:row + 3] for row in range(height)}, radial, write)
@@ -292,7 +310,7 @@
         out[owner] = jnp.where(slot < counts[0, owner], joined, 0.0)
 
     copies[-1].wait()
-    pack_sides([latent[row] for row in range(height)], to_partner, to_outer)
+    pack_four([latent[row] for row in range(height)], to_partner, to_outer)
 
 
 def behind_of(got, part, cuts, runs, rows_of, *, height, width, radial):
@@ -364,13 +382,15 @@
     pl.when(jnp.logical_not(middle))(lambda: body(LEAST // LANES))
 
 
-def bin_sides_kernel(got, _, behind, rows_of):
+def bin_sides_kernel(got, _, behind, to_partner, to_outer, rows_of):
     height, width, radial = behind.shape
 
     def body(runs):
         packed = behind_of(got, 0, 2, runs, rows_of, height=height, width=width, radial=radial)
-        for row, values in enumerate(column_rows(packed, 0, height)):
+        lines = column_rows(packed, 0, height)
+        for row, values in enumerate(lines):
             behind[row] = values
+        pack_sides(lines, to_partner, to_outer)
 
     for_load(body)
 
@@ -382,7 +402,7 @@
     def body(runs):
         packed = behind_of(got, 1, 2, runs, rows_of, height=height, width=width, radial=radial)
         for row, values in enumerate(column_rows(packed, 1, height)):
-            upstream[row] = density[row] * jnp.where((sub < 2) | (sub >= 6), behind[row], values)
+            upstream[row] = density[row, :width] * jnp.where((sub < 2) | (sub >= 6), behind[row], values)
 
     for_load(body)
 
@@ -421,14 +441,15 @@
     i32 = jnp.int32
     tile = jax.ShapeDtypeStruct((height, width, radial), f32)
     sides = jax.ShapeDtypeStruct((height // 4, SUBLANES, radial), f32)
-    ends = jax.ShapeDtypeStruct((3, SUBLANES, radial), f32)
+    ends = jax.ShapeDtypeStruct((4, SUBLANES, radial), f32)
 
     def table(values):
         return values.reshape(slots // LANES, LANES)
 
+    four = jax.ShapeDtypeStruct((height // 2, SUBLANES, radial), f32)
     packed, latent, *to_sides = pl.pallas_call(
         open_kernel,
-        out_shape=(jax.ShapeDtypeStruct((shards, 2 * RUNS, LANES), f32), tile, sides, sides),
+        out_shape=(jax.ShapeDtypeStruct((shards, 2 * RUNS, LANES), f32), tile, four, four),
         in_specs=[HBM] * 6,
         out_specs=(VMEM, VMEM, VMEM, VMEM),
         scratch_shapes=[pltpu.SMEM((1, shards), i32)] * 2
@@ -446,7 +467,7 @@
     rows = pltpu.VMEM((height, 2 * width, radial), f32)
     moved = pltpu.VMEM((2, height, 2 * width, radial), f32)
     edge = (3, 3, 4, width, radial)
-    star_rows = pltpu.VMEM((3, shards * 2 * RUNS, LANES), f32)
+    star_rows = [pltpu.VMEM((3, shards * 2 * RUNS, LANES), f32)]
     inner_rows = (3, 3, height - 2, width, radial)
 
     def call(kernel, name, outs, scratch, *operands):
@@ -466,27 +487,30 @@
     beside = swap(*to_sides, "lon", True)
     to_ends = call(pack_ends_kernel, "density_pack", (ends, ends), [], latent, *beside)
     above = swap(*to_ends, "lat", False, outer_first=True)
+    broad = 2 * width
     inner, middle = call(
-        density_inside_kernel, "density_inside", (shape(height - 4, width, radial), shape(*inner_rows)), [rows, moved],
+        density_inside_kernel, "density_inside",
+        (shape(height - 4, broad, radial), shape(3, 3, height - 2, broad, radial)), [rows, moved],
         latent, *beside, stencils,
     )
-    behind = call(bin_sides_kernel, "bin_sides", tile, [star_rows], got, inner)
-    density, *to_sides = call(
-        density_ends_kernel, "density_ends", (tile, sides, sides), [pltpu.VMEM(edge, f32), rows, moved],
+    behind, *to_sides = call(bin_sides_kernel, "bin_sides", (tile, sides, sides), star_rows, got, inner)
+    density = call(
+        density_ends_kernel, "density_ends", shape(height, broad, radial),
+        [pltpu.VMEM((3, 3, 4, broad, radial), f32), rows, moved],
         latent, *beside, *above[::-1], stencils, middle, inner, behind,
     )
-    upstream = call(bin_rest_kernel, "bin_rest", tile, [star_rows], got, density, behind)
+    upstream = call(bin_rest_kernel, "bin_rest", tile, star_rows, got, density, behind)
 
     mirrored = mirror(stencils)[::-1]
     beside = swap(*to_sides, "lon", True, outer_first=True)
     *to_ends, middle = call(
         back_reach_kernel, "back_reach", (shape(2, width, radial), shape(2, width, radial), shape(*edge)),
-        [rows, moved, pltpu.VMEM((4, width, radial), f32)], upstream, *beside[::-1], mirrored,
+        [rows, moved, pltpu.VMEM((4, width, radial), f32)], upstream, *beside[::-1], density, mirrored,
     )
     above = swap(*to_ends, "lat", False)
     own = call(
         back_own_kernel, "back_own", tile, [rows, moved, pltpu.VMEM(inner_rows, f32)],
-        upstream, *beside[::-1], mirrored, latent, middle,
+        upstream, *beside[::-1], density, mirrored, latent, middle,
     )
     return pl.pallas_call(
         close_kernel,

time: 31.9 us -> 31.6 us (level)
  waiting for transfers between devices: 7.3 us -> 3.32 us
  local copies, waits for them, and re-layouts: 0.26 us -> 2.06 us
  starting transfers between devices: 14.6 us -> 16.2 us
  Pallas kernels: 9.21 us -> 9.56 us
    ppermute x8, waiting for transfers between devices: 4.57 us -> 2.54 us  [swap(): lax.ppermute(values, axis, both_ways(pairs))]
    all_to_all x1, waiting for transfers between devices: 2.73 us -> 0.78 us  [on_device(): lax.all_to_all(packed, ('lat', 'lon'), split_axis=0, concat_axis=0, tiled...]
    ppermute x8, starting transfers between devices: 11.5 us -> 13.1 us  [swap(): lax.ppermute(values, axis, both_ways(pairs))]
    rev x1, local copies, waits for them, and re-layouts: 0.01 us -> 0.91 us  [mirror(): jnp.flip(stencils, axis=1)]
    unnamed x3 -> x1, local copies, waits for them, and re-layouts: 0.03 us -> 0.92 us
    pallas_call x7, Pallas kernels: 6.78 us -> 7.12 us  [call(): pl.pallas_call(kernel, out_shape=outs, in_specs=[VMEM] * len(operands), o...]
  transfers between devices with their start and end apart: 9 -> 9, of which waited for: 3 -> 2; matrix products, arithmetic and copies ran while one was open for 1% -> 7% of each run, Pallas kernels for 19% -> 22%
where the time goes in v18:
time: 31.6 us; the launch traced here: 31.4 us
  starting transfers between devices  16.2 us (51%)
  Pallas kernels  9.56 us (30%)
  waiting for transfers between devices  3.32 us (11%)
  local copies, waits for them, and re-layouts  2.06 us (7%)
    ppermute x8, starting transfers between devices, swap(): lax.ppermute(values, axis, both_ways(pairs))  13.1 us
    pallas_call x7, Pallas kernels, call(): pl.pallas_call(kernel, out_shape=outs, in_specs=[VMEM] * len(operands), o...  7.12 us
    all_to_all x1, starting transfers between devices, on_device(): lax.all_to_all(packed, ('lat', 'lon'), split_axis=0, concat_axis=0, tiled...  3.09 us
    ppermute x8, waiting for transfers between devices, swap(): lax.ppermute(values, axis, both_ways(pairs))  2.54 us
    pallas_call x1, Pallas kernels, on_device(): pl.pallas_call(open_kernel, out_shape=(jax.ShapeDtypeStruct((shards, 2 *...  1.76 us
    unnamed x1, local copies, waits for them, and re-layouts  0.92 us
    rev x1, local copies, waits for them, and re-layouts, mirror(): jnp.flip(stencils, axis=1)  0.91 us
    all_to_all x1, waiting for transfers between devices, on_device(): lax.all_to_all(packed, ('lat', 'lon'), split_axis=0, concat_axis=0, tiled...  0.78 us
  transfers between devices with their start and end apart: 9, of which 2 were waited for; matrix products, arithmetic and copies ran while one was open for 7% of the time, Pallas kernels for 22%

profile of v18, /device:TPU:2, one launch (start us, length us, event | category | flops | bytes accessed | tf_op | source)
XLA Modules:
  0.0 31.4 jit_solution(5263583406810280970)
XLA Ops:
  0.0 1.8 %opening.1 = (f32[32,8,128]{2,1,0:T(8,128)}, f32[8,8,512]{2,1,0:T(8,128)S(1)}, f32[4,8,512]{2,1,0:T(8,128)S(1)}, f32[4,8,512]{2,1,0:T(8,128)S(1)}) custom-call(s32[1,32]{1,0:T(1,128)} %counts_in.1, s32[1,32]{1,0:T(1,128)} %offsets_in.1, f32[128,128]{1,0:T(8,128)} %bitcast.20, s32[128,128]{1,0:T(8,128)} %bitcast.21, s32[128,128]{1,0:T(8,128)} %bitcast.22, ...), custom_call_target="tpu_custom_call" | custom-call | tf_op jit(solution)/shard_map/opening/pallas_call | solution.py:450
  1.8 0.1 collective-permute-start
  1.9 3.7 %collective-permute-start.1 = (f32[4,8,512]{2,1,0:T(8,128)S(1)}, f32[4,8,512]{2,1,0:T(8,128)S(1)}, u32[]{:S(2)}, u32[]{:S(2)}) collective-permute-start(f32[4,8,512]{2,1,0:T(8,128)S(1)} %get-tuple-element.22), channel_id=1, source_target_pairs={{1,2},{3,4},{5,6},{7,0},{2,1},{4,3},{6,5},{0,7},{9,10},{11,12},{13... | collective-permute-start | bytes 196616 | tf_op jit(solution)/shard_map/ppermute | solution.py:427
  5.6 3.1 %all-to-all-start = ((f32[32,8,128]{2,1,0:T(8,128)}), f32[32,8,128]{2,1,0:T(8,128)S(1)}, u32[]{:S(2)}, u32[]{:S(2)}) async-start(f32[32,8,128]{2,1,0:T(8,128)} %get-tuple-element.19), calls=%async_computation | async-start | bytes 262144 | tf_op jit(solution)/shard_map/all_to_all | solution.py:465
  8.7 0.9 %copy.18.stencils = f32[2,27,512]{2,1,0:T(8,128)S(1)} copy(f32[2,27,512]{2,0,1:T(2,128)} %param.13) | data formatting | bytes 221184 | tf_op args[6]
  9.6 0.9 %rev.7 = f32[2,27,512]{2,0,1:T(2,128)S(1)} reverse(f32[2,27,512]{2,0,1:T(2,128)} %param.13), dimensions={1} | reverse | bytes 221184 | tf_op jit(solution)/shard_map/jit(_flip)/rev | solution.py:411
  10.5 0.1 slice_bitcast_fusion.1
  10.6 0.1 pad_bitcast_fusion
  10.8 3.4 %collective-permute-start.2 = (f32[4,8,512]{2,1,0:T(8,128)S(1)}, f32[4,8,512]{2,1,0:T(8,128)S(1)}, u32[]{:S(2)}, u32[]{:S(2)}) collective-permute-start(f32[4,8,512]{2,1,0:T(8,128)S(1)} %get-tuple-element.23), channel_id=1, source_target_pairs={{8,16},{16,8},{9,17},{17,9},{10,18},{18,10},{11,19},{19,11},{12,20... | collective-permute-start | bytes 196616 | tf_op jit(solution)/shard_map/ppermute | solution.py:427
  14.1 0.1 collective-permute-start.3
  14.2 0.9 %density_inside.1 = (f32[4,16,512]{2,1,0:T(8,128)S(1)}, f32[3,3,6,16,512]{4,3,2,1,0:T(8,128)S(1)}) custom-call(f32[8,8,512]{2,1,0:T(8,128)S(1)} %get-tuple-element.20.field.latent, f32[4,8,512]{2,1,0:T(8,128)S(1)} %collective-permute-done.side_0, f32[4,8,512]{2,1,0:T(8,128)S(1)} %collective-permute-done.1.side_1, f32[2,27,512]{2,1,0:T(8,128)S(1)} %copy.18.stencils), custom_call_target="tpu_custom_call" | custom-call | tf_op jit(solution)/shard_map/density_inside/pallas_call | solution.py:474
  15.1 0.8 %all-to-all-done.got = f32[32,8,128]{2,1,0:T(8,128)S(1)} async-done(((f32[32,8,128]{2,1,0:T(8,128)}), f32[32,8,128]{2,1,0:T(8,128)S(1)}, u32[]{:S(2)}, u32[]{:S(2)}) %all-to-all-start) | async-done | bytes 131104 | tf_op jit(solution)/shard_map/all_to_all | solution.py:465
  15.9 2.2 %bin_sides.1 = (f32[8,8,512]{2,1,0:T(8,128)S(1)}, f32[2,8,512]{2,1,0:T(8,128)S(1)}, f32[2,8,512]{2,1,0:T(8,128)S(1)}) custom-call(f32[32,8,128]{2,1,0:T(8,128)S(1)} %all-to-all-done.got, f32[4,16,512]{2,1,0:T(8,128)S(1)} %get-tuple-element.26._.inner), custom_call_target="tpu_custom_call" | custom-call | tf_op jit(solution)/shard_map/bin_sides/pallas_call | solution.py:474
  18.1 2.1 %collective-permute-start.4 = (f32[2,8,512]{2,1,0:T(8,128)S(1)}, f32[2,8,512]{2,1,0:T(8,128)S(1)}, u32[]{:S(2)}, u32[]{:S(2)}) collective-permute-start(f32[2,8,512]{2,1,0:T(8,128)S(1)} %get-tuple-element.28), channel_id=1, source_target_pairs={{1,2},{3,4},{5,6},{7,0},{2,1},{4,3},{6,5},{0,7},{9,10},{11,12},{13... | collective-permute-start | bytes 98312 | tf_op jit(solution)/shard_map/ppermute | solution.py:427
  20.2 0.1 pad_maximum_fusion
  20.3 0.7 %density_ends.1.density = f32[8,16,512]{2,1,0:T(8,128)S(1)} custom-call(f32[8,8,512]{2,1,0:T(8,128)S(1)} %get-tuple-element.20.field.latent, f32[4,8,512]{2,1,0:T(8,128)S(1)} %collective-permute-done.side_0, f32[4,8,512]{2,1,0:T(8,128)S(1)} %collective-permute-done.1.side_1, f32[4,8,512]{2,1,0:T(8,128)S(1)} %collective-permute-done.2.end_1, ...), custom_call_target="tpu_custom_call" | custom-call | tf_op jit(solution)/shard_map/density_ends/pallas_call | solution.py:474
  21.0 2.2 %bin_rest.1.field = f32[8,8,512]{2,1,0:T(8,128)S(1)} custom-call(f32[32,8,128]{2,1,0:T(8,128)S(1)} %all-to-all-done.got, f32[8,16,512]{2,1,0:T(8,128)S(1)} %density_ends.1.density, f32[8,8,512]{2,1,0:T(8,128)S(1)} %get-tuple-element.27._.behind), custom_call_target="tpu_custom_call" | custom-call | tf_op jit(solution)/shard_map/bin_rest/pallas_call | solution.py:474
  23.2 0.0 collective-permute-done.4.side_1
  23.3 0.4 %back_reach.1 = (f32[2,8,512]{2,1,0:T(8,128)S(1)}, f32[2,8,512]{2,1,0:T(8,128)S(1)}, f32[3,3,4,8,512]{4,3,2,1,0:T(8,128)S(1)}) custom-call(f32[8,8,512]{2,1,0:T(8,128)S(1)} %bin_rest.1.field, f32[2,8,512]{2,1,0:T(8,128)S(1)} %collective-permute-done.4.side_1, f32[2,8,512]{2,1,0:T(8,128)S(1)} %collective-permute-done.5.side_0, ...), custom_call_target="tpu_custom_call" | custom-call | tf_op jit(solution)/shard_map/back_reach/pallas_call | solution.py:474
  23.6 0.4 %collective-permute-start.6 = (f32[2,8,512]{2,1,0:T(8,128)S(1)}, f32[2,8,512]{2,1,0:T(8,128)S(1)}, u32[]{:S(2)}, u32[]{:S(2)}) collective-permute-start(f32[2,8,512]{2,1,0:T(8,128)S(1)} %get-tuple-element.31), channel_id=1, source_target_pairs={{0,8},{16,24},{8,0},{24,16},{1,9},{17,25},{9,1},{25,17},{2,10},{18... | collective-permute-start | bytes 98312 | tf_op jit(solution)/shard_map/ppermute | solution.py:427
  24.0 3.4 %collective-permute-start.7 = (f32[2,8,512]{2,1,0:T(8,128)S(1)}, f32[2,8,512]{2,1,0:T(8,128)S(1)}, u32[]{:S(2)}, u32[]{:S(2)}) collective-permute-start(f32[2,8,512]{2,1,0:T(8,128)S(1)} %get-tuple-element.32), channel_id=1, source_target_pairs={{8,16},{16,8},{9,17},{17,9},{10,18},{18,10},{11,19},{19,11},{12,20... | collective-permute-start | bytes 98312 | tf_op jit(solution)/shard_map/ppermute | solution.py:427
  27.4 0.8 %back_own.1.own = f32[8,8,512]{2,1,0:T(8,128)S(1)} custom-call(f32[8,8,512]{2,1,0:T(8,128)S(1)} %bin_rest.1.field, f32[2,8,512]{2,1,0:T(8,128)S(1)} %collective-permute-done.4.side_1, f32[2,8,512]{2,1,0:T(8,128)S(1)} %collective-permute-done.5.side_0, f32[8,16,512]{2,1,0:T(8,128)S(1)} %density_ends.1.density, f32[2,27,512]{2,1,0:T(8,128)S(1)} %rev.8.stencils, ...), custom_call_target="tpu_custom_call" | custom-call | tf_op jit(solution)/shard_map/back_own/pallas_call | solution.py:474
  28.2 2.5 %collective-permute-done.7.end_1 = f32[2,8,512]{2,1,0:T(8,128)S(1)} collective-permute-done((f32[2,8,512]{2,1,0:T(8,128)S(1)}, f32[2,8,512]{2,1,0:T(8,128)S(1)}, u32[]{:S(2)}, u32[]{:S(2)}) %collective-permute-start.7) | collective-permute-done | bytes 32800 | tf_op jit(solution)/shard_map/ppermute | solution.py:427
  30.7 0.7 %close.1 = f32[8,8,512]{2,1,0:T(8,128)} custom-call(f32[8,8,512]{2,1,0:T(8,128)S(1)} %back_own.1.own, f32[2,8,512]{2,1,0:T(8,128)S(1)} %collective-permute-done.6.end_0, f32[2,8,512]{2,1,0:T(8,128)S(1)} %collective-permute-done.7.end_1), custom_call_target="tpu_custom_call" | custom-call | tf_op jit(solution)/shard_map/close/pallas_call | solution.py:515
  (11 shorter events, 0.1 us)
Async XLA Ops:
  1.8 8.9 %collective-permute-start = (f32[4,8,512]{2,1,0:T(8,128)S(1)}, f32[4,8,512]{2,1,0:T(8,128)S(1)}, u32[]{:S(2)}, u32[]{:S(2)}) collective-permute-start(f32[4,8,512]{2,1,0:T(8,128)S(1)} %get-tuple-element.21), channel_id=1, source_target_pairs={{0,1},{2,3},{4,5},{6,7},{1,0},{3,2},{5,4},{7,6},{8,9},{10,11},{12,... | collective-permute-start | bytes 196616 | tf_op jit(solution)/shard_map/ppermute | solution.py:427
  1.9 8.9 %collective-permute-start.1 = (f32[4,8,512]{2,1,0:T(8,128)S(1)}, f32[4,8,512]{2,1,0:T(8,128)S(1)}, u32[]{:S(2)}, u32[]{:S(2)}) collective-permute-start(f32[4,8,512]{2,1,0:T(8,128)S(1)} %get-tuple-element.22), channel_id=1, source_target_pairs={{1,2},{3,4},{5,6},{7,0},{2,1},{4,3},{6,5},{0,7},{9,10},{11,12},{13... | collective-permute-start | bytes 196616 | tf_op jit(solution)/shard_map/ppermute | solution.py:427
  5.6 10.3 %all-to-all-start = ((f32[32,8,128]{2,1,0:T(8,128)}), f32[32,8,128]{2,1,0:T(8,128)S(1)}, u32[]{:S(2)}, u32[]{:S(2)}) async-start(f32[32,8,128]{2,1,0:T(8,128)} %get-tuple-element.19), calls=%async_computation | async-start | bytes 262144 | tf_op jit(solution)/shard_map/all_to_all | solution.py:465
  10.8 9.5 %collective-permute-start.2 = (f32[4,8,512]{2,1,0:T(8,128)S(1)}, f32[4,8,512]{2,1,0:T(8,128)S(1)}, u32[]{:S(2)}, u32[]{:S(2)}) collective-permute-start(f32[4,8,512]{2,1,0:T(8,128)S(1)} %get-tuple-element.23), channel_id=1, source_target_pairs={{8,16},{16,8},{9,17},{17,9},{10,18},{18,10},{11,19},{19,11},{12,20... | collective-permute-start | bytes 196616 | tf_op jit(solution)/shard_map/ppermute | solution.py:427
  14.1 6.2 %collective-permute-start.3 = (f32[4,8,512]{2,1,0:T(8,128)S(1)}, f32[4,8,512]{2,1,0:T(8,128)S(1)}, u32[]{:S(2)}, u32[]{:S(2)}) collective-permute-start(f32[4,8,512]{2,1,0:T(8,128)S(1)} %get-tuple-element.24), channel_id=1, source_target_pairs={{0,8},{16,24},{8,0},{24,16},{1,9},{17,25},{9,1},{25,17},{2,10},{18... | collective-permute-start | bytes 196616 | tf_op jit(solution)/shard_map/ppermute | solution.py:427
  18.1 5.2 %collective-permute-start.4 = (f32[2,8,512]{2,1,0:T(8,128)S(1)}, f32[2,8,512]{2,1,0:T(8,128)S(1)}, u32[]{:S(2)}, u32[]{:S(2)}) collective-permute-start(f32[2,8,512]{2,1,0:T(8,128)S(1)} %get-tuple-element.28), channel_id=1, source_target_pairs={{1,2},{3,4},{5,6},{7,0},{2,1},{4,3},{6,5},{0,7},{9,10},{11,12},{13... | collective-permute-start | bytes 98312 | tf_op jit(solution)/shard_map/ppermute | solution.py:427
  20.2 3.1 %collective-permute-start.5 = (f32[2,8,512]{2,1,0:T(8,128)S(1)}, f32[2,8,512]{2,1,0:T(8,128)S(1)}, u32[]{:S(2)}, u32[]{:S(2)}) collective-permute-start(f32[2,8,512]{2,1,0:T(8,128)S(1)} %get-tuple-element.29), channel_id=1, source_target_pairs={{0,1},{2,3},{4,5},{6,7},{1,0},{3,2},{5,4},{7,6},{8,9},{10,11},{12,... | collective-permute-start | bytes 98312 | tf_op jit(solution)/shard_map/ppermute | solution.py:427
  23.6 4.6 %collective-permute-start.6 = (f32[2,8,512]{2,1,0:T(8,128)S(1)}, f32[2,8,512]{2,1,0:T(8,128)S(1)}, u32[]{:S(2)}, u32[]{:S(2)}) collective-permute-start(f32[2,8,512]{2,1,0:T(8,128)S(1)} %get-tuple-element.31), channel_id=1, source_target_pairs={{0,8},{16,24},{8,0},{24,16},{1,9},{17,25},{9,1},{25,17},{2,10},{18... | collective-permute-start | bytes 98312 | tf_op jit(solution)/shard_map/ppermute | solution.py:427
  24.0 6.7 %collective-permute-start.7 = (f32[2,8,512]{2,1,0:T(8,128)S(1)}, f32[2,8,512]{2,1,0:T(8,128)S(1)}, u32[]{:S(2)}, u32[]{:S(2)}) collective-permute-start(f32[2,8,512]{2,1,0:T(8,128)S(1)} %get-tuple-element.32), channel_id=1, source_target_pairs={{8,16},{16,8},{9,17},{17,9},{10,18},{18,10},{11,19},{19,11},{12,20... | collective-permute-start | bytes 98312 | tf_op jit(solution)/shard_map/ppermute | solution.py:427

commit v19 on v18

--- a/solution.py
+++ b/solution.py
@@ -279,17 +279,17 @@
 
 
 def open_kernel(
-    counts_in, offsets_in, residual_in, pixel_in, bins_in, latent_in, out, latent, to_partner, to_outer,
+    counts_in, offsets_in, residual_in, pixel_in, bins_in, latent_in, taps_in, out, latent, to_partner, to_outer, taps,
     counts, offsets, residual, pixel, bins, table, arrived,
 ):
     pairs = (
         (counts_in, counts), (offsets_in, offsets), (residual_in, residual), (pixel_in, pixel), (bins_in, bins),
-        (latent_in, latent),
+        (latent_in, latent), (taps_in, taps),
     )
     copies = [pltpu.make_async_copy(source, target, arrived.at[i]) for i, (source, target) in enumerate(pairs)]
     for copy in copies:
         copy.start()
-    for copy in copies[:-1]:
+    for copy in copies[:-2]:
         copy.wait()
     height, _, radial = latent.shape
     length = residual.shape[0]
@@ -309,8 +309,9 @@
         joined = jnp.where(lane < LANES - part, here, after)
         out[owner] = jnp.where(slot < counts[0, owner], joined, 0.0)
 
+    copies[-2].wait()
+    pack_four([latent[row] for row in range(height)], to_partner, to_outer)
     copies[-1].wait()
-    pack_four([latent[row] for row in range(height)], to_partner, to_outer)
 
 
 def behind_of(got, part, cuts, runs, rows_of, *, height, width, radial):
@@ -407,12 +408,16 @@
     for_load(body)
 
 
-def mirror(stencils):
-    turned = jnp.flip(stencils, axis=1).reshape(stencils.shape[0], 9, 3, stencils.shape[2])
-    edge = jnp.zeros_like(turned[:, :, 0, :1])
-    back = jnp.concatenate([edge, turned[:, :, 0, :-1]], axis=-1)
-    ahead = jnp.concatenate([turned[:, :, 2, 1:], edge], axis=-1)
-    return jnp.stack([back, turned[:, :, 1], ahead], axis=2).reshape(stencils.shape)
+def tables_kernel(taps, stencils, mirrored):
+    count, levels, _ = taps.shape
+    for level in range(levels):
+        for tap in range(count):
+            row = taps[tap, level:level + 1, :]
+            stencils[level, tap:tap + 1, :] = row
+            turned = count - 1 - tap
+            if turned % 3 != 1:
+                row = radial_shifts(row)[turned % 3 // 2]
+            mirrored[levels - 1 - level, turned:turned + 1, :] = row
 
 
 def swap(to_partner, to_outer, axis, closed, outer_first=False):
@@ -447,20 +452,21 @@
         return values.reshape(slots // LANES, LANES)
 
     four = jax.ShapeDtypeStruct((height // 2, SUBLANES, radial), f32)
-    packed, latent, *to_sides = pl.pallas_call(
+    taps = jax.ShapeDtypeStruct((stencils.shape[1], stencils.shape[0], radial), f32)
+    packed, latent, *to_sides, taps = pl.pallas_call(
         open_kernel,
-        out_shape=(jax.ShapeDtypeStruct((shards, 2 * RUNS, LANES), f32), tile, four, four),
-        in_specs=[HBM] * 6,
-        out_specs=(VMEM, VMEM, VMEM, VMEM),
+        out_shape=(jax.ShapeDtypeStruct((shards, 2 * RUNS, LANES), f32), tile, four, four, taps),
+        in_specs=[HBM] * 7,
+        out_specs=(VMEM,) * 5,
         scratch_shapes=[pltpu.SMEM((1, shards), i32)] * 2
         + [pltpu.VMEM((slots // LANES, LANES), kind) for kind in (f32, i32, i32)]
         + [pltpu.VMEM((2 * slots // LANES, LANES), f32)]
-        + [pltpu.SemaphoreType.DMA((6,))],
+        + [pltpu.SemaphoreType.DMA((7,))],
         compiler_params=LIMIT,
         name="opening",
     )(*[
         pltpu.with_memory_space_constraint(values, pltpu.HBM)
-        for values in (send_counts, send_offsets, table(residual), table(star_pixel), table(star_bin), latent)
+        for values in (send_counts, send_offsets, table(residual), table(star_pixel), table(star_bin), latent, stencils.transpose(1, 0, 2))
     ])
     got = lax.all_to_all(packed, ("lat", "lon"), split_axis=0, concat_axis=0, tiled=True)
 
@@ -488,6 +494,8 @@
     to_ends = call(pack_ends_kernel, "density_pack", (ends, ends), [], latent, *beside)
     above = swap(*to_ends, "lat", False, outer_first=True)
     broad = 2 * width
+    coefs = jax.ShapeDtypeStruct(stencils.shape, f32)
+    stencils, mirrored = call(tables_kernel, "tables", (coefs, coefs), [], taps)
     inner, middle = call(
         density_inside_kernel, "density_inside",
         (shape(height - 4, broad, radial), shape(3, 3, height - 2, broad, radial)), [rows, moved],
@@ -501,7 +509,6 @@
     )
     upstream = call(bin_rest_kernel, "bin_rest", tile, star_rows, got, density, behind)
 
-    mirrored = mirror(stencils)[::-1]
     beside = swap(*to_sides, "lon", True, outer_first=True)
     *to_ends, middle = call(
         back_reach_kernel, "back_reach", (shape(2, width, radial), shape(2, width, radial), shape(*edge)),

time: 31.6 us -> 36.3 us (1.15)
  waiting for transfers between devices: 3.32 us -> 7.45 us
  starting transfers between devices: 16.2 us -> 18.7 us
  local copies, waits for them, and re-layouts: 2.06 us -> 0 us
    ppermute x8, waiting for transfers between devices: 2.54 us -> 7.45 us  [swap(): lax.ppermute(values, axis, both_ways(pairs))]
    all_to_all x1, starting transfers between devices: 3.09 us -> 6.13 us  [on_device(): lax.all_to_all(packed, ('lat', 'lon'), split_axis=0, concat_axis=0, tiled...]
    unnamed x1 -> x0, local copies, waits for them, and re-layouts: 0.92 us -> none
    rev x2 -> x0, local copies, waits for them, and re-layouts: 0.92 us -> none  [the longest x1 0.91 us: mirror(): jnp.flip(stencils, axis=1)]
    all_to_all x1, waiting for transfers between devices: 0.78 us -> 0.01 us  [on_device(): lax.all_to_all(packed, ('lat', 'lon'), split_axis=0, concat_axis=0, tiled...]
    ppermute x8, starting transfers between devices: 13.1 us -> 12.5 us  [swap(): lax.ppermute(values, axis, both_ways(pairs))]
    pallas_call x7 -> x8, Pallas kernels: 7.12 us -> 7.35 us  [call(): pl.pallas_call(kernel, out_shape=outs, in_specs=[VMEM] * len(operands), o...]
  transfers between devices with their start and end apart: 9 -> 9, of which waited for: 2 -> 3; matrix products, arithmetic and copies ran while one was open for 7% -> 0% of each run, Pallas kernels for 22% -> 19%
where the time goes in v19:
time: 36.3 us; the launch traced here: 36.1 us
  starting transfers between devices  18.7 us (52%)
  Pallas kernels  9.82 us (27%)
  waiting for transfers between devices  7.45 us (21%)
    ppermute x8, starting transfers between devices, swap(): lax.ppermute(values, axis, both_ways(pairs))  12.5 us
    ppermute x8, waiting for transfers between devices, swap(): lax.ppermute(values, axis, both_ways(pairs))  7.45 us
    pallas_call x8, Pallas kernels, call(): pl.pallas_call(kernel, out_shape=outs, in_specs=[VMEM] * len(operands), o...  7.35 us
    all_to_all x1, starting transfers between devices, on_device(): lax.all_to_all(packed, ('lat', 'lon'), split_axis=0, concat_axis=0, tiled...  6.13 us
    pallas_call x1, Pallas kernels, on_device(): pl.pallas_call(open_kernel, out_shape=(jax.ShapeDtypeStruct((shards, 2 *...  1.79 us
  transfers between devices with their start and end apart: 9, of which 3 were waited for; matrix products, arithmetic and copies ran while one was open for 0% of the time, Pallas kernels for 19%

profile of v19, /device:TPU:2, one launch (start us, length us, event | category | flops | bytes accessed | tf_op | source)
XLA Modules:
  0.0 36.1 jit_solution(16654351998308985288)
XLA Ops:
  0.0 1.8 %opening.1 = (f32[32,8,128]{2,1,0:T(8,128)}, f32[8,8,512]{2,1,0:T(8,128)S(1)}, f32[4,8,512]{2,1,0:T(8,128)S(1)}, f32[4,8,512]{2,1,0:T(8,128)S(1)}, f32[27,2,512]{2,1,0:T(2,128)S(1)}) custom-call(s32[1,32]{1,0:T(1,128)} %counts_in.1, s32[1,32]{1,0:T(1,128)} %offsets_in.1, f32[128,128]{1,0:T(8,128)} %bitcast.5, s32[128,128]{1,0:T(8,128)} %bitcast.6, ...), custom_call_target="tpu_custom_call" | custom-call | tf_op jit(solution)/shard_map/opening/pallas_call | solution.py:456
  1.8 6.1 %all-to-all-start = ((f32[32,8,128]{2,1,0:T(8,128)}), f32[32,8,128]{2,1,0:T(8,128)S(1)}, u32[]{:S(2)}, u32[]{:S(2)}) async-start(f32[32,8,128]{2,1,0:T(8,128)} %get-tuple-element.22), calls=%async_computation | async-start | bytes 262144 | tf_op jit(solution)/shard_map/all_to_all | solution.py:471
  7.9 0.2 collective-permute-start
  8.2 3.3 %collective-permute-start.1 = (f32[4,8,512]{2,1,0:T(8,128)S(1)}, f32[4,8,512]{2,1,0:T(8,128)S(1)}, u32[]{:S(2)}, u32[]{:S(2)}) collective-permute-start(f32[4,8,512]{2,1,0:T(8,128)S(1)} %get-tuple-element.25), channel_id=1, source_target_pairs={{1,2},{3,4},{5,6},{7,0},{2,1},{4,3},{6,5},{0,7},{9,10},{11,12},{13... | collective-permute-start | bytes 196616 | tf_op jit(solution)/shard_map/ppermute | solution.py:432
  11.5 0.0 collective-permute-done.side_0
  11.5 3.9 %collective-permute-done.1.side_1 = f32[4,8,512]{2,1,0:T(8,128)S(1)} collective-permute-done((f32[4,8,512]{2,1,0:T(8,128)S(1)}, f32[4,8,512]{2,1,0:T(8,128)S(1)}, u32[]{:S(2)}, u32[]{:S(2)}) %collective-permute-start.1) | collective-permute-done | bytes 65568 | tf_op jit(solution)/shard_map/ppermute | solution.py:432
  15.4 3.4 %collective-permute-start.2 = (f32[4,8,512]{2,1,0:T(8,128)S(1)}, f32[4,8,512]{2,1,0:T(8,128)S(1)}, u32[]{:S(2)}, u32[]{:S(2)}) collective-permute-start(f32[4,8,512]{2,1,0:T(8,128)S(1)} %get-tuple-element.26), channel_id=1, source_target_pairs={{8,16},{16,8},{9,17},{17,9},{10,18},{18,10},{11,19},{19,11},{12,20... | collective-permute-start | bytes 196616 | tf_op jit(solution)/shard_map/ppermute | solution.py:432
  18.8 0.1 collective-permute-start.3
  18.9 0.2 tables.1
  19.1 0.9 %density_inside.1 = (f32[4,16,512]{2,1,0:T(8,128)S(1)}, f32[3,3,6,16,512]{4,3,2,1,0:T(8,128)S(1)}) custom-call(f32[8,8,512]{2,1,0:T(8,128)S(1)} %get-tuple-element.23.field.latent, f32[4,8,512]{2,1,0:T(8,128)S(1)} %collective-permute-done.side_0, f32[4,8,512]{2,1,0:T(8,128)S(1)} %collective-permute-done.1.side_1, f32[2,27,512]{2,1,0:T(8,128)S(1)} %get-tuple-element.29.stencils), custom_call_target="tpu_custom_call" | custom-call | tf_op jit(solution)/shard_map/density_inside/pallas_call | solution.py:480
  20.0 0.0 all-to-all-done.got
  20.0 2.2 %bin_sides.1 = (f32[8,8,512]{2,1,0:T(8,128)S(1)}, f32[2,8,512]{2,1,0:T(8,128)S(1)}, f32[2,8,512]{2,1,0:T(8,128)S(1)}) custom-call(f32[32,8,128]{2,1,0:T(8,128)S(1)} %all-to-all-done.got, f32[4,16,512]{2,1,0:T(8,128)S(1)} %get-tuple-element.31._.inner), custom_call_target="tpu_custom_call" | custom-call | tf_op jit(solution)/shard_map/bin_sides/pallas_call | solution.py:480
  22.2 1.3 %collective-permute-start.4 = (f32[2,8,512]{2,1,0:T(8,128)S(1)}, f32[2,8,512]{2,1,0:T(8,128)S(1)}, u32[]{:S(2)}, u32[]{:S(2)}) collective-permute-start(f32[2,8,512]{2,1,0:T(8,128)S(1)} %get-tuple-element.33), channel_id=1, source_target_pairs={{1,2},{3,4},{5,6},{7,0},{2,1},{4,3},{6,5},{0,7},{9,10},{11,12},{13... | collective-permute-start | bytes 98312 | tf_op jit(solution)/shard_map/ppermute | solution.py:432
  23.5 0.0 collective-permute-start.5
  23.6 0.7 %density_ends.1.density = f32[8,16,512]{2,1,0:T(8,128)S(1)} custom-call(f32[8,8,512]{2,1,0:T(8,128)S(1)} %get-tuple-element.23.field.latent, f32[4,8,512]{2,1,0:T(8,128)S(1)} %collective-permute-done.side_0, f32[4,8,512]{2,1,0:T(8,128)S(1)} %collective-permute-done.1.side_1, f32[4,8,512]{2,1,0:T(8,128)S(1)} %collective-permute-done.2.end_1, ...), custom_call_target="tpu_custom_call" | custom-call | tf_op jit(solution)/shard_map/density_ends/pallas_call | solution.py:480
  24.3 2.2 %bin_rest.1.field = f32[8,8,512]{2,1,0:T(8,128)S(1)} custom-call(f32[32,8,128]{2,1,0:T(8,128)S(1)} %all-to-all-done.got, f32[8,16,512]{2,1,0:T(8,128)S(1)} %density_ends.1.density, f32[8,8,512]{2,1,0:T(8,128)S(1)} %get-tuple-element.32._.behind), custom_call_target="tpu_custom_call" | custom-call | tf_op jit(solution)/shard_map/bin_rest/pallas_call | solution.py:480
  26.5 1.0 %collective-permute-done.4.side_1 = f32[2,8,512]{2,1,0:T(8,128)S(1)} collective-permute-done((f32[2,8,512]{2,1,0:T(8,128)S(1)}, f32[2,8,512]{2,1,0:T(8,128)S(1)}, u32[]{:S(2)}, u32[]{:S(2)}) %collective-permute-start.4) | collective-permute-done | bytes 32800 | tf_op jit(solution)/shard_map/ppermute | solution.py:432
  27.4 0.0 collective-permute-done.5.side_0
  27.4 0.4 back_reach.1
  27.8 0.9 %collective-permute-start.6 = (f32[2,8,512]{2,1,0:T(8,128)S(1)}, f32[2,8,512]{2,1,0:T(8,128)S(1)}, u32[]{:S(2)}, u32[]{:S(2)}) collective-permute-start(f32[2,8,512]{2,1,0:T(8,128)S(1)} %get-tuple-element.37), channel_id=1, source_target_pairs={{0,8},{16,24},{8,0},{24,16},{1,9},{17,25},{9,1},{25,17},{2,10},{18... | collective-permute-start | bytes 98312 | tf_op jit(solution)/shard_map/ppermute | solution.py:432
  28.7 3.3 %collective-permute-start.7 = (f32[2,8,512]{2,1,0:T(8,128)S(1)}, f32[2,8,512]{2,1,0:T(8,128)S(1)}, u32[]{:S(2)}, u32[]{:S(2)}) collective-permute-start(f32[2,8,512]{2,1,0:T(8,128)S(1)} %get-tuple-element.38), channel_id=1, source_target_pairs={{8,16},{16,8},{9,17},{17,9},{10,18},{18,10},{11,19},{19,11},{12,20... | collective-permute-start | bytes 98312 | tf_op jit(solution)/shard_map/ppermute | solution.py:432
  32.0 0.8 %back_own.1.own = f32[8,8,512]{2,1,0:T(8,128)S(1)} custom-call(f32[8,8,512]{2,1,0:T(8,128)S(1)} %bin_rest.1.field, f32[2,8,512]{2,1,0:T(8,128)S(1)} %collective-permute-done.4.side_1, f32[2,8,512]{2,1,0:T(8,128)S(1)} %collective-permute-done.5.side_0, f32[8,16,512]{2,1,0:T(8,128)S(1)} %density_ends.1.density, f32[2,27,512]{2,1,0:T(8,128)S(1)} %get-tuple-element.35.stencils, ...), custom_call_target="tpu_custom_call" | custom-call | tf_op jit(solution)/shard_map/back_own/pallas_call | solution.py:480
  32.9 2.5 %collective-permute-done.7.end_1 = f32[2,8,512]{2,1,0:T(8,128)S(1)} collective-permute-done((f32[2,8,512]{2,1,0:T(8,128)S(1)}, f32[2,8,512]{2,1,0:T(8,128)S(1)}, u32[]{:S(2)}, u32[]{:S(2)}) %collective-permute-start.7) | collective-permute-done | bytes 32800 | tf_op jit(solution)/shard_map/ppermute | solution.py:432
  35.4 0.7 %close.1 = f32[8,8,512]{2,1,0:T(8,128)} custom-call(f32[8,8,512]{2,1,0:T(8,128)S(1)} %back_own.1.own, f32[2,8,512]{2,1,0:T(8,128)S(1)} %collective-permute-done.6.end_0, f32[2,8,512]{2,1,0:T(8,128)S(1)} %collective-permute-done.7.end_1), custom_call_target="tpu_custom_call" | custom-call | tf_op jit(solution)/shard_map/close/pallas_call | solution.py:522
  (4 shorter events, 0.0 us)
Async XLA Ops:
  1.8 18.2 %all-to-all-start = ((f32[32,8,128]{2,1,0:T(8,128)}), f32[32,8,128]{2,1,0:T(8,128)S(1)}, u32[]{:S(2)}, u32[]{:S(2)}) async-start(f32[32,8,128]{2,1,0:T(8,128)} %get-tuple-element.22), calls=%async_computation | async-start | bytes 262144 | tf_op jit(solution)/shard_map/all_to_all | solution.py:471
  7.9 3.5 %collective-permute-start = (f32[4,8,512]{2,1,0:T(8,128)S(1)}, f32[4,8,512]{2,1,0:T(8,128)S(1)}, u32[]{:S(2)}, u32[]{:S(2)}) collective-permute-start(f32[4,8,512]{2,1,0:T(8,128)S(1)} %get-tuple-element.24), channel_id=1, source_target_pairs={{0,1},{2,3},{4,5},{6,7},{1,0},{3,2},{5,4},{7,6},{8,9},{10,11},{12,... | collective-permute-start | bytes 196616 | tf_op jit(solution)/shard_map/ppermute | solution.py:432
  8.2 7.2 %collective-permute-start.1 = (f32[4,8,512]{2,1,0:T(8,128)S(1)}, f32[4,8,512]{2,1,0:T(8,128)S(1)}, u32[]{:S(2)}, u32[]{:S(2)}) collective-permute-start(f32[4,8,512]{2,1,0:T(8,128)S(1)} %get-tuple-element.25), channel_id=1, source_target_pairs={{1,2},{3,4},{5,6},{7,0},{2,1},{4,3},{6,5},{0,7},{9,10},{11,12},{13... | collective-permute-start | bytes 196616 | tf_op jit(solution)/shard_map/ppermute | solution.py:432
  15.4 8.1 %collective-permute-start.2 = (f32[4,8,512]{2,1,0:T(8,128)S(1)}, f32[4,8,512]{2,1,0:T(8,128)S(1)}, u32[]{:S(2)}, u32[]{:S(2)}) collective-permute-start(f32[4,8,512]{2,1,0:T(8,128)S(1)} %get-tuple-element.26), channel_id=1, source_target_pairs={{8,16},{16,8},{9,17},{17,9},{10,18},{18,10},{11,19},{19,11},{12,20... | collective-permute-start | bytes 196616 | tf_op jit(solution)/shard_map/ppermute | solution.py:432
  18.8 4.7 %collective-permute-start.3 = (f32[4,8,512]{2,1,0:T(8,128)S(1)}, f32[4,8,512]{2,1,0:T(8,128)S(1)}, u32[]{:S(2)}, u32[]{:S(2)}) collective-permute-start(f32[4,8,512]{2,1,0:T(8,128)S(1)} %get-tuple-element.27), channel_id=1, source_target_pairs={{0,8},{16,24},{8,0},{24,16},{1,9},{17,25},{9,1},{25,17},{2,10},{18... | collective-permute-start | bytes 196616 | tf_op jit(solution)/shard_map/ppermute | solution.py:432
  22.2 5.2 %collective-permute-start.4 = (f32[2,8,512]{2,1,0:T(8,128)S(1)}, f32[2,8,512]{2,1,0:T(8,128)S(1)}, u32[]{:S(2)}, u32[]{:S(2)}) collective-permute-start(f32[2,8,512]{2,1,0:T(8,128)S(1)} %get-tuple-element.33), channel_id=1, source_target_pairs={{1,2},{3,4},{5,6},{7,0},{2,1},{4,3},{6,5},{0,7},{9,10},{11,12},{13... | collective-permute-start | bytes 98312 | tf_op jit(solution)/shard_map/ppermute | solution.py:432
  23.5 3.9 %collective-permute-start.5 = (f32[2,8,512]{2,1,0:T(8,128)S(1)}, f32[2,8,512]{2,1,0:T(8,128)S(1)}, u32[]{:S(2)}, u32[]{:S(2)}) collective-permute-start(f32[2,8,512]{2,1,0:T(8,128)S(1)} %get-tuple-element.34), channel_id=1, source_target_pairs={{0,1},{2,3},{4,5},{6,7},{1,0},{3,2},{5,4},{7,6},{8,9},{10,11},{12,... | collective-permute-start | bytes 98312 | tf_op jit(solution)/shard_map/ppermute | solution.py:432
  27.8 5.1 %collective-permute-start.6 = (f32[2,8,512]{2,1,0:T(8,128)S(1)}, f32[2,8,512]{2,1,0:T(8,128)S(1)}, u32[]{:S(2)}, u32[]{:S(2)}) collective-permute-start(f32[2,8,512]{2,1,0:T(8,128)S(1)} %get-tuple-element.37), channel_id=1, source_target_pairs={{0,8},{16,24},{8,0},{24,16},{1,9},{17,25},{9,1},{25,17},{2,10},{18... | collective-permute-start | bytes 98312 | tf_op jit(solution)/shard_map/ppermute | solution.py:432
  28.7 6.7 %collective-permute-start.7 = (f32[2,8,512]{2,1,0:T(8,128)S(1)}, f32[2,8,512]{2,1,0:T(8,128)S(1)}, u32[]{:S(2)}, u32[]{:S(2)}) collective-permute-start(f32[2,8,512]{2,1,0:T(8,128)S(1)} %get-tuple-element.38), channel_id=1, source_target_pairs={{8,16},{16,8},{9,17},{17,9},{10,18},{18,10},{11,19},{19,11},{12,20... | collective-permute-start | bytes 98312 | tf_op jit(solution)/shard_map/ppermute | solution.py:432

commit v20 on v19

--- a/solution.py
+++ b/solution.py
@@ -408,16 +408,12 @@
     for_load(body)
 
 
-def tables_kernel(taps, stencils, mirrored):
-    count, levels, _ = taps.shape
-    for level in range(levels):
-        for tap in range(count):
-            row = taps[tap, level:level + 1, :]
-            stencils[level, tap:tap + 1, :] = row
-            turned = count - 1 - tap
-            if turned % 3 != 1:
-                row = radial_shifts(row)[turned % 3 // 2]
-            mirrored[levels - 1 - level, turned:turned + 1, :] = row
+def mirror(stencils):
+    turned = jnp.flip(stencils, axis=1).reshape(stencils.shape[0], 9, 3, stencils.shape[2])
+    edge = jnp.zeros_like(turned[:, :, 0, :1])
+    back = jnp.concatenate([edge, turned[:, :, 0, :-1]], axis=-1)
+    ahead = jnp.concatenate([turned[:, :, 2, 1:], edge], axis=-1)
+    return jnp.stack([back, turned[:, :, 1], ahead], axis=2).reshape(stencils.shape)
 
 
 def swap(to_partner, to_outer, axis, closed, outer_first=False):
@@ -494,8 +490,8 @@
     to_ends = call(pack_ends_kernel, "density_pack", (ends, ends), [], latent, *beside)
     above = swap(*to_ends, "lat", False, outer_first=True)
     broad = 2 * width
-    coefs = jax.ShapeDtypeStruct(stencils.shape, f32)
-    stencils, mirrored = call(tables_kernel, "tables", (coefs, coefs), [], taps)
+    stencils = taps.transpose(1, 0, 2)
+    mirrored = mirror(stencils)[::-1]
     inner, middle = call(
         density_inside_kernel, "density_inside",
         (shape(height - 4, broad, radial), shape(3, 3, height - 2, broad, radial)), [rows, moved],

time: 36.3 us -> 31.4 us (0.87)
  starting transfers between devices: 18.7 us -> 14.4 us
  waiting for transfers between devices: 7.45 us -> 6.41 us
  local copies, waits for them, and re-layouts: 0 us -> 0.5 us
    ppermute x8, waiting for transfers between devices: 7.45 us -> 4.01 us  [swap(): lax.ppermute(values, axis, both_ways(pairs))]
    all_to_all x1, starting transfers between devices: 6.13 us -> 3.09 us  [on_device(): lax.all_to_all(packed, ('lat', 'lon'), split_axis=0, concat_axis=0, tiled...]
    all_to_all x1, waiting for transfers between devices: 0.01 us -> 2.4 us  [on_device(): lax.all_to_all(packed, ('lat', 'lon'), split_axis=0, concat_axis=0, tiled...]
    ppermute x8, starting transfers between devices: 12.5 us -> 11.3 us  [swap(): lax.ppermute(values, axis, both_ways(pairs))]
    pallas_call x8 -> x7, Pallas kernels: 7.35 us -> 7.12 us  [call(): pl.pallas_call(kernel, out_shape=outs, in_specs=[VMEM] * len(operands), o...]
  transfers between devices with their start and end apart: 9 -> 9, of which waited for: 3 -> 3; matrix products, arithmetic and copies ran while one was open for 0% -> 2% of each run, Pallas kernels for 19% -> 22%
where the time goes in v20:
time: 31.4 us; the launch traced here: 31.2 us
  starting transfers between devices  14.4 us (46%)
  Pallas kernels  9.59 us (31%)
  waiting for transfers between devices  6.41 us (20%)
  local copies, waits for them, and re-layouts  0.5 us (2%)
    ppermute x8, starting transfers between devices, swap(): lax.ppermute(values, axis, both_ways(pairs))  11.3 us
    pallas_call x7, Pallas kernels, call(): pl.pallas_call(kernel, out_shape=outs, in_specs=[VMEM] * len(operands), o...  7.12 us
    ppermute x8, waiting for transfers between devices, swap(): lax.ppermute(values, axis, both_ways(pairs))  4.01 us
    all_to_all x1, starting transfers between devices, on_device(): lax.all_to_all(packed, ('lat', 'lon'), split_axis=0, concat_axis=0, tiled...  3.09 us
    all_to_all x1, waiting for transfers between devices, on_device(): lax.all_to_all(packed, ('lat', 'lon'), split_axis=0, concat_axis=0, tiled...  2.4 us
    pallas_call x1, Pallas kernels, on_device(): pl.pallas_call(open_kernel, out_shape=(jax.ShapeDtypeStruct((shards, 2 *...  1.79 us
    pallas_call x1, Pallas kernels, on_device(): pl.pallas_call(close_kernel, out_shape=tile, in_specs=[VMEM] * 3, out_spe...  0.67 us
  transfers between devices with their start and end apart: 9, of which 3 were waited for; matrix products, arithmetic and copies ran while one was open for 2% of the time, Pallas kernels for 22%

profile of v20, /device:TPU:2, one launch (start us, length us, event | category | flops | bytes accessed | tf_op | source)
XLA Modules:
  0.0 31.2 jit_solution(1628900741825335849)
XLA Ops:
  0.0 1.8 %opening.1 = (f32[32,8,128]{2,1,0:T(8,128)}, f32[8,8,512]{2,1,0:T(8,128)S(1)}, f32[4,8,512]{2,1,0:T(8,128)S(1)}, f32[4,8,512]{2,1,0:T(8,128)S(1)}, f32[27,2,512]{2,1,0:T(2,128)S(1)}) custom-call(s32[1,32]{1,0:T(1,128)} %counts_in.1, s32[1,32]{1,0:T(1,128)} %offsets_in.1, f32[128,128]{1,0:T(8,128)} %bitcast.26, s32[128,128]{1,0:T(8,128)} %bitcast.27, ...), custom_call_target="tpu_custom_call" | custom-call | tf_op jit(solution)/shard_map/opening/pallas_call | solution.py:452
  1.8 0.1 collective-permute-start
  1.9 3.7 %collective-permute-start.1 = (f32[4,8,512]{2,1,0:T(8,128)S(1)}, f32[4,8,512]{2,1,0:T(8,128)S(1)}, u32[]{:S(2)}, u32[]{:S(2)}) collective-permute-start(f32[4,8,512]{2,1,0:T(8,128)S(1)} %get-tuple-element.23), channel_id=1, source_target_pairs={{1,2},{3,4},{5,6},{7,0},{2,1},{4,3},{6,5},{0,7},{9,10},{11,12},{13... | collective-permute-start | bytes 196616 | tf_op jit(solution)/shard_map/ppermute | solution.py:428
  5.6 3.1 %all-to-all-start = ((f32[32,8,128]{2,1,0:T(8,128)}), f32[32,8,128]{2,1,0:T(8,128)S(1)}, u32[]{:S(2)}, u32[]{:S(2)}) async-start(f32[32,8,128]{2,1,0:T(8,128)} %get-tuple-element.20), calls=%async_computation | async-start | bytes 262144 | tf_op jit(solution)/shard_map/all_to_all | solution.py:467
  8.7 0.2 rev.7
  8.9 0.1 copy.12
  9.0 0.1 slice_bitcast_fusion.1
  9.1 0.1 pad_bitcast_fusion
  9.2 3.4 %collective-permute-start.2 = (f32[4,8,512]{2,1,0:T(8,128)S(1)}, f32[4,8,512]{2,1,0:T(8,128)S(1)}, u32[]{:S(2)}, u32[]{:S(2)}) collective-permute-start(f32[4,8,512]{2,1,0:T(8,128)S(1)} %get-tuple-element.24), channel_id=1, source_target_pairs={{8,16},{16,8},{9,17},{17,9},{10,18},{18,10},{11,19},{19,11},{12,20... | collective-permute-start | bytes 196616 | tf_op jit(solution)/shard_map/ppermute | solution.py:428
  12.6 0.1 collective-permute-start.3
  12.7 0.9 %density_inside.1 = (f32[4,16,512]{2,1,0:T(8,128)S(1)}, f32[3,3,6,16,512]{4,3,2,1,0:T(8,128)S(1)}) custom-call(f32[8,8,512]{2,1,0:T(8,128)S(1)} %get-tuple-element.21.field.latent, f32[4,8,512]{2,1,0:T(8,128)S(1)} %collective-permute-done.side_0, f32[4,8,512]{2,1,0:T(8,128)S(1)} %collective-permute-done.1.side_1, f32[2,27,512]{2,1,0:T(8,128)S(1)} %bitcast.20), custom_call_target="tpu_custom_call" | custom-call | tf_op jit(solution)/shard_map/density_inside/pallas_call | solution.py:476
  13.6 2.4 %all-to-all-done.got = f32[32,8,128]{2,1,0:T(8,128)S(1)} async-done(((f32[32,8,128]{2,1,0:T(8,128)}), f32[32,8,128]{2,1,0:T(8,128)S(1)}, u32[]{:S(2)}, u32[]{:S(2)}) %all-to-all-start) | async-done | bytes 131104 | tf_op jit(solution)/shard_map/all_to_all | solution.py:467
  16.0 2.2 %bin_sides.1 = (f32[8,8,512]{2,1,0:T(8,128)S(1)}, f32[2,8,512]{2,1,0:T(8,128)S(1)}, f32[2,8,512]{2,1,0:T(8,128)S(1)}) custom-call(f32[32,8,128]{2,1,0:T(8,128)S(1)} %all-to-all-done.got, f32[4,16,512]{2,1,0:T(8,128)S(1)} %get-tuple-element.28._.inner), custom_call_target="tpu_custom_call" | custom-call | tf_op jit(solution)/shard_map/bin_sides/pallas_call | solution.py:476
  18.2 0.8 %collective-permute-start.4 = (f32[2,8,512]{2,1,0:T(8,128)S(1)}, f32[2,8,512]{2,1,0:T(8,128)S(1)}, u32[]{:S(2)}, u32[]{:S(2)}) collective-permute-start(f32[2,8,512]{2,1,0:T(8,128)S(1)} %get-tuple-element.30), channel_id=1, source_target_pairs={{1,2},{3,4},{5,6},{7,0},{2,1},{4,3},{6,5},{0,7},{9,10},{11,12},{13... | collective-permute-start | bytes 98312 | tf_op jit(solution)/shard_map/ppermute | solution.py:428
  18.9 0.1 pad_maximum_fusion
  19.1 0.7 %density_ends.1.density = f32[8,16,512]{2,1,0:T(8,128)S(1)} custom-call(f32[8,8,512]{2,1,0:T(8,128)S(1)} %get-tuple-element.21.field.latent, f32[4,8,512]{2,1,0:T(8,128)S(1)} %collective-permute-done.side_0, f32[4,8,512]{2,1,0:T(8,128)S(1)} %collective-permute-done.1.side_1, f32[4,8,512]{2,1,0:T(8,128)S(1)} %collective-permute-done.2.end_1, ...), custom_call_target="tpu_custom_call" | custom-call | tf_op jit(solution)/shard_map/density_ends/pallas_call | solution.py:476
  19.8 2.2 %bin_rest.1.field = f32[8,8,512]{2,1,0:T(8,128)S(1)} custom-call(f32[32,8,128]{2,1,0:T(8,128)S(1)} %all-to-all-done.got, f32[8,16,512]{2,1,0:T(8,128)S(1)} %density_ends.1.density, f32[8,8,512]{2,1,0:T(8,128)S(1)} %get-tuple-element.29._.behind), custom_call_target="tpu_custom_call" | custom-call | tf_op jit(solution)/shard_map/bin_rest/pallas_call | solution.py:476
  22.0 1.4 %collective-permute-done.4.side_1 = f32[2,8,512]{2,1,0:T(8,128)S(1)} collective-permute-done((f32[2,8,512]{2,1,0:T(8,128)S(1)}, f32[2,8,512]{2,1,0:T(8,128)S(1)}, u32[]{:S(2)}, u32[]{:S(2)}) %collective-permute-start.4) | collective-permute-done | bytes 32800 | tf_op jit(solution)/shard_map/ppermute | solution.py:428
  23.4 0.4 %back_reach.1 = (f32[2,8,512]{2,1,0:T(8,128)S(1)}, f32[2,8,512]{2,1,0:T(8,128)S(1)}, f32[3,3,4,8,512]{4,3,2,1,0:T(8,128)S(1)}) custom-call(f32[8,8,512]{2,1,0:T(8,128)S(1)} %bin_rest.1.field, f32[2,8,512]{2,1,0:T(8,128)S(1)} %collective-permute-done.4.side_1, f32[2,8,512]{2,1,0:T(8,128)S(1)} %collective-permute-done.5.side_0, ...), custom_call_target="tpu_custom_call" | custom-call | tf_op jit(solution)/shard_map/back_reach/pallas_call | solution.py:476
  23.7 0.1 collective-permute-start.6
  23.8 3.3 %collective-permute-start.7 = (f32[2,8,512]{2,1,0:T(8,128)S(1)}, f32[2,8,512]{2,1,0:T(8,128)S(1)}, u32[]{:S(2)}, u32[]{:S(2)}) collective-permute-start(f32[2,8,512]{2,1,0:T(8,128)S(1)} %get-tuple-element.34), channel_id=1, source_target_pairs={{8,16},{16,8},{9,17},{17,9},{10,18},{18,10},{11,19},{19,11},{12,20... | collective-permute-start | bytes 98312 | tf_op jit(solution)/shard_map/ppermute | solution.py:428
  27.1 0.8 %back_own.1.own = f32[8,8,512]{2,1,0:T(8,128)S(1)} custom-call(f32[8,8,512]{2,1,0:T(8,128)S(1)} %bin_rest.1.field, f32[2,8,512]{2,1,0:T(8,128)S(1)} %collective-permute-done.4.side_1, f32[2,8,512]{2,1,0:T(8,128)S(1)} %collective-permute-done.5.side_0, f32[8,16,512]{2,1,0:T(8,128)S(1)} %density_ends.1.density, f32[2,27,512]{2,1,0:T(8,128)S(1)} %rev.8.stencils, ...), custom_call_target="tpu_custom_call" | custom-call | tf_op jit(solution)/shard_map/back_own/pallas_call | solution.py:476
  28.0 2.6 %collective-permute-done.7.end_1 = f32[2,8,512]{2,1,0:T(8,128)S(1)} collective-permute-done((f32[2,8,512]{2,1,0:T(8,128)S(1)}, f32[2,8,512]{2,1,0:T(8,128)S(1)}, u32[]{:S(2)}, u32[]{:S(2)}) %collective-permute-start.7) | collective-permute-done | bytes 32800 | tf_op jit(solution)/shard_map/ppermute | solution.py:428
  30.5 0.7 %close.1 = f32[8,8,512]{2,1,0:T(8,128)} custom-call(f32[8,8,512]{2,1,0:T(8,128)S(1)} %back_own.1.own, f32[2,8,512]{2,1,0:T(8,128)S(1)} %collective-permute-done.6.end_0, f32[2,8,512]{2,1,0:T(8,128)S(1)} %collective-permute-done.7.end_1), custom_call_target="tpu_custom_call" | custom-call | tf_op jit(solution)/shard_map/close/pallas_call | solution.py:518
  (12 shorter events, 0.1 us)
Async XLA Ops:
  1.8 7.4 %collective-permute-start = (f32[4,8,512]{2,1,0:T(8,128)S(1)}, f32[4,8,512]{2,1,0:T(8,128)S(1)}, u32[]{:S(2)}, u32[]{:S(2)}) collective-permute-start(f32[4,8,512]{2,1,0:T(8,128)S(1)} %get-tuple-element.22), channel_id=1, source_target_pairs={{0,1},{2,3},{4,5},{6,7},{1,0},{3,2},{5,4},{7,6},{8,9},{10,11},{12,... | collective-permute-start | bytes 196616 | tf_op jit(solution)/shard_map/ppermute | solution.py:428
  1.9 7.3 %collective-permute-start.1 = (f32[4,8,512]{2,1,0:T(8,128)S(1)}, f32[4,8,512]{2,1,0:T(8,128)S(1)}, u32[]{:S(2)}, u32[]{:S(2)}) collective-permute-start(f32[4,8,512]{2,1,0:T(8,128)S(1)} %get-tuple-element.23), channel_id=1, source_target_pairs={{1,2},{3,4},{5,6},{7,0},{2,1},{4,3},{6,5},{0,7},{9,10},{11,12},{13... | collective-permute-start | bytes 196616 | tf_op jit(solution)/shard_map/ppermute | solution.py:428
  5.6 10.4 %all-to-all-start = ((f32[32,8,128]{2,1,0:T(8,128)}), f32[32,8,128]{2,1,0:T(8,128)S(1)}, u32[]{:S(2)}, u32[]{:S(2)}) async-start(f32[32,8,128]{2,1,0:T(8,128)} %get-tuple-element.20), calls=%async_computation | async-start | bytes 262144 | tf_op jit(solution)/shard_map/all_to_all | solution.py:467
  9.2 9.8 %collective-permute-start.2 = (f32[4,8,512]{2,1,0:T(8,128)S(1)}, f32[4,8,512]{2,1,0:T(8,128)S(1)}, u32[]{:S(2)}, u32[]{:S(2)}) collective-permute-start(f32[4,8,512]{2,1,0:T(8,128)S(1)} %get-tuple-element.24), channel_id=1, source_target_pairs={{8,16},{16,8},{9,17},{17,9},{10,18},{18,10},{11,19},{19,11},{12,20... | collective-permute-start | bytes 196616 | tf_op jit(solution)/shard_map/ppermute | solution.py:428
  12.6 6.4 %collective-permute-start.3 = (f32[4,8,512]{2,1,0:T(8,128)S(1)}, f32[4,8,512]{2,1,0:T(8,128)S(1)}, u32[]{:S(2)}, u32[]{:S(2)}) collective-permute-start(f32[4,8,512]{2,1,0:T(8,128)S(1)} %get-tuple-element.25), channel_id=1, source_target_pairs={{0,8},{16,24},{8,0},{24,16},{1,9},{17,25},{9,1},{25,17},{2,10},{18... | collective-permute-start | bytes 196616 | tf_op jit(solution)/shard_map/ppermute | solution.py:428
  18.2 5.2 %collective-permute-start.4 = (f32[2,8,512]{2,1,0:T(8,128)S(1)}, f32[2,8,512]{2,1,0:T(8,128)S(1)}, u32[]{:S(2)}, u32[]{:S(2)}) collective-permute-start(f32[2,8,512]{2,1,0:T(8,128)S(1)} %get-tuple-element.30), channel_id=1, source_target_pairs={{1,2},{3,4},{5,6},{7,0},{2,1},{4,3},{6,5},{0,7},{9,10},{11,12},{13... | collective-permute-start | bytes 98312 | tf_op jit(solution)/shard_map/ppermute | solution.py:428
  18.9 4.5 %collective-permute-start.5 = (f32[2,8,512]{2,1,0:T(8,128)S(1)}, f32[2,8,512]{2,1,0:T(8,128)S(1)}, u32[]{:S(2)}, u32[]{:S(2)}) collective-permute-start(f32[2,8,512]{2,1,0:T(8,128)S(1)} %get-tuple-element.31), channel_id=1, source_target_pairs={{0,1},{2,3},{4,5},{6,7},{1,0},{3,2},{5,4},{7,6},{8,9},{10,11},{12,... | collective-permute-start | bytes 98312 | tf_op jit(solution)/shard_map/ppermute | solution.py:428
  23.7 4.2 %collective-permute-start.6 = (f32[2,8,512]{2,1,0:T(8,128)S(1)}, f32[2,8,512]{2,1,0:T(8,128)S(1)}, u32[]{:S(2)}, u32[]{:S(2)}) collective-permute-start(f32[2,8,512]{2,1,0:T(8,128)S(1)} %get-tuple-element.33), channel_id=1, source_target_pairs={{0,8},{16,24},{8,0},{24,16},{1,9},{17,25},{9,1},{25,17},{2,10},{18... | collective-permute-start | bytes 98312 | tf_op jit(solution)/shard_map/ppermute | solution.py:428
  23.8 6.7 %collective-permute-start.7 = (f32[2,8,512]{2,1,0:T(8,128)S(1)}, f32[2,8,512]{2,1,0:T(8,128)S(1)}, u32[]{:S(2)}, u32[]{:S(2)}) collective-permute-start(f32[2,8,512]{2,1,0:T(8,128)S(1)} %get-tuple-element.34), channel_id=1, source_target_pairs={{8,16},{16,8},{9,17},{17,9},{10,18},{18,10},{11,19},{19,11},{12,20... | collective-permute-start | bytes 98312 | tf_op jit(solution)/shard_map/ppermute | solution.py:428

commit v21 on v20

--- a/solution.py
+++ b/solution.py
@@ -344,9 +344,9 @@
     rows_of[1] = coarse
     rows_of[2] = tiles - coarse
 
-    total = jnp.zeros((2 * classes, span), jnp.float32)
+    sums = [jnp.zeros((2 * classes, span), jnp.float32) for _ in range(2)]
     group = 2 * RUNS // runs
-    for first in range(0, shards, group):
+    for turn, first in enumerate(range(0, shards, group)):
         left, right = [], []
         for run in range(group * runs):
             row = (first + run // runs) * rows + run % runs * 2
@@ -354,9 +354,10 @@
             left.append(jnp.concatenate([jnp.where(mine, tall(kind, row), zero) for kind in (1, 2)], axis=0))
             low = jnp.broadcast_to(lows[:, row + 1:row + 2], (LANES, LANES))
             right.append(jnp.concatenate([jnp.maximum(low, place) for place in places], axis=1))
-        total = total + jnp.dot(
+        sums[turn % 2] = sums[turn % 2] + jnp.dot(
             jnp.concatenate(left, axis=1), jnp.concatenate(right, axis=0), preferred_element_type=jnp.float32
         )
+    total = sums[0] + sums[1]
     both = (total[:classes] + total[classes:]) * bin_width
     every = both[:, span - 1:] * (1.0 / span)
     lane = lax.broadcasted_iota(jnp.int32, both.shape, 1)

time: 31.4 us -> 31.4 us (level)
  no operation moved by 1% of the time
where the time goes in v21:
time: 31.4 us; the launch traced here: 31.2 us
  starting transfers between devices  14.4 us (46%)
  Pallas kernels  9.58 us (31%)
  waiting for transfers between devices  6.41 us (20%)
  local copies, waits for them, and re-layouts  0.5 us (2%)
    ppermute x8, starting transfers between devices, swap(): lax.ppermute(values, axis, both_ways(pairs))  11.3 us
    pallas_call x7, Pallas kernels, call(): pl.pallas_call(kernel, out_shape=outs, in_specs=[VMEM] * len(operands), o...  7.12 us
    ppermute x8, waiting for transfers between devices, swap(): lax.ppermute(values, axis, both_ways(pairs))  4.01 us
    all_to_all x1, starting transfers between devices, on_device(): lax.all_to_all(packed, ('lat', 'lon'), split_axis=0, concat_axis=0, tiled...  3.09 us
    all_to_all x1, waiting for transfers between devices, on_device(): lax.all_to_all(packed, ('lat', 'lon'), split_axis=0, concat_axis=0, tiled...  2.4 us
    pallas_call x1, Pallas kernels, on_device(): pl.pallas_call(open_kernel, out_shape=(jax.ShapeDtypeStruct((shards, 2 *...  1.79 us
    pallas_call x1, Pallas kernels, on_device(): pl.pallas_call(close_kernel, out_shape=tile, in_specs=[VMEM] * 3, out_spe...  0.67 us
  transfers between devices with their start and end apart: 9, of which 3 were waited for; matrix products, arithmetic and copies ran while one was open for 2% of the time, Pallas kernels for 22%

profile of v21, /device:TPU:2, one launch (start us, length us, event | category | flops | bytes accessed | tf_op | source)
XLA Modules:
  0.0 31.2 jit_solution(6790423895660632231)
XLA Ops:
  0.0 1.8 %opening.1 = (f32[32,8,128]{2,1,0:T(8,128)}, f32[8,8,512]{2,1,0:T(8,128)S(1)}, f32[4,8,512]{2,1,0:T(8,128)S(1)}, f32[4,8,512]{2,1,0:T(8,128)S(1)}, f32[27,2,512]{2,1,0:T(2,128)S(1)}) custom-call(s32[1,32]{1,0:T(1,128)} %counts_in.1, s32[1,32]{1,0:T(1,128)} %offsets_in.1, f32[128,128]{1,0:T(8,128)} %bitcast.26, s32[128,128]{1,0:T(8,128)} %bitcast.27, ...), custom_call_target="tpu_custom_call" | custom-call | tf_op jit(solution)/shard_map/opening/pallas_call | solution.py:453
  1.8 0.1 collective-permute-start
  1.9 3.7 %collective-permute-start.1 = (f32[4,8,512]{2,1,0:T(8,128)S(1)}, f32[4,8,512]{2,1,0:T(8,128)S(1)}, u32[]{:S(2)}, u32[]{:S(2)}) collective-permute-start(f32[4,8,512]{2,1,0:T(8,128)S(1)} %get-tuple-element.23), channel_id=1, source_target_pairs={{1,2},{3,4},{5,6},{7,0},{2,1},{4,3},{6,5},{0,7},{9,10},{11,12},{13... | collective-permute-start | bytes 196616 | tf_op jit(solution)/shard_map/ppermute | solution.py:429
  5.6 3.1 %all-to-all-start = ((f32[32,8,128]{2,1,0:T(8,128)}), f32[32,8,128]{2,1,0:T(8,128)S(1)}, u32[]{:S(2)}, u32[]{:S(2)}) async-start(f32[32,8,128]{2,1,0:T(8,128)} %get-tuple-element.20), calls=%async_computation | async-start | bytes 262144 | tf_op jit(solution)/shard_map/all_to_all | solution.py:468
  8.7 0.2 rev.7
  8.9 0.1 copy.12
  9.0 0.1 slice_bitcast_fusion.1
  9.1 0.1 pad_bitcast_fusion
  9.2 3.4 %collective-permute-start.2 = (f32[4,8,512]{2,1,0:T(8,128)S(1)}, f32[4,8,512]{2,1,0:T(8,128)S(1)}, u32[]{:S(2)}, u32[]{:S(2)}) collective-permute-start(f32[4,8,512]{2,1,0:T(8,128)S(1)} %get-tuple-element.24), channel_id=1, source_target_pairs={{8,16},{16,8},{9,17},{17,9},{10,18},{18,10},{11,19},{19,11},{12,20... | collective-permute-start | bytes 196616 | tf_op jit(solution)/shard_map/ppermute | solution.py:429
  12.6 0.1 collective-permute-start.3
  12.7 0.9 %density_inside.1 = (f32[4,16,512]{2,1,0:T(8,128)S(1)}, f32[3,3,6,16,512]{4,3,2,1,0:T(8,128)S(1)}) custom-call(f32[8,8,512]{2,1,0:T(8,128)S(1)} %get-tuple-element.21.field.latent, f32[4,8,512]{2,1,0:T(8,128)S(1)} %collective-permute-done.side_0, f32[4,8,512]{2,1,0:T(8,128)S(1)} %collective-permute-done.1.side_1, f32[2,27,512]{2,1,0:T(8,128)S(1)} %bitcast.20), custom_call_target="tpu_custom_call" | custom-call | tf_op jit(solution)/shard_map/density_inside/pallas_call | solution.py:477
  13.6 2.4 %all-to-all-done.got = f32[32,8,128]{2,1,0:T(8,128)S(1)} async-done(((f32[32,8,128]{2,1,0:T(8,128)}), f32[32,8,128]{2,1,0:T(8,128)S(1)}, u32[]{:S(2)}, u32[]{:S(2)}) %all-to-all-start) | async-done | bytes 131104 | tf_op jit(solution)/shard_map/all_to_all | solution.py:468
  16.0 2.2 %bin_sides.1 = (f32[8,8,512]{2,1,0:T(8,128)S(1)}, f32[2,8,512]{2,1,0:T(8,128)S(1)}, f32[2,8,512]{2,1,0:T(8,128)S(1)}) custom-call(f32[32,8,128]{2,1,0:T(8,128)S(1)} %all-to-all-done.got, f32[4,16,512]{2,1,0:T(8,128)S(1)} %get-tuple-element.28._.inner), custom_call_target="tpu_custom_call" | custom-call | tf_op jit(solution)/shard_map/bin_sides/pallas_call | solution.py:477
  18.2 0.8 %collective-permute-start.4 = (f32[2,8,512]{2,1,0:T(8,128)S(1)}, f32[2,8,512]{2,1,0:T(8,128)S(1)}, u32[]{:S(2)}, u32[]{:S(2)}) collective-permute-start(f32[2,8,512]{2,1,0:T(8,128)S(1)} %get-tuple-element.30), channel_id=1, source_target_pairs={{1,2},{3,4},{5,6},{7,0},{2,1},{4,3},{6,5},{0,7},{9,10},{11,12},{13... | collective-permute-start | bytes 98312 | tf_op jit(solution)/shard_map/ppermute | solution.py:429
  18.9 0.1 pad_maximum_fusion
  19.1 0.7 %density_ends.1.density = f32[8,16,512]{2,1,0:T(8,128)S(1)} custom-call(f32[8,8,512]{2,1,0:T(8,128)S(1)} %get-tuple-element.21.field.latent, f32[4,8,512]{2,1,0:T(8,128)S(1)} %collective-permute-done.side_0, f32[4,8,512]{2,1,0:T(8,128)S(1)} %collective-permute-done.1.side_1, f32[4,8,512]{2,1,0:T(8,128)S(1)} %collective-permute-done.2.end_1, ...), custom_call_target="tpu_custom_call" | custom-call | tf_op jit(solution)/shard_map/density_ends/pallas_call | solution.py:477
  19.8 2.2 %bin_rest.1.field = f32[8,8,512]{2,1,0:T(8,128)S(1)} custom-call(f32[32,8,128]{2,1,0:T(8,128)S(1)} %all-to-all-done.got, f32[8,16,512]{2,1,0:T(8,128)S(1)} %density_ends.1.density, f32[8,8,512]{2,1,0:T(8,128)S(1)} %get-tuple-element.29._.behind), custom_call_target="tpu_custom_call" | custom-call | tf_op jit(solution)/shard_map/bin_rest/pallas_call | solution.py:477
  22.0 1.4 %collective-permute-done.4.side_1 = f32[2,8,512]{2,1,0:T(8,128)S(1)} collective-permute-done((f32[2,8,512]{2,1,0:T(8,128)S(1)}, f32[2,8,512]{2,1,0:T(8,128)S(1)}, u32[]{:S(2)}, u32[]{:S(2)}) %collective-permute-start.4) | collective-permute-done | bytes 32800 | tf_op jit(solution)/shard_map/ppermute | solution.py:429
  23.4 0.4 %back_reach.1 = (f32[2,8,512]{2,1,0:T(8,128)S(1)}, f32[2,8,512]{2,1,0:T(8,128)S(1)}, f32[3,3,4,8,512]{4,3,2,1,0:T(8,128)S(1)}) custom-call(f32[8,8,512]{2,1,0:T(8,128)S(1)} %bin_rest.1.field, f32[2,8,512]{2,1,0:T(8,128)S(1)} %collective-permute-done.4.side_1, f32[2,8,512]{2,1,0:T(8,128)S(1)} %collective-permute-done.5.side_0, ...), custom_call_target="tpu_custom_call" | custom-call | tf_op jit(solution)/shard_map/back_reach/pallas_call | solution.py:477
  23.7 0.1 collective-permute-start.6
  23.8 3.3 %collective-permute-start.7 = (f32[2,8,512]{2,1,0:T(8,128)S(1)}, f32[2,8,512]{2,1,0:T(8,128)S(1)}, u32[]{:S(2)}, u32[]{:S(2)}) collective-permute-start(f32[2,8,512]{2,1,0:T(8,128)S(1)} %get-tuple-element.34), channel_id=1, source_target_pairs={{8,16},{16,8},{9,17},{17,9},{10,18},{18,10},{11,19},{19,11},{12,20... | collective-permute-start | bytes 98312 | tf_op jit(solution)/shard_map/ppermute | solution.py:429
  27.1 0.8 %back_own.1.own = f32[8,8,512]{2,1,0:T(8,128)S(1)} custom-call(f32[8,8,512]{2,1,0:T(8,128)S(1)} %bin_rest.1.field, f32[2,8,512]{2,1,0:T(8,128)S(1)} %collective-permute-done.4.side_1, f32[2,8,512]{2,1,0:T(8,128)S(1)} %collective-permute-done.5.side_0, f32[8,16,512]{2,1,0:T(8,128)S(1)} %density_ends.1.density, f32[2,27,512]{2,1,0:T(8,128)S(1)} %rev.8.stencils, ...), custom_call_target="tpu_custom_call" | custom-call | tf_op jit(solution)/shard_map/back_own/pallas_call | solution.py:477
  28.0 2.6 %collective-permute-done.7.end_1 = f32[2,8,512]{2,1,0:T(8,128)S(1)} collective-permute-done((f32[2,8,512]{2,1,0:T(8,128)S(1)}, f32[2,8,512]{2,1,0:T(8,128)S(1)}, u32[]{:S(2)}, u32[]{:S(2)}) %collective-permute-start.7) | collective-permute-done | bytes 32800 | tf_op jit(solution)/shard_map/ppermute | solution.py:429
  30.5 0.7 %close.1 = f32[8,8,512]{2,1,0:T(8,128)} custom-call(f32[8,8,512]{2,1,0:T(8,128)S(1)} %back_own.1.own, f32[2,8,512]{2,1,0:T(8,128)S(1)} %collective-permute-done.6.end_0, f32[2,8,512]{2,1,0:T(8,128)S(1)} %collective-permute-done.7.end_1), custom_call_target="tpu_custom_call" | custom-call | tf_op jit(solution)/shard_map/close/pallas_call | solution.py:519
  (12 shorter events, 0.1 us)
Async XLA Ops:
  1.8 7.4 %collective-permute-start = (f32[4,8,512]{2,1,0:T(8,128)S(1)}, f32[4,8,512]{2,1,0:T(8,128)S(1)}, u32[]{:S(2)}, u32[]{:S(2)}) collective-permute-start(f32[4,8,512]{2,1,0:T(8,128)S(1)} %get-tuple-element.22), channel_id=1, source_target_pairs={{0,1},{2,3},{4,5},{6,7},{1,0},{3,2},{5,4},{7,6},{8,9},{10,11},{12,... | collective-permute-start | bytes 196616 | tf_op jit(solution)/shard_map/ppermute | solution.py:429
  1.9 7.3 %collective-permute-start.1 = (f32[4,8,512]{2,1,0:T(8,128)S(1)}, f32[4,8,512]{2,1,0:T(8,128)S(1)}, u32[]{:S(2)}, u32[]{:S(2)}) collective-permute-start(f32[4,8,512]{2,1,0:T(8,128)S(1)} %get-tuple-element.23), channel_id=1, source_target_pairs={{1,2},{3,4},{5,6},{7,0},{2,1},{4,3},{6,5},{0,7},{9,10},{11,12},{13... | collective-permute-start | bytes 196616 | tf_op jit(solution)/shard_map/ppermute | solution.py:429
  5.6 10.4 %all-to-all-start = ((f32[32,8,128]{2,1,0:T(8,128)}), f32[32,8,128]{2,1,0:T(8,128)S(1)}, u32[]{:S(2)}, u32[]{:S(2)}) async-start(f32[32,8,128]{2,1,0:T(8,128)} %get-tuple-element.20), calls=%async_computation | async-start | bytes 262144 | tf_op jit(solution)/shard_map/all_to_all | solution.py:468
  9.2 9.8 %collective-permute-start.2 = (f32[4,8,512]{2,1,0:T(8,128)S(1)}, f32[4,8,512]{2,1,0:T(8,128)S(1)}, u32[]{:S(2)}, u32[]{:S(2)}) collective-permute-start(f32[4,8,512]{2,1,0:T(8,128)S(1)} %get-tuple-element.24), channel_id=1, source_target_pairs={{8,16},{16,8},{9,17},{17,9},{10,18},{18,10},{11,19},{19,11},{12,20... | collective-permute-start | bytes 196616 | tf_op jit(solution)/shard_map/ppermute | solution.py:429
  12.6 6.4 %collective-permute-start.3 = (f32[4,8,512]{2,1,0:T(8,128)S(1)}, f32[4,8,512]{2,1,0:T(8,128)S(1)}, u32[]{:S(2)}, u32[]{:S(2)}) collective-permute-start(f32[4,8,512]{2,1,0:T(8,128)S(1)} %get-tuple-element.25), channel_id=1, source_target_pairs={{0,8},{16,24},{8,0},{24,16},{1,9},{17,25},{9,1},{25,17},{2,10},{18... | collective-permute-start | bytes 196616 | tf_op jit(solution)/shard_map/ppermute | solution.py:429
  18.2 5.2 %collective-permute-start.4 = (f32[2,8,512]{2,1,0:T(8,128)S(1)}, f32[2,8,512]{2,1,0:T(8,128)S(1)}, u32[]{:S(2)}, u32[]{:S(2)}) collective-permute-start(f32[2,8,512]{2,1,0:T(8,128)S(1)} %get-tuple-element.30), channel_id=1, source_target_pairs={{1,2},{3,4},{5,6},{7,0},{2,1},{4,3},{6,5},{0,7},{9,10},{11,12},{13... | collective-permute-start | bytes 98312 | tf_op jit(solution)/shard_map/ppermute | solution.py:429
  18.9 4.5 %collective-permute-start.5 = (f32[2,8,512]{2,1,0:T(8,128)S(1)}, f32[2,8,512]{2,1,0:T(8,128)S(1)}, u32[]{:S(2)}, u32[]{:S(2)}) collective-permute-start(f32[2,8,512]{2,1,0:T(8,128)S(1)} %get-tuple-element.31), channel_id=1, source_target_pairs={{0,1},{2,3},{4,5},{6,7},{1,0},{3,2},{5,4},{7,6},{8,9},{10,11},{12,... | collective-permute-start | bytes 98312 | tf_op jit(solution)/shard_map/ppermute | solution.py:429
  23.7 4.2 %collective-permute-start.6 = (f32[2,8,512]{2,1,0:T(8,128)S(1)}, f32[2,8,512]{2,1,0:T(8,128)S(1)}, u32[]{:S(2)}, u32[]{:S(2)}) collective-permute-start(f32[2,8,512]{2,1,0:T(8,128)S(1)} %get-tuple-element.33), channel_id=1, source_target_pairs={{0,8},{16,24},{8,0},{24,16},{1,9},{17,25},{9,1},{25,17},{2,10},{18... | collective-permute-start | bytes 98312 | tf_op jit(solution)/shard_map/ppermute | solution.py:429
  23.8 6.7 %collective-permute-start.7 = (f32[2,8,512]{2,1,0:T(8,128)S(1)}, f32[2,8,512]{2,1,0:T(8,128)S(1)}, u32[]{:S(2)}, u32[]{:S(2)}) collective-permute-start(f32[2,8,512]{2,1,0:T(8,128)S(1)} %get-tuple-element.34), channel_id=1, source_target_pairs={{8,16},{16,8},{9,17},{17,9},{10,18},{18,10},{11,19},{19,11},{12,20... | collective-permute-start | bytes 98312 | tf_op jit(solution)/shard_map/ppermute | solution.py:429

commit v22 on v20

--- a/solution.py
+++ b/solution.py
@@ -26,20 +26,6 @@
 
 def sublane(radial):
     return lax.broadcasted_iota(jnp.int32, (SUBLANES, radial), 0)
-
-
-def pack_sides(rows, to_partner, to_outer):
-    _, odd = position("lon")
-    sub = sublane(rows[0].shape[1])
-    for group in range(len(rows) // 4):
-        before, after = rows[4 * group], rows[4 * group]
-        for k in range(1, 4):
-            row = rows[4 * group + k]
-            pair = lax.shift_right_logical(sub, 1)
-            before = jnp.where(pair == k, pltpu.roll(row, 2 * k, 0), before)
-            after = jnp.where(pair == 3 - k, pltpu.roll(row, SUBLANES - 2 * k, 0), after)
-        to_partner[group] = either(odd, before, after)
-        to_outer[group] = either(odd, after, before)
 
 
 def unpack_sides(from_partner, from_outer, height):
@@ -50,10 +36,8 @@
         partner, outer = from_partner[group], from_outer[group]
         before, after = either(odd, partner, outer), either(odd, outer, partner)
         for k in range(4):
-            if k:
-                tiles.append(jnp.where(sub < 4, pltpu.roll(after, SUBLANES - 2 * k, 0), pltpu.roll(before, 2 * k, 0)))
-            else:
-                tiles.append(jnp.where(sub < 4, after, before))
+            ahead = pltpu.roll(after, -2 * k % SUBLANES, 0)
+            tiles.append(jnp.where(sub < 4, ahead, pltpu.roll(before, SUBLANES - 2 - 2 * k, 0)))
     return tiles
 
 
@@ -314,18 +298,18 @@
     copies[-1].wait()
 
 
-def behind_of(got, part, cuts, runs, rows_of, *, height, width, radial):
-    span = radial // cuts
-    pixels = height * width // 2
-    classes = cuts * pixels
+def behind_of(got, index_of, pixels, runs, rows_of, *, width, radial):
+    span = radial // 2
+    classes = 2 * pixels
     shards, rows, _ = got.shape
     bf16 = jnp.bfloat16
     column = lax.broadcasted_iota(jnp.int32, (classes, LANES), 0).astype(jnp.float32).astype(bf16)
     places = [
-        (lax.broadcasted_iota(jnp.int32, (LANES, LANES), 1) + (first + 1)).astype(jnp.float32).astype(bf16)
+        (lax.broadcasted_iota(jnp.int32, (LANES, LANES), 1) + first).astype(jnp.float32).astype(bf16)
         for first in range(0, span, LANES)
     ]
     zero = jnp.zeros((), bf16)
+    one = jnp.ones((), bf16)
 
     def tall(kind, row):
         line = jnp.broadcast_to(rows_of[kind, row:row + 1, :], (16, LANES))
@@ -335,11 +319,10 @@
     cell = tiles.astype(jnp.int32)
     pixel = lax.shift_right_logical(cell, radial.bit_length() - 1)
     bins = lax.bitwise_and(cell, radial - 1)
-    cut = lax.shift_right_logical(bins, span.bit_length() - 1)
-    place = lax.bitwise_and(pixel + 2, width - 1)
-    own = cut * pixels + lax.shift_right_logical(pixel, 3) * 4 + lax.bitwise_and(place, 3)
-    rows_of[0] = jnp.where(lax.shift_right_logical(place, 2) == part, own, classes).astype(jnp.float32)
-    lows = jnp.transpose((lax.bitwise_and(bins, span - 1) + 1).astype(jnp.float32)).astype(bf16)
+    upper = lax.shift_right_logical(bins, span.bit_length() - 1)
+    index = index_of(lax.shift_right_logical(pixel, width.bit_length() - 1), lax.bitwise_and(pixel, width - 1))
+    rows_of[0] = jnp.where(index < pixels, upper * pixels + index, classes).astype(jnp.float32)
+    lows = jnp.transpose(lax.bitwise_and(bins, span - 1).astype(jnp.float32)).astype(bf16)
     coarse = tiles.astype(bf16).astype(jnp.float32)
     rows_of[1] = coarse
     rows_of[2] = tiles - coarse
@@ -353,27 +336,13 @@
             mine = tall(0, row + 1) == column
             left.append(jnp.concatenate([jnp.where(mine, tall(kind, row), zero) for kind in (1, 2)], axis=0))
             low = jnp.broadcast_to(lows[:, row + 1:row + 2], (LANES, LANES))
-            right.append(jnp.concatenate([jnp.maximum(low, place) for place in places], axis=1))
+            right.append(jnp.concatenate([jnp.where(low >= place, one, zero) for place in places], axis=1))
         total = total + jnp.dot(
             jnp.concatenate(left, axis=1), jnp.concatenate(right, axis=0), preferred_element_type=jnp.float32
         )
     both = (total[:classes] + total[classes:]) * bin_width
-    every = both[:, span - 1:] * (1.0 / span)
-    lane = lax.broadcasted_iota(jnp.int32, both.shape, 1)
-    at_least = jnp.where(lane == 0, every, pltpu.roll(both, 1, 1) - both + every)
-    ranges = [at_least[start:start + pixels] for start in range(0, classes, pixels)]
-    for k in reversed(range(cuts - 1)):
-        ranges[k] = ranges[k] + ranges[k + 1][:, :1]
-    return jnp.concatenate(ranges, axis=1)
-
-
-def column_rows(packed, part, height):
-    rows = []
-    for row in range(height):
-        tile = packed[row // 2 * SUBLANES:(row // 2 + 1) * SUBLANES]
-        turn = row % 2 * 4 + (2 if part == 0 else SUBLANES - 2)
-        rows.append(pltpu.roll(tile, (SUBLANES - turn) % SUBLANES, 0))
-    return rows
+    near, far = both[:pixels], both[pixels:]
+    return jnp.concatenate([near + far[:, :1], far], axis=1)
 
 
 def for_load(body):
@@ -383,27 +352,42 @@
     pl.when(jnp.logical_not(middle))(lambda: body(LEAST // LANES))
 
 
-def bin_sides_kernel(got, _, behind, to_partner, to_outer, rows_of):
-    height, width, radial = behind.shape
+def bin_sides_kernel(got, _, to_partner, to_outer, rows_of):
+    _, odd = position("lon")
+
+    def index_of(row, col):
+        side = lax.bitwise_xor(lax.shift_right_logical(col, 2), odd)
+        return jnp.where((col < 2) | (col >= 6), side * 16 + row * 2 + lax.bitwise_and(col, 1), 32)
 
     def body(runs):
-        packed = behind_of(got, 0, 2, runs, rows_of, height=height, width=width, radial=radial)
-        lines = column_rows(packed, 0, height)
-        for row, values in enumerate(lines):
-            behind[row] = values
-        pack_sides(lines, to_partner, to_outer)
+        packed = behind_of(got, index_of, 32, runs, rows_of, width=SUBLANES, radial=to_outer.shape[2])
+        for place in range(2):
+            to_outer[place] = packed[place * SUBLANES:(place + 1) * SUBLANES]
+            to_partner[place] = packed[(2 + place) * SUBLANES:(3 + place) * SUBLANES]
 
     for_load(body)
 
 
-def bin_rest_kernel(got, density, behind, upstream, rows_of):
-    height, width, radial = behind.shape
+def bin_rest_kernel(got, density, to_partner, to_outer, upstream, rows_of):
+    height, width, radial = upstream.shape
+    _, odd = position("lon")
     sub = sublane(radial)
 
     def body(runs):
-        packed = behind_of(got, 1, 2, runs, rows_of, height=height, width=width, radial=radial)
-        for row, values in enumerate(column_rows(packed, 1, height)):
-            upstream[row] = density[row, :width] * jnp.where((sub < 2) | (sub >= 6), behind[row], values)
+        packed = behind_of(
+            got, lambda row, col: jnp.where((col >= 2) & (col < 6), row * 4 + col - 2, 32), 32, runs, rows_of,
+            width=width, radial=radial,
+        )
+        for row in range(height):
+            group, k = row // 4, row % 4
+            partner, outer = to_partner[group], to_outer[group]
+            first, last = either(odd, partner, outer), either(odd, outer, partner)
+            first = pltpu.roll(first, -2 * k % SUBLANES, 0)
+            last = pltpu.roll(last, SUBLANES - 2 - 2 * k, 0)
+            inner = packed[row // 2 * SUBLANES:(row // 2 + 1) * SUBLANES]
+            inner = pltpu.roll(inner, 6 if row % 2 else 2, 0)
+            mine = jnp.where(sub < 2, first, jnp.where(sub < 6, inner, last))
+            upstream[row] = density[row, :width] * mine
 
     for_load(body)
 
@@ -497,13 +481,13 @@
         (shape(height - 4, broad, radial), shape(3, 3, height - 2, broad, radial)), [rows, moved],
         latent, *beside, stencils,
     )
-    behind, *to_sides = call(bin_sides_kernel, "bin_sides", (tile, sides, sides), star_rows, got, inner)
+    to_sides = call(bin_sides_kernel, "bin_sides", (sides, sides), star_rows, got, inner)
     density = call(
         density_ends_kernel, "density_ends", shape(height, broad, radial),
         [pltpu.VMEM((3, 3, 4, broad, radial), f32), rows, moved],
-        latent, *beside, *above[::-1], stencils, middle, inner, behind,
-    )
-    upstream = call(bin_rest_kernel, "bin_rest", tile, star_rows, got, density, behind)
+        latent, *beside, *above[::-1], stencils, middle, inner, to_sides[1],
+    )
+    upstream = call(bin_rest_kernel, "bin_rest", tile, star_rows, got, density, *to_sides)
 
     beside = swap(*to_sides, "lon", True, outer_first=True)
     *to_ends, middle = call(

time: 31.4 us -> 31.3 us (level)
  transfers between devices with their start and end apart: 9 -> 9, of which waited for: 3 -> 3; matrix products, arithmetic and copies ran while one was open for 2% -> 2% of each run, Pallas kernels for 22% -> 21%
where the time goes in v22:
time: 31.3 us; the launch traced here: 31.1 us
  starting transfers between devices  14.4 us (46%)
  Pallas kernels  9.46 us (30%)
  waiting for transfers between devices  6.46 us (21%)
  local copies, waits for them, and re-layouts  0.5 us (2%)
    ppermute x8, starting transfers between devices, swap(): lax.ppermute(values, axis, both_ways(pairs))  11.3 us
    pallas_call x7, Pallas kernels, call(): pl.pallas_call(kernel, out_shape=outs, in_specs=[VMEM] * len(operands), o...  6.99 us
    ppermute x8, waiting for transfers between devices, swap(): lax.ppermute(values, axis, both_ways(pairs))  4.06 us
    all_to_all x1, starting transfers between devices, on_device(): lax.all_to_all(packed, ('lat', 'lon'), split_axis=0, concat_axis=0, tiled...  3.09 us
    all_to_all x1, waiting for transfers between devices, on_device(): lax.all_to_all(packed, ('lat', 'lon'), split_axis=0, concat_axis=0, tiled...  2.4 us
    pallas_call x1, Pallas kernels, on_device(): pl.pallas_call(open_kernel, out_shape=(jax.ShapeDtypeStruct((shards, 2 *...  1.79 us
    pallas_call x1, Pallas kernels, on_device(): pl.pallas_call(close_kernel, out_shape=tile, in_specs=[VMEM] * 3, out_spe...  0.67 us
  transfers between devices with their start and end apart: 9, of which 3 were waited for; matrix products, arithmetic and copies ran while one was open for 2% of the time, Pallas kernels for 21%

profile of v22, /device:TPU:2, one launch (start us, length us, event | category | flops | bytes accessed | tf_op | source)
XLA Modules:
  0.0 31.1 jit_solution(7617256497365290846)
XLA Ops:
  0.0 1.8 %opening.1 = (f32[32,8,128]{2,1,0:T(8,128)}, f32[8,8,512]{2,1,0:T(8,128)S(1)}, f32[4,8,512]{2,1,0:T(8,128)S(1)}, f32[4,8,512]{2,1,0:T(8,128)S(1)}, f32[27,2,512]{2,1,0:T(2,128)S(1)}) custom-call(s32[1,32]{1,0:T(1,128)} %counts_in.1, s32[1,32]{1,0:T(1,128)} %offsets_in.1, f32[128,128]{1,0:T(8,128)} %bitcast.26, s32[128,128]{1,0:T(8,128)} %bitcast.27, ...), custom_call_target="tpu_custom_call" | custom-call | tf_op jit(solution)/shard_map/opening/pallas_call | solution.py:436
  1.8 0.1 collective-permute-start
  1.9 3.7 %collective-permute-start.1 = (f32[4,8,512]{2,1,0:T(8,128)S(1)}, f32[4,8,512]{2,1,0:T(8,128)S(1)}, u32[]{:S(2)}, u32[]{:S(2)}) collective-permute-start(f32[4,8,512]{2,1,0:T(8,128)S(1)} %get-tuple-element.22), channel_id=1, source_target_pairs={{1,2},{3,4},{5,6},{7,0},{2,1},{4,3},{6,5},{0,7},{9,10},{11,12},{13... | collective-permute-start | bytes 196616 | tf_op jit(solution)/shard_map/ppermute | solution.py:412
  5.6 3.1 %all-to-all-start = ((f32[32,8,128]{2,1,0:T(8,128)}), f32[32,8,128]{2,1,0:T(8,128)S(1)}, u32[]{:S(2)}, u32[]{:S(2)}) async-start(f32[32,8,128]{2,1,0:T(8,128)} %get-tuple-element.19), calls=%async_computation | async-start | bytes 262144 | tf_op jit(solution)/shard_map/all_to_all | solution.py:451
  8.7 0.2 rev.7
  8.9 0.1 copy.12
  9.0 0.1 slice_bitcast_fusion.1
  9.1 0.1 pad_bitcast_fusion
  9.2 3.4 %collective-permute-start.2 = (f32[4,8,512]{2,1,0:T(8,128)S(1)}, f32[4,8,512]{2,1,0:T(8,128)S(1)}, u32[]{:S(2)}, u32[]{:S(2)}) collective-permute-start(f32[4,8,512]{2,1,0:T(8,128)S(1)} %get-tuple-element.23), channel_id=1, source_target_pairs={{8,16},{16,8},{9,17},{17,9},{10,18},{18,10},{11,19},{19,11},{12,20... | collective-permute-start | bytes 196616 | tf_op jit(solution)/shard_map/ppermute | solution.py:412
  12.6 0.1 collective-permute-start.3
  12.7 0.9 %density_inside.1 = (f32[4,16,512]{2,1,0:T(8,128)S(1)}, f32[3,3,6,16,512]{4,3,2,1,0:T(8,128)S(1)}) custom-call(f32[8,8,512]{2,1,0:T(8,128)S(1)} %get-tuple-element.20.field.latent, f32[4,8,512]{2,1,0:T(8,128)S(1)} %collective-permute-done.side_0, f32[4,8,512]{2,1,0:T(8,128)S(1)} %collective-permute-done.1.side_1, f32[2,27,512]{2,1,0:T(8,128)S(1)} %bitcast.20), custom_call_target="tpu_custom_call" | custom-call | tf_op jit(solution)/shard_map/density_inside/pallas_call | solution.py:460
  13.6 2.4 %all-to-all-done.got = f32[32,8,128]{2,1,0:T(8,128)S(1)} async-done(((f32[32,8,128]{2,1,0:T(8,128)}), f32[32,8,128]{2,1,0:T(8,128)S(1)}, u32[]{:S(2)}, u32[]{:S(2)}) %all-to-all-start) | async-done | bytes 131104 | tf_op jit(solution)/shard_map/all_to_all | solution.py:451
  16.0 2.1 %bin_sides.1 = (f32[2,8,512]{2,1,0:T(8,128)S(1)}, f32[2,8,512]{2,1,0:T(8,128)S(1)}) custom-call(f32[32,8,128]{2,1,0:T(8,128)S(1)} %all-to-all-done.got, f32[4,16,512]{2,1,0:T(8,128)S(1)} %get-tuple-element.27._.inner), custom_call_target="tpu_custom_call" | custom-call | tf_op jit(solution)/shard_map/bin_sides/pallas_call | solution.py:460
  18.1 0.7 %collective-permute-start.4 = (f32[2,8,512]{2,1,0:T(8,128)S(1)}, f32[2,8,512]{2,1,0:T(8,128)S(1)}, u32[]{:S(2)}, u32[]{:S(2)}) collective-permute-start(f32[2,8,512]{2,1,0:T(8,128)S(1)} %get-tuple-element.28._.to_outer), channel_id=1, source_target_pairs={{1,2},{3,4},{5,6},{7,0},{2,1},{4,3},{6,5},{0,7},{9,10},{11,12},{13... | collective-permute-start | bytes 98312 | tf_op jit(solution)/shard_map/ppermute | solution.py:412
  18.8 0.1 pad_maximum_fusion
  18.9 0.7 %density_ends.1.density = f32[8,16,512]{2,1,0:T(8,128)S(1)} custom-call(f32[8,8,512]{2,1,0:T(8,128)S(1)} %get-tuple-element.20.field.latent, f32[4,8,512]{2,1,0:T(8,128)S(1)} %collective-permute-done.side_0, f32[4,8,512]{2,1,0:T(8,128)S(1)} %collective-permute-done.1.side_1, f32[4,8,512]{2,1,0:T(8,128)S(1)} %collective-permute-done.2.end_1, ...), custom_call_target="tpu_custom_call" | custom-call | tf_op jit(solution)/shard_map/density_ends/pallas_call | solution.py:460
  19.7 2.1 %bin_rest.1.field = f32[8,8,512]{2,1,0:T(8,128)S(1)} custom-call(f32[32,8,128]{2,1,0:T(8,128)S(1)} %all-to-all-done.got, f32[8,16,512]{2,1,0:T(8,128)S(1)} %density_ends.1.density, f32[2,8,512]{2,1,0:T(8,128)S(1)} %get-tuple-element.29.to_partner, f32[2,8,512]{2,1,0:T(8,128)S(1)} %get-tuple-element.28._.to_outer), custom_call_target="tpu_custom_call" | custom-call | tf_op jit(solution)/shard_map/bin_rest/pallas_call | solution.py:460
  21.8 1.5 %collective-permute-done.4.side_1 = f32[2,8,512]{2,1,0:T(8,128)S(1)} collective-permute-done((f32[2,8,512]{2,1,0:T(8,128)S(1)}, f32[2,8,512]{2,1,0:T(8,128)S(1)}, u32[]{:S(2)}, u32[]{:S(2)}) %collective-permute-start.4) | collective-permute-done | bytes 32800 | tf_op jit(solution)/shard_map/ppermute | solution.py:412
  23.3 0.3 %back_reach.1 = (f32[2,8,512]{2,1,0:T(8,128)S(1)}, f32[2,8,512]{2,1,0:T(8,128)S(1)}, f32[3,3,4,8,512]{4,3,2,1,0:T(8,128)S(1)}) custom-call(f32[8,8,512]{2,1,0:T(8,128)S(1)} %bin_rest.1.field, f32[2,8,512]{2,1,0:T(8,128)S(1)} %collective-permute-done.4.side_1, f32[2,8,512]{2,1,0:T(8,128)S(1)} %collective-permute-done.5.side_0, ...), custom_call_target="tpu_custom_call" | custom-call | tf_op jit(solution)/shard_map/back_reach/pallas_call | solution.py:460
  23.6 0.1 collective-permute-start.6
  23.7 3.3 %collective-permute-start.7 = (f32[2,8,512]{2,1,0:T(8,128)S(1)}, f32[2,8,512]{2,1,0:T(8,128)S(1)}, u32[]{:S(2)}, u32[]{:S(2)}) collective-permute-start(f32[2,8,512]{2,1,0:T(8,128)S(1)} %get-tuple-element.32), channel_id=1, source_target_pairs={{8,16},{16,8},{9,17},{17,9},{10,18},{18,10},{11,19},{19,11},{12,20... | collective-permute-start | bytes 98312 | tf_op jit(solution)/shard_map/ppermute | solution.py:412
  27.0 0.8 %back_own.1.own = f32[8,8,512]{2,1,0:T(8,128)S(1)} custom-call(f32[8,8,512]{2,1,0:T(8,128)S(1)} %bin_rest.1.field, f32[2,8,512]{2,1,0:T(8,128)S(1)} %collective-permute-done.4.side_1, f32[2,8,512]{2,1,0:T(8,128)S(1)} %collective-permute-done.5.side_0, f32[8,16,512]{2,1,0:T(8,128)S(1)} %density_ends.1.density, f32[2,27,512]{2,1,0:T(8,128)S(1)} %rev.8.stencils, ...), custom_call_target="tpu_custom_call" | custom-call | tf_op jit(solution)/shard_map/back_own/pallas_call | solution.py:460
  27.8 2.6 %collective-permute-done.7.end_1 = f32[2,8,512]{2,1,0:T(8,128)S(1)} collective-permute-done((f32[2,8,512]{2,1,0:T(8,128)S(1)}, f32[2,8,512]{2,1,0:T(8,128)S(1)}, u32[]{:S(2)}, u32[]{:S(2)}) %collective-permute-start.7) | collective-permute-done | bytes 32800 | tf_op jit(solution)/shard_map/ppermute | solution.py:412
  30.4 0.7 %close.1 = f32[8,8,512]{2,1,0:T(8,128)} custom-call(f32[8,8,512]{2,1,0:T(8,128)S(1)} %back_own.1.own, f32[2,8,512]{2,1,0:T(8,128)S(1)} %collective-permute-done.6.end_0, f32[2,8,512]{2,1,0:T(8,128)S(1)} %collective-permute-done.7.end_1), custom_call_target="tpu_custom_call" | custom-call | tf_op jit(solution)/shard_map/close/pallas_call | solution.py:502
  (12 shorter events, 0.1 us)
Async XLA Ops:
  1.8 7.4 %collective-permute-start = (f32[4,8,512]{2,1,0:T(8,128)S(1)}, f32[4,8,512]{2,1,0:T(8,128)S(1)}, u32[]{:S(2)}, u32[]{:S(2)}) collective-permute-start(f32[4,8,512]{2,1,0:T(8,128)S(1)} %get-tuple-element.21), channel_id=1, source_target_pairs={{0,1},{2,3},{4,5},{6,7},{1,0},{3,2},{5,4},{7,6},{8,9},{10,11},{12,... | collective-permute-start | bytes 196616 | tf_op jit(solution)/shard_map/ppermute | solution.py:412
  1.9 7.3 %collective-permute-start.1 = (f32[4,8,512]{2,1,0:T(8,128)S(1)}, f32[4,8,512]{2,1,0:T(8,128)S(1)}, u32[]{:S(2)}, u32[]{:S(2)}) collective-permute-start(f32[4,8,512]{2,1,0:T(8,128)S(1)} %get-tuple-element.22), channel_id=1, source_target_pairs={{1,2},{3,4},{5,6},{7,0},{2,1},{4,3},{6,5},{0,7},{9,10},{11,12},{13... | collective-permute-start | bytes 196616 | tf_op jit(solution)/shard_map/ppermute | solution.py:412
  5.6 10.4 %all-to-all-start = ((f32[32,8,128]{2,1,0:T(8,128)}), f32[32,8,128]{2,1,0:T(8,128)S(1)}, u32[]{:S(2)}, u32[]{:S(2)}) async-start(f32[32,8,128]{2,1,0:T(8,128)} %get-tuple-element.19), calls=%async_computation | async-start | bytes 262144 | tf_op jit(solution)/shard_map/all_to_all | solution.py:451
  9.2 9.7 %collective-permute-start.2 = (f32[4,8,512]{2,1,0:T(8,128)S(1)}, f32[4,8,512]{2,1,0:T(8,128)S(1)}, u32[]{:S(2)}, u32[]{:S(2)}) collective-permute-start(f32[4,8,512]{2,1,0:T(8,128)S(1)} %get-tuple-element.23), channel_id=1, source_target_pairs={{8,16},{16,8},{9,17},{17,9},{10,18},{18,10},{11,19},{19,11},{12,20... | collective-permute-start | bytes 196616 | tf_op jit(solution)/shard_map/ppermute | solution.py:412
  12.6 6.3 %collective-permute-start.3 = (f32[4,8,512]{2,1,0:T(8,128)S(1)}, f32[4,8,512]{2,1,0:T(8,128)S(1)}, u32[]{:S(2)}, u32[]{:S(2)}) collective-permute-start(f32[4,8,512]{2,1,0:T(8,128)S(1)} %get-tuple-element.24), channel_id=1, source_target_pairs={{0,8},{16,24},{8,0},{24,16},{1,9},{17,25},{9,1},{25,17},{2,10},{18... | collective-permute-start | bytes 196616 | tf_op jit(solution)/shard_map/ppermute | solution.py:412
  18.1 5.2 %collective-permute-start.4 = (f32[2,8,512]{2,1,0:T(8,128)S(1)}, f32[2,8,512]{2,1,0:T(8,128)S(1)}, u32[]{:S(2)}, u32[]{:S(2)}) collective-permute-start(f32[2,8,512]{2,1,0:T(8,128)S(1)} %get-tuple-element.28._.to_outer), channel_id=1, source_target_pairs={{1,2},{3,4},{5,6},{7,0},{2,1},{4,3},{6,5},{0,7},{9,10},{11,12},{13... | collective-permute-start | bytes 98312 | tf_op jit(solution)/shard_map/ppermute | solution.py:412
  18.8 4.4 %collective-permute-start.5 = (f32[2,8,512]{2,1,0:T(8,128)S(1)}, f32[2,8,512]{2,1,0:T(8,128)S(1)}, u32[]{:S(2)}, u32[]{:S(2)}) collective-permute-start(f32[2,8,512]{2,1,0:T(8,128)S(1)} %get-tuple-element.29.to_partner), channel_id=1, source_target_pairs={{0,1},{2,3},{4,5},{6,7},{1,0},{3,2},{5,4},{7,6},{8,9},{10,11},{12,... | collective-permute-start | bytes 98312 | tf_op jit(solution)/shard_map/ppermute | solution.py:412
  23.6 4.2 %collective-permute-start.6 = (f32[2,8,512]{2,1,0:T(8,128)S(1)}, f32[2,8,512]{2,1,0:T(8,128)S(1)}, u32[]{:S(2)}, u32[]{:S(2)}) collective-permute-start(f32[2,8,512]{2,1,0:T(8,128)S(1)} %get-tuple-element.31), channel_id=1, source_target_pairs={{0,8},{16,24},{8,0},{24,16},{1,9},{17,25},{9,1},{25,17},{2,10},{18... | collective-permute-start | bytes 98312 | tf_op jit(solution)/shard_map/ppermute | solution.py:412
  23.7 6.7 %collective-permute-start.7 = (f32[2,8,512]{2,1,0:T(8,128)S(1)}, f32[2,8,512]{2,1,0:T(8,128)S(1)}, u32[]{:S(2)}, u32[]{:S(2)}) collective-permute-start(f32[2,8,512]{2,1,0:T(8,128)S(1)} %get-tuple-element.32), channel_id=1, source_target_pairs={{8,16},{16,8},{9,17},{17,9},{10,18},{18,10},{11,19},{19,11},{12,20... | collective-permute-start | bytes 98312 | tf_op jit(solution)/shard_map/ppermute | solution.py:412

commit v23 on v22

--- a/solution.py
+++ b/solution.py
@@ -30,7 +30,7 @@
 
 def unpack_sides(from_partner, from_outer, height):
     _, odd = position("lon")
-    sub = sublane(from_partner.shape[2])
+    sub = sublane(from_outer.shape[2])
     tiles = []
     for group in range(height // 4):
         partner, outer = from_partner[group], from_outer[group]
@@ -202,15 +202,17 @@
         out[row] = inner[row - 2]
 
 
-def beside_tiles(side_0, side_1, density):
+def beside_tiles(pair, side_1, density):
+    _, odd = position("lon")
+    side_0 = [either(odd, pair[0, group], pair[1, group]) for group in range(2)]
     tiles = unpack_sides(side_0, side_1, density.shape[0])
     return [tile * density[row, SUBLANES:] for row, tile in enumerate(tiles)]
 
 
-def back_reach_kernel(field, side_1, side_0, density, stencils, to_partner, to_outer, middle, wide, shifted, reach):
+def back_reach_kernel(field, side_1, pair, density, stencils, to_partner, to_outer, middle, wide, shifted, reach):
     height, _, radial = field.shape
     last = height - 1
-    fill_wide(wide, field, beside_tiles(side_0, side_1, density), (0, 1, last - 1, last))
+    fill_wide(wide, field, beside_tiles(pair, side_1, density), (0, 1, last - 1, last))
     lat, odd = position("lat")
     above = (lat > 0).astype(jnp.int32)
     below = (lat < lax.axis_size("lat") - 1).astype(jnp.int32)
@@ -232,9 +234,9 @@
         to_outer[place] = either(odd, reach[2 + place], reach[place])
 
 
-def back_own_kernel(field, side_1, side_0, density, stencils, latent, edge, out, wide, shifted, middle):
+def back_own_kernel(field, side_1, pair, density, stencils, latent, edge, out, wide, shifted, middle):
     height, _, radial = field.shape
-    fill_wide(wide, field, beside_tiles(side_0, side_1, density), range(height))
+    fill_wide(wide, field, beside_tiles(pair, side_1, density), range(height))
     centers = [(row, ALL) for row in range(1, height - 1)]
     first_level(wide, shifted, stencils.at[0], centers, middle, [None] * len(centers))
 
@@ -352,42 +354,46 @@
     pl.when(jnp.logical_not(middle))(lambda: body(LEAST // LANES))
 
 
-def bin_sides_kernel(got, _, to_partner, to_outer, rows_of):
+def bin_outer_kernel(got, _, to_outer, rows_of):
     _, odd = position("lon")
 
     def index_of(row, col):
-        side = lax.bitwise_xor(lax.shift_right_logical(col, 2), odd)
-        return jnp.where((col < 2) | (col >= 6), side * 16 + row * 2 + lax.bitwise_and(col, 1), 32)
+        return jnp.where(lax.shift_right_logical(col, 1) == 3 * odd, row * 2 + lax.bitwise_and(col, 1), 16)
 
     def body(runs):
-        packed = behind_of(got, index_of, 32, runs, rows_of, width=SUBLANES, radial=to_outer.shape[2])
+        packed = behind_of(got, index_of, 16, runs, rows_of, width=SUBLANES, radial=to_outer.shape[2])
         for place in range(2):
             to_outer[place] = packed[place * SUBLANES:(place + 1) * SUBLANES]
-            to_partner[place] = packed[(2 + place) * SUBLANES:(3 + place) * SUBLANES]
 
     for_load(body)
 
 
-def bin_rest_kernel(got, density, to_partner, to_outer, upstream, rows_of):
+def bin_rest_kernel(got, density, to_outer, upstream, to_pair, rows_of):
     height, width, radial = upstream.shape
     _, odd = position("lon")
-    sub = sublane(radial)
+    pair = lax.shift_right_logical(sublane(radial), 1)
+
+    def index_of(row, col):
+        place = lax.bitwise_and(col + 2 * odd, width - 1) - 2
+        return jnp.where(place >= 0, lax.shift_right_logical(place, 1) * 16 + row * 2 + lax.bitwise_and(place, 1), 48)
 
     def body(runs):
-        packed = behind_of(
-            got, lambda row, col: jnp.where((col >= 2) & (col < 6), row * 4 + col - 2, 32), 32, runs, rows_of,
-            width=width, radial=radial,
-        )
+        packed = behind_of(got, index_of, 48, runs, rows_of, width=width, radial=radial)
+
+        def part(step, group):
+            at = (2 * step + group) * SUBLANES
+            return packed[at:at + SUBLANES]
+
         for row in range(height):
             group, k = row // 4, row % 4
-            partner, outer = to_partner[group], to_outer[group]
-            first, last = either(odd, partner, outer), either(odd, outer, partner)
-            first = pltpu.roll(first, -2 * k % SUBLANES, 0)
-            last = pltpu.roll(last, SUBLANES - 2 - 2 * k, 0)
-            inner = packed[row // 2 * SUBLANES:(row // 2 + 1) * SUBLANES]
-            inner = pltpu.roll(inner, 6 if row % 2 else 2, 0)
-            mine = jnp.where(sub < 2, first, jnp.where(sub < 6, inner, last))
-            upstream[row] = density[row, :width] * mine
+            mine = pltpu.roll(to_outer[group], -2 * k % SUBLANES, 0)
+            for step in range(3):
+                mine = jnp.where(pair == step + 1, pltpu.roll(part(step, group), (2 * (step + 1 - k)) % SUBLANES, 0), mine)
+            upstream[row] = density[row, :width] * either(odd, pltpu.roll(mine, SUBLANES - 2, 0), mine)
+        for group in range(2):
+            side = either(odd, part(0, group), part(2, group))
+            to_pair[0, group] = side
+            to_pair[1, group] = side
 
     for_load(body)
 
@@ -481,23 +487,31 @@
         (shape(height - 4, broad, radial), shape(3, 3, height - 2, broad, radial)), [rows, moved],
         latent, *beside, stencils,
     )
-    to_sides = call(bin_sides_kernel, "bin_sides", (sides, sides), star_rows, got, inner)
+    to_outer = call(bin_outer_kernel, "bin_outer", sides, star_rows, got, inner)
     density = call(
         density_ends_kernel, "density_ends", shape(height, broad, radial),
         [pltpu.VMEM((3, 3, 4, broad, radial), f32), rows, moved],
-        latent, *beside, *above[::-1], stencils, middle, inner, to_sides[1],
-    )
-    upstream = call(bin_rest_kernel, "bin_rest", tile, star_rows, got, density, *to_sides)
-
-    beside = swap(*to_sides, "lon", True, outer_first=True)
+        latent, *beside, *above[::-1], stencils, middle, inner, to_outer,
+    )
+    upstream, to_pair = call(
+        bin_rest_kernel, "bin_rest", (tile, shape(2, 2, SUBLANES, radial)), star_rows, got, density, to_outer
+    )
+
+    count = lax.axis_size("lon")
+    from_outer = lax.ppermute(
+        to_outer, "lon", [(i, (i + 1) % count) for i in range(1, count, 2)] + [((i + 1) % count, i) for i in range(1, count, 2)]
+    )
+    pair = lax.all_to_all(
+        to_pair, "lon", 0, 0, axis_index_groups=[[i, i + 1] for i in range(0, count, 2)], tiled=True
+    )
     *to_ends, middle = call(
         back_reach_kernel, "back_reach", (shape(2, width, radial), shape(2, width, radial), shape(*edge)),
-        [rows, moved, pltpu.VMEM((4, width, radial), f32)], upstream, *beside[::-1], density, mirrored,
+        [rows, moved, pltpu.VMEM((4, width, radial), f32)], upstream, from_outer, pair, density, mirrored,
     )
     above = swap(*to_ends, "lat", False)
     own = call(
         back_own_kernel, "back_own", tile, [rows, moved, pltpu.VMEM(inner_rows, f32)],
-        upstream, *beside[::-1], density, mirrored, latent, middle,
+        upstream, from_outer, pair, density, mirrored, latent, middle,
     )
     return pl.pallas_call(
         close_kernel,

time: 31.3 us -> 33.9 us (1.083)
  blocking collectives: 0 us -> 3.79 us
  waiting for transfers between devices: 6.46 us -> 5.01 us
    all_to_all x0 -> x1, blocking collectives: none -> 3.79 us  [on_device(): lax.all_to_all(to_pair, 'lon', 0, 0, axis_index_groups=[[i, i + 1] for i...]
    ppermute x8 -> x6, waiting for transfers between devices: 4.06 us -> 2.61 us  [swap(): lax.ppermute(values, axis, both_ways(pairs))]
    ppermute x8 -> x6, starting transfers between devices: 11.3 us -> 10.6 us  [swap(): lax.ppermute(values, axis, both_ways(pairs))]
    ppermute x0 -> x1, starting transfers between devices: none -> 0.72 us  [on_device(): lax.ppermute(to_outer, 'lon', [(i, (i + 1) % count) for i in range(1, cou...]
  transfers between devices with their start and end apart: 9 -> 8, of which waited for: 3 -> 2; matrix products, arithmetic and copies ran while one was open for 2% -> 2% of each run, Pallas kernels for 21% -> 21%
where the time goes in v23:
time: 33.9 us; the launch traced here: 33.7 us
  starting transfers between devices  14.4 us (42%)
  Pallas kernels  9.75 us (29%)
  waiting for transfers between devices  5.01 us (15%)
  blocking collectives  3.79 us (11%)
  local copies, waits for them, and re-layouts  0.5 us (1%)
    ppermute x6, starting transfers between devices, swap(): lax.ppermute(values, axis, both_ways(pairs))  10.6 us
    pallas_call x7, Pallas kernels, call(): pl.pallas_call(kernel, out_shape=outs, in_specs=[VMEM] * len(operands), o...  7.29 us
    all_to_all x1, blocking collectives, on_device(): lax.all_to_all(to_pair, 'lon', 0, 0, axis_index_groups=[[i, i + 1] for i...  3.79 us
    all_to_all x1, starting transfers between devices, on_device(): lax.all_to_all(packed, ('lat', 'lon'), split_axis=0, concat_axis=0, tiled...  3.09 us
    ppermute x6, waiting for transfers between devices, swap(): lax.ppermute(values, axis, both_ways(pairs))  2.61 us
    all_to_all x1, waiting for transfers between devices, on_device(): lax.all_to_all(packed, ('lat', 'lon'), split_axis=0, concat_axis=0, tiled...  2.4 us
    pallas_call x1, Pallas kernels, on_device(): pl.pallas_call(open_kernel, out_shape=(jax.ShapeDtypeStruct((shards, 2 *...  1.79 us
    ppermute x1, starting transfers between devices, on_device(): lax.ppermute(to_outer, 'lon', [(i, (i + 1) % count) for i in range(1, cou...  0.72 us
  transfers between devices with their start and end apart: 8, of which 2 were waited for; matrix products, arithmetic and copies ran while one was open for 2% of the time, Pallas kernels for 21%

profile of v23, /device:TPU:2, one launch (start us, length us, event | category | flops | bytes accessed | tf_op | source)
XLA Modules:
  0.0 33.7 jit_solution(7033163253797659582)
XLA Ops:
  0.0 1.8 %opening.1 = (f32[32,8,128]{2,1,0:T(8,128)}, f32[8,8,512]{2,1,0:T(8,128)S(1)}, f32[4,8,512]{2,1,0:T(8,128)S(1)}, f32[4,8,512]{2,1,0:T(8,128)S(1)}, f32[27,2,512]{2,1,0:T(2,128)S(1)}) custom-call(s32[1,32]{1,0:T(1,128)} %counts_in.1, s32[1,32]{1,0:T(1,128)} %offsets_in.1, f32[128,128]{1,0:T(8,128)} %bitcast.26, s32[128,128]{1,0:T(8,128)} %bitcast.27, ...), custom_call_target="tpu_custom_call" | custom-call | tf_op jit(solution)/shard_map/opening/pallas_call | solution.py:442
  1.8 0.1 collective-permute-start
  1.9 3.7 %collective-permute-start.1 = (f32[4,8,512]{2,1,0:T(8,128)S(1)}, f32[4,8,512]{2,1,0:T(8,128)S(1)}, u32[]{:S(2)}, u32[]{:S(2)}) collective-permute-start(f32[4,8,512]{2,1,0:T(8,128)S(1)} %get-tuple-element.22), channel_id=1, source_target_pairs={{1,2},{3,4},{5,6},{7,0},{2,1},{4,3},{6,5},{0,7},{9,10},{11,12},{13... | collective-permute-start | bytes 196616 | tf_op jit(solution)/shard_map/ppermute | solution.py:418
  5.6 3.1 %all-to-all-start = ((f32[32,8,128]{2,1,0:T(8,128)}), f32[32,8,128]{2,1,0:T(8,128)S(1)}, u32[]{:S(2)}, u32[]{:S(2)}) async-start(f32[32,8,128]{2,1,0:T(8,128)} %get-tuple-element.19), calls=%async_computation | async-start | bytes 262144 | tf_op jit(solution)/shard_map/all_to_all | solution.py:457
  8.7 0.2 rev.7
  8.9 0.1 copy.12
  9.0 0.1 slice_bitcast_fusion.1
  9.1 0.1 pad_bitcast_fusion
  9.2 3.4 %collective-permute-start.2 = (f32[4,8,512]{2,1,0:T(8,128)S(1)}, f32[4,8,512]{2,1,0:T(8,128)S(1)}, u32[]{:S(2)}, u32[]{:S(2)}) collective-permute-start(f32[4,8,512]{2,1,0:T(8,128)S(1)} %get-tuple-element.23), channel_id=1, source_target_pairs={{8,16},{16,8},{9,17},{17,9},{10,18},{18,10},{11,19},{19,11},{12,20... | collective-permute-start | bytes 196616 | tf_op jit(solution)/shard_map/ppermute | solution.py:418
  12.6 0.1 collective-permute-start.3
  12.7 0.9 %density_inside.1 = (f32[4,16,512]{2,1,0:T(8,128)S(1)}, f32[3,3,6,16,512]{4,3,2,1,0:T(8,128)S(1)}) custom-call(f32[8,8,512]{2,1,0:T(8,128)S(1)} %get-tuple-element.20.field.latent, f32[4,8,512]{2,1,0:T(8,128)S(1)} %collective-permute-done.side_0, f32[4,8,512]{2,1,0:T(8,128)S(1)} %collective-permute-done.1.side_1, f32[2,27,512]{2,1,0:T(8,128)S(1)} %bitcast.20), custom_call_target="tpu_custom_call" | custom-call | tf_op jit(solution)/shard_map/density_inside/pallas_call | solution.py:466
  13.6 2.4 %all-to-all-done.got = f32[32,8,128]{2,1,0:T(8,128)S(1)} async-done(((f32[32,8,128]{2,1,0:T(8,128)}), f32[32,8,128]{2,1,0:T(8,128)S(1)}, u32[]{:S(2)}, u32[]{:S(2)}) %all-to-all-start) | async-done | bytes 131104 | tf_op jit(solution)/shard_map/all_to_all | solution.py:457
  16.0 2.2 %bin_outer.1._.to_outer = f32[2,8,512]{2,1,0:T(8,128)S(1)} custom-call(f32[32,8,128]{2,1,0:T(8,128)S(1)} %all-to-all-done.got, f32[4,16,512]{2,1,0:T(8,128)S(1)} %get-tuple-element.27._.inner), custom_call_target="tpu_custom_call" | custom-call | tf_op jit(solution)/shard_map/bin_outer/pallas_call | solution.py:466
  18.2 0.7 %collective-permute-start.4 = (f32[2,8,512]{2,1,0:T(8,128)S(1)}, f32[2,8,512]{2,1,0:T(8,128)S(1)}, u32[]{:S(2)}, u32[]{:S(2)}) collective-permute-start(f32[2,8,512]{2,1,0:T(8,128)S(1)} %bin_outer.1._.to_outer), channel_id=1, source_target_pairs={{1,2},{3,4},{5,6},{7,0},{2,1},{4,3},{6,5},{0,7},{9,10},{11,12},{13... | collective-permute-start | bytes 98312 | tf_op jit(solution)/shard_map/ppermute | solution.py:501
  18.9 0.1 pad_maximum_fusion
  19.0 0.7 %density_ends.1.density = f32[8,16,512]{2,1,0:T(8,128)S(1)} custom-call(f32[8,8,512]{2,1,0:T(8,128)S(1)} %get-tuple-element.20.field.latent, f32[4,8,512]{2,1,0:T(8,128)S(1)} %collective-permute-done.side_0, f32[4,8,512]{2,1,0:T(8,128)S(1)} %collective-permute-done.1.side_1, f32[4,8,512]{2,1,0:T(8,128)S(1)} %collective-permute-done.2.end_1, ...), custom_call_target="tpu_custom_call" | custom-call | tf_op jit(solution)/shard_map/density_ends/pallas_call | solution.py:466
  19.7 2.3 %bin_rest.1 = (f32[8,8,512]{2,1,0:T(8,128)S(1)}, f32[2,2,8,512]{3,2,1,0:T(8,128)S(1)}) custom-call(f32[32,8,128]{2,1,0:T(8,128)S(1)} %all-to-all-done.got, f32[8,16,512]{2,1,0:T(8,128)S(1)} %density_ends.1.density, f32[2,8,512]{2,1,0:T(8,128)S(1)} %bin_outer.1._.to_outer), custom_call_target="tpu_custom_call" | custom-call | tf_op jit(solution)/shard_map/bin_rest/pallas_call | solution.py:466
  22.1 3.8 %all_to_all.10.pair = f32[2,2,8,512]{3,2,1,0:T(8,128)S(1)} all-to-all(f32[2,2,8,512]{3,2,1,0:T(8,128)S(1)} %get-tuple-element.29), channel_id=1, replica_groups={{0,1},{2,3},{4,5},{6,7},{8,9},{10,11},{12,13},{14,15},{16,17},{18,19},{..., dimensions={0} | all-to-all | bytes 131072 | tf_op jit(solution)/shard_map/all_to_all | solution.py:504
  25.9 0.4 %back_reach.1 = (f32[2,8,512]{2,1,0:T(8,128)S(1)}, f32[2,8,512]{2,1,0:T(8,128)S(1)}, f32[3,3,4,8,512]{4,3,2,1,0:T(8,128)S(1)}) custom-call(f32[8,8,512]{2,1,0:T(8,128)S(1)} %get-tuple-element.28.field, f32[2,8,512]{2,1,0:T(8,128)S(1)} %collective-permute-done.4.side_1, f32[2,2,8,512]{3,2,1,0:T(8,128)S(1)} %all_to_all.10.pair, ...), custom_call_target="tpu_custom_call" | custom-call | tf_op jit(solution)/shard_map/back_reach/pallas_call | solution.py:466
  26.2 0.1 collective-permute-start.5
  26.3 3.3 %collective-permute-start.6 = (f32[2,8,512]{2,1,0:T(8,128)S(1)}, f32[2,8,512]{2,1,0:T(8,128)S(1)}, u32[]{:S(2)}, u32[]{:S(2)}) collective-permute-start(f32[2,8,512]{2,1,0:T(8,128)S(1)} %get-tuple-element.32), channel_id=1, source_target_pairs={{8,16},{16,8},{9,17},{17,9},{10,18},{18,10},{11,19},{19,11},{12,20... | collective-permute-start | bytes 98312 | tf_op jit(solution)/shard_map/ppermute | solution.py:418
  29.6 0.8 %back_own.1.own = f32[8,8,512]{2,1,0:T(8,128)S(1)} custom-call(f32[8,8,512]{2,1,0:T(8,128)S(1)} %get-tuple-element.28.field, f32[2,8,512]{2,1,0:T(8,128)S(1)} %collective-permute-done.4.side_1, f32[2,2,8,512]{3,2,1,0:T(8,128)S(1)} %all_to_all.10.pair, f32[8,16,512]{2,1,0:T(8,128)S(1)} %density_ends.1.density, f32[2,27,512]{2,1,0:T(8,128)S(1)} %rev.8.stencils, ...), custom_call_target="tpu_custom_call" | custom-call | tf_op jit(solution)/shard_map/back_own/pallas_call | solution.py:466
  30.4 2.6 %collective-permute-done.6.end_1 = f32[2,8,512]{2,1,0:T(8,128)S(1)} collective-permute-done((f32[2,8,512]{2,1,0:T(8,128)S(1)}, f32[2,8,512]{2,1,0:T(8,128)S(1)}, u32[]{:S(2)}, u32[]{:S(2)}) %collective-permute-start.6) | collective-permute-done | bytes 32800 | tf_op jit(solution)/shard_map/ppermute | solution.py:418
  33.0 0.7 %close.1 = f32[8,8,512]{2,1,0:T(8,128)} custom-call(f32[8,8,512]{2,1,0:T(8,128)S(1)} %back_own.1.own, f32[2,8,512]{2,1,0:T(8,128)S(1)} %collective-permute-done.5.end_0, f32[2,8,512]{2,1,0:T(8,128)S(1)} %collective-permute-done.6.end_1), custom_call_target="tpu_custom_call" | custom-call | tf_op jit(solution)/shard_map/close/pallas_call | solution.py:516
  (11 shorter events, 0.1 us)
Async XLA Ops:
  1.8 7.4 %collective-permute-start = (f32[4,8,512]{2,1,0:T(8,128)S(1)}, f32[4,8,512]{2,1,0:T(8,128)S(1)}, u32[]{:S(2)}, u32[]{:S(2)}) collective-permute-start(f32[4,8,512]{2,1,0:T(8,128)S(1)} %get-tuple-element.21), channel_id=1, source_target_pairs={{0,1},{2,3},{4,5},{6,7},{1,0},{3,2},{5,4},{7,6},{8,9},{10,11},{12,... | collective-permute-start | bytes 196616 | tf_op jit(solution)/shard_map/ppermute | solution.py:418
  1.9 7.3 %collective-permute-start.1 = (f32[4,8,512]{2,1,0:T(8,128)S(1)}, f32[4,8,512]{2,1,0:T(8,128)S(1)}, u32[]{:S(2)}, u32[]{:S(2)}) collective-permute-start(f32[4,8,512]{2,1,0:T(8,128)S(1)} %get-tuple-element.22), channel_id=1, source_target_pairs={{1,2},{3,4},{5,6},{7,0},{2,1},{4,3},{6,5},{0,7},{9,10},{11,12},{13... | collective-permute-start | bytes 196616 | tf_op jit(solution)/shard_map/ppermute | solution.py:418
  5.6 10.4 %all-to-all-start = ((f32[32,8,128]{2,1,0:T(8,128)}), f32[32,8,128]{2,1,0:T(8,128)S(1)}, u32[]{:S(2)}, u32[]{:S(2)}) async-start(f32[32,8,128]{2,1,0:T(8,128)} %get-tuple-element.19), calls=%async_computation | async-start | bytes 262144 | tf_op jit(solution)/shard_map/all_to_all | solution.py:457
  9.2 9.7 %collective-permute-start.2 = (f32[4,8,512]{2,1,0:T(8,128)S(1)}, f32[4,8,512]{2,1,0:T(8,128)S(1)}, u32[]{:S(2)}, u32[]{:S(2)}) collective-permute-start(f32[4,8,512]{2,1,0:T(8,128)S(1)} %get-tuple-element.23), channel_id=1, source_target_pairs={{8,16},{16,8},{9,17},{17,9},{10,18},{18,10},{11,19},{19,11},{12,20... | collective-permute-start | bytes 196616 | tf_op jit(solution)/shard_map/ppermute | solution.py:418
  12.6 6.4 %collective-permute-start.3 = (f32[4,8,512]{2,1,0:T(8,128)S(1)}, f32[4,8,512]{2,1,0:T(8,128)S(1)}, u32[]{:S(2)}, u32[]{:S(2)}) collective-permute-start(f32[4,8,512]{2,1,0:T(8,128)S(1)} %get-tuple-element.24), channel_id=1, source_target_pairs={{0,8},{16,24},{8,0},{24,16},{1,9},{17,25},{9,1},{25,17},{2,10},{18... | collective-permute-start | bytes 196616 | tf_op jit(solution)/shard_map/ppermute | solution.py:418
  18.2 7.7 %collective-permute-start.4 = (f32[2,8,512]{2,1,0:T(8,128)S(1)}, f32[2,8,512]{2,1,0:T(8,128)S(1)}, u32[]{:S(2)}, u32[]{:S(2)}) collective-permute-start(f32[2,8,512]{2,1,0:T(8,128)S(1)} %bin_outer.1._.to_outer), channel_id=1, source_target_pairs={{1,2},{3,4},{5,6},{7,0},{2,1},{4,3},{6,5},{0,7},{9,10},{11,12},{13... | collective-permute-start | bytes 98312 | tf_op jit(solution)/shard_map/ppermute | solution.py:501
  26.2 4.2 %collective-permute-start.5 = (f32[2,8,512]{2,1,0:T(8,128)S(1)}, f32[2,8,512]{2,1,0:T(8,128)S(1)}, u32[]{:S(2)}, u32[]{:S(2)}) collective-permute-start(f32[2,8,512]{2,1,0:T(8,128)S(1)} %get-tuple-element.31), channel_id=1, source_target_pairs={{0,8},{16,24},{8,0},{24,16},{1,9},{17,25},{9,1},{25,17},{2,10},{18... | collective-permute-start | bytes 98312 | tf_op jit(solution)/shard_map/ppermute | solution.py:418
  26.3 6.7 %collective-permute-start.6 = (f32[2,8,512]{2,1,0:T(8,128)S(1)}, f32[2,8,512]{2,1,0:T(8,128)S(1)}, u32[]{:S(2)}, u32[]{:S(2)}) collective-permute-start(f32[2,8,512]{2,1,0:T(8,128)S(1)} %get-tuple-element.32), channel_id=1, source_target_pairs={{8,16},{16,8},{9,17},{17,9},{10,18},{18,10},{11,19},{19,11},{12,20... | collective-permute-start | bytes 98312 | tf_op jit(solution)/shard_map/ppermute | solution.py:418

commit v24 on v22

--- a/solution.py
+++ b/solution.py
@@ -315,31 +315,34 @@
         line = jnp.broadcast_to(rows_of[kind, row:row + 1, :], (16, LANES))
         return jnp.concatenate([line.astype(bf16)] * (classes // 16), axis=0)
 
-    tiles = got[...].reshape(shards * rows, LANES)
-    cell = tiles.astype(jnp.int32)
-    pixel = lax.shift_right_logical(cell, radial.bit_length() - 1)
-    bins = lax.bitwise_and(cell, radial - 1)
-    upper = lax.shift_right_logical(bins, span.bit_length() - 1)
-    index = index_of(lax.shift_right_logical(pixel, width.bit_length() - 1), lax.bitwise_and(pixel, width - 1))
-    rows_of[0] = jnp.where(index < pixels, upper * pixels + index, classes).astype(jnp.float32)
-    lows = jnp.transpose(lax.bitwise_and(bins, span - 1).astype(jnp.float32)).astype(bf16)
-    coarse = tiles.astype(bf16).astype(jnp.float32)
-    rows_of[1] = coarse
-    rows_of[2] = tiles - coarse
-
     total = jnp.zeros((2 * classes, span), jnp.float32)
     group = 2 * RUNS // runs
-    for first in range(0, shards, group):
-        left, right = [], []
-        for run in range(group * runs):
-            row = (first + run // runs) * rows + run % runs * 2
-            mine = tall(0, row + 1) == column
-            left.append(jnp.concatenate([jnp.where(mine, tall(kind, row), zero) for kind in (1, 2)], axis=0))
-            low = jnp.broadcast_to(lows[:, row + 1:row + 2], (LANES, LANES))
-            right.append(jnp.concatenate([jnp.where(low >= place, one, zero) for place in places], axis=1))
-        total = total + jnp.dot(
-            jnp.concatenate(left, axis=1), jnp.concatenate(right, axis=0), preferred_element_type=jnp.float32
-        )
+    block = LANES // rows
+    for start in range(0, shards, block):
+        tiles = got[start:start + block].reshape(LANES, LANES)
+        cell = tiles.astype(jnp.int32)
+        pixel = lax.shift_right_logical(cell, radial.bit_length() - 1)
+        bins = lax.bitwise_and(cell, radial - 1)
+        upper = lax.shift_right_logical(bins, span.bit_length() - 1)
+        index = index_of(lax.shift_right_logical(pixel, width.bit_length() - 1), lax.bitwise_and(pixel, width - 1))
+        at = slice(start * rows, start * rows + LANES)
+        lows = jnp.transpose(lax.bitwise_and(bins, span - 1).astype(jnp.float32)).astype(bf16)
+        coarse = tiles.astype(bf16).astype(jnp.float32)
+        rows_of[0, at] = jnp.where(index < pixels, upper * pixels + index, classes).astype(jnp.float32)
+        rows_of[1, at] = coarse
+        rows_of[2, at] = tiles - coarse
+        for first in range(0, block, group):
+            left, right = [], []
+            for run in range(group * runs):
+                here = (first + run // runs) * rows + run % runs * 2
+                row = start * rows + here
+                mine = tall(0, row + 1) == column
+                left.append(jnp.concatenate([jnp.where(mine, tall(kind, row), zero) for kind in (1, 2)], axis=0))
+                low = jnp.broadcast_to(lows[:, here + 1:here + 2], (LANES, LANES))
+                right.append(jnp.concatenate([jnp.where(low >= place, one, zero) for place in places], axis=1))
+            total = total + jnp.dot(
+                jnp.concatenate(left, axis=1), jnp.concatenate(right, axis=0), preferred_element_type=jnp.float32
+            )
     both = (total[:classes] + total[classes:]) * bin_width
     near, far = both[:pixels], both[pixels:]
     return jnp.concatenate([near + far[:, :1], far], axis=1)

time: 31.3 us -> 31.3 us (level)
  no operation moved by 1% of the time
where the time goes in v24:
time: 31.3 us; the launch traced here: 31.1 us
  starting transfers between devices  14.4 us (46%)
  Pallas kernels  9.47 us (30%)
  waiting for transfers between devices  6.45 us (21%)
  local copies, waits for them, and re-layouts  0.5 us (2%)
    ppermute x8, starting transfers between devices, swap(): lax.ppermute(values, axis, both_ways(pairs))  11.3 us
    pallas_call x7, Pallas kernels, call(): pl.pallas_call(kernel, out_shape=outs, in_specs=[VMEM] * len(operands), o...  7.01 us
    ppermute x8, waiting for transfers between devices, swap(): lax.ppermute(values, axis, both_ways(pairs))  4.05 us
    all_to_all x1, starting transfers between devices, on_device(): lax.all_to_all(packed, ('lat', 'lon'), split_axis=0, concat_axis=0, tiled...  3.09 us
    all_to_all x1, waiting for transfers between devices, on_device(): lax.all_to_all(packed, ('lat', 'lon'), split_axis=0, concat_axis=0, tiled...  2.4 us
    pallas_call x1, Pallas kernels, on_device(): pl.pallas_call(open_kernel, out_shape=(jax.ShapeDtypeStruct((shards, 2 *...  1.79 us
    pallas_call x1, Pallas kernels, on_device(): pl.pallas_call(close_kernel, out_shape=tile, in_specs=[VMEM] * 3, out_spe...  0.67 us
  transfers between devices with their start and end apart: 9, of which 3 were waited for; matrix products, arithmetic and copies ran while one was open for 2% of the time, Pallas kernels for 21%

profile of v24, /device:TPU:2, one launch (start us, length us, event | category | flops | bytes accessed | tf_op | source)
XLA Modules:
  0.0 31.1 jit_solution(15726005515722384274)
XLA Ops:
  0.0 1.8 %opening.1 = (f32[32,8,128]{2,1,0:T(8,128)}, f32[8,8,512]{2,1,0:T(8,128)S(1)}, f32[4,8,512]{2,1,0:T(8,128)S(1)}, f32[4,8,512]{2,1,0:T(8,128)S(1)}, f32[27,2,512]{2,1,0:T(2,128)S(1)}) custom-call(s32[1,32]{1,0:T(1,128)} %counts_in.1, s32[1,32]{1,0:T(1,128)} %offsets_in.1, f32[128,128]{1,0:T(8,128)} %bitcast.26, s32[128,128]{1,0:T(8,128)} %bitcast.27, ...), custom_call_target="tpu_custom_call" | custom-call | tf_op jit(solution)/shard_map/opening/pallas_call | solution.py:439
  1.8 0.1 collective-permute-start
  1.9 3.7 %collective-permute-start.1 = (f32[4,8,512]{2,1,0:T(8,128)S(1)}, f32[4,8,512]{2,1,0:T(8,128)S(1)}, u32[]{:S(2)}, u32[]{:S(2)}) collective-permute-start(f32[4,8,512]{2,1,0:T(8,128)S(1)} %get-tuple-element.22), channel_id=1, source_target_pairs={{1,2},{3,4},{5,6},{7,0},{2,1},{4,3},{6,5},{0,7},{9,10},{11,12},{13... | collective-permute-start | bytes 196616 | tf_op jit(solution)/shard_map/ppermute | solution.py:415
  5.6 3.1 %all-to-all-start = ((f32[32,8,128]{2,1,0:T(8,128)}), f32[32,8,128]{2,1,0:T(8,128)S(1)}, u32[]{:S(2)}, u32[]{:S(2)}) async-start(f32[32,8,128]{2,1,0:T(8,128)} %get-tuple-element.19), calls=%async_computation | async-start | bytes 262144 | tf_op jit(solution)/shard_map/all_to_all | solution.py:454
  8.7 0.2 rev.7
  8.9 0.1 copy.12
  9.0 0.1 slice_bitcast_fusion.1
  9.1 0.1 pad_bitcast_fusion
  9.2 3.4 %collective-permute-start.2 = (f32[4,8,512]{2,1,0:T(8,128)S(1)}, f32[4,8,512]{2,1,0:T(8,128)S(1)}, u32[]{:S(2)}, u32[]{:S(2)}) collective-permute-start(f32[4,8,512]{2,1,0:T(8,128)S(1)} %get-tuple-element.23), channel_id=1, source_target_pairs={{8,16},{16,8},{9,17},{17,9},{10,18},{18,10},{11,19},{19,11},{12,20... | collective-permute-start | bytes 196616 | tf_op jit(solution)/shard_map/ppermute | solution.py:415
  12.6 0.1 collective-permute-start.3
  12.7 0.9 %density_inside.1 = (f32[4,16,512]{2,1,0:T(8,128)S(1)}, f32[3,3,6,16,512]{4,3,2,1,0:T(8,128)S(1)}) custom-call(f32[8,8,512]{2,1,0:T(8,128)S(1)} %get-tuple-element.20.field.latent, f32[4,8,512]{2,1,0:T(8,128)S(1)} %collective-permute-done.side_0, f32[4,8,512]{2,1,0:T(8,128)S(1)} %collective-permute-done.1.side_1, f32[2,27,512]{2,1,0:T(8,128)S(1)} %bitcast.20), custom_call_target="tpu_custom_call" | custom-call | tf_op jit(solution)/shard_map/density_inside/pallas_call | solution.py:463
  13.6 2.4 %all-to-all-done.got = f32[32,8,128]{2,1,0:T(8,128)S(1)} async-done(((f32[32,8,128]{2,1,0:T(8,128)}), f32[32,8,128]{2,1,0:T(8,128)S(1)}, u32[]{:S(2)}, u32[]{:S(2)}) %all-to-all-start) | async-done | bytes 131104 | tf_op jit(solution)/shard_map/all_to_all | solution.py:454
  16.0 2.1 %bin_sides.1 = (f32[2,8,512]{2,1,0:T(8,128)S(1)}, f32[2,8,512]{2,1,0:T(8,128)S(1)}) custom-call(f32[32,8,128]{2,1,0:T(8,128)S(1)} %all-to-all-done.got, f32[4,16,512]{2,1,0:T(8,128)S(1)} %get-tuple-element.27._.inner), custom_call_target="tpu_custom_call" | custom-call | tf_op jit(solution)/shard_map/bin_sides/pallas_call | solution.py:463
  18.1 0.7 %collective-permute-start.4 = (f32[2,8,512]{2,1,0:T(8,128)S(1)}, f32[2,8,512]{2,1,0:T(8,128)S(1)}, u32[]{:S(2)}, u32[]{:S(2)}) collective-permute-start(f32[2,8,512]{2,1,0:T(8,128)S(1)} %get-tuple-element.28._.to_outer), channel_id=1, source_target_pairs={{1,2},{3,4},{5,6},{7,0},{2,1},{4,3},{6,5},{0,7},{9,10},{11,12},{13... | collective-permute-start | bytes 98312 | tf_op jit(solution)/shard_map/ppermute | solution.py:415
  18.8 0.1 pad_maximum_fusion
  18.9 0.7 %density_ends.1.density = f32[8,16,512]{2,1,0:T(8,128)S(1)} custom-call(f32[8,8,512]{2,1,0:T(8,128)S(1)} %get-tuple-element.20.field.latent, f32[4,8,512]{2,1,0:T(8,128)S(1)} %collective-permute-done.side_0, f32[4,8,512]{2,1,0:T(8,128)S(1)} %collective-permute-done.1.side_1, f32[4,8,512]{2,1,0:T(8,128)S(1)} %collective-permute-done.2.end_1, ...), custom_call_target="tpu_custom_call" | custom-call | tf_op jit(solution)/shard_map/density_ends/pallas_call | solution.py:463
  19.7 2.1 %bin_rest.1.field = f32[8,8,512]{2,1,0:T(8,128)S(1)} custom-call(f32[32,8,128]{2,1,0:T(8,128)S(1)} %all-to-all-done.got, f32[8,16,512]{2,1,0:T(8,128)S(1)} %density_ends.1.density, f32[2,8,512]{2,1,0:T(8,128)S(1)} %get-tuple-element.29.to_partner, f32[2,8,512]{2,1,0:T(8,128)S(1)} %get-tuple-element.28._.to_outer), custom_call_target="tpu_custom_call" | custom-call | tf_op jit(solution)/shard_map/bin_rest/pallas_call | solution.py:463
  21.8 1.5 %collective-permute-done.4.side_1 = f32[2,8,512]{2,1,0:T(8,128)S(1)} collective-permute-done((f32[2,8,512]{2,1,0:T(8,128)S(1)}, f32[2,8,512]{2,1,0:T(8,128)S(1)}, u32[]{:S(2)}, u32[]{:S(2)}) %collective-permute-start.4) | collective-permute-done | bytes 32800 | tf_op jit(solution)/shard_map/ppermute | solution.py:415
  23.3 0.3 %back_reach.1 = (f32[2,8,512]{2,1,0:T(8,128)S(1)}, f32[2,8,512]{2,1,0:T(8,128)S(1)}, f32[3,3,4,8,512]{4,3,2,1,0:T(8,128)S(1)}) custom-call(f32[8,8,512]{2,1,0:T(8,128)S(1)} %bin_rest.1.field, f32[2,8,512]{2,1,0:T(8,128)S(1)} %collective-permute-done.4.side_1, f32[2,8,512]{2,1,0:T(8,128)S(1)} %collective-permute-done.5.side_0, ...), custom_call_target="tpu_custom_call" | custom-call | tf_op jit(solution)/shard_map/back_reach/pallas_call | solution.py:463
  23.6 0.1 collective-permute-start.6
  23.7 3.3 %collective-permute-start.7 = (f32[2,8,512]{2,1,0:T(8,128)S(1)}, f32[2,8,512]{2,1,0:T(8,128)S(1)}, u32[]{:S(2)}, u32[]{:S(2)}) collective-permute-start(f32[2,8,512]{2,1,0:T(8,128)S(1)} %get-tuple-element.32), channel_id=1, source_target_pairs={{8,16},{16,8},{9,17},{17,9},{10,18},{18,10},{11,19},{19,11},{12,20... | collective-permute-start | bytes 98312 | tf_op jit(solution)/shard_map/ppermute | solution.py:415
  27.0 0.8 %back_own.1.own = f32[8,8,512]{2,1,0:T(8,128)S(1)} custom-call(f32[8,8,512]{2,1,0:T(8,128)S(1)} %bin_rest.1.field, f32[2,8,512]{2,1,0:T(8,128)S(1)} %collective-permute-done.4.side_1, f32[2,8,512]{2,1,0:T(8,128)S(1)} %collective-permute-done.5.side_0, f32[8,16,512]{2,1,0:T(8,128)S(1)} %density_ends.1.density, f32[2,27,512]{2,1,0:T(8,128)S(1)} %rev.8.stencils, ...), custom_call_target="tpu_custom_call" | custom-call | tf_op jit(solution)/shard_map/back_own/pallas_call | solution.py:463
  27.8 2.6 %collective-permute-done.7.end_1 = f32[2,8,512]{2,1,0:T(8,128)S(1)} collective-permute-done((f32[2,8,512]{2,1,0:T(8,128)S(1)}, f32[2,8,512]{2,1,0:T(8,128)S(1)}, u32[]{:S(2)}, u32[]{:S(2)}) %collective-permute-start.7) | collective-permute-done | bytes 32800 | tf_op jit(solution)/shard_map/ppermute | solution.py:415
  30.4 0.7 %close.1 = f32[8,8,512]{2,1,0:T(8,128)} custom-call(f32[8,8,512]{2,1,0:T(8,128)S(1)} %back_own.1.own, f32[2,8,512]{2,1,0:T(8,128)S(1)} %collective-permute-done.6.end_0, f32[2,8,512]{2,1,0:T(8,128)S(1)} %collective-permute-done.7.end_1), custom_call_target="tpu_custom_call" | custom-call | tf_op jit(solution)/shard_map/close/pallas_call | solution.py:505
  (12 shorter events, 0.1 us)
Async XLA Ops:
  1.8 7.4 %collective-permute-start = (f32[4,8,512]{2,1,0:T(8,128)S(1)}, f32[4,8,512]{2,1,0:T(8,128)S(1)}, u32[]{:S(2)}, u32[]{:S(2)}) collective-permute-start(f32[4,8,512]{2,1,0:T(8,128)S(1)} %get-tuple-element.21), channel_id=1, source_target_pairs={{0,1},{2,3},{4,5},{6,7},{1,0},{3,2},{5,4},{7,6},{8,9},{10,11},{12,... | collective-permute-start | bytes 196616 | tf_op jit(solution)/shard_map/ppermute | solution.py:415
  1.9 7.3 %collective-permute-start.1 = (f32[4,8,512]{2,1,0:T(8,128)S(1)}, f32[4,8,512]{2,1,0:T(8,128)S(1)}, u32[]{:S(2)}, u32[]{:S(2)}) collective-permute-start(f32[4,8,512]{2,1,0:T(8,128)S(1)} %get-tuple-element.22), channel_id=1, source_target_pairs={{1,2},{3,4},{5,6},{7,0},{2,1},{4,3},{6,5},{0,7},{9,10},{11,12},{13... | collective-permute-start | bytes 196616 | tf_op jit(solution)/shard_map/ppermute | solution.py:415
  5.6 10.4 %all-to-all-start = ((f32[32,8,128]{2,1,0:T(8,128)}), f32[32,8,128]{2,1,0:T(8,128)S(1)}, u32[]{:S(2)}, u32[]{:S(2)}) async-start(f32[32,8,128]{2,1,0:T(8,128)} %get-tuple-element.19), calls=%async_computation | async-start | bytes 262144 | tf_op jit(solution)/shard_map/all_to_all | solution.py:454
  9.2 9.7 %collective-permute-start.2 = (f32[4,8,512]{2,1,0:T(8,128)S(1)}, f32[4,8,512]{2,1,0:T(8,128)S(1)}, u32[]{:S(2)}, u32[]{:S(2)}) collective-permute-start(f32[4,8,512]{2,1,0:T(8,128)S(1)} %get-tuple-element.23), channel_id=1, source_target_pairs={{8,16},{16,8},{9,17},{17,9},{10,18},{18,10},{11,19},{19,11},{12,20... | collective-permute-start | bytes 196616 | tf_op jit(solution)/shard_map/ppermute | solution.py:415
  12.6 6.3 %collective-permute-start.3 = (f32[4,8,512]{2,1,0:T(8,128)S(1)}, f32[4,8,512]{2,1,0:T(8,128)S(1)}, u32[]{:S(2)}, u32[]{:S(2)}) collective-permute-start(f32[4,8,512]{2,1,0:T(8,128)S(1)} %get-tuple-element.24), channel_id=1, source_target_pairs={{0,8},{16,24},{8,0},{24,16},{1,9},{17,25},{9,1},{25,17},{2,10},{18... | collective-permute-start | bytes 196616 | tf_op jit(solution)/shard_map/ppermute | solution.py:415
  18.1 5.2 %collective-permute-start.4 = (f32[2,8,512]{2,1,0:T(8,128)S(1)}, f32[2,8,512]{2,1,0:T(8,128)S(1)}, u32[]{:S(2)}, u32[]{:S(2)}) collective-permute-start(f32[2,8,512]{2,1,0:T(8,128)S(1)} %get-tuple-element.28._.to_outer), channel_id=1, source_target_pairs={{1,2},{3,4},{5,6},{7,0},{2,1},{4,3},{6,5},{0,7},{9,10},{11,12},{13... | collective-permute-start | bytes 98312 | tf_op jit(solution)/shard_map/ppermute | solution.py:415
  18.8 4.5 %collective-permute-start.5 = (f32[2,8,512]{2,1,0:T(8,128)S(1)}, f32[2,8,512]{2,1,0:T(8,128)S(1)}, u32[]{:S(2)}, u32[]{:S(2)}) collective-permute-start(f32[2,8,512]{2,1,0:T(8,128)S(1)} %get-tuple-element.29.to_partner), channel_id=1, source_target_pairs={{0,1},{2,3},{4,5},{6,7},{1,0},{3,2},{5,4},{7,6},{8,9},{10,11},{12,... | collective-permute-start | bytes 98312 | tf_op jit(solution)/shard_map/ppermute | solution.py:415
  23.6 4.2 %collective-permute-start.6 = (f32[2,8,512]{2,1,0:T(8,128)S(1)}, f32[2,8,512]{2,1,0:T(8,128)S(1)}, u32[]{:S(2)}, u32[]{:S(2)}) collective-permute-start(f32[2,8,512]{2,1,0:T(8,128)S(1)} %get-tuple-element.31), channel_id=1, source_target_pairs={{0,8},{16,24},{8,0},{24,16},{1,9},{17,25},{9,1},{25,17},{2,10},{18... | collective-permute-start | bytes 98312 | tf_op jit(solution)/shard_map/ppermute | solution.py:415
  23.7 6.7 %collective-permute-start.7 = (f32[2,8,512]{2,1,0:T(8,128)S(1)}, f32[2,8,512]{2,1,0:T(8,128)S(1)}, u32[]{:S(2)}, u32[]{:S(2)}) collective-permute-start(f32[2,8,512]{2,1,0:T(8,128)S(1)} %get-tuple-element.32), channel_id=1, source_target_pairs={{8,16},{16,8},{9,17},{17,9},{10,18},{18,10},{11,19},{19,11},{12,20... | collective-permute-start | bytes 98312 | tf_op jit(solution)/shard_map/ppermute | solution.py:415

commit v25 on v24

--- a/solution.py
+++ b/solution.py
@@ -267,7 +267,8 @@
     counts, offsets, residual, pixel, bins, table, arrived,
 ):
     pairs = (
-        (counts_in, counts), (offsets_in, offsets), (residual_in, residual), (pixel_in, pixel), (bins_in, bins),
+        (counts_in, counts), (offsets_in, offsets),
+        *((source.at[:target.shape[0]], target) for source, target in ((residual_in, residual), (pixel_in, pixel), (bins_in, bins))),
         (latent_in, latent), (taps_in, taps),
     )
     copies = [pltpu.make_async_copy(source, target, arrived.at[i]) for i, (source, target) in enumerate(pairs)]
@@ -425,6 +426,7 @@
     height, width, radial = latent.shape
     shards = send_counts.shape[1]
     slots = residual.shape[0]
+    filled = min(slots // LANES, shards // 2 * (CAP + LEAST) // LANES + SUBLANES)
     f32 = jnp.float32
     i32 = jnp.int32
     tile = jax.ShapeDtypeStruct((height, width, radial), f32)
@@ -442,8 +444,8 @@
         in_specs=[HBM] * 7,
         out_specs=(VMEM,) * 5,
         scratch_shapes=[pltpu.SMEM((1, shards), i32)] * 2
-        + [pltpu.VMEM((slots // LANES, LANES), kind) for kind in (f32, i32, i32)]
-        + [pltpu.VMEM((2 * slots // LANES, LANES), f32)]
+        + [pltpu.VMEM((filled, LANES), kind) for kind in (f32, i32, i32)]
+        + [pltpu.VMEM((2 * filled, LANES), f32)]
         + [pltpu.SemaphoreType.DMA((7,))],
         compiler_params=LIMIT,
         name="opening",

time: 31.3 us -> 31.2 us (level)
  no operation moved by 1% of the time
where the time goes in v25:
time: 31.2 us; the launch traced here: 31 us
  starting transfers between devices  14.4 us (46%)
  Pallas kernels  9.43 us (30%)
  waiting for transfers between devices  6.45 us (21%)
  local copies, waits for them, and re-layouts  0.5 us (2%)
    ppermute x8, starting transfers between devices, swap(): lax.ppermute(values, axis, both_ways(pairs))  11.3 us
    pallas_call x7, Pallas kernels, call(): pl.pallas_call(kernel, out_shape=outs, in_specs=[VMEM] * len(operands), o...  7 us
    ppermute x8, waiting for transfers between devices, swap(): lax.ppermute(values, axis, both_ways(pairs))  4.05 us
    all_to_all x1, starting transfers between devices, on_device(): lax.all_to_all(packed, ('lat', 'lon'), split_axis=0, concat_axis=0, tiled...  3.09 us
    all_to_all x1, waiting for transfers between devices, on_device(): lax.all_to_all(packed, ('lat', 'lon'), split_axis=0, concat_axis=0, tiled...  2.4 us
    pallas_call x1, Pallas kernels, on_device(): pl.pallas_call(open_kernel, out_shape=(jax.ShapeDtypeStruct((shards, 2 *...  1.75 us
    pallas_call x1, Pallas kernels, on_device(): pl.pallas_call(close_kernel, out_shape=tile, in_specs=[VMEM] * 3, out_spe...  0.67 us
  transfers between devices with their start and end apart: 9, of which 3 were waited for; matrix products, arithmetic and copies ran while one was open for 2% of the time, Pallas kernels for 21%

profile of v25, /device:TPU:2, one launch (start us, length us, event | category | flops | bytes accessed | tf_op | source)
XLA Modules:
  0.0 31.0 jit_solution(16457024649957320033)
XLA Ops:
  0.0 1.8 %opening.1 = (f32[32,8,128]{2,1,0:T(8,128)}, f32[8,8,512]{2,1,0:T(8,128)S(1)}, f32[4,8,512]{2,1,0:T(8,128)S(1)}, f32[4,8,512]{2,1,0:T(8,128)S(1)}, f32[27,2,512]{2,1,0:T(2,128)S(1)}) custom-call(s32[1,32]{1,0:T(1,128)} %counts_in.1, s32[1,32]{1,0:T(1,128)} %offsets_in.1, f32[128,128]{1,0:T(8,128)} %bitcast.26, s32[128,128]{1,0:T(8,128)} %bitcast.27, ...), custom_call_target="tpu_custom_call" | custom-call | tf_op jit(solution)/shard_map/opening/pallas_call | solution.py:441
  1.8 0.1 collective-permute-start
  1.8 3.7 %collective-permute-start.1 = (f32[4,8,512]{2,1,0:T(8,128)S(1)}, f32[4,8,512]{2,1,0:T(8,128)S(1)}, u32[]{:S(2)}, u32[]{:S(2)}) collective-permute-start(f32[4,8,512]{2,1,0:T(8,128)S(1)} %get-tuple-element.22), channel_id=1, source_target_pairs={{1,2},{3,4},{5,6},{7,0},{2,1},{4,3},{6,5},{0,7},{9,10},{11,12},{13... | collective-permute-start | bytes 196616 | tf_op jit(solution)/shard_map/ppermute | solution.py:416
  5.5 3.1 %all-to-all-start = ((f32[32,8,128]{2,1,0:T(8,128)}), f32[32,8,128]{2,1,0:T(8,128)S(1)}, u32[]{:S(2)}, u32[]{:S(2)}) async-start(f32[32,8,128]{2,1,0:T(8,128)} %get-tuple-element.19), calls=%async_computation | async-start | bytes 262144 | tf_op jit(solution)/shard_map/all_to_all | solution.py:456
  8.7 0.2 rev.7
  8.8 0.1 copy.12
  8.9 0.1 slice_bitcast_fusion.1
  9.1 0.1 pad_bitcast_fusion
  9.2 3.4 %collective-permute-start.2 = (f32[4,8,512]{2,1,0:T(8,128)S(1)}, f32[4,8,512]{2,1,0:T(8,128)S(1)}, u32[]{:S(2)}, u32[]{:S(2)}) collective-permute-start(f32[4,8,512]{2,1,0:T(8,128)S(1)} %get-tuple-element.23), channel_id=1, source_target_pairs={{8,16},{16,8},{9,17},{17,9},{10,18},{18,10},{11,19},{19,11},{12,20... | collective-permute-start | bytes 196616 | tf_op jit(solution)/shard_map/ppermute | solution.py:416
  12.6 0.1 collective-permute-start.3
  12.7 0.9 %density_inside.1 = (f32[4,16,512]{2,1,0:T(8,128)S(1)}, f32[3,3,6,16,512]{4,3,2,1,0:T(8,128)S(1)}) custom-call(f32[8,8,512]{2,1,0:T(8,128)S(1)} %get-tuple-element.20.field.latent, f32[4,8,512]{2,1,0:T(8,128)S(1)} %collective-permute-done.side_0, f32[4,8,512]{2,1,0:T(8,128)S(1)} %collective-permute-done.1.side_1, f32[2,27,512]{2,1,0:T(8,128)S(1)} %bitcast.20), custom_call_target="tpu_custom_call" | custom-call | tf_op jit(solution)/shard_map/density_inside/pallas_call | solution.py:465
  13.6 2.4 %all-to-all-done.got = f32[32,8,128]{2,1,0:T(8,128)S(1)} async-done(((f32[32,8,128]{2,1,0:T(8,128)}), f32[32,8,128]{2,1,0:T(8,128)S(1)}, u32[]{:S(2)}, u32[]{:S(2)}) %all-to-all-start) | async-done | bytes 131104 | tf_op jit(solution)/shard_map/all_to_all | solution.py:456
  16.0 2.1 %bin_sides.1 = (f32[2,8,512]{2,1,0:T(8,128)S(1)}, f32[2,8,512]{2,1,0:T(8,128)S(1)}) custom-call(f32[32,8,128]{2,1,0:T(8,128)S(1)} %all-to-all-done.got, f32[4,16,512]{2,1,0:T(8,128)S(1)} %get-tuple-element.27._.inner), custom_call_target="tpu_custom_call" | custom-call | tf_op jit(solution)/shard_map/bin_sides/pallas_call | solution.py:465
  18.1 0.7 %collective-permute-start.4 = (f32[2,8,512]{2,1,0:T(8,128)S(1)}, f32[2,8,512]{2,1,0:T(8,128)S(1)}, u32[]{:S(2)}, u32[]{:S(2)}) collective-permute-start(f32[2,8,512]{2,1,0:T(8,128)S(1)} %get-tuple-element.28._.to_outer), channel_id=1, source_target_pairs={{1,2},{3,4},{5,6},{7,0},{2,1},{4,3},{6,5},{0,7},{9,10},{11,12},{13... | collective-permute-start | bytes 98312 | tf_op jit(solution)/shard_map/ppermute | solution.py:416
  18.8 0.1 pad_maximum_fusion
  18.9 0.7 %density_ends.1.density = f32[8,16,512]{2,1,0:T(8,128)S(1)} custom-call(f32[8,8,512]{2,1,0:T(8,128)S(1)} %get-tuple-element.20.field.latent, f32[4,8,512]{2,1,0:T(8,128)S(1)} %collective-permute-done.side_0, f32[4,8,512]{2,1,0:T(8,128)S(1)} %collective-permute-done.1.side_1, f32[4,8,512]{2,1,0:T(8,128)S(1)} %collective-permute-done.2.end_1, ...), custom_call_target="tpu_custom_call" | custom-call | tf_op jit(solution)/shard_map/density_ends/pallas_call | solution.py:465
  19.6 2.1 %bin_rest.1.field = f32[8,8,512]{2,1,0:T(8,128)S(1)} custom-call(f32[32,8,128]{2,1,0:T(8,128)S(1)} %all-to-all-done.got, f32[8,16,512]{2,1,0:T(8,128)S(1)} %density_ends.1.density, f32[2,8,512]{2,1,0:T(8,128)S(1)} %get-tuple-element.29.to_partner, f32[2,8,512]{2,1,0:T(8,128)S(1)} %get-tuple-element.28._.to_outer), custom_call_target="tpu_custom_call" | custom-call | tf_op jit(solution)/shard_map/bin_rest/pallas_call | solution.py:465
  21.8 1.5 %collective-permute-done.4.side_1 = f32[2,8,512]{2,1,0:T(8,128)S(1)} collective-permute-done((f32[2,8,512]{2,1,0:T(8,128)S(1)}, f32[2,8,512]{2,1,0:T(8,128)S(1)}, u32[]{:S(2)}, u32[]{:S(2)}) %collective-permute-start.4) | collective-permute-done | bytes 32800 | tf_op jit(solution)/shard_map/ppermute | solution.py:416
  23.2 0.3 %back_reach.1 = (f32[2,8,512]{2,1,0:T(8,128)S(1)}, f32[2,8,512]{2,1,0:T(8,128)S(1)}, f32[3,3,4,8,512]{4,3,2,1,0:T(8,128)S(1)}) custom-call(f32[8,8,512]{2,1,0:T(8,128)S(1)} %bin_rest.1.field, f32[2,8,512]{2,1,0:T(8,128)S(1)} %collective-permute-done.4.side_1, f32[2,8,512]{2,1,0:T(8,128)S(1)} %collective-permute-done.5.side_0, ...), custom_call_target="tpu_custom_call" | custom-call | tf_op jit(solution)/shard_map/back_reach/pallas_call | solution.py:465
  23.6 0.1 collective-permute-start.6
  23.7 3.3 %collective-permute-start.7 = (f32[2,8,512]{2,1,0:T(8,128)S(1)}, f32[2,8,512]{2,1,0:T(8,128)S(1)}, u32[]{:S(2)}, u32[]{:S(2)}) collective-permute-start(f32[2,8,512]{2,1,0:T(8,128)S(1)} %get-tuple-element.32), channel_id=1, source_target_pairs={{8,16},{16,8},{9,17},{17,9},{10,18},{18,10},{11,19},{19,11},{12,20... | collective-permute-start | bytes 98312 | tf_op jit(solution)/shard_map/ppermute | solution.py:416
  27.0 0.8 %back_own.1.own = f32[8,8,512]{2,1,0:T(8,128)S(1)} custom-call(f32[8,8,512]{2,1,0:T(8,128)S(1)} %bin_rest.1.field, f32[2,8,512]{2,1,0:T(8,128)S(1)} %collective-permute-done.4.side_1, f32[2,8,512]{2,1,0:T(8,128)S(1)} %collective-permute-done.5.side_0, f32[8,16,512]{2,1,0:T(8,128)S(1)} %density_ends.1.density, f32[2,27,512]{2,1,0:T(8,128)S(1)} %rev.8.stencils, ...), custom_call_target="tpu_custom_call" | custom-call | tf_op jit(solution)/shard_map/back_own/pallas_call | solution.py:465
  27.8 2.6 %collective-permute-done.7.end_1 = f32[2,8,512]{2,1,0:T(8,128)S(1)} collective-permute-done((f32[2,8,512]{2,1,0:T(8,128)S(1)}, f32[2,8,512]{2,1,0:T(8,128)S(1)}, u32[]{:S(2)}, u32[]{:S(2)}) %collective-permute-start.7) | collective-permute-done | bytes 32800 | tf_op jit(solution)/shard_map/ppermute | solution.py:416
  30.4 0.7 %close.1 = f32[8,8,512]{2,1,0:T(8,128)} custom-call(f32[8,8,512]{2,1,0:T(8,128)S(1)} %back_own.1.own, f32[2,8,512]{2,1,0:T(8,128)S(1)} %collective-permute-done.6.end_0, f32[2,8,512]{2,1,0:T(8,128)S(1)} %collective-permute-done.7.end_1), custom_call_target="tpu_custom_call" | custom-call | tf_op jit(solution)/shard_map/close/pallas_call | solution.py:507
  (12 shorter events, 0.1 us)
Async XLA Ops:
  1.8 7.4 %collective-permute-start = (f32[4,8,512]{2,1,0:T(8,128)S(1)}, f32[4,8,512]{2,1,0:T(8,128)S(1)}, u32[]{:S(2)}, u32[]{:S(2)}) collective-permute-start(f32[4,8,512]{2,1,0:T(8,128)S(1)} %get-tuple-element.21), channel_id=1, source_target_pairs={{0,1},{2,3},{4,5},{6,7},{1,0},{3,2},{5,4},{7,6},{8,9},{10,11},{12,... | collective-permute-start | bytes 196616 | tf_op jit(solution)/shard_map/ppermute | solution.py:416
  1.8 7.3 %collective-permute-start.1 = (f32[4,8,512]{2,1,0:T(8,128)S(1)}, f32[4,8,512]{2,1,0:T(8,128)S(1)}, u32[]{:S(2)}, u32[]{:S(2)}) collective-permute-start(f32[4,8,512]{2,1,0:T(8,128)S(1)} %get-tuple-element.22), channel_id=1, source_target_pairs={{1,2},{3,4},{5,6},{7,0},{2,1},{4,3},{6,5},{0,7},{9,10},{11,12},{13... | collective-permute-start | bytes 196616 | tf_op jit(solution)/shard_map/ppermute | solution.py:416
  5.5 10.4 %all-to-all-start = ((f32[32,8,128]{2,1,0:T(8,128)}), f32[32,8,128]{2,1,0:T(8,128)S(1)}, u32[]{:S(2)}, u32[]{:S(2)}) async-start(f32[32,8,128]{2,1,0:T(8,128)} %get-tuple-element.19), calls=%async_computation | async-start | bytes 262144 | tf_op jit(solution)/shard_map/all_to_all | solution.py:456
  9.2 9.7 %collective-permute-start.2 = (f32[4,8,512]{2,1,0:T(8,128)S(1)}, f32[4,8,512]{2,1,0:T(8,128)S(1)}, u32[]{:S(2)}, u32[]{:S(2)}) collective-permute-start(f32[4,8,512]{2,1,0:T(8,128)S(1)} %get-tuple-element.23), channel_id=1, source_target_pairs={{8,16},{16,8},{9,17},{17,9},{10,18},{18,10},{11,19},{19,11},{12,20... | collective-permute-start | bytes 196616 | tf_op jit(solution)/shard_map/ppermute | solution.py:416
  12.6 6.3 %collective-permute-start.3 = (f32[4,8,512]{2,1,0:T(8,128)S(1)}, f32[4,8,512]{2,1,0:T(8,128)S(1)}, u32[]{:S(2)}, u32[]{:S(2)}) collective-permute-start(f32[4,8,512]{2,1,0:T(8,128)S(1)} %get-tuple-element.24), channel_id=1, source_target_pairs={{0,8},{16,24},{8,0},{24,16},{1,9},{17,25},{9,1},{25,17},{2,10},{18... | collective-permute-start | bytes 196616 | tf_op jit(solution)/shard_map/ppermute | solution.py:416
  18.1 5.2 %collective-permute-start.4 = (f32[2,8,512]{2,1,0:T(8,128)S(1)}, f32[2,8,512]{2,1,0:T(8,128)S(1)}, u32[]{:S(2)}, u32[]{:S(2)}) collective-permute-start(f32[2,8,512]{2,1,0:T(8,128)S(1)} %get-tuple-element.28._.to_outer), channel_id=1, source_target_pairs={{1,2},{3,4},{5,6},{7,0},{2,1},{4,3},{6,5},{0,7},{9,10},{11,12},{13... | collective-permute-start | bytes 98312 | tf_op jit(solution)/shard_map/ppermute | solution.py:416
  18.8 4.4 %collective-permute-start.5 = (f32[2,8,512]{2,1,0:T(8,128)S(1)}, f32[2,8,512]{2,1,0:T(8,128)S(1)}, u32[]{:S(2)}, u32[]{:S(2)}) collective-permute-start(f32[2,8,512]{2,1,0:T(8,128)S(1)} %get-tuple-element.29.to_partner), channel_id=1, source_target_pairs={{0,1},{2,3},{4,5},{6,7},{1,0},{3,2},{5,4},{7,6},{8,9},{10,11},{12,... | collective-permute-start | bytes 98312 | tf_op jit(solution)/shard_map/ppermute | solution.py:416
  23.6 4.2 %collective-permute-start.6 = (f32[2,8,512]{2,1,0:T(8,128)S(1)}, f32[2,8,512]{2,1,0:T(8,128)S(1)}, u32[]{:S(2)}, u32[]{:S(2)}) collective-permute-start(f32[2,8,512]{2,1,0:T(8,128)S(1)} %get-tuple-element.31), channel_id=1, source_target_pairs={{0,8},{16,24},{8,0},{24,16},{1,9},{17,25},{9,1},{25,17},{2,10},{18... | collective-permute-start | bytes 98312 | tf_op jit(solution)/shard_map/ppermute | solution.py:416
  23.7 6.7 %collective-permute-start.7 = (f32[2,8,512]{2,1,0:T(8,128)S(1)}, f32[2,8,512]{2,1,0:T(8,128)S(1)}, u32[]{:S(2)}, u32[]{:S(2)}) collective-permute-start(f32[2,8,512]{2,1,0:T(8,128)S(1)} %get-tuple-element.32), channel_id=1, source_target_pairs={{8,16},{16,8},{9,17},{17,9},{10,18},{18,10},{11,19},{19,11},{12,20... | collective-permute-start | bytes 98312 | tf_op jit(solution)/shard_map/ppermute | solution.py:416
